TPU v7x, 32 devices: a whole 2x2x4 slice. The times are simulated.
32 devices in a mesh: groups: 2 (over x), ctx: 16 (over z, y, core).
Axes of the slice: x: 2, y: 2, z: 4, core: 2. Of those that a mesh axis runs over, the one named last changes fastest.
Arguments:
- tokens: bfloat16 [8192, 1024], P(('groups', 'ctx')), parts along dimension 0, may hold values from -4 to 4
- routes: int32 [8192, 2], P(('groups', 'ctx')), parts along dimension 0, may hold values from 0 to 31, all different within a row; in each aligned block of 256 rows (0 to 255, 256 to 511, ...) at most 20 rows name the same one
- gates: float32 [8192, 2], P(('groups', 'ctx')), parts along dimension 0, may hold values from 0.2 to 1
- qkv_weight: bfloat16 [1024, 3072], P('ctx'), may hold values from -2 to 2
- out_weight: bfloat16 [1024, 1024], P('ctx'), may hold values from -0.75 to 0.75
- w_in: bfloat16 [1024, 131072], P(None, 'ctx'), may hold values from -0.1875 to 0.1875
- w_out: bfloat16 [131072, 1024], P('ctx'), may hold values from -0.09375 to 0.09375
Outputs:
- layer_out: bfloat16 [8192, 1024], P(('groups', 'ctx')), parts along dimension 0
There are 2 independent parts, one for each index of `groups`. A program takes and returns all parts, laid end to end along the dimension named above; an argument that names none is the same for every part. Nothing has to cross between parts.
Inputs may be any that keep to these rules, and one draw needn't show every extreme that they name: The 2 ids of a row differ; in each aligned block of 256 rows (the rows of one device) no expert is named by more than 20 routes, a bound that some block reaches.
All inputs are finite; a program needn't handle non-finite values.
Results may differ from a plain program's by a relative error of at most 0.004.
The roundings to bfloat16 on the way count: a program that leaves them out, or rounds other values in their place, can miss the bound.
Values may be sent and summed in bfloat16 or wider, within the bound.
No kernel may reach another device: no remote copies, remote signals or barrier semaphores. Data moves between devices by JAX's collectives and lax.ppermute only.
A program may use at most 128 MiB of HBM per device.

v0:
```python
import jax
import jax.numpy as jnp
from jax import lax
from jax.sharding import PartitionSpec as P

HEADS = 16
HD = 64
EXPERTS = 32
SPAN = 4
CAP = 20


eps = 1e-06


def from_partner(block, axis, stride):
    count = lax.axis_size(axis)
    route = []
    for low in range(count):
        high = low | 1 << stride
        if high != low and high < count:
            route += [(low, high), (high, low)]
    return lax.ppermute(block, axis, route)


def normalize(values):
    values = values.astype(jnp.float32)
    center = values - jnp.mean(values, axis=-1, keepdims=True)
    spread = jnp.mean(center * center, axis=-1, keepdims=True)
    return (center * lax.rsqrt(spread + eps)).astype(jnp.bfloat16)


def attend(queries, keys_all, values_all):
    rows, width = queries.shape
    length = keys_all.shape[0]
    q_heads = queries.reshape(rows, HEADS, HD)
    k_heads = keys_all.reshape(length, HEADS, HD)
    v_heads = values_all.reshape(length, HEADS, HD)
    scores = jnp.einsum(
        "thd,shd->hts", q_heads, k_heads, preferred_element_type=jnp.float32
    ) * HD ** (-0.5)
    peak = jnp.max(scores, axis=-1, keepdims=True)
    weights = jnp.exp(scores - peak)
    probs = (weights / jnp.sum(weights, axis=-1, keepdims=True)).astype(jnp.bfloat16)
    mixed = jnp.einsum("hts,shd->thd", probs, v_heads, preferred_element_type=jnp.float32)
    return mixed.reshape(rows, width).astype(jnp.bfloat16)


def add_parts(returned, parts_ff):
    grouped = returned.reshape(EXPERTS, parts_ff, returned.shape[2], returned.shape[3])
    if parts_ff > 1:
        return jnp.sum(grouped.astype(jnp.float32), axis=1).astype(jnp.bfloat16)
    return grouped[:, 0]


def per_device(tokens, routes, gates, qkv_weight, out_weight, w_in, w_out):
    rows, width = tokens.shape
    devices = lax.axis_size("ctx")
    parts_ff = max(1, devices // EXPERTS)
    local_experts = max(1, EXPERTS // devices)
    capacity = CAP
    top_routes = routes.shape[1]
    normed = normalize(tokens)
    columns = normed
    projected = jnp.dot(
        columns,
        lax.all_gather(qkv_weight, "ctx", axis=0, tiled=True),
        preferred_element_type=jnp.float32,
    )
    projected = projected.astype(jnp.bfloat16)
    queries = projected[:, :width]
    key_value = jnp.stack([projected[:, width : 2 * width], projected[:, 2 * width :]])
    for bit_level in range(SPAN.bit_length() - 1):
        partner = from_partner(key_value, "ctx", bit_level)
        key_value = jnp.concatenate([key_value, partner], axis=1)
    context = attend(queries, key_value[0], key_value[1])
    columns = context
    attended = jnp.dot(
        columns,
        lax.all_gather(out_weight, "ctx", axis=0, tiled=True),
        preferred_element_type=jnp.float32,
    )
    resid = tokens.astype(jnp.float32) + attended
    moe_in = normalize(resid)
    flat_ids = routes.reshape(-1)
    onehot = (flat_ids[:, None] == jnp.arange(EXPERTS, dtype=jnp.int32)[None, :]).astype(jnp.int32)
    before = jnp.cumsum(onehot, axis=0) - onehot
    position = jnp.sum(before * onehot, axis=1)
    slot = flat_ids * capacity + position
    source = jnp.repeat(moe_in, top_routes, axis=0)
    table = jnp.zeros((EXPERTS * capacity, width), jnp.bfloat16).at[slot].set(source)
    table = table.reshape(EXPERTS, capacity, width)
    hidden_units = w_in.shape[1] // local_experts
    repeated = table
    if parts_ff > 1:
        repeated = jnp.repeat(table, parts_ff, axis=0)
    outgoing = repeated.reshape(devices, local_experts, capacity, width)
    arrived = lax.all_to_all(outgoing, "ctx", split_axis=0, concat_axis=0, tiled=True)
    results = []
    for local in range(arrived.shape[1]):
        block = arrived[:, local]
        flat = block.reshape(-1, width)
        first = w_in[:, local * hidden_units : (local + 1) * hidden_units]
        second = w_out[local * hidden_units : (local + 1) * hidden_units]
        hidden = jax.nn.gelu(jnp.dot(flat, first, preferred_element_type=jnp.float32)).astype(
            jnp.bfloat16
        )
        term = jnp.dot(hidden, second, preferred_element_type=jnp.float32).astype(jnp.bfloat16)
        results.append(term.reshape(block.shape))
    produced = jnp.stack(results, axis=1)
    returned = lax.all_to_all(produced, "ctx", split_axis=0, concat_axis=0, tiled=True)
    merged = add_parts(returned, parts_ff)
    picked = merged.reshape(EXPERTS * capacity, width)[slot].reshape(rows, top_routes, width)
    mixture = jnp.sum(picked.astype(jnp.float32) * gates[:, :, None], axis=1)
    return (resid + mixture).astype(jnp.bfloat16)


def solution(mesh):
    in_specs = (
        P(("groups", "ctx"), None),
        P(("groups", "ctx"), None),
        P(("groups", "ctx"), None),
        P("ctx", None),
        P("ctx", None),
        P(None, "ctx"),
        P("ctx", None),
    )
    out_specs = P(("groups", "ctx"), None)
    return jax.shard_map(
        per_device, mesh=mesh, in_specs=in_specs, out_specs=out_specs, check_vma=False
    )
```

profile of v0, /device:TPU:1, one launch (start us, length us, event | category | flops | bytes accessed | tf_op | source)
XLA Modules:
  0.0 301.4 jit_solution(12954528116929934952)
XLA Ops:
  7.3 1.2 convert_reduce_fusion
  8.5 1.3 fusion.49
  9.8 64.2 %all-gather.3.cloned.1.call-done = bf16[1024,3072]{1,0:T(8,128)(2,1)} async-done(((bf16[64,3072]{1,0:T(8,128)(2,1)}), bf16[1024,3072]{1,0:T(8,128)(2,1)}) %all-gather.3.cloned.1.call-update) | async-done | bytes 6291472 | tf_op jit(solution)/shard_map/all_gather | solution.py:67
  74.0 4.9 %convolution_convert_fusion = bf16[256,3072]{1,0:T(8,128)(2,1)S(1)} fusion(bf16[1024,3072]{1,0:T(8,128)(2,1)} %all-gather.3.cloned.1.call-done, bf16[256,1024]{1,0:T(8,128)(2,1)} %param.7, f32[256]{0:T(256)S(1)} %add_rsqrt_fusion.1, f32[256]{0:T(256)S(1)} %broadcast_multiply_fusion.2), kind=kOutput, calls=%fused_computation.36 | convolution fusion | flops 1612447744 | bytes 8390656 | tf_op jit(solution)/shard_map/dot_general | solution.py:65
  79.5 2.4 collective-permute-done
  81.9 1.5 pad_maximum_fusion.1
  84.0 1.3 reduce-window.6
  86.4 51.3 %collective-permute-done.1 = bf16[2,512,1024]{2,1,0:T(8,128)(2,1)} collective-permute-done((bf16[2,512,1024]{2,1,0:T(8,128)(2,1)}, bf16[2,512,1024]{2,1,0:T(8,128)(2,1)}, u32[]{:S(2)}, u32[]{:S(2)}) %collective-permute-start.1) | collective-permute-done | bytes 2097184 | tf_op jit(solution)/shard_map/ppermute | solution.py:23
  137.7 1.8 pad_maximum_fusion
  139.5 1.8 fusion.69
  141.3 4.0 %copy.22 = bf16[1,1024,1024]{1,2,0:T(8,128)(2,1)} copy(bf16[1,1024,1024]{2,1,0:T(8,128)(2,1)} %get-tuple-element.8) | data formatting | bytes 4194304 | tf_op jit(solution)/shard_map/slice | solution.py:76
  145.3 2.6 copy.24
  147.8 9.7 %fusion.71 = (f32[16,256]{1,0:T(8,128)S(1)}, f32[16,256,1024]{2,1,0:T(8,128)}) fusion(bf16[256,16,64]{0,2,1:T(8,128)(2,1)S(1)} %bitcast.44, bf16[1024,16,64]{0,2,1:T(8,128)(2,1)} %bitcast.42), kind=kOutput, calls=%fused_computation.90 | convolution fusion | flops 549454848 | bytes 19415040 | tf_op jit(solution)/shard_map/sub | solution.py:43
  157.6 9.2 %fusion.42 = bf16[16,64,256]{2,1,0:T(8,128)(2,1)S(1)} fusion(bf16[1024,16,64]{0,2,1:T(8,128)(2,1)} %bitcast.41, f32[16,256,1024]{2,1,0:T(8,128)} %get-tuple-element.13, f32[16,256]{1,0:T(8,128)S(1)} %get-tuple-element.12), kind=kOutput, calls=%fused_computation.48 | convolution fusion | flops 545521664 | bytes 19415040 | tf_op jit(solution)/shard_map/hts,shd->thd/dot_general | solution.py:45
  166.8 2.4 fusion.72
  170.7 3.7 %scatter_custom_fusion = bf16[640,1024]{1,0:T(8,128)(2,1)} fusion(s32[512]{0:T(512)S(1)} %bitcast.45, bf16[512,1024]{1,0:T(8,128)(2,1)S(1)} %reshape.100, bf16[]{:T(256)} %constant.10.clone.1), kind=kCustom, calls=%fused_computation.57 | custom fusion | bytes 1310722 | tf_op jit(solution)/shard_map/scatter | solution.py:91
  174.4 2.4 reshape_reshape.3
  176.8 1.4 copy.29
  178.1 36.0 %all_to_all.10 = bf16[16,2,20,1024]{3,1,2,0:T(2,128)(2,1)S(1)} all-to-all(bf16[16,2,20,1024]{3,1,2,0:T(2,128)(2,1)S(1)} %copy.29), channel_id=1, replica_groups=mesh['groups'=2,'ctx'=16] {'ctx'}, dimensions={0} | all-to-all | bytes 2621440 | tf_op jit(solution)/shard_map/all_to_all | solution.py:98
  214.1 5.7 %slice_reduce_fusion.1 = (bf16[16,20,1024]{2,1,0:T(8,128)(2,1)S(1)}, bf16[16,20,1024]{2,1,0:T(8,128)(2,1)S(1)}) fusion(bf16[16,2,20,1024]{3,1,2,0:T(2,128)(2,1)S(1)} %all_to_all.10), kind=kLoop, calls=%fused_computation.47 | loop fusion | bytes 2621440 | tf_op jit(solution)/shard_map/slice | solution.py:101
  220.0 12.4 %fusion.39 = bf16[320,1024]{1,0:T(8,128)(2,1)} fusion(bf16[8192,1024]{1,0:T(8,128)(2,1)} %param.13, bf16[320,1024]{1,0:T(8,128)(2,1)S(1)} %reshape_squeeze.15, bf16[1024,8192]{1,0:T(8,128)(2,1)} %param.12), kind=kOutput, calls=%fused_computation.45 | convolution fusion | flops 5380833280 | bytes 18087936 | tf_op jit(solution)/shard_map/dot_general | solution.py:108
  232.4 1.6 stack_reshape.7
  234.2 12.4 %fusion.36 = bf16[320,1024]{1,0:T(8,128)(2,1)} fusion(bf16[8192,1024]{1,0:T(8,128)(2,1)} %param.13, bf16[320,1024]{1,0:T(8,128)(2,1)S(1)} %reshape_squeeze.14, bf16[1024,8192]{1,0:T(8,128)(2,1)} %param.12), kind=kOutput, calls=%fused_computation.44 | convolution fusion | flops 5380833280 | bytes 18087936 | tf_op jit(solution)/shard_map/dot_general | solution.py:108
  246.6 1.2 stack_reshape.6
  248.0 2.4 copy.30
  250.4 3.6 %all-to-all-start.1 = ((bf16[16,2,20,1024]{3,1,2,0:T(2,128)(2,1)}), bf16[16,2,20,1024]{3,1,2,0:T(2,128)(2,1)S(1)}, u32[]{:S(2)}, u32[]{:S(2)}) async-start(bf16[16,2,20,1024]{3,1,2,0:T(2,128)(2,1)} %copy.30), calls=%async_computation.1 | async-start | bytes 2621440 | tf_op jit(solution)/shard_map/all_to_all | solution.py:111
  254.2 27.6 %all-to-all-done.1 = bf16[16,2,20,1024]{3,1,2,0:T(2,128)(2,1)S(1)} async-done(((bf16[16,2,20,1024]{3,1,2,0:T(2,128)(2,1)}), bf16[16,2,20,1024]{3,1,2,0:T(2,128)(2,1)S(1)}, u32[]{:S(2)}, u32[]{:S(2)}) %all-to-all-start.1) | async-done | bytes 1310752 | tf_op jit(solution)/shard_map/all_to_all | solution.py:111
  281.8 1.5 copy.31
  283.3 2.3 reshape_squeeze_reshape.3
  285.6 2.8 gather_fusion
  288.4 2.4 reshape.87
  290.8 2.6 multiply_reduce_fusion.1
  (42 shorter events, 5.9 us)
Async XLA Ops:
  6.5 67.5 %all-gather.3.cloned.1.call-start = ((), (), s32[]{:S(2)}) async-start(), calls=%async_computation.2 | async-start | bytes 6684672 | tf_op jit(solution)/shard_map/all_gather | solution.py:67
  7.3 159.5 %all-gather.5.cloned.1.call-start = ((), (), s32[]{:S(2)}) async-start(), calls=%async_computation.3 | async-start | bytes 2228224 | tf_op jit(solution)/shard_map/all_gather | solution.py:80
  78.9 4.8 %copy-start.1 = (s32[256,2]{0,1:T(2,128)S(1)}, s32[256,2]{0,1:T(2,128)}, u32[]{:S(2)}) copy-start(s32[256,2]{0,1:T(2,128)} %param.8) | copy-start | bytes 6148
  79.1 2.7 collective-permute-start
  83.4 54.3 %collective-permute-start.1 = (bf16[2,512,1024]{2,1,0:T(8,128)(2,1)}, bf16[2,512,1024]{2,1,0:T(8,128)(2,1)}, u32[]{:S(2)}, u32[]{:S(2)}) collective-permute-start(bf16[2,512,1024]{2,1,0:T(8,128)(2,1)} %pad_maximum_fusion.1), channel_id=1, source_target_pairs={{0,2},{2,0},{1,3},{3,1},{4,6},{6,4},{5,7},{7,5},{8,10},{10,8},{9,1... | collective-permute-start | bytes 6291464 | tf_op jit(solution)/shard_map/ppermute | solution.py:23
  157.6 9.2 %copy-start = (bf16[256,1024]{1,0:T(8,128)(2,1)S(1)}, bf16[256,1024]{1,0:T(8,128)(2,1)}, u32[]{:S(2)}) copy-start(bf16[256,1024]{1,0:T(8,128)(2,1)} %param.7) | copy-start | bytes 1572868
  246.6 7.4 %copy-start.2 = (f32[256,2]{0,1:T(2,128)S(1)}, f32[256,2]{0,1:T(2,128)}, u32[]{:S(2)}) copy-start(f32[256,2]{0,1:T(2,128)} %param.9) | copy-start | bytes 6148
  250.4 31.4 %all-to-all-start.1 = ((bf16[16,2,20,1024]{3,1,2,0:T(2,128)(2,1)}), bf16[16,2,20,1024]{3,1,2,0:T(2,128)(2,1)S(1)}, u32[]{:S(2)}, u32[]{:S(2)}) async-start(bf16[16,2,20,1024]{3,1,2,0:T(2,128)(2,1)} %copy.30), calls=%async_computation.1 | async-start | bytes 2621440 | tf_op jit(solution)/shard_map/all_to_all | solution.py:111
Sparse Core Ops, SparseCore 0:
  9.6 64.3 all-gather.2
  83.8 46.7 all-gather.4
where the time goes:
time: 307 us; the launch traced here: 301 us
  waiting for transfers between devices  146 us (48%)
  matrix products  51 us (17%)
  local copies, waits for them, and re-layouts  38.3 us (12%)
  blocking collectives  36 us (12%)
  between operations  13.8 us (4%)
  other arithmetic  11.7 us (4%)
  starting transfers between devices  4.26 us (1%)
    all_gather x1, waiting for transfers between devices, per_device(): lax.all_gather(qkv_weight, 'ctx', axis=0, tiled=True)  64.2 us
    ppermute x2, waiting for transfers between devices, from_partner(): return lax.ppermute(block, axis, route)  53.7 us
    all_to_all x1, blocking collectives, per_device(): lax.all_to_all(outgoing, 'ctx', split_axis=0, concat_axis=0, tiled=True)  36 us
    all_to_all x1, waiting for transfers between devices, per_device(): lax.all_to_all(produced, 'ctx', split_axis=0, concat_axis=0, tiled=True)  27.6 us
    dot_general x2, matrix products, per_device(): jnp.dot(hidden, second, preferred_element_type=jnp.float32)  24.9 us
    sub x1, matrix products, attend(): weights = jnp.exp(scores - peak)  9.71 us
    dot_general x1, matrix products, attend(): jnp.einsum('hts,shd->thd', probs, v_heads, preferred_element_type=jnp.flo...  9.18 us
    slice x3, local copies, waits for them, and re-layouts, per_device(): context = attend(queries, key_value[0], key_value[1])  8.31 us
  transfers between devices with their start and end apart: 5, of which 4 were waited for; matrix products, arithmetic and copies ran while one was open for 11% of the time, Pallas kernels for 0%

commit v1 on v0

v1 whole, which is shorter than its diff:
```python
import functools

import jax
import jax.numpy as jnp
from jax import lax
from jax.experimental import pallas as pl
from jax.experimental.pallas import tpu as pltpu
from jax.sharding import PartitionSpec as P

HEADS = 16
HD = 64
EXPERTS = 32
SPAN = 4
CAP = 20
TOP = 2
MIB = 1 << 20

eps = 1e-06
bf16 = jnp.bfloat16
f32 = jnp.float32


def params(mib=40):
    return pltpu.CompilerParams(vmem_limit_bytes=mib * MIB)


def cost(flops, nbytes, trans=0):
    return pl.CostEstimate(flops=int(flops), bytes_accessed=int(nbytes), transcendentals=int(trans))


def mm(a, b, dims=(((1,), (0,)), ((), ()))):
    return lax.dot_general(a, b, dims, preferred_element_type=f32)


def normalize(values):
    center = values - jnp.mean(values, axis=-1, keepdims=True)
    spread = jnp.mean(center * center, axis=-1, keepdims=True)
    return (center * lax.rsqrt(spread + eps)).astype(bf16)


def norm_kernel(x_ref, o_ref):
    o_ref[...] = normalize(x_ref[...].astype(f32))


def norm_call(tokens):
    return pl.pallas_call(
        norm_kernel,
        out_shape=jax.ShapeDtypeStruct(tokens.shape, bf16),
        compiler_params=params(),
        cost_estimate=cost(8 * tokens.size, 4 * tokens.size),
        name="norm_tokens",
    )(tokens)


def route_kernel(routes_ref, gates_ref, d_ref, hi_ref, mid_ref, lo_ref):
    rows = routes_ref.shape[1]
    slots = d_ref.shape[0]
    expert = lax.broadcasted_iota(jnp.int32, (EXPERTS, rows), 0)
    names = [expert == routes_ref[r : r + 1, :] for r in range(TOP)]
    counts = names[0]
    for other in names[1:]:
        counts = counts | other
    counts = jnp.where(counts, 1.0, 0.0).astype(bf16)
    earlier = lax.broadcasted_iota(jnp.int32, (rows, rows), 0) < lax.broadcasted_iota(
        jnp.int32, (rows, rows), 1
    )
    before = mm(counts, jnp.where(earlier, 1.0, 0.0).astype(bf16))
    place = lax.broadcasted_iota(jnp.int32, (slots, rows), 0)
    marks = jnp.zeros((slots, rows), f32)
    weights = jnp.zeros((slots, rows), f32)
    for r in range(TOP):
        position = jnp.sum(jnp.where(names[r], before, 0.0), axis=0, keepdims=True)
        slot = routes_ref[r : r + 1, :] * CAP + position.astype(jnp.int32)
        here = place == slot
        marks = jnp.where(here, 1.0, marks)
        weights = jnp.where(here, gates_ref[r : r + 1, :], weights)
    d_ref[...] = marks.astype(bf16)
    high = weights.astype(bf16)
    rest = weights - high.astype(f32)
    middle = rest.astype(bf16)
    hi_ref[...] = high
    mid_ref[...] = middle
    lo_ref[...] = (rest - middle.astype(f32)).astype(bf16)


def route_call(routes, gates):
    rows = routes.shape[0]
    shape = jax.ShapeDtypeStruct((EXPERTS * CAP, rows), bf16)
    return pl.pallas_call(
        route_kernel,
        out_shape=[shape] * 4,
        compiler_params=params(),
        cost_estimate=cost(20 * EXPERTS * CAP * rows, 8 * EXPERTS * CAP * rows),
        name="route_slots",
    )(routes.T, gates.T)


def project_kernel(place_ref, *refs, count, blocks, share):
    xs = refs[:count]
    ws = refs[count : count + blocks * share]
    o_ref = refs[count + blocks * share]
    full = refs[count + blocks * share + 1]
    size = ws[0].shape[0]
    rows = xs[0].shape[0]
    for s in range(share):
        for m in range(blocks):
            start = pl.multiple_of((place_ref[0] ^ m) * size, size)
            full[s, pl.ds(start, size), :] = ws[s * blocks + m][...]
    for s in range(share):
        for j in range(count):
            o_ref[s, j * rows : (j + 1) * rows, :] = mm(xs[j][...], full[s]).astype(bf16)


def project_call(place, xs, ws, blocks, share):
    rows, width = xs[0].shape
    count = len(xs)
    cols = ws[0].shape[1]
    vm = pl.BlockSpec(memory_space=pltpu.VMEM)
    return pl.pallas_call(
        functools.partial(project_kernel, count=count, blocks=blocks, share=share),
        out_shape=jax.ShapeDtypeStruct((share, count * rows, cols), bf16),
        in_specs=[pl.BlockSpec(memory_space=pltpu.SMEM)] + [vm] * (count + blocks * share),
        out_specs=vm,
        scratch_shapes=[pltpu.VMEM((share, width, cols), bf16)],
        compiler_params=params(),
        cost_estimate=cost(2 * count * rows * width * cols * share, 2 * width * (count * rows + 2 * cols * share)),
        name="project",
    )(place, *xs, *ws)


def attend_kernel(p_ref, *o_refs, blocks, share):
    cols = p_ref.shape[2] // 3
    rows = o_refs[0].shape[0]
    heads = cols // HD
    lane = lax.broadcasted_iota(jnp.int32, (rows, cols), 1) // HD
    for o_ref, j in zip(o_refs, blocks):
        for s in range(share):
            queries = p_ref[s, j * rows : (j + 1) * rows, :cols] * jnp.asarray(HD ** (-0.5), bf16)
            keys = p_ref[s, :, cols : 2 * cols]
            values = p_ref[s, :, 2 * cols :]
            mixed = None
            for h in range(heads):
                mine = lane == h
                q = jnp.where(mine, queries, jnp.zeros_like(queries)) if heads > 1 else queries
                scores = mm(q, keys, (((1,), (1,)), ((), ())))
                weights = jnp.exp(scores - jnp.max(scores, axis=-1, keepdims=True))
                probs = (weights * (1.0 / jnp.sum(weights, axis=-1, keepdims=True))).astype(bf16)
                part = mm(probs, values)
                mixed = part if mixed is None else jnp.where(mine, part, mixed)
            o_ref[:, s * cols : (s + 1) * cols] = mixed.astype(bf16)


def attend_call(projected, blocks, rows):
    share, length, cols = projected.shape
    width = share * cols // 3
    return pl.pallas_call(
        functools.partial(attend_kernel, blocks=blocks, share=share),
        out_shape=[jax.ShapeDtypeStruct((rows, width), bf16)] * len(blocks),
        compiler_params=params(),
        cost_estimate=cost(
            16 * len(blocks) * rows * length * width, 4 * projected.size, len(blocks) * rows * length * width // HD
        ),
        name="attend",
    )(projected)


def output_kernel(place_ref, t_ref, d_ref, w_ref, *refs):
    ctxs = refs[:SPAN]
    r_ref, o_ref = refs[SPAN:]
    width = ctxs[0].shape[1]
    total = t_ref[...].astype(f32)
    attended = None
    for j in range(SPAN):
        start = pl.multiple_of((place_ref[0] ^ j) * width, width)
        part = mm(ctxs[j][...], w_ref[pl.ds(start, width), :])
        attended = part if attended is None else attended + part
    total = total + attended
    r_ref[...] = total
    o_ref[...] = mm(d_ref[...], normalize(total)).astype(bf16)


def output_call(place, tokens, marks, weight, ctxs):
    rows, width = tokens.shape
    vm = pl.BlockSpec(memory_space=pltpu.VMEM)
    return pl.pallas_call(
        output_kernel,
        out_shape=[
            jax.ShapeDtypeStruct((rows, width), f32),
            jax.ShapeDtypeStruct((marks.shape[0], width), bf16),
        ],
        in_specs=[pl.BlockSpec(memory_space=pltpu.SMEM)] + [vm] * (3 + SPAN),
        out_specs=[vm, vm],
        compiler_params=params(),
        cost_estimate=cost(2 * rows * width * (width + marks.shape[0]), 6 * width * width),
        name="out_projection",
    )(place, tokens, marks, weight, *ctxs)


def gelu(x):
    return jax.nn.gelu(x, approximate=True)


def expert_kernel(x_ref, win_ref, wout_ref, o_ref, rows_ref, acc_ref, term_ref, *, local, sources):
    e = pl.program_id(0)
    step = pl.program_id(1)
    last = pl.num_programs(1) - 1
    count = sources * CAP

    def pick(which):
        out_row = lax.broadcasted_iota(jnp.int32, (count, local * count), 0)
        in_row = lax.broadcasted_iota(jnp.int32, (count, local * count), 1)
        source = out_row // CAP
        wanted = source * (local * CAP) + which * CAP + (out_row - source * CAP)
        return jnp.where(in_row == wanted, 1.0, 0.0).astype(bf16)

    if local > 1:

        @pl.when(step == 0)
        def _():
            rows_ref[...] = mm(pick(e), x_ref[...]).astype(bf16)

        rows = rows_ref
    else:
        rows = x_ref

    @pl.when(step == 0)
    def _():
        acc_ref[...] = jnp.zeros_like(acc_ref)

    hidden = gelu(mm(rows[...], win_ref[...])).astype(bf16)
    acc_ref[...] += mm(hidden, wout_ref[...])

    @pl.when(step == last)
    def _():
        if local > 1:
            term_ref[e] = acc_ref[...].astype(bf16)
        else:
            o_ref[...] = acc_ref[...].astype(bf16)

    if local > 1:

        @pl.when((step == last) & (e == local - 1))
        def _():
            total = None
            for which in range(local):
                part = mm(pick(which), term_ref[which], (((0,), (0,)), ((), ())))
                total = part if total is None else total + part
            o_ref[...] = total.astype(bf16)


def expert_call(arrived, w_in, w_out, local, sources, block=512):
    count = sources * CAP
    width = arrived.shape[1]
    hidden = w_in.shape[1] // local
    steps = hidden // block
    return pl.pallas_call(
        functools.partial(expert_kernel, local=local, sources=sources),
        grid=(local, steps),
        out_shape=jax.ShapeDtypeStruct(arrived.shape, bf16),
        in_specs=[
            pl.BlockSpec(arrived.shape, lambda e, i: (0, 0)),
            pl.BlockSpec((width, block), lambda e, i: (0, e * steps + i)),
            pl.BlockSpec((block, width), lambda e, i: (e * steps + i, 0)),
        ],
        out_specs=pl.BlockSpec(arrived.shape, lambda e, i: (0, 0)),
        scratch_shapes=[
            pltpu.VMEM((count, width), bf16),
            pltpu.VMEM((count, width), f32),
            pltpu.VMEM((local, count, width), bf16),
        ],
        compiler_params=params(),
        cost_estimate=cost(4 * count * width * hidden * local, 4 * width * hidden * local, count * hidden * local),
        name="experts",
    )(arrived, w_in, w_out)


def combine_kernel(r_ref, b_ref, hi_ref, mid_ref, lo_ref, o_ref):
    dims = (((0,), (0,)), ((), ()))
    back = b_ref[...]
    mixture = mm(lo_ref[...], back, dims)
    mixture = mixture + mm(mid_ref[...], back, dims)
    mixture = mixture + mm(hi_ref[...], back, dims)
    o_ref[...] = (r_ref[...] + mixture).astype(bf16)


def combine_call(resid, back, parts):
    return pl.pallas_call(
        combine_kernel,
        out_shape=jax.ShapeDtypeStruct(resid.shape, bf16),
        compiler_params=params(),
        cost_estimate=cost(6 * back.size * resid.shape[0], 6 * resid.size + 2 * back.size),
        name="combine",
    )(resid, back, *parts)


def swap(value, axis, bits):
    size = lax.axis_size(axis)
    return lax.ppermute(value, axis, [(i, i ^ bits) for i in range(size)])


def per_device(tokens, routes, gates, qkv_weight, out_weight, w_in, w_out):
    rows, width = tokens.shape
    devices = lax.axis_size("ctx")
    groups = lax.axis_size("groups")
    upper = devices // SPAN
    me = lax.axis_index("ctx")
    member = me % SPAN
    line = me // SPAN
    group = lax.axis_index("groups")
    parts_ff = max(1, devices // EXPERTS)
    local_experts = max(1, EXPERTS // devices)

    mine = width // SPAN
    share = SHARE(groups, mine // HD)
    cols = mine // share
    offset = (group % share) * cols

    def columns(to):
        pieces = [
            lax.dynamic_slice_in_dim(qkv_weight, t * width + to * mine + offset, cols, 1)
            for t in range(3)
        ]
        return jnp.concatenate(pieces, axis=1)

    pieces = [columns(member)] + [swap(columns(member ^ j), "ctx", j) for j in range(1, SPAN)]
    block = jnp.zeros((SPAN,) + pieces[0].shape, bf16)
    for j in range(SPAN):
        block = lax.dynamic_update_slice(block, pieces[j][None], (member ^ j, 0, 0))
    block = block.reshape(-1, 3 * cols)
    lines = [block] + [swap(block, "ctx", m * SPAN) for m in range(1, upper)]
    shares = lines
    for s in range(1, share):
        shares = shares + [swap(piece, "groups", s) for piece in lines]

    normed = norm_call(tokens)
    far = swap(normed, "ctx", 2)
    near = swap(normed, "ctx", 1)
    both = swap(far, "ctx", 1)
    marks, *gate_parts = route_call(routes, gates)

    projected = project_call(line.reshape(1), [normed, near, far, both], shares, upper, share)
    sent = attend_call(projected, (3, 2), rows)
    back = {3: swap(sent[0], "ctx", 3), 2: swap(sent[1], "ctx", 2)}
    kept = attend_call(projected, (1, 0), rows)
    back[1] = swap(kept[0], "ctx", 1)
    back[0] = kept[1]
    ctxs = []
    for j in range(SPAN):
        if share > 1:
            split = back[j].reshape(rows, share, cols)
            order = [lax.dynamic_index_in_dim(split, (group % share) ^ s, 1, keepdims=False) for s in range(share)]
            ctxs.append(jnp.concatenate(order, axis=1))
        else:
            ctxs.append(back[j])
    whole_out = lax.all_gather(out_weight, "ctx", axis=0, tiled=True)
    resid, table = output_call(member.reshape(1), tokens, marks, whole_out, ctxs)

    table = table.reshape(EXPERTS, CAP, width)
    if parts_ff > 1:
        table = jnp.repeat(table, parts_ff, axis=0)
    outgoing = table.reshape(devices, local_experts * CAP, width)
    arrived = lax.all_to_all(outgoing, "ctx", split_axis=0, concat_axis=0, tiled=True)
    produced = expert_call(arrived.reshape(-1, width), w_in, w_out, local_experts, devices)
    produced = produced.reshape(devices, local_experts * CAP, width)
    returned = lax.all_to_all(produced, "ctx", split_axis=0, concat_axis=0, tiled=True)
    if parts_ff > 1:
        grouped = returned.reshape(EXPERTS, parts_ff, CAP, width)
        returned = jnp.sum(grouped.astype(f32), axis=1).astype(bf16)
    return combine_call(resid, returned.reshape(EXPERTS * CAP, width), gate_parts)


def SHARE(groups, heads):
    return 1


def solution(mesh):
    in_specs = (
        P(("groups", "ctx"), None),
        P(("groups", "ctx"), None),
        P(("groups", "ctx"), None),
        P("ctx", None),
        P("ctx", None),
        P(None, "ctx"),
        P("ctx", None),
    )
    out_specs = P(("groups", "ctx"), None)
    return jax.shard_map(
        per_device, mesh=mesh, in_specs=in_specs, out_specs=out_specs, check_vma=False
    )
```

time: 307 us -> 202 us (0.66); the launches traced: 301 us -> 201 us
  waiting for transfers between devices: 146 us -> 50.6 us
  matrix products: 51 us -> 0 us
  blocking collectives: 36 us -> 79.9 us
  Pallas kernels: 0 us -> 40 us
  local copies, waits for them, and re-layouts: 38.3 us -> 3.67 us
  other arithmetic: 11.7 us -> 0.04 us
  starting transfers between devices: 4.26 us -> 13.6 us
    all_gather x2 -> x1, waiting for transfers between devices: 64.2 us -> 0.01 us  [per_device(): whole_out = lax.all_gather(out_weight, 'ctx', axis=0, tiled=True)]
    dot_general x5 -> x0, matrix products: 41.3 us -> none  [the longest x2 24.9 us: per_device(): jnp.dot(hidden, second, preferred_element_type=jnp.float32)]
    pallas_call x0 -> x8, Pallas kernels: none -> 40 us  [the longest x1 25.1 us: expert_call(): pl.pallas_call(functools.partial(expert_kernel, local=local, sources=sour...]
    all_to_all x0 -> x1, blocking collectives: none -> 35.3 us  [per_device(): lax.all_to_all(produced, 'ctx', split_axis=0, concat_axis=0, tiled=True)]
    all_to_all x1 -> x0, waiting for transfers between devices: 27.6 us -> none  [per_device(): lax.all_to_all(produced, 'ctx', split_axis=0, concat_axis=0, tiled=True)]
    slice x7 -> x0, local copies, waits for them, and re-layouts: 14.6 us -> none  [the longest x3 8.31 us: per_device(): context = attend(queries, key_value[0], key_value[1])]
    ppermute x2 -> x12, starting transfers between devices: 0.59 us -> 13.6 us  [swap(): return lax.ppermute(value, axis, [(i, i ^ bits) for i in range(size)])]
    another operation x9 -> x0, local copies, waits for them, and re-layouts: 11.5 us -> none  [the longest x3 5.25 us: per_device(): produced = jnp.stack(results, axis=1)]
  transfers between devices with their start and end apart: 5 -> 13, of which waited for: 4 -> 5; matrix products, arithmetic and copies ran while one was open for 11% -> 1% of each run, Pallas kernels for 0% -> 6%
where the time goes in v1:
time: 202 us; the launch traced here: 201 us
  blocking collectives  79.9 us (40%)
  waiting for transfers between devices  50.6 us (25%)
  Pallas kernels  40 us (20%)
  starting transfers between devices  13.6 us (7%)
  between operations  13.6 us (7%)
  local copies, waits for them, and re-layouts  3.67 us (2%)
    ppermute x12, waiting for transfers between devices, swap(): return lax.ppermute(value, axis, [(i, i ^ bits) for i in range(size)])  49.9 us
    all_to_all x1, blocking collectives, per_device(): lax.all_to_all(outgoing, 'ctx', split_axis=0, concat_axis=0, tiled=True)  44.6 us
    all_to_all x1, blocking collectives, per_device(): lax.all_to_all(produced, 'ctx', split_axis=0, concat_axis=0, tiled=True)  35.3 us
    pallas_call x1, Pallas kernels, expert_call(): pl.pallas_call(functools.partial(expert_kernel, local=local, sources=sour...  25.1 us
    ppermute x12, starting transfers between devices, swap(): return lax.ppermute(value, axis, [(i, i ^ bits) for i in range(size)])  13.6 us
    pallas_call x2, Pallas kernels, attend_call(): pl.pallas_call(functools.partial(attend_kernel, blocks=blocks, share=shar...  7.24 us
  transfers between devices with their start and end apart: 13, of which 5 were waited for; matrix products, arithmetic and copies ran while one was open for 1% of the time, Pallas kernels for 6%

profile of v1, /device:TPU:1, one launch (start us, length us, event | category | flops | bytes accessed | tf_op | source)
XLA Modules:
  0.0 201.3 jit_solution(5414149627924848936)
XLA Ops:
  6.5 0.7 all-gather.2.cloned.1.call-update
  7.3 0.0 copy-start.1
  7.3 1.0 copy-done.1
  8.3 0.3 norm_tokens.1.refs_0_
  8.6 2.1 %collective-permute-start.1 = (bf16[256,1024]{1,0:T(8,128)(2,1)S(1)}, bf16[256,1024]{1,0:T(8,128)(2,1)S(1)}, u32[]{:S(2)}, u32[]{:S(2)}) collective-permute-start(bf16[256,1024]{1,0:T(8,128)(2,1)S(1)} %norm_tokens.1.refs_0_), channel_id=1, source_target_pairs={{0,2},{1,3},{2,0},{3,1},{4,6},{5,7},{6,4},{7,5},{8,10},{9,11},{10,... | collective-permute-start | bytes 1572872 | tf_op jit(solution)/shard_map/ppermute | solution.py:298
  10.8 1.0 collective-permute-start
  11.7 1.0 constant_dynamic-slice_fusion.2
  12.7 0.1 collective-permute-start.3
  12.8 0.1 collective-permute-start.4
  12.9 2.2 %collective-permute-start.5 = (bf16[64,768]{1,0:T(8,128)(2,1)S(1)}, bf16[64,768]{1,0:T(8,128)(2,1)S(1)}, u32[]{:S(2)}, u32[]{:S(2)}) collective-permute-start(bf16[64,768]{1,0:T(8,128)(2,1)S(1)} %pad_maximum_fusion.2), channel_id=1, source_target_pairs={{0,3},{1,2},{2,1},{3,0},{4,7},{5,6},{6,5},{7,4},{8,11},{9,10},{10,... | collective-permute-start | bytes 294920 | tf_op jit(solution)/shard_map/ppermute | solution.py:298
  15.1 10.8 %collective-permute-done.4 = bf16[64,768]{1,0:T(8,128)(2,1)S(1)} collective-permute-done((bf16[64,768]{1,0:T(8,128)(2,1)S(1)}, bf16[64,768]{1,0:T(8,128)(2,1)S(1)}, u32[]{:S(2)}, u32[]{:S(2)}) %collective-permute-start.4) | collective-permute-done | bytes 98336 | tf_op jit(solution)/shard_map/ppermute | solution.py:298
  26.0 2.1 %collective-permute-start.2 = (bf16[256,1024]{1,0:T(8,128)(2,1)S(1)}, bf16[256,1024]{1,0:T(8,128)(2,1)S(1)}, u32[]{:S(2)}, u32[]{:S(2)}) collective-permute-start(bf16[256,1024]{1,0:T(8,128)(2,1)S(1)} %collective-permute-done.1.refs_2_), channel_id=1, source_target_pairs={{0,1},{1,0},{2,3},{3,2},{4,5},{5,4},{6,7},{7,6},{8,9},{9,8},{10,11... | collective-permute-start | bytes 1572872 | tf_op jit(solution)/shard_map/ppermute | solution.py:298
  28.1 0.9 collective-permute-done.5
  29.0 1.6 collective-permute-start.6
  30.5 2.3 %collective-permute-start.7 = (bf16[256,768]{1,0:T(8,128)(2,1)S(1)}, bf16[256,768]{1,0:T(8,128)(2,1)S(1)}, u32[]{:S(2)}, u32[]{:S(2)}) collective-permute-start(bf16[256,768]{1,0:T(8,128)(2,1)S(1)} %bitcast.24), channel_id=1, source_target_pairs={{0,8},{1,9},{2,10},{3,11},{4,12},{5,13},{6,14},{7,15},{8,0},{9,1},... | collective-permute-start | bytes 1179656 | tf_op jit(solution)/shard_map/ppermute | solution.py:298
  32.9 22.8 %collective-permute-done.6.refs_5_ = bf16[256,768]{1,0:T(8,128)(2,1)S(1)} collective-permute-done((bf16[256,768]{1,0:T(8,128)(2,1)S(1)}, bf16[256,768]{1,0:T(8,128)(2,1)S(1)}, u32[]{:S(2)}, u32[]{:S(2)}) %collective-permute-start.6) | collective-permute-done | bytes 393248 | tf_op jit(solution)/shard_map/ppermute | solution.py:298
  55.7 10.8 %collective-permute-done.8.refs_7_ = bf16[256,768]{1,0:T(8,128)(2,1)} collective-permute-done((bf16[256,768]{1,0:T(8,128)(2,1)S(1)}, bf16[256,768]{1,0:T(8,128)(2,1)}, u32[]{:S(2)}, u32[]{:S(2)}) %collective-permute-start.8) | collective-permute-done | bytes 393248 | tf_op jit(solution)/shard_map/ppermute | solution.py:298
  66.6 2.9 %project.1.p_ref = bf16[1,1024,768]{2,1,0:T(8,128)(2,1)S(1)} custom-call(s32[1]{0:T(128)} %bitcast.3.place_ref, bf16[256,1024]{1,0:T(8,128)(2,1)S(1)} %norm_tokens.1.refs_0_, bf16[256,1024]{1,0:T(8,128)(2,1)S(1)} %collective-permute-done.refs_1_, bf16[256,1024]{1,0:T(8,128)(2,1)S(1)} %collective-permute-done.1.refs_2_, ...), custom_call_target="tpu_custom_call" | custom-call | flops 1610612736 | bytes 5242880 | tf_op jit(solution)/shard_map/project/pallas_call | solution.py:119
  69.5 3.6 %attend.3 = (bf16[256,256]{1,0:T(8,128)(2,1)S(1)}, bf16[256,256]{1,0:T(8,128)(2,1)S(1)}) custom-call(bf16[1,1024,768]{2,1,0:T(8,128)(2,1)S(1)} %project.1.p_ref), custom_call_target="tpu_custom_call" | custom-call | flops 2147483648 | bytes 3145728 | tf_op jit(solution)/shard_map/attend/pallas_call | solution.py:156
  73.1 0.0 copy-start.3
  73.1 0.0 copy-start.2
  73.1 1.3 collective-permute-start.10
  74.4 3.6 %attend.2 = (bf16[256,256]{1,0:T(8,128)(2,1)S(1)}, bf16[256,256]{1,0:T(8,128)(2,1)S(1)}) custom-call(bf16[1,1024,768]{2,1,0:T(8,128)(2,1)S(1)} %project.1.p_ref), custom_call_target="tpu_custom_call" | custom-call | flops 2147483648 | bytes 3145728 | tf_op jit(solution)/shard_map/attend/pallas_call | solution.py:156
  78.1 0.9 collective-permute-start.11
  78.9 0.7 route_slots.1
  79.7 4.5 %collective-permute-done.11.refs_3_ = bf16[256,256]{1,0:T(8,128)(2,1)S(1)} collective-permute-done((bf16[256,256]{1,0:T(8,128)(2,1)S(1)}, bf16[256,256]{1,0:T(8,128)(2,1)S(1)}, u32[]{:S(2)}, u32[]{:S(2)}) %collective-permute-start.11) | collective-permute-done | bytes 131104 | tf_op jit(solution)/shard_map/ppermute | solution.py:298
  84.2 1.6 copy-done
  85.8 1.4 out_projection.1
  87.2 44.6 %all_to_all.10 = bf16[16,40,1024]{2,1,0:T(8,128)(2,1)S(1)} all-to-all(bf16[16,40,1024]{2,1,0:T(8,128)(2,1)S(1)} %bitcast.20), channel_id=1, replica_groups=mesh['groups'=2,'ctx'=16] {'ctx'}, dimensions={0} | all-to-all | bytes 2621440 | tf_op jit(solution)/shard_map/all_to_all | solution.py:362
  131.9 25.1 %experts.1 = bf16[640,1024]{1,0:T(8,128)(2,1)S(1)} custom-call(bf16[640,1024]{1,0:T(8,128)(2,1)S(1)} %bitcast.21, bf16[1024,8192]{1,0:T(8,128)(2,1)} %win_ref.1, bf16[8192,1024]{1,0:T(8,128)(2,1)} %wout_ref.1), custom_call_target="tpu_custom_call" | custom-call | flops 10737418240 | bytes 33554432 | tf_op jit(solution)/shard_map/experts/pallas_call | solution.py:256
  157.0 35.3 %all_to_all.11 = bf16[16,40,1024]{2,1,0:T(8,128)(2,1)S(1)} all-to-all(bf16[16,40,1024]{2,1,0:T(8,128)(2,1)S(1)} %bitcast.22), channel_id=1, replica_groups=mesh['groups'=2,'ctx'=16] {'ctx'}, dimensions={0} | all-to-all | bytes 2621440 | tf_op jit(solution)/shard_map/all_to_all | solution.py:365
  192.3 2.2 %combine.1 = bf16[256,1024]{1,0:T(8,128)(2,1)} custom-call(f32[256,1024]{1,0:T(8,128)S(1)} %get-tuple-element.20.r_ref, bf16[640,1024]{1,0:T(8,128)(2,1)S(1)} %bitcast.19, bf16[640,256]{1,0:T(8,128)(2,1)S(1)} %get-tuple-element.22.hi_ref, bf16[640,256]{1,0:T(8,128)(2,1)S(1)} %get-tuple-element.23.mid_ref, bf16[640,256]{1,0:T(8,128)(2,1)S(1)} %get-tuple-element.24.lo_ref), custom_call_target="tpu_custom_call" | custom-call | flops 1006632960 | bytes 2883584 | tf_op jit(solution)/shard_map/combine/pallas_call | solution.py:287
  (24 shorter events, 0.1 us)
Async XLA Ops:
  6.5 77.7 %all-gather.2.cloned.1.call-start = ((), (), s32[]{:S(2)}) async-start(), calls=%async_computation.2 | async-start | bytes 2228224 | tf_op jit(solution)/shard_map/all_gather | solution.py:355
  7.3 1.0 copy-start.1
  8.6 17.3 %collective-permute-start.1 = (bf16[256,1024]{1,0:T(8,128)(2,1)S(1)}, bf16[256,1024]{1,0:T(8,128)(2,1)S(1)}, u32[]{:S(2)}, u32[]{:S(2)}) collective-permute-start(bf16[256,1024]{1,0:T(8,128)(2,1)S(1)} %norm_tokens.1.refs_0_), channel_id=1, source_target_pairs={{0,2},{1,3},{2,0},{3,1},{4,6},{5,7},{6,4},{7,5},{8,10},{9,11},{10,... | collective-permute-start | bytes 1572872 | tf_op jit(solution)/shard_map/ppermute | solution.py:298
  10.8 55.8 %collective-permute-start = (bf16[256,1024]{1,0:T(8,128)(2,1)S(1)}, bf16[256,1024]{1,0:T(8,128)(2,1)S(1)}, u32[]{:S(2)}, u32[]{:S(2)}) collective-permute-start(bf16[256,1024]{1,0:T(8,128)(2,1)S(1)} %norm_tokens.1.refs_0_), channel_id=1, source_target_pairs={{0,1},{1,0},{2,3},{3,2},{4,5},{5,4},{6,7},{7,6},{8,9},{9,8},{10,11... | collective-permute-start | bytes 1572872 | tf_op jit(solution)/shard_map/ppermute | solution.py:298
  12.7 2.4 %collective-permute-start.3 = (bf16[64,768]{1,0:T(8,128)(2,1)S(1)}, bf16[64,768]{1,0:T(8,128)(2,1)S(1)}, u32[]{:S(2)}, u32[]{:S(2)}) collective-permute-start(bf16[64,768]{1,0:T(8,128)(2,1)S(1)} %pad_maximum_fusion), channel_id=1, source_target_pairs={{0,1},{1,0},{2,3},{3,2},{4,5},{5,4},{6,7},{7,6},{8,9},{9,8},{10,11... | collective-permute-start | bytes 294920 | tf_op jit(solution)/shard_map/ppermute | solution.py:298
  12.8 13.1 %collective-permute-start.4 = (bf16[64,768]{1,0:T(8,128)(2,1)S(1)}, bf16[64,768]{1,0:T(8,128)(2,1)S(1)}, u32[]{:S(2)}, u32[]{:S(2)}) collective-permute-start(bf16[64,768]{1,0:T(8,128)(2,1)S(1)} %pad_maximum_fusion.1), channel_id=1, source_target_pairs={{0,2},{1,3},{2,0},{3,1},{4,6},{5,7},{6,4},{7,5},{8,10},{9,11},{10,... | collective-permute-start | bytes 294920 | tf_op jit(solution)/shard_map/ppermute | solution.py:298
  12.9 16.1 %collective-permute-start.5 = (bf16[64,768]{1,0:T(8,128)(2,1)S(1)}, bf16[64,768]{1,0:T(8,128)(2,1)S(1)}, u32[]{:S(2)}, u32[]{:S(2)}) collective-permute-start(bf16[64,768]{1,0:T(8,128)(2,1)S(1)} %pad_maximum_fusion.2), channel_id=1, source_target_pairs={{0,3},{1,2},{2,1},{3,0},{4,7},{5,6},{6,5},{7,4},{8,11},{9,10},{10,... | collective-permute-start | bytes 294920 | tf_op jit(solution)/shard_map/ppermute | solution.py:298
  26.0 40.6 %collective-permute-start.2 = (bf16[256,1024]{1,0:T(8,128)(2,1)S(1)}, bf16[256,1024]{1,0:T(8,128)(2,1)S(1)}, u32[]{:S(2)}, u32[]{:S(2)}) collective-permute-start(bf16[256,1024]{1,0:T(8,128)(2,1)S(1)} %collective-permute-done.1.refs_2_), channel_id=1, source_target_pairs={{0,1},{1,0},{2,3},{3,2},{4,5},{5,4},{6,7},{7,6},{8,9},{9,8},{10,11... | collective-permute-start | bytes 1572872 | tf_op jit(solution)/shard_map/ppermute | solution.py:298
  29.0 26.7 %collective-permute-start.6 = (bf16[256,768]{1,0:T(8,128)(2,1)S(1)}, bf16[256,768]{1,0:T(8,128)(2,1)S(1)}, u32[]{:S(2)}, u32[]{:S(2)}) collective-permute-start(bf16[256,768]{1,0:T(8,128)(2,1)S(1)} %bitcast.23), channel_id=1, source_target_pairs={{0,4},{1,5},{2,6},{3,7},{4,0},{5,1},{6,2},{7,3},{8,12},{9,13},{10,... | collective-permute-start | bytes 1179656 | tf_op jit(solution)/shard_map/ppermute | solution.py:298
  30.5 25.2 %collective-permute-start.7 = (bf16[256,768]{1,0:T(8,128)(2,1)S(1)}, bf16[256,768]{1,0:T(8,128)(2,1)S(1)}, u32[]{:S(2)}, u32[]{:S(2)}) collective-permute-start(bf16[256,768]{1,0:T(8,128)(2,1)S(1)} %bitcast.24), channel_id=1, source_target_pairs={{0,8},{1,9},{2,10},{3,11},{4,12},{5,13},{6,14},{7,15},{8,0},{9,1},... | collective-permute-start | bytes 1179656 | tf_op jit(solution)/shard_map/ppermute | solution.py:298
  32.9 33.7 %collective-permute-start.8 = (bf16[256,768]{1,0:T(8,128)(2,1)S(1)}, bf16[256,768]{1,0:T(8,128)(2,1)}, u32[]{:S(2)}, u32[]{:S(2)}) collective-permute-start(bf16[256,768]{1,0:T(8,128)(2,1)S(1)} %bitcast.25), channel_id=1, source_target_pairs={{0,12},{1,13},{2,14},{3,15},{4,8},{5,9},{6,10},{7,11},{8,4},{9,5},... | collective-permute-start | bytes 1179656 | tf_op jit(solution)/shard_map/ppermute | solution.py:298
  73.1 5.8 %copy-start.3 = (s32[256,2]{0,1:T(2,128)S(1)}, s32[256,2]{0,1:T(2,128)}, u32[]{:S(2)}) copy-start(s32[256,2]{0,1:T(2,128)} %param.8) | copy-start | bytes 6148
  73.1 5.8 %copy-start.4 = (f32[256,2]{0,1:T(2,128)S(1)}, f32[256,2]{0,1:T(2,128)}, u32[]{:S(2)}) copy-start(f32[256,2]{0,1:T(2,128)} %param.9) | copy-start | bytes 6148
  73.1 11.1 %copy-start.2 = (bf16[256,1024]{1,0:T(8,128)(2,1)S(1)}, bf16[256,1024]{1,0:T(8,128)(2,1)}, u32[]{:S(2)}) copy-start(bf16[256,1024]{1,0:T(8,128)(2,1)} %t_ref.1) | copy-start | bytes 1572868
  73.1 6.5 %collective-permute-start.10 = (bf16[256,256]{1,0:T(8,128)(2,1)S(1)}, bf16[256,256]{1,0:T(8,128)(2,1)S(1)}, u32[]{:S(2)}, u32[]{:S(2)}) collective-permute-start(bf16[256,256]{1,0:T(8,128)(2,1)S(1)} %get-tuple-element.18), channel_id=1, source_target_pairs={{0,2},{1,3},{2,0},{3,1},{4,6},{5,7},{6,4},{7,5},{8,10},{9,11},{10,... | collective-permute-start | bytes 393224 | tf_op jit(solution)/shard_map/ppermute | solution.py:298
  78.1 6.1 %collective-permute-start.11 = (bf16[256,256]{1,0:T(8,128)(2,1)S(1)}, bf16[256,256]{1,0:T(8,128)(2,1)S(1)}, u32[]{:S(2)}, u32[]{:S(2)}) collective-permute-start(bf16[256,256]{1,0:T(8,128)(2,1)S(1)} %get-tuple-element.19), channel_id=1, source_target_pairs={{0,3},{1,2},{2,1},{3,0},{4,7},{5,6},{6,5},{7,4},{8,11},{9,10},{10,... | collective-permute-start | bytes 393224 | tf_op jit(solution)/shard_map/ppermute | solution.py:298
  78.9 5.3 %collective-permute-start.9 = (bf16[256,256]{1,0:T(8,128)(2,1)S(1)}, bf16[256,256]{1,0:T(8,128)(2,1)S(1)}, u32[]{:S(2)}, u32[]{:S(2)}) collective-permute-start(bf16[256,256]{1,0:T(8,128)(2,1)S(1)} %get-tuple-element.17), channel_id=1, source_target_pairs={{0,1},{1,0},{2,3},{3,2},{4,5},{5,4},{6,7},{7,6},{8,9},{9,8},{10,11... | collective-permute-start | bytes 393224 | tf_op jit(solution)/shard_map/ppermute | solution.py:298
  84.2 1.6 copy-start
Sparse Core Ops, SparseCore 0:
  9.5 62.9 all-gather.1

commit v2 on v1

--- a/solution.py
+++ b/solution.py
@@ -95,35 +95,40 @@
     )(routes.T, gates.T)
 
 
-def project_kernel(place_ref, *refs, count, blocks, share):
+def project_kernel(place_ref, *refs, count, lines, share):
     xs = refs[:count]
-    ws = refs[count : count + blocks * share]
-    o_ref = refs[count + blocks * share]
-    full = refs[count + blocks * share + 1]
-    size = ws[0].shape[0]
+    ws = refs[count : count + lines * share]
+    o_ref, part_ref, full = refs[count + lines * share :]
+    size, wide = ws[0].shape
+    cols = wide // 4
     rows = xs[0].shape[0]
     for s in range(share):
-        for m in range(blocks):
+        for m in range(lines):
             start = pl.multiple_of((place_ref[0] ^ m) * size, size)
-            full[s, pl.ds(start, size), :] = ws[s * blocks + m][...]
+            full[place_ref[1] ^ s, pl.ds(start, size), :] = ws[s * lines + m][...]
     for s in range(share):
         for j in range(count):
-            o_ref[s, j * rows : (j + 1) * rows, :] = mm(xs[j][...], full[s]).astype(bf16)
-
-
-def project_call(place, xs, ws, blocks, share):
+            o_ref[s, j * rows : (j + 1) * rows, :] = mm(xs[j][...], full[s, :, : 3 * cols]).astype(bf16)
+        part_ref[:, s * cols : (s + 1) * cols] = full[s, :, 3 * cols :]
+
+
+def project_call(place, xs, ws, lines, share):
     rows, width = xs[0].shape
     count = len(xs)
-    cols = ws[0].shape[1]
+    wide = ws[0].shape[1]
+    cols = wide // 4
     vm = pl.BlockSpec(memory_space=pltpu.VMEM)
     return pl.pallas_call(
-        functools.partial(project_kernel, count=count, blocks=blocks, share=share),
-        out_shape=jax.ShapeDtypeStruct((share, count * rows, cols), bf16),
-        in_specs=[pl.BlockSpec(memory_space=pltpu.SMEM)] + [vm] * (count + blocks * share),
-        out_specs=vm,
-        scratch_shapes=[pltpu.VMEM((share, width, cols), bf16)],
-        compiler_params=params(),
-        cost_estimate=cost(2 * count * rows * width * cols * share, 2 * width * (count * rows + 2 * cols * share)),
+        functools.partial(project_kernel, count=count, lines=lines, share=share),
+        out_shape=[
+            jax.ShapeDtypeStruct((share, count * rows, 3 * cols), bf16),
+            jax.ShapeDtypeStruct((width, share * cols), bf16),
+        ],
+        in_specs=[pl.BlockSpec(memory_space=pltpu.SMEM)] + [vm] * (count + lines * share),
+        out_specs=[vm, vm],
+        scratch_shapes=[pltpu.VMEM((share, width, wide), bf16)],
+        compiler_params=params(),
+        cost_estimate=cost(6 * count * rows * width * cols * share, 2 * width * (count * rows + 2 * wide * share)),
         name="project",
     )(place, *xs, *ws)
 
@@ -164,22 +169,21 @@
     )(projected)
 
 
-def output_kernel(place_ref, t_ref, d_ref, w_ref, *refs):
-    ctxs = refs[:SPAN]
-    r_ref, o_ref = refs[SPAN:]
-    width = ctxs[0].shape[1]
-    total = t_ref[...].astype(f32)
-    attended = None
+def output_kernel(place_ref, t_ref, d_ref, *refs):
+    ctxs, parts = refs[:SPAN], refs[SPAN : 2 * SPAN]
+    r_ref, o_ref, c_ref, a_ref = refs[2 * SPAN :]
+    wide = ctxs[0].shape[1]
+    starts = [pl.multiple_of((place_ref[0] ^ j) * wide, wide) for j in range(SPAN)]
     for j in range(SPAN):
-        start = pl.multiple_of((place_ref[0] ^ j) * width, width)
-        part = mm(ctxs[j][...], w_ref[pl.ds(start, width), :])
-        attended = part if attended is None else attended + part
-    total = total + attended
+        c_ref[:, pl.ds(starts[j], wide)] = ctxs[j][...]
+    for j in range(SPAN):
+        a_ref[:, pl.ds(starts[j], wide)] = mm(c_ref[...], parts[j][...])
+    total = t_ref[...].astype(f32) + a_ref[...]
     r_ref[...] = total
     o_ref[...] = mm(d_ref[...], normalize(total)).astype(bf16)
 
 
-def output_call(place, tokens, marks, weight, ctxs):
+def output_call(place, tokens, marks, parts, ctxs):
     rows, width = tokens.shape
     vm = pl.BlockSpec(memory_space=pltpu.VMEM)
     return pl.pallas_call(
@@ -188,87 +192,114 @@
             jax.ShapeDtypeStruct((rows, width), f32),
             jax.ShapeDtypeStruct((marks.shape[0], width), bf16),
         ],
-        in_specs=[pl.BlockSpec(memory_space=pltpu.SMEM)] + [vm] * (3 + SPAN),
+        in_specs=[pl.BlockSpec(memory_space=pltpu.SMEM)] + [vm] * (2 + 2 * SPAN),
         out_specs=[vm, vm],
+        scratch_shapes=[pltpu.VMEM((rows, width), bf16), pltpu.VMEM((rows, width), f32)],
         compiler_params=params(),
         cost_estimate=cost(2 * rows * width * (width + marks.shape[0]), 6 * width * width),
         name="out_projection",
-    )(place, tokens, marks, weight, *ctxs)
+    )(place, tokens, marks, *ctxs, *parts)
 
 
 def gelu(x):
     return jax.nn.gelu(x, approximate=True)
 
 
-def expert_kernel(x_ref, win_ref, wout_ref, o_ref, rows_ref, acc_ref, term_ref, *, local, sources):
-    e = pl.program_id(0)
-    step = pl.program_id(1)
-    last = pl.num_programs(1) - 1
+def expert_kernel(x_ref, win_ref, wout_ref, o_ref, *scratch, local, sources, step, ahead):
+    rows_ref, hid_ref, pre_ref, acc_ref, term_ref, in_buf, out_buf, in_sem, out_sem = scratch
     count = sources * CAP
-
-    def pick(which):
-        out_row = lax.broadcasted_iota(jnp.int32, (count, local * count), 0)
-        in_row = lax.broadcasted_iota(jnp.int32, (count, local * count), 1)
-        source = out_row // CAP
-        wanted = source * (local * CAP) + which * CAP + (out_row - source * CAP)
-        return jnp.where(in_row == wanted, 1.0, 0.0).astype(bf16)
+    width = x_ref.shape[1]
+    hidden = win_ref.shape[1] // local
+    steps = hidden // step
+    pack = 4 * CAP
+
+    def load_in(e, n):
+        return pltpu.make_async_copy(
+            win_ref.at[:, pl.ds(e * hidden + n * step, step)], in_buf.at[n], in_sem.at[n]
+        )
+
+    def load_out(e, n):
+        return pltpu.make_async_copy(
+            wout_ref.at[pl.ds(e * hidden + n * step, step), :],
+            out_buf.at[pl.ds(n * step, step), :],
+            out_sem.at[n],
+        )
+
+    chain = [load(e, n) for e in range(local) for load in (load_in, load_out) for n in range(steps)]
+
+    def arrive(t):
+        chain[t].wait()
+        if t + ahead < len(chain):
+            chain[t + ahead].start()
+
+    for load in chain[:ahead]:
+        load.start()
 
     if local > 1:
-
-        @pl.when(step == 0)
-        def _():
-            rows_ref[...] = mm(pick(e), x_ref[...]).astype(bf16)
-
-        rows = rows_ref
-    else:
-        rows = x_ref
-
-    @pl.when(step == 0)
-    def _():
-        acc_ref[...] = jnp.zeros_like(acc_ref)
-
-    hidden = gelu(mm(rows[...], win_ref[...])).astype(bf16)
-    acc_ref[...] += mm(hidden, wout_ref[...])
-
-    @pl.when(step == last)
-    def _():
-        if local > 1:
-            term_ref[e] = acc_ref[...].astype(bf16)
-        else:
-            o_ref[...] = acc_ref[...].astype(bf16)
+        to = lax.broadcasted_iota(jnp.int32, (local * pack, local * pack), 0)
+        have = lax.broadcasted_iota(jnp.int32, (local * pack, local * pack), 1)
+        expert = to // pack
+        inner = to - expert * pack
+        source = inner // CAP
+        wanted = source * (local * CAP) + expert * CAP + (inner - source * CAP)
+        order = jnp.where(have == wanted, 1.0, 0.0).astype(bf16)
+        for g in range(count // pack):
+            part = mm(order, x_ref[g * local * pack : (g + 1) * local * pack, :]).astype(bf16)
+            for e in range(local):
+                rows_ref[e, g * pack : (g + 1) * pack, :] = part[e * pack : (e + 1) * pack, :]
+
+    for e in range(local):
+        for n in range(steps):
+            arrive(2 * e * steps + n)
+            rows = rows_ref[e] if local > 1 else x_ref[...]
+            pre_ref[n % 2] = mm(rows, in_buf[n])
+            if n:
+                hid_ref[:, (n - 1) * step : n * step] = gelu(pre_ref[(n - 1) % 2]).astype(bf16)
+        hid_ref[:, (steps - 1) * step :] = gelu(pre_ref[(steps - 1) % 2]).astype(bf16)
+        for n in range(steps):
+            arrive((2 * e + 1) * steps + n)
+            part = mm(hid_ref[:, n * step : (n + 1) * step], out_buf[n * step : (n + 1) * step, :])
+            if n:
+                part = acc_ref[...] + part
+            if n + 1 < steps:
+                acc_ref[...] = part
+            elif local > 1:
+                term_ref[e] = part.astype(bf16)
+            else:
+                o_ref[...] = part.astype(bf16)
 
     if local > 1:
-
-        @pl.when((step == last) & (e == local - 1))
-        def _():
-            total = None
-            for which in range(local):
-                part = mm(pick(which), term_ref[which], (((0,), (0,)), ((), ())))
-                total = part if total is None else total + part
-            o_ref[...] = total.astype(bf16)
-
-
-def expert_call(arrived, w_in, w_out, local, sources, block=512):
+        for g in range(count // pack):
+            part = jnp.concatenate([term_ref[e, g * pack : (g + 1) * pack, :] for e in range(local)], axis=0)
+            back = mm(order, part, (((0,), (0,)), ((), ())))
+            o_ref[g * local * pack : (g + 1) * local * pack, :] = back.astype(bf16)
+
+
+def expert_call(arrived, w_in, w_out, local, sources, step=2048, ahead=2):
     count = sources * CAP
     width = arrived.shape[1]
     hidden = w_in.shape[1] // local
-    steps = hidden // block
-    return pl.pallas_call(
-        functools.partial(expert_kernel, local=local, sources=sources),
-        grid=(local, steps),
+    steps = hidden // step
+    kept = (local, count, width) if local > 1 else (1, 16, 128)
+    vm = pl.BlockSpec(memory_space=pltpu.VMEM)
+    hbm = pl.BlockSpec(memory_space=pl.ANY)
+    return pl.pallas_call(
+        functools.partial(expert_kernel, local=local, sources=sources, step=step, ahead=ahead),
         out_shape=jax.ShapeDtypeStruct(arrived.shape, bf16),
-        in_specs=[
-            pl.BlockSpec(arrived.shape, lambda e, i: (0, 0)),
-            pl.BlockSpec((width, block), lambda e, i: (0, e * steps + i)),
-            pl.BlockSpec((block, width), lambda e, i: (e * steps + i, 0)),
+        in_specs=[vm, hbm, hbm],
+        out_specs=vm,
+        scratch_shapes=[
+            pltpu.VMEM(kept, bf16),
+            pltpu.VMEM((count, hidden), bf16),
+            pltpu.VMEM((2, count, step), f32),
+            pltpu.VMEM((count, width), f32),
+            pltpu.VMEM(kept, bf16),
+            pltpu.VMEM((steps, width, step), bf16),
+            pltpu.VMEM((hidden, width), bf16),
+            pltpu.SemaphoreType.DMA((steps,)),
+            pltpu.SemaphoreType.DMA((steps,)),
         ],
-        out_specs=pl.BlockSpec(arrived.shape, lambda e, i: (0, 0)),
-        scratch_shapes=[
-            pltpu.VMEM((count, width), bf16),
-            pltpu.VMEM((count, width), f32),
-            pltpu.VMEM((local, count, width), bf16),
-        ],
-        compiler_params=params(),
+        compiler_params=params(52),
         cost_estimate=cost(4 * count * width * hidden * local, 4 * width * hidden * local, count * hidden * local),
         name="experts",
     )(arrived, w_in, w_out)
@@ -302,7 +333,7 @@
     rows, width = tokens.shape
     devices = lax.axis_size("ctx")
     groups = lax.axis_size("groups")
-    upper = devices // SPAN
+    lines_total = devices // SPAN
     me = lax.axis_index("ctx")
     member = me % SPAN
     line = me // SPAN
@@ -311,7 +342,7 @@
     local_experts = max(1, EXPERTS // devices)
 
     mine = width // SPAN
-    share = SHARE(groups, mine // HD)
+    share = groups if (mine // HD) % groups == 0 else 1
     cols = mine // share
     offset = (group % share) * cols
 
@@ -320,40 +351,44 @@
             lax.dynamic_slice_in_dim(qkv_weight, t * width + to * mine + offset, cols, 1)
             for t in range(3)
         ]
+        pieces.append(lax.dynamic_slice_in_dim(out_weight, to * mine + offset, cols, 1))
         return jnp.concatenate(pieces, axis=1)
 
     pieces = [columns(member)] + [swap(columns(member ^ j), "ctx", j) for j in range(1, SPAN)]
     block = jnp.zeros((SPAN,) + pieces[0].shape, bf16)
     for j in range(SPAN):
         block = lax.dynamic_update_slice(block, pieces[j][None], (member ^ j, 0, 0))
-    block = block.reshape(-1, 3 * cols)
-    lines = [block] + [swap(block, "ctx", m * SPAN) for m in range(1, upper)]
-    shares = lines
-    for s in range(1, share):
-        shares = shares + [swap(piece, "groups", s) for piece in lines]
-
-    normed = norm_call(tokens)
+    block = block.reshape(-1, 4 * cols)
+    normed, block = lax.optimization_barrier((norm_call(tokens), block))
+    lines = {0: block}
+    bit = lines_total // 2
+    while bit:
+        for known in list(lines):
+            lines[known | bit] = swap(lines[known], "ctx", bit * SPAN)
+        bit //= 2
+    shares = []
+    for s in range(share):
+        shares += [lines[m] if s == 0 else swap(lines[m], "groups", s) for m in range(lines_total)]
+
     far = swap(normed, "ctx", 2)
     near = swap(normed, "ctx", 1)
     both = swap(far, "ctx", 1)
     marks, *gate_parts = route_call(routes, gates)
 
-    projected = project_call(line.reshape(1), [normed, near, far, both], shares, upper, share)
+    place = jnp.stack([line, group % share])
+    projected, part = project_call(place, [normed, near, far, both], shares, lines_total, share)
+    part_far = swap(part, "ctx", 2)
+    part_near = swap(part, "ctx", 1)
+    part_both = swap(part_far, "ctx", 1)
     sent = attend_call(projected, (3, 2), rows)
     back = {3: swap(sent[0], "ctx", 3), 2: swap(sent[1], "ctx", 2)}
     kept = attend_call(projected, (1, 0), rows)
     back[1] = swap(kept[0], "ctx", 1)
     back[0] = kept[1]
-    ctxs = []
-    for j in range(SPAN):
-        if share > 1:
-            split = back[j].reshape(rows, share, cols)
-            order = [lax.dynamic_index_in_dim(split, (group % share) ^ s, 1, keepdims=False) for s in range(share)]
-            ctxs.append(jnp.concatenate(order, axis=1))
-        else:
-            ctxs.append(back[j])
-    whole_out = lax.all_gather(out_weight, "ctx", axis=0, tiled=True)
-    resid, table = output_call(member.reshape(1), tokens, marks, whole_out, ctxs)
+    ctxs = [back[j] for j in range(SPAN)]
+    resid, table = output_call(
+        member.reshape(1), tokens, marks, [part, part_near, part_far, part_both], ctxs
+    )
 
     table = table.reshape(EXPERTS, CAP, width)
     if parts_ff > 1:
@@ -367,10 +402,6 @@
         grouped = returned.reshape(EXPERTS, parts_ff, CAP, width)
         returned = jnp.sum(grouped.astype(f32), axis=1).astype(bf16)
     return combine_call(resid, returned.reshape(EXPERTS * CAP, width), gate_parts)
-
-
-def SHARE(groups, heads):
-    return 1
 
 
 def solution(mesh):

time: 202 us -> 175 us (0.87)
  between operations: 13.6 us -> 0.21 us
  waiting for transfers between devices: 50.6 us -> 42.1 us
  blocking collectives: 79.9 us -> 72.7 us
  starting transfers between devices: 13.6 us -> 20.2 us
  local copies, waits for them, and re-layouts: 3.67 us -> 1.06 us
    ppermute x12 -> x19, waiting for transfers between devices: 49.9 us -> 42.1 us  [swap(): return lax.ppermute(value, axis, [(i, i ^ bits) for i in range(size)])]
    all_to_all x1, blocking collectives: 44.6 us -> 37.4 us  [per_device(): lax.all_to_all(outgoing, 'ctx', split_axis=0, concat_axis=0, tiled=True)]
    ppermute x12 -> x19, starting transfers between devices: 13.6 us -> 20.2 us  [swap(): return lax.ppermute(value, axis, [(i, i ^ bits) for i in range(size)])]
    pallas_call x1, Pallas kernels: 25.1 us -> 19.9 us  [expert_call(): pl.pallas_call(functools.partial(expert_kernel, local=local, sources=sour...]
    pallas_call x2, Pallas kernels: 7.24 us -> 10.2 us  [attend_call(): pl.pallas_call(functools.partial(attend_kernel, blocks=blocks, share=shar...]
    unnamed x10 -> x6, local copies, waits for them, and re-layouts: 2.64 us -> 0.02 us
  transfers between devices with their start and end apart: 13 -> 19, of which waited for: 5 -> 9; matrix products, arithmetic and copies ran while one was open for 1% -> 0% of each run, Pallas kernels for 6% -> 6%
where the time goes in v2:
time: 175 us
  blocking collectives  72.7 us (42%)
  waiting for transfers between devices  42.1 us (24%)
  Pallas kernels  38.7 us (22%)
  starting transfers between devices  20.2 us (12%)
    ppermute x19, waiting for transfers between devices, swap(): return lax.ppermute(value, axis, [(i, i ^ bits) for i in range(size)])  42.1 us
    all_to_all x1, blocking collectives, per_device(): lax.all_to_all(outgoing, 'ctx', split_axis=0, concat_axis=0, tiled=True)  37.4 us
    all_to_all x1, blocking collectives, per_device(): lax.all_to_all(produced, 'ctx', split_axis=0, concat_axis=0, tiled=True)  35.3 us
    ppermute x19, starting transfers between devices, swap(): return lax.ppermute(value, axis, [(i, i ^ bits) for i in range(size)])  20.2 us
    pallas_call x1, Pallas kernels, expert_call(): pl.pallas_call(functools.partial(expert_kernel, local=local, sources=sour...  19.9 us
    pallas_call x2, Pallas kernels, attend_call(): pl.pallas_call(functools.partial(attend_kernel, blocks=blocks, share=shar...  10.2 us
    pallas_call x1, Pallas kernels, project_call(): pl.pallas_call(functools.partial(project_kernel, count=count, lines=lines...  3.76 us
  transfers between devices with their start and end apart: 19, of which 9 were waited for; matrix products, arithmetic and copies ran while one was open for 0% of the time, Pallas kernels for 6%

profile of v2, /device:TPU:1, one launch (start us, length us, event | category | flops | bytes accessed | tf_op | source)
XLA Modules:
  0.0 175.0 jit_solution(1597587346837318523)
XLA Ops:
  0.0 1.0 constant_dynamic-slice_fusion
  1.0 2.1 %collective-permute-start.1 = (bf16[64,512]{1,0:T(8,128)(2,1)S(1)}, bf16[64,512]{1,0:T(8,128)(2,1)S(1)}, u32[]{:S(2)}, u32[]{:S(2)}) collective-permute-start(bf16[64,512]{1,0:T(8,128)(2,1)S(1)} %pad_maximum_fusion.1), channel_id=1, source_target_pairs={{0,2},{1,3},{2,0},{3,1},{4,6},{5,7},{6,4},{7,5},{8,10},{9,11},{10,... | collective-permute-start | bytes 196616 | tf_op jit(solution)/shard_map/ppermute | solution.py:329
  3.2 1.0 collective-permute-start
  5.1 2.9 %collective-permute-done.2 = bf16[64,512]{1,0:T(8,128)(2,1)S(1)} collective-permute-done((bf16[64,512]{1,0:T(8,128)(2,1)S(1)}, bf16[64,512]{1,0:T(8,128)(2,1)S(1)}, u32[]{:S(2)}, u32[]{:S(2)}) %collective-permute-start.2) | collective-permute-done | bytes 65568 | tf_op jit(solution)/shard_map/ppermute | solution.py:329
  8.0 0.9 collective-permute-start.4
  8.9 2.3 %collective-permute-start.7 = (bf16[256,512]{1,0:T(8,128)(2,1)S(1)}, bf16[256,512]{1,0:T(8,128)(2,1)S(1)}, u32[]{:S(2)}, u32[]{:S(2)}) collective-permute-start(bf16[256,512]{1,0:T(8,128)(2,1)S(1)} %bitcast.23), channel_id=1, source_target_pairs={{0,8},{1,9},{2,10},{3,11},{4,12},{5,13},{6,14},{7,15},{8,0},{9,1},... | collective-permute-start | bytes 786440 | tf_op jit(solution)/shard_map/ppermute | solution.py:329
  11.2 1.2 collective-permute-start.9
  12.4 1.3 collective-permute-start.6
  13.7 1.2 collective-permute-start.3
  14.9 8.1 %collective-permute-done.7.refs_6_ = bf16[256,512]{1,0:T(8,128)(2,1)S(1)} collective-permute-done((bf16[256,512]{1,0:T(8,128)(2,1)S(1)}, bf16[256,512]{1,0:T(8,128)(2,1)S(1)}, u32[]{:S(2)}, u32[]{:S(2)}) %collective-permute-start.7) | collective-permute-done | bytes 262176 | tf_op jit(solution)/shard_map/ppermute | solution.py:329
  23.0 1.1 collective-permute-start.8
  24.1 0.8 collective-permute-start.5
  24.9 1.2 collective-permute-start.11
  26.4 3.4 %collective-permute-done.8.refs_7_ = bf16[256,512]{1,0:T(8,128)(2,1)} collective-permute-done((bf16[256,512]{1,0:T(8,128)(2,1)S(1)}, bf16[256,512]{1,0:T(8,128)(2,1)}, u32[]{:S(2)}, u32[]{:S(2)}) %collective-permute-start.8) | collective-permute-done | bytes 262176 | tf_op jit(solution)/shard_map/ppermute | solution.py:329
  29.8 1.1 collective-permute-start.12
  30.9 1.9 %collective-permute-done.11.refs_10_ = bf16[256,512]{1,0:T(8,128)(2,1)} collective-permute-done((bf16[256,512]{1,0:T(8,128)(2,1)S(1)}, bf16[256,512]{1,0:T(8,128)(2,1)}, u32[]{:S(2)}, u32[]{:S(2)}) %collective-permute-start.11) | collective-permute-done | bytes 262176 | tf_op jit(solution)/shard_map/ppermute | solution.py:329
  32.8 5.6 %collective-permute-done.10.refs_9_ = bf16[256,512]{1,0:T(8,128)(2,1)} collective-permute-done((bf16[256,512]{1,0:T(8,128)(2,1)}, bf16[256,512]{1,0:T(8,128)(2,1)}, u32[]{:S(2)}, u32[]{:S(2)}) %collective-permute-start.10) | collective-permute-done | bytes 262176 | tf_op jit(solution)/shard_map/ppermute | solution.py:329
  38.5 5.6 %collective-permute-done.12.refs_11_ = bf16[256,512]{1,0:T(8,128)(2,1)} collective-permute-done((bf16[256,512]{1,0:T(8,128)(2,1)}, bf16[256,512]{1,0:T(8,128)(2,1)}, u32[]{:S(2)}, u32[]{:S(2)}) %collective-permute-start.12) | collective-permute-done | bytes 262176 | tf_op jit(solution)/shard_map/ppermute | solution.py:329
  44.1 3.8 %project.1 = (bf16[2,1024,384]{2,1,0:T(8,128)(2,1)S(1)}, bf16[1024,256]{1,0:T(8,128)(2,1)S(1)}) custom-call(s32[2]{0:T(128)S(1)} %pad_add_fusion.place_ref, bf16[256,1024]{1,0:T(8,128)(2,1)S(1)} %norm_tokens.1.refs_0_, bf16[256,1024]{1,0:T(8,128)(2,1)S(1)} %collective-permute-done.3.refs_1_, bf16[256,1024]{1,0:T(8,128)(2,1)S(1)} %collective-permute-done.4.refs_2_, ...), custom_call_target="tpu_custom_call" | custom-call | flops 1610612736 | bytes 6291456 | tf_op jit(solution)/shard_map/project/pallas_call | solution.py:121
  48.5 1.1 collective-permute-start.16
  49.7 10.8 %collective-permute-done.17.refs_6_ = bf16[1024,256]{1,0:T(8,128)(2,1)S(1)} collective-permute-done((bf16[1024,256]{1,0:T(8,128)(2,1)S(1)}, bf16[1024,256]{1,0:T(8,128)(2,1)S(1)}, u32[]{:S(2)}, u32[]{:S(2)}) %collective-permute-start.17) | collective-permute-done | bytes 524320 | tf_op jit(solution)/shard_map/ppermute | solution.py:329
  60.5 1.8 %collective-permute-start.18 = (bf16[1024,256]{1,0:T(8,128)(2,1)S(1)}, bf16[1024,256]{1,0:T(8,128)(2,1)S(1)}, u32[]{:S(2)}, u32[]{:S(2)}) collective-permute-start(bf16[1024,256]{1,0:T(8,128)(2,1)S(1)} %collective-permute-done.17.refs_6_), channel_id=1, source_target_pairs={{0,1},{1,0},{2,3},{3,2},{4,5},{5,4},{6,7},{7,6},{8,9},{9,8},{10,11... | collective-permute-start | bytes 1572872 | tf_op jit(solution)/shard_map/ppermute | solution.py:329
  62.3 5.0 %attend.3 = (bf16[256,256]{1,0:T(8,128)(2,1)S(1)}, bf16[256,256]{1,0:T(8,128)(2,1)S(1)}) custom-call(bf16[2,1024,384]{2,1,0:T(8,128)(2,1)S(1)} %get-tuple-element.22.p_ref), custom_call_target="tpu_custom_call" | custom-call | flops 2147483648 | bytes 3145728 | tf_op jit(solution)/shard_map/attend/pallas_call | solution.py:161
  68.0 5.2 %attend.2 = (bf16[256,256]{1,0:T(8,128)(2,1)S(1)}, bf16[256,256]{1,0:T(8,128)(2,1)S(1)}) custom-call(bf16[2,1024,384]{2,1,0:T(8,128)(2,1)S(1)} %get-tuple-element.22.p_ref), custom_call_target="tpu_custom_call" | custom-call | flops 2147483648 | bytes 3145728 | tf_op jit(solution)/shard_map/attend/pallas_call | solution.py:161
  73.2 1.1 collective-permute-start.15
  74.5 0.7 route_slots.1
  75.2 3.4 %collective-permute-done.15.refs_3_ = bf16[256,256]{1,0:T(8,128)(2,1)S(1)} collective-permute-done((bf16[256,256]{1,0:T(8,128)(2,1)S(1)}, bf16[256,256]{1,0:T(8,128)(2,1)S(1)}, u32[]{:S(2)}, u32[]{:S(2)}) %collective-permute-start.15) | collective-permute-done | bytes 131104 | tf_op jit(solution)/shard_map/ppermute | solution.py:329
  78.7 1.6 out_projection.1
  80.3 37.4 %all_to_all.10 = bf16[16,40,1024]{2,1,0:T(8,128)(2,1)} all-to-all(bf16[16,40,1024]{2,1,0:T(8,128)(2,1)S(1)} %bitcast.21), channel_id=1, replica_groups=mesh['groups'=2,'ctx'=16] {'ctx'}, dimensions={0} | all-to-all | bytes 2621440 | tf_op jit(solution)/shard_map/all_to_all | solution.py:397
  117.6 19.9 %experts.1 = bf16[640,1024]{1,0:T(8,128)(2,1)S(1)} custom-call(bf16[640,1024]{1,0:T(8,128)(2,1)} %bitcast.29, bf16[1024,8192]{1,0:T(8,128)(2,1)} %win_ref.1, bf16[8192,1024]{1,0:T(8,128)(2,1)} %wout_ref.1), custom_call_target="tpu_custom_call" | custom-call | flops 10737418240 | bytes 33554432 | tf_op jit(solution)/shard_map/experts/pallas_call | solution.py:286
  137.5 35.3 %all_to_all.11 = bf16[16,40,1024]{2,1,0:T(8,128)(2,1)S(1)} all-to-all(bf16[16,40,1024]{2,1,0:T(8,128)(2,1)S(1)} %bitcast.22), channel_id=1, replica_groups=mesh['groups'=2,'ctx'=16] {'ctx'}, dimensions={0} | all-to-all | bytes 2621440 | tf_op jit(solution)/shard_map/all_to_all | solution.py:400
  172.8 2.2 %combine.1 = bf16[256,1024]{1,0:T(8,128)(2,1)} custom-call(f32[256,1024]{1,0:T(8,128)S(1)} %get-tuple-element.28.r_ref, bf16[640,1024]{1,0:T(8,128)(2,1)S(1)} %bitcast.20, bf16[640,256]{1,0:T(8,128)(2,1)S(1)} %get-tuple-element.30.hi_ref, bf16[640,256]{1,0:T(8,128)(2,1)S(1)} %get-tuple-element.31.mid_ref, bf16[640,256]{1,0:T(8,128)(2,1)S(1)} %get-tuple-element.32.lo_ref), custom_call_target="tpu_custom_call" | custom-call | flops 1006632960 | bytes 2883584 | tf_op jit(solution)/shard_map/combine/pallas_call | solution.py:318
  (32 shorter events, 2.9 us)
Async XLA Ops:
  0.0 4.3 %copy-start = (bf16[256,1024]{1,0:T(8,128)(2,1)S(1)}, bf16[256,1024]{1,0:T(8,128)(2,1)}, u32[]{:S(2)}) copy-start(bf16[256,1024]{1,0:T(8,128)(2,1)} %t_ref.1) | copy-start | bytes 1572868
  1.0 4.1 %collective-permute-start.1 = (bf16[64,512]{1,0:T(8,128)(2,1)S(1)}, bf16[64,512]{1,0:T(8,128)(2,1)S(1)}, u32[]{:S(2)}, u32[]{:S(2)}) collective-permute-start(bf16[64,512]{1,0:T(8,128)(2,1)S(1)} %pad_maximum_fusion.1), channel_id=1, source_target_pairs={{0,2},{1,3},{2,0},{3,1},{4,6},{5,7},{6,4},{7,5},{8,10},{9,11},{10,... | collective-permute-start | bytes 196616 | tf_op jit(solution)/shard_map/ppermute | solution.py:329
  3.2 1.9 %collective-permute-start = (bf16[64,512]{1,0:T(8,128)(2,1)S(1)}, bf16[64,512]{1,0:T(8,128)(2,1)S(1)}, u32[]{:S(2)}, u32[]{:S(2)}) collective-permute-start(bf16[64,512]{1,0:T(8,128)(2,1)S(1)} %pad_maximum_fusion), channel_id=1, source_target_pairs={{0,1},{1,0},{2,3},{3,2},{4,5},{5,4},{6,7},{7,6},{8,9},{9,8},{10,11... | collective-permute-start | bytes 196616 | tf_op jit(solution)/shard_map/ppermute | solution.py:329
  4.2 3.8 %collective-permute-start.2 = (bf16[64,512]{1,0:T(8,128)(2,1)S(1)}, bf16[64,512]{1,0:T(8,128)(2,1)S(1)}, u32[]{:S(2)}, u32[]{:S(2)}) collective-permute-start(bf16[64,512]{1,0:T(8,128)(2,1)S(1)} %pad_maximum_fusion.2), channel_id=1, source_target_pairs={{0,3},{1,2},{2,1},{3,0},{4,7},{5,6},{6,5},{7,4},{8,11},{9,10},{10,... | collective-permute-start | bytes 196616 | tf_op jit(solution)/shard_map/ppermute | solution.py:329
  8.0 16.1 %collective-permute-start.4 = (bf16[256,1024]{1,0:T(8,128)(2,1)S(1)}, bf16[256,1024]{1,0:T(8,128)(2,1)S(1)}, u32[]{:S(2)}, u32[]{:S(2)}) collective-permute-start(bf16[256,1024]{1,0:T(8,128)(2,1)S(1)} %norm_tokens.1.refs_0_), channel_id=1, source_target_pairs={{0,2},{1,3},{2,0},{3,1},{4,6},{5,7},{6,4},{7,5},{8,10},{9,11},{10,... | collective-permute-start | bytes 1572872 | tf_op jit(solution)/shard_map/ppermute | solution.py:329
  8.9 14.2 %collective-permute-start.7 = (bf16[256,512]{1,0:T(8,128)(2,1)S(1)}, bf16[256,512]{1,0:T(8,128)(2,1)S(1)}, u32[]{:S(2)}, u32[]{:S(2)}) collective-permute-start(bf16[256,512]{1,0:T(8,128)(2,1)S(1)} %bitcast.23), channel_id=1, source_target_pairs={{0,8},{1,9},{2,10},{3,11},{4,12},{5,13},{6,14},{7,15},{8,0},{9,1},... | collective-permute-start | bytes 786440 | tf_op jit(solution)/shard_map/ppermute | solution.py:329
  11.2 13.7 %collective-permute-start.9 = (bf16[256,512]{1,0:T(8,128)(2,1)S(1)}, bf16[256,512]{1,0:T(8,128)(2,1)S(1)}, u32[]{:S(2)}, u32[]{:S(2)}) collective-permute-start(bf16[256,512]{1,0:T(8,128)(2,1)S(1)} %bitcast.24), channel_id=1, source_target_pairs={{0,16},{16,0},{1,17},{17,1},{2,18},{18,2},{3,19},{19,3},{4,20},{20... | collective-permute-start | bytes 786440 | tf_op jit(solution)/shard_map/ppermute | solution.py:329
  12.4 13.6 %collective-permute-start.6 = (bf16[256,512]{1,0:T(8,128)(2,1)S(1)}, bf16[256,512]{1,0:T(8,128)(2,1)}, u32[]{:S(2)}, u32[]{:S(2)}) collective-permute-start(bf16[256,512]{1,0:T(8,128)(2,1)S(1)} %bitcast.25), channel_id=1, source_target_pairs={{0,4},{1,5},{2,6},{3,7},{4,0},{5,1},{6,2},{7,3},{8,12},{9,13},{10,... | collective-permute-start | bytes 786440 | tf_op jit(solution)/shard_map/ppermute | solution.py:329
  13.7 24.7 %collective-permute-start.3 = (bf16[256,1024]{1,0:T(8,128)(2,1)S(1)}, bf16[256,1024]{1,0:T(8,128)(2,1)S(1)}, u32[]{:S(2)}, u32[]{:S(2)}) collective-permute-start(bf16[256,1024]{1,0:T(8,128)(2,1)S(1)} %norm_tokens.1.refs_0_), channel_id=1, source_target_pairs={{0,1},{1,0},{2,3},{3,2},{4,5},{5,4},{6,7},{7,6},{8,9},{9,8},{10,11... | collective-permute-start | bytes 1572872 | tf_op jit(solution)/shard_map/ppermute | solution.py:329
  23.0 6.7 %collective-permute-start.8 = (bf16[256,512]{1,0:T(8,128)(2,1)S(1)}, bf16[256,512]{1,0:T(8,128)(2,1)}, u32[]{:S(2)}, u32[]{:S(2)}) collective-permute-start(bf16[256,512]{1,0:T(8,128)(2,1)S(1)} %collective-permute-done.7.refs_6_), channel_id=1, source_target_pairs={{0,4},{1,5},{2,6},{3,7},{4,0},{5,1},{6,2},{7,3},{8,12},{9,13},{10,... | collective-permute-start | bytes 786440 | tf_op jit(solution)/shard_map/ppermute | solution.py:329
  24.1 20.0 %collective-permute-start.5 = (bf16[256,1024]{1,0:T(8,128)(2,1)S(1)}, bf16[256,1024]{1,0:T(8,128)(2,1)S(1)}, u32[]{:S(2)}, u32[]{:S(2)}) collective-permute-start(bf16[256,1024]{1,0:T(8,128)(2,1)S(1)} %collective-permute-done.4.refs_2_), channel_id=1, source_target_pairs={{0,1},{1,0},{2,3},{3,2},{4,5},{5,4},{6,7},{7,6},{8,9},{9,8},{10,11... | collective-permute-start | bytes 1572872 | tf_op jit(solution)/shard_map/ppermute | solution.py:329
  24.9 8.0 %collective-permute-start.11 = (bf16[256,512]{1,0:T(8,128)(2,1)S(1)}, bf16[256,512]{1,0:T(8,128)(2,1)}, u32[]{:S(2)}, u32[]{:S(2)}) collective-permute-start(bf16[256,512]{1,0:T(8,128)(2,1)S(1)} %collective-permute-done.7.refs_6_), channel_id=1, source_target_pairs={{0,16},{16,0},{1,17},{17,1},{2,18},{18,2},{3,19},{19,3},{4,20},{20... | collective-permute-start | bytes 786440 | tf_op jit(solution)/shard_map/ppermute | solution.py:329
  26.0 12.4 %collective-permute-start.10 = (bf16[256,512]{1,0:T(8,128)(2,1)}, bf16[256,512]{1,0:T(8,128)(2,1)}, u32[]{:S(2)}, u32[]{:S(2)}) collective-permute-start(bf16[256,512]{1,0:T(8,128)(2,1)} %collective-permute-done.6.refs_5_), channel_id=1, source_target_pairs={{0,16},{16,0},{1,17},{17,1},{2,18},{18,2},{3,19},{19,3},{4,20},{20... | collective-permute-start | bytes 786440 | tf_op jit(solution)/shard_map/ppermute | solution.py:329
  29.8 14.3 %collective-permute-start.12 = (bf16[256,512]{1,0:T(8,128)(2,1)}, bf16[256,512]{1,0:T(8,128)(2,1)}, u32[]{:S(2)}, u32[]{:S(2)}) collective-permute-start(bf16[256,512]{1,0:T(8,128)(2,1)} %collective-permute-done.8.refs_7_), channel_id=1, source_target_pairs={{0,16},{16,0},{1,17},{17,1},{2,18},{18,2},{3,19},{19,3},{4,20},{20... | collective-permute-start | bytes 786440 | tf_op jit(solution)/shard_map/ppermute | solution.py:329
  47.9 12.6 %collective-permute-start.17 = (bf16[1024,256]{1,0:T(8,128)(2,1)S(1)}, bf16[1024,256]{1,0:T(8,128)(2,1)S(1)}, u32[]{:S(2)}, u32[]{:S(2)}) collective-permute-start(bf16[1024,256]{1,0:T(8,128)(2,1)S(1)} %get-tuple-element.27.refs_4_), channel_id=1, source_target_pairs={{0,2},{1,3},{2,0},{3,1},{4,6},{5,7},{6,4},{7,5},{8,10},{9,11},{10,... | collective-permute-start | bytes 1572872 | tf_op jit(solution)/shard_map/ppermute | solution.py:329
  48.5 30.1 %collective-permute-start.16 = (bf16[1024,256]{1,0:T(8,128)(2,1)S(1)}, bf16[1024,256]{1,0:T(8,128)(2,1)S(1)}, u32[]{:S(2)}, u32[]{:S(2)}) collective-permute-start(bf16[1024,256]{1,0:T(8,128)(2,1)S(1)} %get-tuple-element.27.refs_4_), channel_id=1, source_target_pairs={{0,1},{1,0},{2,3},{3,2},{4,5},{5,4},{6,7},{7,6},{8,9},{9,8},{10,11... | collective-permute-start | bytes 1572872 | tf_op jit(solution)/shard_map/ppermute | solution.py:329
  60.5 18.2 %collective-permute-start.18 = (bf16[1024,256]{1,0:T(8,128)(2,1)S(1)}, bf16[1024,256]{1,0:T(8,128)(2,1)S(1)}, u32[]{:S(2)}, u32[]{:S(2)}) collective-permute-start(bf16[1024,256]{1,0:T(8,128)(2,1)S(1)} %collective-permute-done.17.refs_6_), channel_id=1, source_target_pairs={{0,1},{1,0},{2,3},{3,2},{4,5},{5,4},{6,7},{7,6},{8,9},{9,8},{10,11... | collective-permute-start | bytes 1572872 | tf_op jit(solution)/shard_map/ppermute | solution.py:329
  67.3 7.2 %copy-start.1 = (s32[256,2]{0,1:T(2,128)S(1)}, s32[256,2]{0,1:T(2,128)}, u32[]{:S(2)}) copy-start(s32[256,2]{0,1:T(2,128)} %param.8) | copy-start | bytes 6148
  67.3 7.2 %copy-start.2 = (f32[256,2]{0,1:T(2,128)S(1)}, f32[256,2]{0,1:T(2,128)}, u32[]{:S(2)}) copy-start(f32[256,2]{0,1:T(2,128)} %param.9) | copy-start | bytes 6148
  67.3 7.9 %collective-permute-start.14 = (bf16[256,256]{1,0:T(8,128)(2,1)S(1)}, bf16[256,256]{1,0:T(8,128)(2,1)S(1)}, u32[]{:S(2)}, u32[]{:S(2)}) collective-permute-start(bf16[256,256]{1,0:T(8,128)(2,1)S(1)} %get-tuple-element.25), channel_id=1, source_target_pairs={{0,2},{1,3},{2,0},{3,1},{4,6},{5,7},{6,4},{7,5},{8,10},{9,11},{10,... | collective-permute-start | bytes 393224 | tf_op jit(solution)/shard_map/ppermute | solution.py:329
  73.2 5.5 %collective-permute-start.15 = (bf16[256,256]{1,0:T(8,128)(2,1)S(1)}, bf16[256,256]{1,0:T(8,128)(2,1)S(1)}, u32[]{:S(2)}, u32[]{:S(2)}) collective-permute-start(bf16[256,256]{1,0:T(8,128)(2,1)S(1)} %get-tuple-element.26), channel_id=1, source_target_pairs={{0,3},{1,2},{2,1},{3,0},{4,7},{5,6},{6,5},{7,4},{8,11},{9,10},{10,... | collective-permute-start | bytes 393224 | tf_op jit(solution)/shard_map/ppermute | solution.py:329
  74.3 4.4 %collective-permute-start.13 = (bf16[256,256]{1,0:T(8,128)(2,1)S(1)}, bf16[256,256]{1,0:T(8,128)(2,1)S(1)}, u32[]{:S(2)}, u32[]{:S(2)}) collective-permute-start(bf16[256,256]{1,0:T(8,128)(2,1)S(1)} %get-tuple-element.24), channel_id=1, source_target_pairs={{0,1},{1,0},{2,3},{3,2},{4,5},{5,4},{6,7},{7,6},{8,9},{9,8},{10,11... | collective-permute-start | bytes 393224 | tf_op jit(solution)/shard_map/ppermute | solution.py:329

commit v3 on v2

--- a/solution.py
+++ b/solution.py
@@ -1,4 +1,5 @@
 import functools
+import math
 
 import jax
 import jax.numpy as jnp
@@ -106,9 +107,14 @@
         for m in range(lines):
             start = pl.multiple_of((place_ref[0] ^ m) * size, size)
             full[place_ref[1] ^ s, pl.ds(start, size), :] = ws[s * lines + m][...]
+    mine = share * cols
     for s in range(share):
         for j in range(count):
-            o_ref[s, j * rows : (j + 1) * rows, :] = mm(xs[j][...], full[s, :, : 3 * cols]).astype(bf16)
+            got = mm(xs[j][...], full[s, :, : 3 * cols]).astype(bf16)
+            for t in range(3):
+                o_ref[j * rows : (j + 1) * rows, t * mine + s * cols : t * mine + (s + 1) * cols] = got[
+                    :, t * cols : (t + 1) * cols
+                ]
         part_ref[:, s * cols : (s + 1) * cols] = full[s, :, 3 * cols :]
 
 
@@ -121,7 +127,7 @@
     return pl.pallas_call(
         functools.partial(project_kernel, count=count, lines=lines, share=share),
         out_shape=[
-            jax.ShapeDtypeStruct((share, count * rows, 3 * cols), bf16),
+            jax.ShapeDtypeStruct((count * rows, 3 * share * cols), bf16),
             jax.ShapeDtypeStruct((width, share * cols), bf16),
         ],
         in_specs=[pl.BlockSpec(memory_space=pltpu.SMEM)] + [vm] * (count + lines * share),
@@ -133,37 +139,34 @@
     )(place, *xs, *ws)
 
 
-def attend_kernel(p_ref, *o_refs, blocks, share):
-    cols = p_ref.shape[2] // 3
+def attend_kernel(p_ref, *o_refs, blocks):
+    cols = p_ref.shape[1] // 3
     rows = o_refs[0].shape[0]
-    heads = cols // HD
     lane = lax.broadcasted_iota(jnp.int32, (rows, cols), 1) // HD
+    keys = p_ref[:, cols : 2 * cols]
+    values = p_ref[:, 2 * cols :]
     for o_ref, j in zip(o_refs, blocks):
-        for s in range(share):
-            queries = p_ref[s, j * rows : (j + 1) * rows, :cols] * jnp.asarray(HD ** (-0.5), bf16)
-            keys = p_ref[s, :, cols : 2 * cols]
-            values = p_ref[s, :, 2 * cols :]
-            mixed = None
-            for h in range(heads):
-                mine = lane == h
-                q = jnp.where(mine, queries, jnp.zeros_like(queries)) if heads > 1 else queries
-                scores = mm(q, keys, (((1,), (1,)), ((), ())))
-                weights = jnp.exp(scores - jnp.max(scores, axis=-1, keepdims=True))
-                probs = (weights * (1.0 / jnp.sum(weights, axis=-1, keepdims=True))).astype(bf16)
-                part = mm(probs, values)
-                mixed = part if mixed is None else jnp.where(mine, part, mixed)
-            o_ref[:, s * cols : (s + 1) * cols] = mixed.astype(bf16)
+        queries = p_ref[j * rows : (j + 1) * rows, :cols] * jnp.asarray(HD ** (-0.5), bf16)
+        mixed = None
+        for h in range(cols // HD):
+            mine = lane == h
+            q = jnp.where(mine, queries, jnp.zeros_like(queries))
+            scores = mm(q, keys, (((1,), (1,)), ((), ())))
+            weights = jnp.exp(scores - jnp.max(scores, axis=-1, keepdims=True))
+            probs = (weights * (1.0 / jnp.sum(weights, axis=-1, keepdims=True))).astype(bf16)
+            part = mm(probs, values)
+            mixed = part if mixed is None else jnp.where(mine, part, mixed)
+        o_ref[...] = mixed.astype(bf16)
 
 
 def attend_call(projected, blocks, rows):
-    share, length, cols = projected.shape
-    width = share * cols // 3
-    return pl.pallas_call(
-        functools.partial(attend_kernel, blocks=blocks, share=share),
+    length, width = projected.shape[0], projected.shape[1] // 3
+    return pl.pallas_call(
+        functools.partial(attend_kernel, blocks=blocks),
         out_shape=[jax.ShapeDtypeStruct((rows, width), bf16)] * len(blocks),
-        compiler_params=params(),
+        compiler_params=params(24),
         cost_estimate=cost(
-            16 * len(blocks) * rows * length * width, 4 * projected.size, len(blocks) * rows * length * width // HD
+            16 * len(blocks) * rows * length * width, 2 * projected.size, len(blocks) * rows * length * width // HD
         ),
         name="attend",
     )(projected)
@@ -325,7 +328,7 @@
 
 
 def swap(value, axis, bits):
-    size = lax.axis_size(axis)
+    size = math.prod(lax.axis_size(name) for name in axis) if isinstance(axis, tuple) else lax.axis_size(axis)
     return lax.ppermute(value, axis, [(i, i ^ bits) for i in range(size)])
 
 
@@ -366,9 +369,9 @@
         for known in list(lines):
             lines[known | bit] = swap(lines[known], "ctx", bit * SPAN)
         bit //= 2
-    shares = []
-    for s in range(share):
-        shares += [lines[m] if s == 0 else swap(lines[m], "groups", s) for m in range(lines_total)]
+    shares = [lines[m] for m in range(lines_total)]
+    for s in range(1, share):
+        shares += [swap(block, ("groups", "ctx"), s * devices + m * SPAN) if m < 2 else swap(lines[m], "groups", s) for m in range(lines_total)]
 
     far = swap(normed, "ctx", 2)
     near = swap(normed, "ctx", 1)
@@ -379,10 +382,12 @@
     projected, part = project_call(place, [normed, near, far, both], shares, lines_total, share)
     part_far = swap(part, "ctx", 2)
     part_near = swap(part, "ctx", 1)
-    part_both = swap(part_far, "ctx", 1)
     sent = attend_call(projected, (3, 2), rows)
     back = {3: swap(sent[0], "ctx", 3), 2: swap(sent[1], "ctx", 2)}
+    projected, *sent = lax.optimization_barrier((projected, *sent))
     kept = attend_call(projected, (1, 0), rows)
+    kept, part_far = lax.optimization_barrier((kept, part_far))
+    part_both = swap(part_far, "ctx", 1)
     back[1] = swap(kept[0], "ctx", 1)
     back[0] = kept[1]
     ctxs = [back[j] for j in range(SPAN)]

time: 175 us -> 163 us (0.931)
  waiting for transfers between devices: 42.1 us -> 25.7 us
  starting transfers between devices: 20.2 us -> 24.2 us
  Pallas kernels: 38.7 us -> 36.3 us
    ppermute x19, waiting for transfers between devices: 42.1 us -> 25.7 us  [swap(): return lax.ppermute(value, axis, [(i, i ^ bits) for i in range(size)])]
    ppermute x19, starting transfers between devices: 20.2 us -> 24.2 us  [swap(): return lax.ppermute(value, axis, [(i, i ^ bits) for i in range(size)])]
    pallas_call x2, Pallas kernels: 10.2 us -> 7.68 us  [attend_call(): pl.pallas_call(functools.partial(attend_kernel, blocks=blocks), out_shape...]
  transfers between devices with their start and end apart: 19 -> 19, of which waited for: 9 -> 8; matrix products, arithmetic and copies ran while one was open for 0% -> 0% of each run, Pallas kernels for 6% -> 5%
where the time goes in v3:
time: 163 us
  blocking collectives  73.3 us (45%)
  Pallas kernels  36.3 us (22%)
  waiting for transfers between devices  25.7 us (16%)
  starting transfers between devices  24.2 us (15%)
  local copies, waits for them, and re-layouts  2.71 us (2%)
    all_to_all x1, blocking collectives, per_device(): lax.all_to_all(outgoing, 'ctx', split_axis=0, concat_axis=0, tiled=True)  38 us
    all_to_all x1, blocking collectives, per_device(): lax.all_to_all(produced, 'ctx', split_axis=0, concat_axis=0, tiled=True)  35.3 us
    ppermute x19, waiting for transfers between devices, swap(): return lax.ppermute(value, axis, [(i, i ^ bits) for i in range(size)])  25.7 us
    ppermute x19, starting transfers between devices, swap(): return lax.ppermute(value, axis, [(i, i ^ bits) for i in range(size)])  24.2 us
    pallas_call x1, Pallas kernels, expert_call(): pl.pallas_call(functools.partial(expert_kernel, local=local, sources=sour...  19.9 us
    pallas_call x2, Pallas kernels, attend_call(): pl.pallas_call(functools.partial(attend_kernel, blocks=blocks), out_shape...  7.68 us
    pallas_call x1, Pallas kernels, project_call(): pl.pallas_call(functools.partial(project_kernel, count=count, lines=lines...  3.69 us
  transfers between devices with their start and end apart: 19, of which 8 were waited for; matrix products, arithmetic and copies ran while one was open for 0% of the time, Pallas kernels for 5%

profile of v3, /device:TPU:1, one launch (start us, length us, event | category | flops | bytes accessed | tf_op | source)
XLA Modules:
  0.0 162.6 jit_solution(659529177806311652)
XLA Ops:
  0.0 1.0 constant_dynamic-slice_fusion
  1.0 2.1 %collective-permute-start.1 = (bf16[64,512]{1,0:T(8,128)(2,1)S(1)}, bf16[64,512]{1,0:T(8,128)(2,1)S(1)}, u32[]{:S(2)}, u32[]{:S(2)}) collective-permute-start(bf16[64,512]{1,0:T(8,128)(2,1)S(1)} %pad_maximum_fusion.1), channel_id=1, source_target_pairs={{0,2},{1,3},{2,0},{3,1},{4,6},{5,7},{6,4},{7,5},{8,10},{9,11},{10,... | collective-permute-start | bytes 196616 | tf_op jit(solution)/shard_map/ppermute | solution.py:332
  3.2 1.0 collective-permute-start
  5.1 2.9 %collective-permute-done.2 = bf16[64,512]{1,0:T(8,128)(2,1)S(1)} collective-permute-done((bf16[64,512]{1,0:T(8,128)(2,1)S(1)}, bf16[64,512]{1,0:T(8,128)(2,1)S(1)}, u32[]{:S(2)}, u32[]{:S(2)}) %collective-permute-start.2) | collective-permute-done | bytes 65568 | tf_op jit(solution)/shard_map/ppermute | solution.py:332
  8.0 0.9 collective-permute-start.4
  8.9 2.3 %collective-permute-start.7 = (bf16[256,512]{1,0:T(8,128)(2,1)S(1)}, bf16[256,512]{1,0:T(8,128)(2,1)S(1)}, u32[]{:S(2)}, u32[]{:S(2)}) collective-permute-start(bf16[256,512]{1,0:T(8,128)(2,1)S(1)} %bitcast.23), channel_id=1, source_target_pairs={{0,8},{1,9},{2,10},{3,11},{4,12},{5,13},{6,14},{7,15},{8,0},{9,1},... | collective-permute-start | bytes 786440 | tf_op jit(solution)/shard_map/ppermute | solution.py:332
  11.2 2.2 %collective-permute-start.10 = (bf16[256,512]{1,0:T(8,128)(2,1)S(1)}, bf16[256,512]{1,0:T(8,128)(2,1)S(1)}, u32[]{:S(2)}, u32[]{:S(2)}) collective-permute-start(bf16[256,512]{1,0:T(8,128)(2,1)S(1)} %bitcast.24), channel_id=1, source_target_pairs={{0,20},{1,21},{2,22},{3,23},{4,16},{5,17},{6,18},{7,19},{8,28},{9,... | collective-permute-start | bytes 786440 | tf_op jit(solution)/shard_map/ppermute | solution.py:332
  13.7 1.2 collective-permute-start.3
  14.9 8.1 %collective-permute-done.7.refs_6_ = bf16[256,512]{1,0:T(8,128)(2,1)S(1)} collective-permute-done((bf16[256,512]{1,0:T(8,128)(2,1)S(1)}, bf16[256,512]{1,0:T(8,128)(2,1)S(1)}, u32[]{:S(2)}, u32[]{:S(2)}) %collective-permute-start.7) | collective-permute-done | bytes 262176 | tf_op jit(solution)/shard_map/ppermute | solution.py:332
  23.0 1.1 collective-permute-start.8
  24.1 0.8 collective-permute-start.5
  24.9 1.1 collective-permute-start.6
  26.7 1.2 collective-permute-start.11
  27.9 1.9 %collective-permute-done.8.refs_7_ = bf16[256,512]{1,0:T(8,128)(2,1)} collective-permute-done((bf16[256,512]{1,0:T(8,128)(2,1)S(1)}, bf16[256,512]{1,0:T(8,128)(2,1)}, u32[]{:S(2)}, u32[]{:S(2)}) %collective-permute-start.8) | collective-permute-done | bytes 262176 | tf_op jit(solution)/shard_map/ppermute | solution.py:332
  29.8 1.1 collective-permute-start.12
  31.0 4.4 %collective-permute-done.6.refs_5_ = bf16[256,512]{1,0:T(8,128)(2,1)} collective-permute-done((bf16[256,512]{1,0:T(8,128)(2,1)S(1)}, bf16[256,512]{1,0:T(8,128)(2,1)}, u32[]{:S(2)}, u32[]{:S(2)}) %collective-permute-start.6) | collective-permute-done | bytes 262176 | tf_op jit(solution)/shard_map/ppermute | solution.py:332
  35.4 3.3 %collective-permute-done.12.refs_11_ = bf16[256,512]{1,0:T(8,128)(2,1)} collective-permute-done((bf16[256,512]{1,0:T(8,128)(2,1)}, bf16[256,512]{1,0:T(8,128)(2,1)}, u32[]{:S(2)}, u32[]{:S(2)}) %collective-permute-start.12) | collective-permute-done | bytes 262176 | tf_op jit(solution)/shard_map/ppermute | solution.py:332
  38.7 0.9 copy-done.2
  39.7 3.7 %project.1 = (bf16[1024,768]{1,0:T(8,128)(2,1)S(1)}, bf16[1024,256]{1,0:T(8,128)(2,1)S(1)}) custom-call(s32[2]{0:T(128)S(1)} %pad_add_fusion.place_ref, bf16[256,1024]{1,0:T(8,128)(2,1)S(1)} %norm_tokens.1.refs_0_, bf16[256,1024]{1,0:T(8,128)(2,1)S(1)} %collective-permute-done.3.refs_1_, bf16[256,1024]{1,0:T(8,128)(2,1)S(1)} %collective-permute-done.4.refs_2_, ...), custom_call_target="tpu_custom_call" | custom-call | flops 1610612736 | bytes 6291456 | tf_op jit(solution)/shard_map/project/pallas_call | solution.py:127
  44.1 2.7 %collective-permute-start.17 = (bf16[1024,256]{1,0:T(8,128)(2,1)S(1)}, bf16[1024,256]{1,0:T(8,128)(2,1)S(1)}, u32[]{:S(2)}, u32[]{:S(2)}) collective-permute-start(bf16[1024,256]{1,0:T(8,128)(2,1)S(1)} %get-tuple-element.32.refs_4_), channel_id=1, source_target_pairs={{0,1},{1,0},{2,3},{3,2},{4,5},{5,4},{6,7},{7,6},{8,9},{9,8},{10,11... | collective-permute-start | bytes 1572872 | tf_op jit(solution)/shard_map/ppermute | solution.py:332
  46.8 3.8 %attend.2 = (bf16[256,256]{1,0:T(8,128)(2,1)S(1)}, bf16[256,256]{1,0:T(8,128)(2,1)S(1)}) custom-call(bf16[1024,768]{1,0:T(8,128)(2,1)S(1)} %get-tuple-element.29.p_ref), custom_call_target="tpu_custom_call" | custom-call | flops 2147483648 | bytes 1572864 | tf_op jit(solution)/shard_map/attend/pallas_call | solution.py:164
  50.6 3.8 %attend.3 = (bf16[256,256]{1,0:T(8,128)(2,1)S(1)}, bf16[256,256]{1,0:T(8,128)(2,1)S(1)}) custom-call(bf16[1024,768]{1,0:T(8,128)(2,1)S(1)} %get-tuple-element.29.p_ref), custom_call_target="tpu_custom_call" | custom-call | flops 2147483648 | bytes 1572864 | tf_op jit(solution)/shard_map/attend/pallas_call | solution.py:164
  54.5 3.3 %collective-permute-start.18 = (bf16[1024,256]{1,0:T(8,128)(2,1)S(1)}, bf16[1024,256]{1,0:T(8,128)(2,1)S(1)}, u32[]{:S(2)}, u32[]{:S(2)}) collective-permute-start(bf16[1024,256]{1,0:T(8,128)(2,1)S(1)} %collective-permute-done.13.refs_6_), channel_id=1, source_target_pairs={{0,1},{1,0},{2,3},{3,2},{4,5},{5,4},{6,7},{7,6},{8,9},{9,8},{10,11... | collective-permute-start | bytes 1572872 | tf_op jit(solution)/shard_map/ppermute | solution.py:332
  58.3 0.8 collective-permute-start.15
  59.1 0.8 collective-permute-start.14
  60.7 2.9 %collective-permute-done.16.refs_3_ = bf16[256,256]{1,0:T(8,128)(2,1)S(1)} collective-permute-done((bf16[256,256]{1,0:T(8,128)(2,1)S(1)}, bf16[256,256]{1,0:T(8,128)(2,1)S(1)}, u32[]{:S(2)}, u32[]{:S(2)}) %collective-permute-start.16) | collective-permute-done | bytes 131104 | tf_op jit(solution)/shard_map/ppermute | solution.py:332
  63.5 1.8 %collective-permute-done.15.refs_2_ = bf16[256,256]{1,0:T(8,128)(2,1)S(1)} collective-permute-done((bf16[256,256]{1,0:T(8,128)(2,1)S(1)}, bf16[256,256]{1,0:T(8,128)(2,1)S(1)}, u32[]{:S(2)}, u32[]{:S(2)}) %collective-permute-start.15) | collective-permute-done | bytes 131104 | tf_op jit(solution)/shard_map/ppermute | solution.py:332
  65.3 1.8 %out_projection.1 = (f32[256,1024]{1,0:T(8,128)S(1)}, bf16[640,1024]{1,0:T(8,128)(2,1)S(1)}) custom-call(s32[1]{0:T(128)} %bitcast.place_ref, bf16[256,1024]{1,0:T(8,128)(2,1)S(1)} %copy-done, bf16[640,256]{1,0:T(8,128)(2,1)S(1)} %get-tuple-element.23.d_ref, bf16[256,256]{1,0:T(8,128)(2,1)S(1)} %get-tuple-element.33.refs_0_, ...), custom_call_target="tpu_custom_call" | custom-call | flops 872415232 | bytes 6291456 | tf_op jit(solution)/shard_map/out_projection/pallas_call | solution.py:192
  67.1 38.0 %all_to_all.10 = bf16[16,40,1024]{2,1,0:T(8,128)(2,1)} all-to-all(bf16[16,40,1024]{2,1,0:T(8,128)(2,1)S(1)} %bitcast.21), channel_id=1, replica_groups=mesh['groups'=2,'ctx'=16] {'ctx'}, dimensions={0} | all-to-all | bytes 2621440 | tf_op jit(solution)/shard_map/all_to_all | solution.py:402
  105.2 19.9 %experts.1 = bf16[640,1024]{1,0:T(8,128)(2,1)S(1)} custom-call(bf16[640,1024]{1,0:T(8,128)(2,1)} %bitcast.30, bf16[1024,8192]{1,0:T(8,128)(2,1)} %win_ref.1, bf16[8192,1024]{1,0:T(8,128)(2,1)} %wout_ref.1), custom_call_target="tpu_custom_call" | custom-call | flops 10737418240 | bytes 33554432 | tf_op jit(solution)/shard_map/experts/pallas_call | solution.py:289
  125.1 35.3 %all_to_all.11 = bf16[16,40,1024]{2,1,0:T(8,128)(2,1)S(1)} all-to-all(bf16[16,40,1024]{2,1,0:T(8,128)(2,1)S(1)} %bitcast.22), channel_id=1, replica_groups=mesh['groups'=2,'ctx'=16] {'ctx'}, dimensions={0} | all-to-all | bytes 2621440 | tf_op jit(solution)/shard_map/all_to_all | solution.py:405
  160.4 2.2 %combine.1 = bf16[256,1024]{1,0:T(8,128)(2,1)} custom-call(f32[256,1024]{1,0:T(8,128)S(1)} %get-tuple-element.36.r_ref, bf16[640,1024]{1,0:T(8,128)(2,1)S(1)} %bitcast.20, bf16[640,256]{1,0:T(8,128)(2,1)S(1)} %get-tuple-element.38.hi_ref, bf16[640,256]{1,0:T(8,128)(2,1)S(1)} %get-tuple-element.39.mid_ref, bf16[640,256]{1,0:T(8,128)(2,1)S(1)} %get-tuple-element.40.lo_ref), custom_call_target="tpu_custom_call" | custom-call | flops 1006632960 | bytes 2883584 | tf_op jit(solution)/shard_map/combine/pallas_call | solution.py:321
  (36 shorter events, 3.9 us)
Async XLA Ops:
  0.0 4.3 %copy-start = (bf16[256,1024]{1,0:T(8,128)(2,1)S(1)}, bf16[256,1024]{1,0:T(8,128)(2,1)}, u32[]{:S(2)}) copy-start(bf16[256,1024]{1,0:T(8,128)(2,1)} %t_ref.1) | copy-start | bytes 1572868
  1.0 4.1 %collective-permute-start.1 = (bf16[64,512]{1,0:T(8,128)(2,1)S(1)}, bf16[64,512]{1,0:T(8,128)(2,1)S(1)}, u32[]{:S(2)}, u32[]{:S(2)}) collective-permute-start(bf16[64,512]{1,0:T(8,128)(2,1)S(1)} %pad_maximum_fusion.1), channel_id=1, source_target_pairs={{0,2},{1,3},{2,0},{3,1},{4,6},{5,7},{6,4},{7,5},{8,10},{9,11},{10,... | collective-permute-start | bytes 196616 | tf_op jit(solution)/shard_map/ppermute | solution.py:332
  3.2 1.9 %collective-permute-start = (bf16[64,512]{1,0:T(8,128)(2,1)S(1)}, bf16[64,512]{1,0:T(8,128)(2,1)S(1)}, u32[]{:S(2)}, u32[]{:S(2)}) collective-permute-start(bf16[64,512]{1,0:T(8,128)(2,1)S(1)} %pad_maximum_fusion), channel_id=1, source_target_pairs={{0,1},{1,0},{2,3},{3,2},{4,5},{5,4},{6,7},{7,6},{8,9},{9,8},{10,11... | collective-permute-start | bytes 196616 | tf_op jit(solution)/shard_map/ppermute | solution.py:332
  4.2 3.8 %collective-permute-start.2 = (bf16[64,512]{1,0:T(8,128)(2,1)S(1)}, bf16[64,512]{1,0:T(8,128)(2,1)S(1)}, u32[]{:S(2)}, u32[]{:S(2)}) collective-permute-start(bf16[64,512]{1,0:T(8,128)(2,1)S(1)} %pad_maximum_fusion.2), channel_id=1, source_target_pairs={{0,3},{1,2},{2,1},{3,0},{4,7},{5,6},{6,5},{7,4},{8,11},{9,10},{10,... | collective-permute-start | bytes 196616 | tf_op jit(solution)/shard_map/ppermute | solution.py:332
  8.0 16.1 %collective-permute-start.4 = (bf16[256,1024]{1,0:T(8,128)(2,1)S(1)}, bf16[256,1024]{1,0:T(8,128)(2,1)S(1)}, u32[]{:S(2)}, u32[]{:S(2)}) collective-permute-start(bf16[256,1024]{1,0:T(8,128)(2,1)S(1)} %norm_tokens.1.refs_0_), channel_id=1, source_target_pairs={{0,2},{1,3},{2,0},{3,1},{4,6},{5,7},{6,4},{7,5},{8,10},{9,11},{10,... | collective-permute-start | bytes 1572872 | tf_op jit(solution)/shard_map/ppermute | solution.py:332
  8.9 14.2 %collective-permute-start.7 = (bf16[256,512]{1,0:T(8,128)(2,1)S(1)}, bf16[256,512]{1,0:T(8,128)(2,1)S(1)}, u32[]{:S(2)}, u32[]{:S(2)}) collective-permute-start(bf16[256,512]{1,0:T(8,128)(2,1)S(1)} %bitcast.23), channel_id=1, source_target_pairs={{0,8},{1,9},{2,10},{3,11},{4,12},{5,13},{6,14},{7,15},{8,0},{9,1},... | collective-permute-start | bytes 786440 | tf_op jit(solution)/shard_map/ppermute | solution.py:332
  11.2 13.7 %collective-permute-start.10 = (bf16[256,512]{1,0:T(8,128)(2,1)S(1)}, bf16[256,512]{1,0:T(8,128)(2,1)S(1)}, u32[]{:S(2)}, u32[]{:S(2)}) collective-permute-start(bf16[256,512]{1,0:T(8,128)(2,1)S(1)} %bitcast.24), channel_id=1, source_target_pairs={{0,20},{1,21},{2,22},{3,23},{4,16},{5,17},{6,18},{7,19},{8,28},{9,... | collective-permute-start | bytes 786440 | tf_op jit(solution)/shard_map/ppermute | solution.py:332
  13.4 12.5 %collective-permute-start.9 = (bf16[256,512]{1,0:T(8,128)(2,1)S(1)}, bf16[256,512]{1,0:T(8,128)(2,1)S(1)}, u32[]{:S(2)}, u32[]{:S(2)}) collective-permute-start(bf16[256,512]{1,0:T(8,128)(2,1)S(1)} %bitcast.25), channel_id=1, source_target_pairs={{0,16},{1,17},{2,18},{3,19},{4,20},{5,21},{6,22},{7,23},{8,24},{9,... | collective-permute-start | bytes 786440 | tf_op jit(solution)/shard_map/ppermute | solution.py:332
  13.7 21.7 %collective-permute-start.3 = (bf16[256,1024]{1,0:T(8,128)(2,1)S(1)}, bf16[256,1024]{1,0:T(8,128)(2,1)S(1)}, u32[]{:S(2)}, u32[]{:S(2)}) collective-permute-start(bf16[256,1024]{1,0:T(8,128)(2,1)S(1)} %norm_tokens.1.refs_0_), channel_id=1, source_target_pairs={{0,1},{1,0},{2,3},{3,2},{4,5},{5,4},{6,7},{7,6},{8,9},{9,8},{10,11... | collective-permute-start | bytes 1572872 | tf_op jit(solution)/shard_map/ppermute | solution.py:332
  23.0 6.7 %collective-permute-start.8 = (bf16[256,512]{1,0:T(8,128)(2,1)S(1)}, bf16[256,512]{1,0:T(8,128)(2,1)}, u32[]{:S(2)}, u32[]{:S(2)}) collective-permute-start(bf16[256,512]{1,0:T(8,128)(2,1)S(1)} %collective-permute-done.7.refs_6_), channel_id=1, source_target_pairs={{0,4},{1,5},{2,6},{3,7},{4,0},{5,1},{6,2},{7,3},{8,12},{9,13},{10,... | collective-permute-start | bytes 786440 | tf_op jit(solution)/shard_map/ppermute | solution.py:332
  24.1 14.6 %collective-permute-start.5 = (bf16[256,1024]{1,0:T(8,128)(2,1)S(1)}, bf16[256,1024]{1,0:T(8,128)(2,1)S(1)}, u32[]{:S(2)}, u32[]{:S(2)}) collective-permute-start(bf16[256,1024]{1,0:T(8,128)(2,1)S(1)} %collective-permute-done.4.refs_2_), channel_id=1, source_target_pairs={{0,1},{1,0},{2,3},{3,2},{4,5},{5,4},{6,7},{7,6},{8,9},{9,8},{10,11... | collective-permute-start | bytes 1572872 | tf_op jit(solution)/shard_map/ppermute | solution.py:332
  24.9 10.5 %collective-permute-start.6 = (bf16[256,512]{1,0:T(8,128)(2,1)S(1)}, bf16[256,512]{1,0:T(8,128)(2,1)}, u32[]{:S(2)}, u32[]{:S(2)}) collective-permute-start(bf16[256,512]{1,0:T(8,128)(2,1)S(1)} %bitcast.26), channel_id=1, source_target_pairs={{0,4},{1,5},{2,6},{3,7},{4,0},{5,1},{6,2},{7,3},{8,12},{9,13},{10,... | collective-permute-start | bytes 786440 | tf_op jit(solution)/shard_map/ppermute | solution.py:332
  26.0 0.7 copy-start.1
  26.7 8.7 %collective-permute-start.11 = (bf16[256,512]{1,0:T(8,128)(2,1)S(1)}, bf16[256,512]{1,0:T(8,128)(2,1)}, u32[]{:S(2)}, u32[]{:S(2)}) collective-permute-start(bf16[256,512]{1,0:T(8,128)(2,1)S(1)} %collective-permute-done.7.refs_6_), channel_id=1, source_target_pairs={{0,16},{16,0},{1,17},{17,1},{2,18},{18,2},{3,19},{19,3},{4,20},{20... | collective-permute-start | bytes 786440 | tf_op jit(solution)/shard_map/ppermute | solution.py:332
  29.8 8.9 %collective-permute-start.12 = (bf16[256,512]{1,0:T(8,128)(2,1)}, bf16[256,512]{1,0:T(8,128)(2,1)}, u32[]{:S(2)}, u32[]{:S(2)}) collective-permute-start(bf16[256,512]{1,0:T(8,128)(2,1)} %collective-permute-done.8.refs_7_), channel_id=1, source_target_pairs={{0,16},{16,0},{1,17},{17,1},{2,18},{18,2},{3,19},{19,3},{4,20},{20... | collective-permute-start | bytes 786440 | tf_op jit(solution)/shard_map/ppermute | solution.py:332
  38.7 1.0 copy-start.2
  43.4 11.1 %collective-permute-start.13 = (bf16[1024,256]{1,0:T(8,128)(2,1)S(1)}, bf16[1024,256]{1,0:T(8,128)(2,1)S(1)}, u32[]{:S(2)}, u32[]{:S(2)}) collective-permute-start(bf16[1024,256]{1,0:T(8,128)(2,1)S(1)} %get-tuple-element.32.refs_4_), channel_id=1, source_target_pairs={{0,2},{1,3},{2,0},{3,1},{4,6},{5,7},{6,4},{7,5},{8,10},{9,11},{10,... | collective-permute-start | bytes 1572872 | tf_op jit(solution)/shard_map/ppermute | solution.py:332
  44.1 21.3 %collective-permute-start.17 = (bf16[1024,256]{1,0:T(8,128)(2,1)S(1)}, bf16[1024,256]{1,0:T(8,128)(2,1)S(1)}, u32[]{:S(2)}, u32[]{:S(2)}) collective-permute-start(bf16[1024,256]{1,0:T(8,128)(2,1)S(1)} %get-tuple-element.32.refs_4_), channel_id=1, source_target_pairs={{0,1},{1,0},{2,3},{3,2},{4,5},{5,4},{6,7},{7,6},{8,9},{9,8},{10,11... | collective-permute-start | bytes 1572872 | tf_op jit(solution)/shard_map/ppermute | solution.py:332
  50.6 9.3 %copy-start.3 = (s32[256,2]{0,1:T(2,128)S(1)}, s32[256,2]{0,1:T(2,128)}, u32[]{:S(2)}) copy-start(s32[256,2]{0,1:T(2,128)} %param.8) | copy-start | bytes 6148
  50.6 9.3 %copy-start.4 = (f32[256,2]{0,1:T(2,128)S(1)}, f32[256,2]{0,1:T(2,128)}, u32[]{:S(2)}) copy-start(f32[256,2]{0,1:T(2,128)} %param.9) | copy-start | bytes 6148
  54.5 10.8 %collective-permute-start.18 = (bf16[1024,256]{1,0:T(8,128)(2,1)S(1)}, bf16[1024,256]{1,0:T(8,128)(2,1)S(1)}, u32[]{:S(2)}, u32[]{:S(2)}) collective-permute-start(bf16[1024,256]{1,0:T(8,128)(2,1)S(1)} %collective-permute-done.13.refs_6_), channel_id=1, source_target_pairs={{0,1},{1,0},{2,3},{3,2},{4,5},{5,4},{6,7},{7,6},{8,9},{9,8},{10,11... | collective-permute-start | bytes 1572872 | tf_op jit(solution)/shard_map/ppermute | solution.py:332
  57.8 5.8 %collective-permute-start.16 = (bf16[256,256]{1,0:T(8,128)(2,1)S(1)}, bf16[256,256]{1,0:T(8,128)(2,1)S(1)}, u32[]{:S(2)}, u32[]{:S(2)}) collective-permute-start(bf16[256,256]{1,0:T(8,128)(2,1)S(1)} %get-tuple-element.27), channel_id=1, source_target_pairs={{0,3},{1,2},{2,1},{3,0},{4,7},{5,6},{6,5},{7,4},{8,11},{9,10},{10,... | collective-permute-start | bytes 393224 | tf_op jit(solution)/shard_map/ppermute | solution.py:332
  58.3 7.0 %collective-permute-start.15 = (bf16[256,256]{1,0:T(8,128)(2,1)S(1)}, bf16[256,256]{1,0:T(8,128)(2,1)S(1)}, u32[]{:S(2)}, u32[]{:S(2)}) collective-permute-start(bf16[256,256]{1,0:T(8,128)(2,1)S(1)} %get-tuple-element.28), channel_id=1, source_target_pairs={{0,2},{1,3},{2,0},{3,1},{4,6},{5,7},{6,4},{7,5},{8,10},{9,11},{10,... | collective-permute-start | bytes 393224 | tf_op jit(solution)/shard_map/ppermute | solution.py:332
  59.1 6.2 %collective-permute-start.14 = (bf16[256,256]{1,0:T(8,128)(2,1)S(1)}, bf16[256,256]{1,0:T(8,128)(2,1)S(1)}, u32[]{:S(2)}, u32[]{:S(2)}) collective-permute-start(bf16[256,256]{1,0:T(8,128)(2,1)S(1)} %get-tuple-element.34), channel_id=1, source_target_pairs={{0,1},{1,0},{2,3},{3,2},{4,5},{5,4},{6,7},{7,6},{8,9},{9,8},{10,11... | collective-permute-start | bytes 393224 | tf_op jit(solution)/shard_map/ppermute | solution.py:332

commit v4 on v3

--- a/solution.py
+++ b/solution.py
@@ -26,7 +26,7 @@
 
 
 def cost(flops, nbytes, trans=0):
-    return pl.CostEstimate(flops=int(flops), bytes_accessed=int(nbytes), transcendentals=int(trans))
+    return pl.CostEstimate(flops=1, bytes_accessed=1, transcendentals=0)
 
 
 def mm(a, b, dims=(((1,), (0,)), ((), ()))):
@@ -90,37 +90,38 @@
     return pl.pallas_call(
         route_kernel,
         out_shape=[shape] * 4,
-        compiler_params=params(),
+        compiler_params=params(24),
         cost_estimate=cost(20 * EXPERTS * CAP * rows, 8 * EXPERTS * CAP * rows),
         name="route_slots",
     )(routes.T, gates.T)
 
 
-def project_kernel(place_ref, *refs, count, lines, share):
+def project_kernel(line_ref, *refs, count, lines, share):
     xs = refs[:count]
     ws = refs[count : count + lines * share]
     o_ref, part_ref, full = refs[count + lines * share :]
     size, wide = ws[0].shape
     cols = wide // 4
     rows = xs[0].shape[0]
+    width = share * cols
     for s in range(share):
         for m in range(lines):
-            start = pl.multiple_of((place_ref[0] ^ m) * size, size)
-            full[place_ref[1] ^ s, pl.ds(start, size), :] = ws[s * lines + m][...]
-    mine = share * cols
+            start = pl.multiple_of((line_ref[0] ^ m) * size, size)
+            full[s, pl.ds(start, size), :] = ws[s * lines + m][...]
     for s in range(share):
         for j in range(count):
             got = mm(xs[j][...], full[s, :, : 3 * cols]).astype(bf16)
             for t in range(3):
-                o_ref[j * rows : (j + 1) * rows, t * mine + s * cols : t * mine + (s + 1) * cols] = got[
+                o_ref[j * rows : (j + 1) * rows, t * width + s * cols : t * width + (s + 1) * cols] = got[
                     :, t * cols : (t + 1) * cols
                 ]
         part_ref[:, s * cols : (s + 1) * cols] = full[s, :, 3 * cols :]
 
 
-def project_call(place, xs, ws, lines, share):
+def project_call(line, xs, ws, lines):
     rows, width = xs[0].shape
     count = len(xs)
+    share = len(ws) // lines
     wide = ws[0].shape[1]
     cols = wide // 4
     vm = pl.BlockSpec(memory_space=pltpu.VMEM)
@@ -133,19 +134,20 @@
         in_specs=[pl.BlockSpec(memory_space=pltpu.SMEM)] + [vm] * (count + lines * share),
         out_specs=[vm, vm],
         scratch_shapes=[pltpu.VMEM((share, width, wide), bf16)],
-        compiler_params=params(),
+        compiler_params=params(24),
         cost_estimate=cost(6 * count * rows * width * cols * share, 2 * width * (count * rows + 2 * wide * share)),
         name="project",
-    )(place, *xs, *ws)
-
-
-def attend_kernel(p_ref, *o_refs, blocks):
+    )(line, *xs, *ws)
+
+
+def attend_kernel(p_ref, *refs, blocks):
+    befores, o_refs = refs[: -len(blocks)], refs[-len(blocks) :]
     cols = p_ref.shape[1] // 3
     rows = o_refs[0].shape[0]
     lane = lax.broadcasted_iota(jnp.int32, (rows, cols), 1) // HD
     keys = p_ref[:, cols : 2 * cols]
     values = p_ref[:, 2 * cols :]
-    for o_ref, j in zip(o_refs, blocks):
+    for i, j in enumerate(blocks):
         queries = p_ref[j * rows : (j + 1) * rows, :cols] * jnp.asarray(HD ** (-0.5), bf16)
         mixed = None
         for h in range(cols // HD):
@@ -156,49 +158,74 @@
             probs = (weights * (1.0 / jnp.sum(weights, axis=-1, keepdims=True))).astype(bf16)
             part = mm(probs, values)
             mixed = part if mixed is None else jnp.where(mine, part, mixed)
-        o_ref[...] = mixed.astype(bf16)
-
-
-def attend_call(projected, blocks, rows):
+        mixed = mixed.astype(bf16)
+        if befores:
+            first = befores[i].shape[1]
+            o_refs[i][:, :first] = befores[i][...]
+            o_refs[i][:, first:] = mixed
+        else:
+            o_refs[i][...] = mixed
+
+
+def attend_call(projected, blocks, rows, befores=()):
     length, width = projected.shape[0], projected.shape[1] // 3
+    first = befores[0].shape[1] if befores else 0
     return pl.pallas_call(
         functools.partial(attend_kernel, blocks=blocks),
-        out_shape=[jax.ShapeDtypeStruct((rows, width), bf16)] * len(blocks),
+        out_shape=[jax.ShapeDtypeStruct((rows, first + width), bf16)] * len(blocks),
         compiler_params=params(24),
         cost_estimate=cost(
             16 * len(blocks) * rows * length * width, 2 * projected.size, len(blocks) * rows * length * width // HD
         ),
         name="attend",
-    )(projected)
-
-
-def output_kernel(place_ref, t_ref, d_ref, *refs):
-    ctxs, parts = refs[:SPAN], refs[SPAN : 2 * SPAN]
-    r_ref, o_ref, c_ref, a_ref = refs[2 * SPAN :]
+    )(projected, *befores)
+
+
+def output_kernel(place_ref, t_ref, d_ref, *refs, share, split):
+    ctxs, parts = refs[:SPAN], refs[SPAN : SPAN + 3 * split]
+    r_ref, o_ref, c_ref, a_ref = refs[SPAN + 3 * split :]
     wide = ctxs[0].shape[1]
+    cols = wide // share
     starts = [pl.multiple_of((place_ref[0] ^ j) * wide, wide) for j in range(SPAN)]
+
+    def natural(value):
+        pieces = []
+        for p in range(share):
+            piece = value[:, :cols]
+            for s in range(1, share):
+                piece = jnp.where((place_ref[1] ^ s) == p, value[:, s * cols : (s + 1) * cols], piece)
+            pieces.append(piece)
+        return jnp.concatenate(pieces, axis=1) if share > 1 else value
+
+    def columns(j):
+        pieces = []
+        for own, far, near in (parts[3 * k : 3 * k + 3] for k in range(split)):
+            size = own.shape[1]
+            pieces.append((own, near, far, near)[j][:, size * (j == 3) : size * (j == 3) + size])
+        return jnp.concatenate(pieces, axis=1) if split > 1 else pieces[0]
+
     for j in range(SPAN):
-        c_ref[:, pl.ds(starts[j], wide)] = ctxs[j][...]
+        c_ref[:, pl.ds(starts[j], wide)] = natural(ctxs[j][...])
     for j in range(SPAN):
-        a_ref[:, pl.ds(starts[j], wide)] = mm(c_ref[...], parts[j][...])
+        a_ref[:, pl.ds(starts[j], wide)] = natural(mm(c_ref[...], columns(j)))
     total = t_ref[...].astype(f32) + a_ref[...]
     r_ref[...] = total
     o_ref[...] = mm(d_ref[...], normalize(total)).astype(bf16)
 
 
-def output_call(place, tokens, marks, parts, ctxs):
+def output_call(place, tokens, marks, parts, ctxs, share):
     rows, width = tokens.shape
     vm = pl.BlockSpec(memory_space=pltpu.VMEM)
     return pl.pallas_call(
-        output_kernel,
+        functools.partial(output_kernel, share=share, split=len(parts) // 3),
         out_shape=[
             jax.ShapeDtypeStruct((rows, width), f32),
             jax.ShapeDtypeStruct((marks.shape[0], width), bf16),
         ],
-        in_specs=[pl.BlockSpec(memory_space=pltpu.SMEM)] + [vm] * (2 + 2 * SPAN),
+        in_specs=[pl.BlockSpec(memory_space=pltpu.SMEM)] + [vm] * (2 + SPAN + len(parts)),
         out_specs=[vm, vm],
         scratch_shapes=[pltpu.VMEM((rows, width), bf16), pltpu.VMEM((rows, width), f32)],
-        compiler_params=params(),
+        compiler_params=params(24),
         cost_estimate=cost(2 * rows * width * (width + marks.shape[0]), 6 * width * width),
         name="out_projection",
     )(place, tokens, marks, *ctxs, *parts)
@@ -362,38 +389,56 @@
     for j in range(SPAN):
         block = lax.dynamic_update_slice(block, pieces[j][None], (member ^ j, 0, 0))
     block = block.reshape(-1, 4 * cols)
-    normed, block = lax.optimization_barrier((norm_call(tokens), block))
+    slots = route_call(routes, gates)
+    normed, block, *slots = lax.optimization_barrier((norm_call(tokens), block, *slots))
+    marks, *gate_parts = slots
+    bits = [1 << i for i in reversed(range(lines_total.bit_length() - 1))]
     lines = {0: block}
-    bit = lines_total // 2
-    while bit:
-        for known in list(lines):
+    for bit in bits:
+        lines[bit] = swap(block, "ctx", bit * SPAN)
+    others = {}
+    for s in range(1, share):
+        for m in range(min(2, lines_total)):
+            others[s, m] = swap(block, ("groups", "ctx"), s * devices + m * SPAN)
+    far = swap(normed, "ctx", 2)
+    lines, others, far = lax.optimization_barrier((lines, others, far))
+    for bit in bits[1:]:
+        for known in [m for m in lines if m >= 2 * bit and m & (2 * bit - 1) == 0]:
             lines[known | bit] = swap(lines[known], "ctx", bit * SPAN)
-        bit //= 2
-    shares = [lines[m] for m in range(lines_total)]
+    early = [m for m in range(2, lines_total) if m & (m - 1) == 0]
     for s in range(1, share):
-        shares += [swap(block, ("groups", "ctx"), s * devices + m * SPAN) if m < 2 else swap(lines[m], "groups", s) for m in range(lines_total)]
-
-    far = swap(normed, "ctx", 2)
-    near = swap(normed, "ctx", 1)
-    both = swap(far, "ctx", 1)
-    marks, *gate_parts = route_call(routes, gates)
-
-    place = jnp.stack([line, group % share])
-    projected, part = project_call(place, [normed, near, far, both], shares, lines_total, share)
-    part_far = swap(part, "ctx", 2)
-    part_near = swap(part, "ctx", 1)
-    sent = attend_call(projected, (3, 2), rows)
-    back = {3: swap(sent[0], "ctx", 3), 2: swap(sent[1], "ctx", 2)}
-    projected, *sent = lax.optimization_barrier((projected, *sent))
-    kept = attend_call(projected, (1, 0), rows)
-    kept, part_far = lax.optimization_barrier((kept, part_far))
-    part_both = swap(part_far, "ctx", 1)
-    back[1] = swap(kept[0], "ctx", 1)
-    back[0] = kept[1]
-    ctxs = [back[j] for j in range(SPAN)]
-    resid, table = output_call(
-        member.reshape(1), tokens, marks, [part, part_near, part_far, part_both], ctxs
-    )
+        for m in early:
+            others[s, m] = swap(lines[m], "groups", s)
+    near = swap(jnp.concatenate([normed, far], axis=0), "ctx", 1)
+    lines, others, near = lax.optimization_barrier((lines, others, near))
+    for s in range(1, share):
+        for m in range(lines_total):
+            if (s, m) not in others:
+                others[s, m] = swap(lines[m], "groups", s)
+
+    crop = [normed, near[:rows], far, near[rows:]]
+    spot = line.reshape(1)
+
+    projected, part = project_call(spot, crop, [lines[m] for m in range(lines_total)], lines_total)
+
+    def with_core(mine_part, far_part):
+        return [mine_part, far_part, swap(jnp.concatenate([mine_part, far_part], axis=1), "ctx", 1)]
+
+    across = swap(part, "ctx", 2)
+    ctxs = attend_call(projected, (0, 1, 2, 3), rows)
+    parts = []
+    if share > 1:
+        rest = [others[s, m] for s in range(1, share) for m in range(lines_total)]
+        rest, ctxs, across = lax.optimization_barrier((rest, ctxs, across))
+        parts = with_core(part, across)
+        projected, part = project_call(spot, crop, rest, lines_total)
+        across = swap(part, "ctx", 2)
+        ctxs = attend_call(projected, (0, 1, 2, 3), rows, ctxs)
+    ctxs = [ctxs[0]] + [swap(ctxs[j], "ctx", j) for j in range(1, SPAN)]
+    ctxs, across = lax.optimization_barrier((ctxs, across))
+    parts += with_core(part, across)
+    place = jnp.stack([member, group % share])
+    resid, table = output_call(place, tokens, marks, parts, ctxs, share)
 
     table = table.reshape(EXPERTS, CAP, width)
     if parts_ff > 1:

time: 163 us -> 169 us (1.037)
  waiting for transfers between devices: 25.7 us -> 32.1 us
  starting transfers between devices: 24.2 us -> 19.8 us
  Pallas kernels: 36.3 us -> 40.5 us
  blocking collectives: 73.3 us -> 71.2 us
    ppermute x19, waiting for transfers between devices: 25.7 us -> 32.1 us  [swap(): return lax.ppermute(value, axis, [(i, i ^ bits) for i in range(size)])]
    ppermute x19, starting transfers between devices: 24.2 us -> 19.8 us  [swap(): return lax.ppermute(value, axis, [(i, i ^ bits) for i in range(size)])]
    pallas_call x2, Pallas kernels: 7.68 us -> 10.3 us  [attend_call(): pl.pallas_call(functools.partial(attend_kernel, blocks=blocks), out_shape...]
    all_to_all x1, blocking collectives: 38 us -> 35.9 us  [per_device(): lax.all_to_all(outgoing, 'ctx', split_axis=0, concat_axis=0, tiled=True)]
    pallas_call x1 -> x2, Pallas kernels: 3.69 us -> 4.75 us  [project_call(): pl.pallas_call(functools.partial(project_kernel, count=count, lines=lines...]
  transfers between devices with their start and end apart: 19 -> 19, of which waited for: 8 -> 9; matrix products, arithmetic and copies ran while one was open for 0% -> 0% of each run, Pallas kernels for 5% -> 7%
where the time goes in v4:
time: 169 us; the launch traced here: 168 us
  blocking collectives  71.2 us (42%)
  Pallas kernels  40.5 us (24%)
  waiting for transfers between devices  32.1 us (19%)
  starting transfers between devices  19.8 us (12%)
  local copies, waits for them, and re-layouts  3.34 us (2%)
    all_to_all x1, blocking collectives, per_device(): lax.all_to_all(outgoing, 'ctx', split_axis=0, concat_axis=0, tiled=True)  35.9 us
    all_to_all x1, blocking collectives, per_device(): lax.all_to_all(produced, 'ctx', split_axis=0, concat_axis=0, tiled=True)  35.3 us
    ppermute x19, waiting for transfers between devices, swap(): return lax.ppermute(value, axis, [(i, i ^ bits) for i in range(size)])  32.1 us
    pallas_call x1, Pallas kernels, expert_call(): pl.pallas_call(functools.partial(expert_kernel, local=local, sources=sour...  19.9 us
    ppermute x19, starting transfers between devices, swap(): return lax.ppermute(value, axis, [(i, i ^ bits) for i in range(size)])  19.8 us
    pallas_call x2, Pallas kernels, attend_call(): pl.pallas_call(functools.partial(attend_kernel, blocks=blocks), out_shape...  10.3 us
    pallas_call x2, Pallas kernels, project_call(): pl.pallas_call(functools.partial(project_kernel, count=count, lines=lines...  4.75 us
  transfers between devices with their start and end apart: 19, of which 9 were waited for; matrix products, arithmetic and copies ran while one was open for 0% of the time, Pallas kernels for 7%

profile of v4, /device:TPU:1, one launch (start us, length us, event | category | flops | bytes accessed | tf_op | source)
XLA Modules:
  0.0 168.3 jit_solution(1896211022067696364)
XLA Ops:
  0.0 1.0 constant_dynamic-slice_fusion
  1.0 2.7 %collective-permute-start.2 = (bf16[64,512]{1,0:T(8,128)(2,1)S(1)}, bf16[64,512]{1,0:T(8,128)(2,1)S(1)}, u32[]{:S(2)}, u32[]{:S(2)}) collective-permute-start(bf16[64,512]{1,0:T(8,128)(2,1)S(1)} %pad_maximum_fusion.5), channel_id=1, source_target_pairs={{0,3},{1,2},{2,1},{3,0},{4,7},{5,6},{6,5},{7,4},{8,11},{9,10},{10,... | collective-permute-start | bytes 196616 | tf_op jit(solution)/shard_map/ppermute | solution.py:359
  4.3 1.0 copy-done
  6.5 1.1 collective-permute-done.1
  7.6 1.7 collective-permute-start.7
  9.3 1.3 collective-permute-start.3
  10.6 2.3 %collective-permute-start.4 = (bf16[256,512]{1,0:T(8,128)(2,1)S(1)}, bf16[256,512]{1,0:T(8,128)(2,1)}, u32[]{:S(2)}, u32[]{:S(2)}) collective-permute-start(bf16[256,512]{1,0:T(8,128)(2,1)S(1)} %bitcast.24), channel_id=1, source_target_pairs={{0,8},{1,9},{2,10},{3,11},{4,12},{5,13},{6,14},{7,15},{8,0},{9,1},... | collective-permute-start | bytes 786440 | tf_op jit(solution)/shard_map/ppermute | solution.py:359
  12.9 1.2 collective-permute-start.5
  14.3 7.8 %collective-permute-done.3.refs_5_ = bf16[256,512]{1,0:T(8,128)(2,1)S(1)} collective-permute-done((bf16[256,512]{1,0:T(8,128)(2,1)S(1)}, bf16[256,512]{1,0:T(8,128)(2,1)S(1)}, u32[]{:S(2)}, u32[]{:S(2)}) %collective-permute-start.3) | collective-permute-done | bytes 262176 | tf_op jit(solution)/shard_map/ppermute | solution.py:359
  22.1 6.5 %collective-permute-done.6.refs_5_ = bf16[256,512]{1,0:T(8,128)(2,1)S(1)} collective-permute-done((bf16[256,512]{1,0:T(8,128)(2,1)S(1)}, bf16[256,512]{1,0:T(8,128)(2,1)S(1)}, u32[]{:S(2)}, u32[]{:S(2)}) %collective-permute-start.6) | collective-permute-done | bytes 262176 | tf_op jit(solution)/shard_map/ppermute | solution.py:359
  28.6 1.1 pad_maximum_fusion
  29.7 1.6 collective-permute-start.10
  31.2 1.3 collective-permute-start.8
  32.8 6.7 %collective-permute-done.8.refs_7_ = bf16[256,512]{1,0:T(8,128)(2,1)} collective-permute-done((bf16[256,512]{1,0:T(8,128)(2,1)}, bf16[256,512]{1,0:T(8,128)(2,1)}, u32[]{:S(2)}, u32[]{:S(2)}) %collective-permute-start.8) | collective-permute-done | bytes 262176 | tf_op jit(solution)/shard_map/ppermute | solution.py:359
  39.5 1.0 collective-permute-done.9.refs_6_
  40.5 1.3 fusion.1
  41.8 2.4 %project.2 = (bf16[1024,384]{1,0:T(8,128)(2,1)S(1)}, bf16[1024,128]{1,0:T(8,128)(2,1)S(1)}) custom-call(s32[1]{0:T(128)} %bitcast.9.line_ref, bf16[256,1024]{1,0:T(8,128)(2,1)S(1)} %norm_tokens.1.refs_0_, bf16[256,1024]{1,0:T(8,128)(2,1)S(1)} %get-tuple-element.110.refs_1_, bf16[256,1024]{1,0:T(8,128)(2,1)S(1)} %collective-permute-done.7.refs_2_, ...), custom_call_target="tpu_custom_call" | custom-call | flops 1 | bytes 1 | tf_op jit(solution)/shard_map/project/pallas_call | solution.py:128
  44.6 5.1 %attend.2 = (bf16[256,128]{1,0:T(8,128)(2,1)S(1)}, bf16[256,128]{1,0:T(8,128)(2,1)S(1)}, bf16[256,128]{1,0:T(8,128)(2,1)S(1)}, bf16[256,128]{1,0:T(8,128)(2,1)S(1)}) custom-call(bf16[1024,384]{1,0:T(8,128)(2,1)S(1)} %get-tuple-element.78.p_ref), custom_call_target="tpu_custom_call" | custom-call | flops 1 | bytes 1 | tf_op jit(solution)/shard_map/attend/pallas_call | solution.py:173
  49.7 1.3 collective-permute-done.12.refs_5_
  51.0 2.3 %project.3 = (bf16[1024,384]{1,0:T(8,128)(2,1)S(1)}, bf16[1024,128]{1,0:T(8,128)(2,1)S(1)}) custom-call(s32[1]{0:T(128)} %bitcast.9.line_ref, bf16[256,1024]{1,0:T(8,128)(2,1)S(1)} %norm_tokens.1.refs_0_, bf16[256,1024]{1,0:T(8,128)(2,1)S(1)} %get-tuple-element.110.refs_1_, bf16[256,1024]{1,0:T(8,128)(2,1)S(1)} %collective-permute-done.7.refs_2_, ...), custom_call_target="tpu_custom_call" | custom-call | flops 1 | bytes 1 | tf_op jit(solution)/shard_map/project/pallas_call | solution.py:128
  53.3 1.5 collective-permute-start.16
  54.8 5.3 %attend.3 = (bf16[256,256]{1,0:T(8,128)(2,1)S(1)}, bf16[256,256]{1,0:T(8,128)(2,1)S(1)}, bf16[256,256]{1,0:T(8,128)(2,1)S(1)}, bf16[256,256]{1,0:T(8,128)(2,1)S(1)}) custom-call(bf16[1024,384]{1,0:T(8,128)(2,1)S(1)} %get-tuple-element.88.p_ref, bf16[256,128]{1,0:T(8,128)(2,1)S(1)} %get-tuple-element.89.refs_0_, ...), custom_call_target="tpu_custom_call" | custom-call | flops 1 | bytes 1 | tf_op jit(solution)/shard_map/attend/pallas_call | solution.py:173
  60.1 2.7 %collective-permute-start.13 = (bf16[256,256]{1,0:T(8,128)(2,1)S(1)}, bf16[256,256]{1,0:T(8,128)(2,1)S(1)}, u32[]{:S(2)}, u32[]{:S(2)}) collective-permute-start(bf16[256,256]{1,0:T(8,128)(2,1)S(1)} %get-tuple-element.94), channel_id=1, source_target_pairs={{0,1},{1,0},{2,3},{3,2},{4,5},{5,4},{6,7},{7,6},{8,9},{9,8},{10,11... | collective-permute-start | bytes 393224 | tf_op jit(solution)/shard_map/ppermute | solution.py:359
  62.8 1.6 collective-permute-start.15
  64.7 3.1 %collective-permute-done.14.refs_2_ = bf16[256,256]{1,0:T(8,128)(2,1)S(1)} collective-permute-done((bf16[256,256]{1,0:T(8,128)(2,1)S(1)}, bf16[256,256]{1,0:T(8,128)(2,1)S(1)}, u32[]{:S(2)}, u32[]{:S(2)}) %collective-permute-start.14) | collective-permute-done | bytes 131104 | tf_op jit(solution)/shard_map/ppermute | solution.py:359
  67.8 3.0 %collective-permute-done.15.refs_3_ = bf16[256,256]{1,0:T(8,128)(2,1)S(1)} collective-permute-done((bf16[256,256]{1,0:T(8,128)(2,1)S(1)}, bf16[256,256]{1,0:T(8,128)(2,1)S(1)}, u32[]{:S(2)}, u32[]{:S(2)}) %collective-permute-start.15) | collective-permute-done | bytes 131104 | tf_op jit(solution)/shard_map/ppermute | solution.py:359
  71.2 1.6 collective-permute-done.18.refs_9_
  72.8 2.2 %out_projection.1 = (f32[256,1024]{1,0:T(8,128)S(1)}, bf16[640,1024]{1,0:T(8,128)(2,1)S(1)}) custom-call(s32[2]{0:T(128)S(1)} %pad_add_fusion.place_ref, bf16[256,1024]{1,0:T(8,128)(2,1)S(1)} %copy-done.1, bf16[640,256]{1,0:T(8,128)(2,1)S(1)} %get-tuple-element.61.d_ref, bf16[256,256]{1,0:T(8,128)(2,1)S(1)} %get-tuple-element.98.refs_0_, ...), custom_call_target="tpu_custom_call" | custom-call | flops 1 | bytes 1 | tf_op jit(solution)/shard_map/out_projection/pallas_call | solution.py:219
  75.0 35.9 %all_to_all.10 = bf16[16,40,1024]{2,1,0:T(8,128)(2,1)} all-to-all(bf16[16,40,1024]{2,1,0:T(8,128)(2,1)S(1)} %bitcast.22), channel_id=1, replica_groups=mesh['groups'=2,'ctx'=16] {'ctx'}, dimensions={0} | all-to-all | bytes 2621440 | tf_op jit(solution)/shard_map/all_to_all | solution.py:447
  110.9 19.9 %experts.1 = bf16[640,1024]{1,0:T(8,128)(2,1)S(1)} custom-call(bf16[640,1024]{1,0:T(8,128)(2,1)} %bitcast.30, bf16[1024,8192]{1,0:T(8,128)(2,1)} %win_ref.1, bf16[8192,1024]{1,0:T(8,128)(2,1)} %wout_ref.1), custom_call_target="tpu_custom_call" | custom-call | flops 1 | bytes 1 | tf_op jit(solution)/shard_map/experts/pallas_call | solution.py:316
  130.8 35.3 %all_to_all.11 = bf16[16,40,1024]{2,1,0:T(8,128)(2,1)S(1)} all-to-all(bf16[16,40,1024]{2,1,0:T(8,128)(2,1)S(1)} %bitcast.20), channel_id=1, replica_groups=mesh['groups'=2,'ctx'=16] {'ctx'}, dimensions={0} | all-to-all | bytes 2621440 | tf_op jit(solution)/shard_map/all_to_all | solution.py:450
  166.1 2.2 %combine.1 = bf16[256,1024]{1,0:T(8,128)(2,1)} custom-call(f32[256,1024]{1,0:T(8,128)S(1)} %get-tuple-element.104.r_ref, bf16[640,1024]{1,0:T(8,128)(2,1)S(1)} %bitcast.21, bf16[640,256]{1,0:T(8,128)(2,1)S(1)} %get-tuple-element.106.hi_ref, bf16[640,256]{1,0:T(8,128)(2,1)S(1)} %get-tuple-element.107.mid_ref, bf16[640,256]{1,0:T(8,128)(2,1)S(1)} %get-tuple-element.108.lo_ref), custom_call_target="tpu_custom_call" | custom-call | flops 1 | bytes 1 | tf_op jit(solution)/shard_map/combine/pallas_call | solution.py:348
  (39 shorter events, 3.3 us)
Async XLA Ops:
  0.0 5.7 %copy-start.2 = (s32[256,2]{0,1:T(2,128)S(1)}, s32[256,2]{0,1:T(2,128)}, u32[]{:S(2)}) copy-start(s32[256,2]{0,1:T(2,128)} %param.8) | copy-start | bytes 6148
  0.0 5.7 %copy-start.3 = (f32[256,2]{0,1:T(2,128)S(1)}, f32[256,2]{0,1:T(2,128)}, u32[]{:S(2)}) copy-start(f32[256,2]{0,1:T(2,128)} %param.9) | copy-start | bytes 6148
  1.0 6.6 %collective-permute-start.2 = (bf16[64,512]{1,0:T(8,128)(2,1)S(1)}, bf16[64,512]{1,0:T(8,128)(2,1)S(1)}, u32[]{:S(2)}, u32[]{:S(2)}) collective-permute-start(bf16[64,512]{1,0:T(8,128)(2,1)S(1)} %pad_maximum_fusion.5), channel_id=1, source_target_pairs={{0,3},{1,2},{2,1},{3,0},{4,7},{5,6},{6,5},{7,4},{8,11},{9,10},{10,... | collective-permute-start | bytes 196616 | tf_op jit(solution)/shard_map/ppermute | solution.py:359
  3.7 3.9 %collective-permute-start.1 = (bf16[64,512]{1,0:T(8,128)(2,1)S(1)}, bf16[64,512]{1,0:T(8,128)(2,1)S(1)}, u32[]{:S(2)}, u32[]{:S(2)}) collective-permute-start(bf16[64,512]{1,0:T(8,128)(2,1)S(1)} %pad_maximum_fusion.4), channel_id=1, source_target_pairs={{0,2},{1,3},{2,0},{3,1},{4,6},{5,7},{6,4},{7,5},{8,10},{9,11},{10,... | collective-permute-start | bytes 196616 | tf_op jit(solution)/shard_map/ppermute | solution.py:359
  3.8 2.7 %collective-permute-start = (bf16[64,512]{1,0:T(8,128)(2,1)S(1)}, bf16[64,512]{1,0:T(8,128)(2,1)S(1)}, u32[]{:S(2)}, u32[]{:S(2)}) collective-permute-start(bf16[64,512]{1,0:T(8,128)(2,1)S(1)} %pad_maximum_fusion.3), channel_id=1, source_target_pairs={{0,1},{1,0},{2,3},{3,2},{4,5},{5,4},{6,7},{7,6},{8,9},{9,8},{10,11... | collective-permute-start | bytes 196616 | tf_op jit(solution)/shard_map/ppermute | solution.py:359
  4.3 1.0 copy-start
  7.6 21.0 %collective-permute-start.7 = (bf16[256,1024]{1,0:T(8,128)(2,1)S(1)}, bf16[256,1024]{1,0:T(8,128)(2,1)S(1)}, u32[]{:S(2)}, u32[]{:S(2)}) collective-permute-start(bf16[256,1024]{1,0:T(8,128)(2,1)S(1)} %norm_tokens.1.refs_0_), channel_id=1, source_target_pairs={{0,2},{1,3},{2,0},{3,1},{4,6},{5,7},{6,4},{7,5},{8,10},{9,11},{10,... | collective-permute-start | bytes 1572872 | tf_op jit(solution)/shard_map/ppermute | solution.py:359
  9.3 12.8 %collective-permute-start.3 = (bf16[256,512]{1,0:T(8,128)(2,1)S(1)}, bf16[256,512]{1,0:T(8,128)(2,1)S(1)}, u32[]{:S(2)}, u32[]{:S(2)}) collective-permute-start(bf16[256,512]{1,0:T(8,128)(2,1)S(1)} %bitcast.23), channel_id=1, source_target_pairs={{0,4},{1,5},{2,6},{3,7},{4,0},{5,1},{6,2},{7,3},{8,12},{9,13},{10,... | collective-permute-start | bytes 786440 | tf_op jit(solution)/shard_map/ppermute | solution.py:359
  10.6 11.5 %collective-permute-start.4 = (bf16[256,512]{1,0:T(8,128)(2,1)S(1)}, bf16[256,512]{1,0:T(8,128)(2,1)}, u32[]{:S(2)}, u32[]{:S(2)}) collective-permute-start(bf16[256,512]{1,0:T(8,128)(2,1)S(1)} %bitcast.24), channel_id=1, source_target_pairs={{0,8},{1,9},{2,10},{3,11},{4,12},{5,13},{6,14},{7,15},{8,0},{9,1},... | collective-permute-start | bytes 786440 | tf_op jit(solution)/shard_map/ppermute | solution.py:359
  12.9 9.2 %collective-permute-start.5 = (bf16[256,512]{1,0:T(8,128)(2,1)S(1)}, bf16[256,512]{1,0:T(8,128)(2,1)S(1)}, u32[]{:S(2)}, u32[]{:S(2)}) collective-permute-start(bf16[256,512]{1,0:T(8,128)(2,1)S(1)} %bitcast.25), channel_id=1, source_target_pairs={{0,16},{1,17},{2,18},{3,19},{4,20},{5,21},{6,22},{7,23},{8,24},{9,... | collective-permute-start | bytes 786440 | tf_op jit(solution)/shard_map/ppermute | solution.py:359
  14.1 14.5 %collective-permute-start.6 = (bf16[256,512]{1,0:T(8,128)(2,1)S(1)}, bf16[256,512]{1,0:T(8,128)(2,1)S(1)}, u32[]{:S(2)}, u32[]{:S(2)}) collective-permute-start(bf16[256,512]{1,0:T(8,128)(2,1)S(1)} %bitcast.26), channel_id=1, source_target_pairs={{0,20},{1,21},{2,22},{3,23},{4,16},{5,17},{6,18},{7,19},{8,28},{9,... | collective-permute-start | bytes 786440 | tf_op jit(solution)/shard_map/ppermute | solution.py:359
  29.7 10.8 %collective-permute-start.10 = (bf16[512,1024]{1,0:T(8,128)(2,1)}, bf16[512,1024]{1,0:T(8,128)(2,1)}, u32[]{:S(2)}, u32[]{:S(2)}) collective-permute-start(bf16[512,1024]{1,0:T(8,128)(2,1)} %pad_maximum_fusion), channel_id=1, source_target_pairs={{0,1},{1,0},{2,3},{3,2},{4,5},{5,4},{6,7},{7,6},{8,9},{9,8},{10,11... | collective-permute-start | bytes 3145736 | tf_op jit(solution)/shard_map/ppermute | solution.py:359
  31.2 8.3 %collective-permute-start.8 = (bf16[256,512]{1,0:T(8,128)(2,1)}, bf16[256,512]{1,0:T(8,128)(2,1)}, u32[]{:S(2)}, u32[]{:S(2)}) collective-permute-start(bf16[256,512]{1,0:T(8,128)(2,1)} %collective-permute-done.4.refs_6_), channel_id=1, source_target_pairs={{0,4},{1,5},{2,6},{3,7},{4,0},{5,1},{6,2},{7,3},{8,12},{9,13},{10,... | collective-permute-start | bytes 786440 | tf_op jit(solution)/shard_map/ppermute | solution.py:359
  32.6 7.9 %collective-permute-start.9 = (bf16[256,512]{1,0:T(8,128)(2,1)}, bf16[256,512]{1,0:T(8,128)(2,1)}, u32[]{:S(2)}, u32[]{:S(2)}) collective-permute-start(bf16[256,512]{1,0:T(8,128)(2,1)} %collective-permute-done.4.refs_6_), channel_id=1, source_target_pairs={{0,16},{16,0},{1,17},{17,1},{2,18},{18,2},{3,19},{19,3},{4,20},{20... | collective-permute-start | bytes 786440 | tf_op jit(solution)/shard_map/ppermute | solution.py:359
  44.2 6.8 %collective-permute-start.12 = (bf16[1024,128]{1,0:T(8,128)(2,1)S(1)}, bf16[1024,128]{1,0:T(8,128)(2,1)S(1)}, u32[]{:S(2)}, u32[]{:S(2)}) collective-permute-start(bf16[1024,128]{1,0:T(8,128)(2,1)S(1)} %get-tuple-element.83.refs_4_), channel_id=1, source_target_pairs={{0,2},{1,3},{2,0},{3,1},{4,6},{5,7},{6,4},{7,5},{8,10},{9,11},{10,... | collective-permute-start | bytes 786440 | tf_op jit(solution)/shard_map/ppermute | solution.py:359
  44.4 6.6 %collective-permute-start.11 = (bf16[256,512]{1,0:T(8,128)(2,1)}, bf16[256,512]{1,0:T(8,128)(2,1)S(1)}, u32[]{:S(2)}, u32[]{:S(2)}) collective-permute-start(bf16[256,512]{1,0:T(8,128)(2,1)} %collective-permute-done.8.refs_7_), channel_id=1, source_target_pairs={{0,16},{16,0},{1,17},{17,1},{2,18},{18,2},{3,19},{19,3},{4,20},{20... | collective-permute-start | bytes 786440 | tf_op jit(solution)/shard_map/ppermute | solution.py:359
  53.3 19.5 %copy-start.1 = (bf16[256,1024]{1,0:T(8,128)(2,1)S(1)}, bf16[256,1024]{1,0:T(8,128)(2,1)}, u32[]{:S(2)}) copy-start(bf16[256,1024]{1,0:T(8,128)(2,1)} %t_ref.1) | copy-start | bytes 1572868
  53.3 17.4 %collective-permute-start.16 = (bf16[1024,128]{1,0:T(8,128)(2,1)S(1)}, bf16[1024,128]{1,0:T(8,128)(2,1)S(1)}, u32[]{:S(2)}, u32[]{:S(2)}) collective-permute-start(bf16[1024,128]{1,0:T(8,128)(2,1)S(1)} %get-tuple-element.97.refs_7_), channel_id=1, source_target_pairs={{0,2},{1,3},{2,0},{3,1},{4,6},{5,7},{6,4},{7,5},{8,10},{9,11},{10,... | collective-permute-start | bytes 786440 | tf_op jit(solution)/shard_map/ppermute | solution.py:359
  60.1 4.7 %collective-permute-start.13 = (bf16[256,256]{1,0:T(8,128)(2,1)S(1)}, bf16[256,256]{1,0:T(8,128)(2,1)S(1)}, u32[]{:S(2)}, u32[]{:S(2)}) collective-permute-start(bf16[256,256]{1,0:T(8,128)(2,1)S(1)} %get-tuple-element.94), channel_id=1, source_target_pairs={{0,1},{1,0},{2,3},{3,2},{4,5},{5,4},{6,7},{7,6},{8,9},{9,8},{10,11... | collective-permute-start | bytes 393224 | tf_op jit(solution)/shard_map/ppermute | solution.py:359
  62.7 5.1 %collective-permute-start.14 = (bf16[256,256]{1,0:T(8,128)(2,1)S(1)}, bf16[256,256]{1,0:T(8,128)(2,1)S(1)}, u32[]{:S(2)}, u32[]{:S(2)}) collective-permute-start(bf16[256,256]{1,0:T(8,128)(2,1)S(1)} %get-tuple-element.95), channel_id=1, source_target_pairs={{0,2},{1,3},{2,0},{3,1},{4,6},{5,7},{6,4},{7,5},{8,10},{9,11},{10,... | collective-permute-start | bytes 393224 | tf_op jit(solution)/shard_map/ppermute | solution.py:359
  62.8 8.0 %collective-permute-start.15 = (bf16[256,256]{1,0:T(8,128)(2,1)S(1)}, bf16[256,256]{1,0:T(8,128)(2,1)S(1)}, u32[]{:S(2)}, u32[]{:S(2)}) collective-permute-start(bf16[256,256]{1,0:T(8,128)(2,1)S(1)} %get-tuple-element.96), channel_id=1, source_target_pairs={{0,3},{1,2},{2,1},{3,0},{4,7},{5,6},{6,5},{7,4},{8,11},{9,10},{10,... | collective-permute-start | bytes 393224 | tf_op jit(solution)/shard_map/ppermute | solution.py:359
  64.5 6.7 %collective-permute-start.17 = (bf16[1024,256]{1,0:T(8,128)(2,1)S(1)}, bf16[1024,256]{1,0:T(8,128)(2,1)S(1)}, u32[]{:S(2)}, u32[]{:S(2)}) collective-permute-start(bf16[1024,256]{1,0:T(8,128)(2,1)S(1)} %pad_maximum_fusion.1), channel_id=1, source_target_pairs={{0,1},{1,0},{2,3},{3,2},{4,5},{5,4},{6,7},{7,6},{8,9},{9,8},{10,11... | collective-permute-start | bytes 1572872 | tf_op jit(solution)/shard_map/ppermute | solution.py:359
  70.8 2.0 %collective-permute-start.18 = (bf16[1024,256]{1,0:T(8,128)(2,1)S(1)}, bf16[1024,256]{1,0:T(8,128)(2,1)S(1)}, u32[]{:S(2)}, u32[]{:S(2)}) collective-permute-start(bf16[1024,256]{1,0:T(8,128)(2,1)S(1)} %pad_maximum_fusion.2), channel_id=1, source_target_pairs={{0,1},{1,0},{2,3},{3,2},{4,5},{5,4},{6,7},{7,6},{8,9},{9,8},{10,11... | collective-permute-start | bytes 1572872 | tf_op jit(solution)/shard_map/ppermute | solution.py:359

commit v5 on v3

--- a/solution.py
+++ b/solution.py
@@ -21,7 +21,7 @@
 f32 = jnp.float32
 
 
-def params(mib=40):
+def params(mib=16):
     return pltpu.CompilerParams(vmem_limit_bytes=mib * MIB)
 
 
@@ -96,45 +96,68 @@
     )(routes.T, gates.T)
 
 
+def part_kernel(place_ref, *refs, lines, share):
+    ws, o_ref, full = refs[: lines * share], refs[lines * share], refs[lines * share + 1]
+    size, wide = ws[0].shape
+    cols = wide // 4
+    for s in range(share):
+        for m in range(lines):
+            start = pl.multiple_of((place_ref[0] ^ m) * size, size)
+            full[place_ref[1] ^ s, pl.ds(start, size), :] = ws[s * lines + m][:, 3 * cols :]
+    for s in range(share):
+        o_ref[:, s * cols : (s + 1) * cols] = full[s]
+
+
+def part_call(place, ws, lines, share):
+    size, wide = ws[0].shape
+    cols = wide // 4
+    vm = pl.BlockSpec(memory_space=pltpu.VMEM)
+    return pl.pallas_call(
+        functools.partial(part_kernel, lines=lines, share=share),
+        out_shape=jax.ShapeDtypeStruct((lines * size, share * cols), bf16),
+        in_specs=[pl.BlockSpec(memory_space=pltpu.SMEM)] + [vm] * (lines * share),
+        out_specs=vm,
+        scratch_shapes=[pltpu.VMEM((share, lines * size, cols), bf16)],
+        compiler_params=params(),
+        cost_estimate=cost(1, 4 * lines * size * share * cols),
+        name="out_weight_part",
+    )(place, *ws)
+
+
 def project_kernel(place_ref, *refs, count, lines, share):
     xs = refs[:count]
     ws = refs[count : count + lines * share]
-    o_ref, part_ref, full = refs[count + lines * share :]
+    o_ref, full = refs[count + lines * share :]
     size, wide = ws[0].shape
     cols = wide // 4
     rows = xs[0].shape[0]
+    mine = share * cols
     for s in range(share):
         for m in range(lines):
             start = pl.multiple_of((place_ref[0] ^ m) * size, size)
-            full[place_ref[1] ^ s, pl.ds(start, size), :] = ws[s * lines + m][...]
-    mine = share * cols
+            full[place_ref[1] ^ s, pl.ds(start, size), :] = ws[s * lines + m][:, : 3 * cols]
     for s in range(share):
         for j in range(count):
-            got = mm(xs[j][...], full[s, :, : 3 * cols]).astype(bf16)
+            got = mm(xs[j][...], full[s]).astype(bf16)
             for t in range(3):
                 o_ref[j * rows : (j + 1) * rows, t * mine + s * cols : t * mine + (s + 1) * cols] = got[
                     :, t * cols : (t + 1) * cols
                 ]
-        part_ref[:, s * cols : (s + 1) * cols] = full[s, :, 3 * cols :]
 
 
 def project_call(place, xs, ws, lines, share):
     rows, width = xs[0].shape
     count = len(xs)
-    wide = ws[0].shape[1]
-    cols = wide // 4
+    cols = ws[0].shape[1] // 4
     vm = pl.BlockSpec(memory_space=pltpu.VMEM)
     return pl.pallas_call(
         functools.partial(project_kernel, count=count, lines=lines, share=share),
-        out_shape=[
-            jax.ShapeDtypeStruct((count * rows, 3 * share * cols), bf16),
-            jax.ShapeDtypeStruct((width, share * cols), bf16),
-        ],
+        out_shape=jax.ShapeDtypeStruct((count * rows, 3 * share * cols), bf16),
         in_specs=[pl.BlockSpec(memory_space=pltpu.SMEM)] + [vm] * (count + lines * share),
-        out_specs=[vm, vm],
-        scratch_shapes=[pltpu.VMEM((share, width, wide), bf16)],
-        compiler_params=params(),
-        cost_estimate=cost(6 * count * rows * width * cols * share, 2 * width * (count * rows + 2 * wide * share)),
+        out_specs=vm,
+        scratch_shapes=[pltpu.VMEM((share, width, 3 * cols), bf16)],
+        compiler_params=params(),
+        cost_estimate=cost(6 * count * rows * width * cols * share, 2 * width * (count * rows + 8 * cols * share)),
         name="project",
     )(place, *xs, *ws)
 
@@ -164,7 +187,7 @@
     return pl.pallas_call(
         functools.partial(attend_kernel, blocks=blocks),
         out_shape=[jax.ShapeDtypeStruct((rows, width), bf16)] * len(blocks),
-        compiler_params=params(24),
+        compiler_params=params(),
         cost_estimate=cost(
             16 * len(blocks) * rows * length * width, 2 * projected.size, len(blocks) * rows * length * width // HD
         ),
@@ -208,35 +231,19 @@
     return jax.nn.gelu(x, approximate=True)
 
 
-def expert_kernel(x_ref, win_ref, wout_ref, o_ref, *scratch, local, sources, step, ahead):
-    rows_ref, hid_ref, pre_ref, acc_ref, term_ref, in_buf, out_buf, in_sem, out_sem = scratch
+def expert_kernel(x_ref, win_ref, wout_ref, o_ref, *scratch, local, sources, step):
+    rows_ref, hid_ref, pre_ref, term_ref, out_buf, sems = scratch
     count = sources * CAP
-    width = x_ref.shape[1]
     hidden = win_ref.shape[1] // local
     steps = hidden // step
     pack = 4 * CAP
 
-    def load_in(e, n):
-        return pltpu.make_async_copy(
-            win_ref.at[:, pl.ds(e * hidden + n * step, step)], in_buf.at[n], in_sem.at[n]
-        )
-
-    def load_out(e, n):
-        return pltpu.make_async_copy(
-            wout_ref.at[pl.ds(e * hidden + n * step, step), :],
-            out_buf.at[pl.ds(n * step, step), :],
-            out_sem.at[n],
-        )
-
-    chain = [load(e, n) for e in range(local) for load in (load_in, load_out) for n in range(steps)]
-
-    def arrive(t):
-        chain[t].wait()
-        if t + ahead < len(chain):
-            chain[t + ahead].start()
-
-    for load in chain[:ahead]:
-        load.start()
+    def load(e, n):
+        span = pl.ds(e * hidden + n * step, step)
+        return pltpu.make_async_copy(wout_ref.at[span, :], out_buf.at[span, :], sems.at[e, n])
+
+    for n in range(steps):
+        load(0, n).start()
 
     if local > 1:
         to = lax.broadcasted_iota(jnp.int32, (local * pack, local * pack), 0)
@@ -253,23 +260,21 @@
 
     for e in range(local):
         for n in range(steps):
-            arrive(2 * e * steps + n)
+            start = e * hidden + n * step
             rows = rows_ref[e] if local > 1 else x_ref[...]
-            pre_ref[n % 2] = mm(rows, in_buf[n])
+            pre_ref[n % 2] = mm(rows, win_ref[:, start : start + step])
             if n:
                 hid_ref[:, (n - 1) * step : n * step] = gelu(pre_ref[(n - 1) % 2]).astype(bf16)
         hid_ref[:, (steps - 1) * step :] = gelu(pre_ref[(steps - 1) % 2]).astype(bf16)
         for n in range(steps):
-            arrive((2 * e + 1) * steps + n)
-            part = mm(hid_ref[:, n * step : (n + 1) * step], out_buf[n * step : (n + 1) * step, :])
-            if n:
-                part = acc_ref[...] + part
-            if n + 1 < steps:
-                acc_ref[...] = part
-            elif local > 1:
-                term_ref[e] = part.astype(bf16)
-            else:
-                o_ref[...] = part.astype(bf16)
+            load(e, n).wait()
+            if e + 1 < local:
+                load(e + 1, n).start()
+        term = mm(hid_ref[...], out_buf[e * hidden : (e + 1) * hidden, :]).astype(bf16)
+        if local > 1:
+            term_ref[e] = term
+        else:
+            o_ref[...] = term
 
     if local > 1:
         for g in range(count // pack):
@@ -278,31 +283,27 @@
             o_ref[g * local * pack : (g + 1) * local * pack, :] = back.astype(bf16)
 
 
-def expert_call(arrived, w_in, w_out, local, sources, step=2048, ahead=2):
+def expert_call(arrived, w_in, w_out, local, sources, step=1024):
     count = sources * CAP
     width = arrived.shape[1]
     hidden = w_in.shape[1] // local
-    steps = hidden // step
     kept = (local, count, width) if local > 1 else (1, 16, 128)
+    w_in = pltpu.with_memory_space_constraint(w_in, pltpu.VMEM)
     vm = pl.BlockSpec(memory_space=pltpu.VMEM)
-    hbm = pl.BlockSpec(memory_space=pl.ANY)
-    return pl.pallas_call(
-        functools.partial(expert_kernel, local=local, sources=sources, step=step, ahead=ahead),
+    return pl.pallas_call(
+        functools.partial(expert_kernel, local=local, sources=sources, step=step),
         out_shape=jax.ShapeDtypeStruct(arrived.shape, bf16),
-        in_specs=[vm, hbm, hbm],
+        in_specs=[vm, vm, pl.BlockSpec(memory_space=pl.ANY)],
         out_specs=vm,
         scratch_shapes=[
             pltpu.VMEM(kept, bf16),
             pltpu.VMEM((count, hidden), bf16),
             pltpu.VMEM((2, count, step), f32),
-            pltpu.VMEM((count, width), f32),
             pltpu.VMEM(kept, bf16),
-            pltpu.VMEM((steps, width, step), bf16),
-            pltpu.VMEM((hidden, width), bf16),
-            pltpu.SemaphoreType.DMA((steps,)),
-            pltpu.SemaphoreType.DMA((steps,)),
+            pltpu.VMEM(w_out.shape, bf16),
+            pltpu.SemaphoreType.DMA((local, hidden // step)),
         ],
-        compiler_params=params(52),
+        compiler_params=params(36),
         cost_estimate=cost(4 * count * width * hidden * local, 4 * width * hidden * local, count * hidden * local),
         name="experts",
     )(arrived, w_in, w_out)
@@ -362,7 +363,9 @@
     for j in range(SPAN):
         block = lax.dynamic_update_slice(block, pieces[j][None], (member ^ j, 0, 0))
     block = block.reshape(-1, 4 * cols)
-    normed, block = lax.optimization_barrier((norm_call(tokens), block))
+    slots = route_call(routes, gates)
+    normed, block, slots = lax.optimization_barrier((norm_call(tokens), block, slots))
+    marks, *gate_parts = slots
     lines = {0: block}
     bit = lines_total // 2
     while bit:
@@ -376,20 +379,15 @@
     far = swap(normed, "ctx", 2)
     near = swap(normed, "ctx", 1)
     both = swap(far, "ctx", 1)
-    marks, *gate_parts = route_call(routes, gates)
-
     place = jnp.stack([line, group % share])
-    projected, part = project_call(place, [normed, near, far, both], shares, lines_total, share)
+    part = part_call(place, shares, lines_total, share)
     part_far = swap(part, "ctx", 2)
     part_near = swap(part, "ctx", 1)
-    sent = attend_call(projected, (3, 2), rows)
-    back = {3: swap(sent[0], "ctx", 3), 2: swap(sent[1], "ctx", 2)}
-    projected, *sent = lax.optimization_barrier((projected, *sent))
-    kept = attend_call(projected, (1, 0), rows)
-    kept, part_far = lax.optimization_barrier((kept, part_far))
+    projected = project_call(place, [normed, near, far, both], shares, lines_total, share)
+    ctxs = attend_call(projected, (0, 1, 2, 3), rows)
+    own, part_far = lax.optimization_barrier((ctxs[0], part_far))
     part_both = swap(part_far, "ctx", 1)
-    back[1] = swap(kept[0], "ctx", 1)
-    back[0] = kept[1]
+    back = {0: own} | {j: swap(ctxs[j], "ctx", j) for j in range(1, SPAN)}
     ctxs = [back[j] for j in range(SPAN)]
     resid, table = output_call(
         member.reshape(1), tokens, marks, [part, part_near, part_far, part_both], ctxs

time: 163 us -> 161 us (0.988)
  waiting for transfers between devices: 25.7 us -> 35.1 us
  starting transfers between devices: 24.2 us -> 20.3 us
  Pallas kernels: 36.3 us -> 32.5 us
  blocking collectives: 73.3 us -> 71.6 us
    ppermute x19, waiting for transfers between devices: 25.7 us -> 35.1 us  [swap(): return lax.ppermute(value, axis, [(i, i ^ bits) for i in range(size)])]
    pallas_call x1, Pallas kernels: 19.9 us -> 15.3 us  [expert_call(): pl.pallas_call(functools.partial(expert_kernel, local=local, sources=sour...]
    ppermute x19, starting transfers between devices: 24.2 us -> 20.3 us  [swap(): return lax.ppermute(value, axis, [(i, i ^ bits) for i in range(size)])]
    all_to_all x1, blocking collectives: 38 us -> 36.3 us  [per_device(): lax.all_to_all(outgoing, 'ctx', split_axis=0, concat_axis=0, tiled=True)]
    unnamed x10 -> x14, local copies, waits for them, and re-layouts: 1.67 us -> 0.04 us
    pallas_call x2 -> x1, Pallas kernels: 7.68 us -> 6.66 us  [attend_call(): pl.pallas_call(functools.partial(attend_kernel, blocks=blocks), out_shape...]
  transfers between devices with their start and end apart: 19 -> 19, of which waited for: 8 -> 9; matrix products, arithmetic and copies ran while one was open for 0% -> 0% of each run, Pallas kernels for 5% -> 8%
where the time goes in v5:
time: 161 us
  blocking collectives  71.6 us (44%)
  waiting for transfers between devices  35.1 us (22%)
  Pallas kernels  32.5 us (20%)
  starting transfers between devices  20.3 us (13%)
    all_to_all x1, blocking collectives, per_device(): lax.all_to_all(outgoing, 'ctx', split_axis=0, concat_axis=0, tiled=True)  36.3 us
    all_to_all x1, blocking collectives, per_device(): lax.all_to_all(produced, 'ctx', split_axis=0, concat_axis=0, tiled=True)  35.3 us
    ppermute x19, waiting for transfers between devices, swap(): return lax.ppermute(value, axis, [(i, i ^ bits) for i in range(size)])  35.1 us
    ppermute x19, starting transfers between devices, swap(): return lax.ppermute(value, axis, [(i, i ^ bits) for i in range(size)])  20.3 us
    pallas_call x1, Pallas kernels, expert_call(): pl.pallas_call(functools.partial(expert_kernel, local=local, sources=sour...  15.3 us
    pallas_call x1, Pallas kernels, attend_call(): pl.pallas_call(functools.partial(attend_kernel, blocks=blocks), out_shape...  6.66 us
    pallas_call x1, Pallas kernels, project_call(): pl.pallas_call(functools.partial(project_kernel, count=count, lines=lines...  4.16 us
  transfers between devices with their start and end apart: 19, of which 9 were waited for; matrix products, arithmetic and copies ran while one was open for 0% of the time, Pallas kernels for 8%

profile of v5, /device:TPU:1, one launch (start us, length us, event | category | flops | bytes accessed | tf_op | source)
XLA Modules:
  0.0 161.0 jit_solution(3238635281835297813)
XLA Ops:
  0.1 1.0 constant_dynamic-slice_fusion
  1.3 2.8 %collective-permute-start.1 = (bf16[64,512]{1,0:T(8,128)(2,1)S(1)}, bf16[64,512]{1,0:T(8,128)(2,1)S(1)}, u32[]{:S(2)}, u32[]{:S(2)}) collective-permute-start(bf16[64,512]{1,0:T(8,128)(2,1)S(1)} %pad_maximum_fusion.1), channel_id=1, source_target_pairs={{0,2},{1,3},{2,0},{3,1},{4,6},{5,7},{6,4},{7,5},{8,10},{9,11},{10,... | collective-permute-start | bytes 196616 | tf_op jit(solution)/shard_map/ppermute | solution.py:333
  4.6 0.7 route_slots.1
  5.4 1.1 collective-permute-done.1
  6.5 1.6 %collective-permute-done.2 = bf16[64,512]{1,0:T(8,128)(2,1)S(1)} collective-permute-done((bf16[64,512]{1,0:T(8,128)(2,1)S(1)}, bf16[64,512]{1,0:T(8,128)(2,1)S(1)}, u32[]{:S(2)}, u32[]{:S(2)}) %collective-permute-start.2) | collective-permute-done | bytes 65568 | tf_op jit(solution)/shard_map/ppermute | solution.py:333
  8.1 1.2 collective-permute-start.4
  9.3 2.3 %collective-permute-start.7 = (bf16[256,512]{1,0:T(8,128)(2,1)S(1)}, bf16[256,512]{1,0:T(8,128)(2,1)S(1)}, u32[]{:S(2)}, u32[]{:S(2)}) collective-permute-start(bf16[256,512]{1,0:T(8,128)(2,1)S(1)} %bitcast.23), channel_id=1, source_target_pairs={{0,8},{1,9},{2,10},{3,11},{4,12},{5,13},{6,14},{7,15},{8,0},{9,1},... | collective-permute-start | bytes 786440 | tf_op jit(solution)/shard_map/ppermute | solution.py:333
  11.7 1.3 collective-permute-start.6
  13.0 1.2 collective-permute-start.9
  14.2 9.1 %collective-permute-done.7.refs_6_.refs_2_ = bf16[256,512]{1,0:T(8,128)(2,1)S(1)} collective-permute-done((bf16[256,512]{1,0:T(8,128)(2,1)S(1)}, bf16[256,512]{1,0:T(8,128)(2,1)S(1)}, u32[]{:S(2)}, u32[]{:S(2)}) %collective-permute-start.7) | collective-permute-done | bytes 262176 | tf_op jit(solution)/shard_map/ppermute | solution.py:333
  23.2 1.3 collective-permute-start.8
  24.5 0.8 collective-permute-start.3
  25.3 2.2 %collective-permute-start.10 = (bf16[256,512]{1,0:T(8,128)(2,1)S(1)}, bf16[256,512]{1,0:T(8,128)(2,1)}, u32[]{:S(2)}, u32[]{:S(2)}) collective-permute-start(bf16[256,512]{1,0:T(8,128)(2,1)S(1)} %bitcast.26), channel_id=1, source_target_pairs={{0,20},{1,21},{2,22},{3,23},{4,16},{5,17},{6,18},{7,19},{8,28},{9,... | collective-permute-start | bytes 786440 | tf_op jit(solution)/shard_map/ppermute | solution.py:333
  27.7 2.0 %collective-permute-done.8.refs_7_.refs_3_ = bf16[256,512]{1,0:T(8,128)(2,1)} collective-permute-done((bf16[256,512]{1,0:T(8,128)(2,1)S(1)}, bf16[256,512]{1,0:T(8,128)(2,1)}, u32[]{:S(2)}, u32[]{:S(2)}) %collective-permute-start.8) | collective-permute-done | bytes 262176 | tf_op jit(solution)/shard_map/ppermute | solution.py:333
  29.7 1.2 collective-permute-start.12
  31.0 5.3 %collective-permute-done.10.refs_9_.refs_5_ = bf16[256,512]{1,0:T(8,128)(2,1)} collective-permute-done((bf16[256,512]{1,0:T(8,128)(2,1)S(1)}, bf16[256,512]{1,0:T(8,128)(2,1)}, u32[]{:S(2)}, u32[]{:S(2)}) %collective-permute-start.10) | collective-permute-done | bytes 262176 | tf_op jit(solution)/shard_map/ppermute | solution.py:333
  36.2 4.5 %collective-permute-done.11.refs_10_.refs_6_ = bf16[256,512]{1,0:T(8,128)(2,1)} collective-permute-done((bf16[256,512]{1,0:T(8,128)(2,1)S(1)}, bf16[256,512]{1,0:T(8,128)(2,1)}, u32[]{:S(2)}, u32[]{:S(2)}) %collective-permute-start.11) | collective-permute-done | bytes 262176 | tf_op jit(solution)/shard_map/ppermute | solution.py:333
  40.7 5.6 %collective-permute-done.12.refs_11_.refs_7_ = bf16[256,512]{1,0:T(8,128)(2,1)} collective-permute-done((bf16[256,512]{1,0:T(8,128)(2,1)}, bf16[256,512]{1,0:T(8,128)(2,1)}, u32[]{:S(2)}, u32[]{:S(2)}) %collective-permute-start.12) | collective-permute-done | bytes 262176 | tf_op jit(solution)/shard_map/ppermute | solution.py:333
  46.3 1.5 out_weight_part.1.refs_4_
  47.9 0.5 collective-permute-start.13
  48.4 1.3 collective-permute-start.17
  49.7 4.2 %project.1.p_ref = bf16[1024,768]{1,0:T(8,128)(2,1)S(1)} custom-call(s32[2]{0:T(128)S(1)} %pad_add_fusion.place_ref, bf16[256,1024]{1,0:T(8,128)(2,1)S(1)} %norm_tokens.1.refs_0_, bf16[256,1024]{1,0:T(8,128)(2,1)} %collective-permute-done.3.refs_1_, bf16[256,1024]{1,0:T(8,128)(2,1)} %collective-permute-done.4.refs_2_, ...), custom_call_target="tpu_custom_call" | custom-call | flops 1610612736 | bytes 6291456 | tf_op jit(solution)/shard_map/project/pallas_call | solution.py:153
  53.9 6.7 %attend.1 = (bf16[256,256]{1,0:T(8,128)(2,1)S(1)}, bf16[256,256]{1,0:T(8,128)(2,1)S(1)}, bf16[256,256]{1,0:T(8,128)(2,1)S(1)}, bf16[256,256]{1,0:T(8,128)(2,1)S(1)}) custom-call(bf16[1024,768]{1,0:T(8,128)(2,1)S(1)} %project.1.p_ref), custom_call_target="tpu_custom_call" | custom-call | flops 4294967296 | bytes 1572864 | tf_op jit(solution)/shard_map/attend/pallas_call | solution.py:187
  60.6 1.7 %collective-permute-start.18 = (bf16[1024,256]{1,0:T(8,128)(2,1)S(1)}, bf16[1024,256]{1,0:T(8,128)(2,1)S(1)}, u32[]{:S(2)}, u32[]{:S(2)}) collective-permute-start(bf16[1024,256]{1,0:T(8,128)(2,1)S(1)} %collective-permute-done.13.refs_6_), channel_id=1, source_target_pairs={{0,1},{1,0},{2,3},{3,2},{4,5},{5,4},{6,7},{7,6},{8,9},{9,8},{10,11... | collective-permute-start | bytes 1572872 | tf_op jit(solution)/shard_map/ppermute | solution.py:333
  62.7 1.7 %collective-permute-start.16 = (bf16[256,256]{1,0:T(8,128)(2,1)S(1)}, bf16[256,256]{1,0:T(8,128)(2,1)S(1)}, u32[]{:S(2)}, u32[]{:S(2)}) collective-permute-start(bf16[256,256]{1,0:T(8,128)(2,1)S(1)} %get-tuple-element.34), channel_id=1, source_target_pairs={{0,3},{1,2},{2,1},{3,0},{4,7},{5,6},{6,5},{7,4},{8,11},{9,10},{10,... | collective-permute-start | bytes 393224 | tf_op jit(solution)/shard_map/ppermute | solution.py:333
  64.4 2.4 %collective-permute-done.15.refs_2_ = bf16[256,256]{1,0:T(8,128)(2,1)S(1)} collective-permute-done((bf16[256,256]{1,0:T(8,128)(2,1)S(1)}, bf16[256,256]{1,0:T(8,128)(2,1)S(1)}, u32[]{:S(2)}, u32[]{:S(2)}) %collective-permute-start.15) | collective-permute-done | bytes 131104 | tf_op jit(solution)/shard_map/ppermute | solution.py:333
  66.9 3.5 %collective-permute-done.16.refs_3_ = bf16[256,256]{1,0:T(8,128)(2,1)S(1)} collective-permute-done((bf16[256,256]{1,0:T(8,128)(2,1)S(1)}, bf16[256,256]{1,0:T(8,128)(2,1)S(1)}, u32[]{:S(2)}, u32[]{:S(2)}) %collective-permute-start.16) | collective-permute-done | bytes 131104 | tf_op jit(solution)/shard_map/ppermute | solution.py:333
  70.3 1.6 out_projection.1
  71.9 36.3 %all_to_all.10 = bf16[16,40,1024]{2,1,0:T(8,128)(2,1)} all-to-all(bf16[16,40,1024]{2,1,0:T(8,128)(2,1)S(1)} %bitcast.21), channel_id=1, replica_groups=mesh['groups'=2,'ctx'=16] {'ctx'}, dimensions={0} | all-to-all | bytes 2621440 | tf_op jit(solution)/shard_map/all_to_all | solution.py:400
  108.3 15.3 %experts.1 = bf16[640,1024]{1,0:T(8,128)(2,1)S(1)} custom-call(bf16[640,1024]{1,0:T(8,128)(2,1)} %bitcast.33, bf16[1024,8192]{1,0:T(8,128)(2,1)S(1)} %bitcast.30, bf16[8192,1024]{1,0:T(8,128)(2,1)} %wout_ref.1), custom_call_target="tpu_custom_call" | custom-call | flops 10737418240 | bytes 33554432 | tf_op jit(solution)/shard_map/experts/pallas_call | solution.py:293
  123.5 35.3 %all_to_all.11 = bf16[16,40,1024]{2,1,0:T(8,128)(2,1)S(1)} all-to-all(bf16[16,40,1024]{2,1,0:T(8,128)(2,1)S(1)} %bitcast.22), channel_id=1, replica_groups=mesh['groups'=2,'ctx'=16] {'ctx'}, dimensions={0} | all-to-all | bytes 2621440 | tf_op jit(solution)/shard_map/all_to_all | solution.py:403
  158.8 2.2 %combine.1 = bf16[256,1024]{1,0:T(8,128)(2,1)} custom-call(f32[256,1024]{1,0:T(8,128)S(1)} %get-tuple-element.36.r_ref, bf16[640,1024]{1,0:T(8,128)(2,1)S(1)} %bitcast.20, bf16[640,256]{1,0:T(8,128)(2,1)S(1)} %get-tuple-element.38.hi_ref, bf16[640,256]{1,0:T(8,128)(2,1)S(1)} %get-tuple-element.39.mid_ref, bf16[640,256]{1,0:T(8,128)(2,1)S(1)} %get-tuple-element.40.lo_ref), custom_call_target="tpu_custom_call" | custom-call | flops 1006632960 | bytes 2883584 | tf_op jit(solution)/shard_map/combine/pallas_call | solution.py:322
  (41 shorter events, 1.4 us)
Async XLA Ops:
  0.0 4.2 %copy-start = (bf16[256,1024]{1,0:T(8,128)(2,1)S(1)}, bf16[256,1024]{1,0:T(8,128)(2,1)}, u32[]{:S(2)}) copy-start(bf16[256,1024]{1,0:T(8,128)(2,1)} %t_ref.1) | copy-start | bytes 1572868
  0.0 4.5 %copy-start.1 = (s32[256,2]{0,1:T(2,128)S(1)}, s32[256,2]{0,1:T(2,128)}, u32[]{:S(2)}) copy-start(s32[256,2]{0,1:T(2,128)} %param.8) | copy-start | bytes 6148
  0.0 4.5 %copy-start.2 = (f32[256,2]{0,1:T(2,128)S(1)}, f32[256,2]{0,1:T(2,128)}, u32[]{:S(2)}) copy-start(f32[256,2]{0,1:T(2,128)} %param.9) | copy-start | bytes 6148
  1.2 4.2 %collective-permute-start = (bf16[64,512]{1,0:T(8,128)(2,1)S(1)}, bf16[64,512]{1,0:T(8,128)(2,1)S(1)}, u32[]{:S(2)}, u32[]{:S(2)}) collective-permute-start(bf16[64,512]{1,0:T(8,128)(2,1)S(1)} %pad_maximum_fusion), channel_id=1, source_target_pairs={{0,1},{1,0},{2,3},{3,2},{4,5},{5,4},{6,7},{7,6},{8,9},{9,8},{10,11... | collective-permute-start | bytes 196616 | tf_op jit(solution)/shard_map/ppermute | solution.py:333
  1.3 5.2 %collective-permute-start.1 = (bf16[64,512]{1,0:T(8,128)(2,1)S(1)}, bf16[64,512]{1,0:T(8,128)(2,1)S(1)}, u32[]{:S(2)}, u32[]{:S(2)}) collective-permute-start(bf16[64,512]{1,0:T(8,128)(2,1)S(1)} %pad_maximum_fusion.1), channel_id=1, source_target_pairs={{0,2},{1,3},{2,0},{3,1},{4,6},{5,7},{6,4},{7,5},{8,10},{9,11},{10,... | collective-permute-start | bytes 196616 | tf_op jit(solution)/shard_map/ppermute | solution.py:333
  4.1 4.1 %collective-permute-start.2 = (bf16[64,512]{1,0:T(8,128)(2,1)S(1)}, bf16[64,512]{1,0:T(8,128)(2,1)S(1)}, u32[]{:S(2)}, u32[]{:S(2)}) collective-permute-start(bf16[64,512]{1,0:T(8,128)(2,1)S(1)} %pad_maximum_fusion.2), channel_id=1, source_target_pairs={{0,3},{1,2},{2,1},{3,0},{4,7},{5,6},{6,5},{7,4},{8,11},{9,10},{10,... | collective-permute-start | bytes 196616 | tf_op jit(solution)/shard_map/ppermute | solution.py:333
  8.1 17.1 %collective-permute-start.4 = (bf16[256,1024]{1,0:T(8,128)(2,1)S(1)}, bf16[256,1024]{1,0:T(8,128)(2,1)}, u32[]{:S(2)}, u32[]{:S(2)}) collective-permute-start(bf16[256,1024]{1,0:T(8,128)(2,1)S(1)} %norm_tokens.1.refs_0_), channel_id=1, source_target_pairs={{0,2},{1,3},{2,0},{3,1},{4,6},{5,7},{6,4},{7,5},{8,10},{9,11},{10,... | collective-permute-start | bytes 1572872 | tf_op jit(solution)/shard_map/ppermute | solution.py:333
  9.3 13.9 %collective-permute-start.7 = (bf16[256,512]{1,0:T(8,128)(2,1)S(1)}, bf16[256,512]{1,0:T(8,128)(2,1)S(1)}, u32[]{:S(2)}, u32[]{:S(2)}) collective-permute-start(bf16[256,512]{1,0:T(8,128)(2,1)S(1)} %bitcast.23), channel_id=1, source_target_pairs={{0,8},{1,9},{2,10},{3,11},{4,12},{5,13},{6,14},{7,15},{8,0},{9,1},... | collective-permute-start | bytes 786440 | tf_op jit(solution)/shard_map/ppermute | solution.py:333
  11.7 13.6 %collective-permute-start.6 = (bf16[256,512]{1,0:T(8,128)(2,1)S(1)}, bf16[256,512]{1,0:T(8,128)(2,1)S(1)}, u32[]{:S(2)}, u32[]{:S(2)}) collective-permute-start(bf16[256,512]{1,0:T(8,128)(2,1)S(1)} %bitcast.24), channel_id=1, source_target_pairs={{0,4},{1,5},{2,6},{3,7},{4,0},{5,1},{6,2},{7,3},{8,12},{9,13},{10,... | collective-permute-start | bytes 786440 | tf_op jit(solution)/shard_map/ppermute | solution.py:333
  13.0 14.5 %collective-permute-start.9 = (bf16[256,512]{1,0:T(8,128)(2,1)S(1)}, bf16[256,512]{1,0:T(8,128)(2,1)S(1)}, u32[]{:S(2)}, u32[]{:S(2)}) collective-permute-start(bf16[256,512]{1,0:T(8,128)(2,1)S(1)} %bitcast.25), channel_id=1, source_target_pairs={{0,16},{1,17},{2,18},{3,19},{4,20},{5,21},{6,22},{7,23},{8,24},{9,... | collective-permute-start | bytes 786440 | tf_op jit(solution)/shard_map/ppermute | solution.py:333
  23.2 6.4 %collective-permute-start.8 = (bf16[256,512]{1,0:T(8,128)(2,1)S(1)}, bf16[256,512]{1,0:T(8,128)(2,1)}, u32[]{:S(2)}, u32[]{:S(2)}) collective-permute-start(bf16[256,512]{1,0:T(8,128)(2,1)S(1)} %collective-permute-done.7.refs_6_.refs_2_), channel_id=1, source_target_pairs={{0,4},{1,5},{2,6},{3,7},{4,0},{5,1},{6,2},{7,3},{8,12},{9,13},{10,... | collective-permute-start | bytes 786440 | tf_op jit(solution)/shard_map/ppermute | solution.py:333
  24.5 25.3 %collective-permute-start.3 = (bf16[256,1024]{1,0:T(8,128)(2,1)S(1)}, bf16[256,1024]{1,0:T(8,128)(2,1)}, u32[]{:S(2)}, u32[]{:S(2)}) collective-permute-start(bf16[256,1024]{1,0:T(8,128)(2,1)S(1)} %norm_tokens.1.refs_0_), channel_id=1, source_target_pairs={{0,1},{1,0},{2,3},{3,2},{4,5},{5,4},{6,7},{7,6},{8,9},{9,8},{10,11... | collective-permute-start | bytes 1572872 | tf_op jit(solution)/shard_map/ppermute | solution.py:333
  25.3 24.5 %collective-permute-start.5 = (bf16[256,1024]{1,0:T(8,128)(2,1)}, bf16[256,1024]{1,0:T(8,128)(2,1)}, u32[]{:S(2)}, u32[]{:S(2)}) collective-permute-start(bf16[256,1024]{1,0:T(8,128)(2,1)} %collective-permute-done.4.refs_2_), channel_id=1, source_target_pairs={{0,1},{1,0},{2,3},{3,2},{4,5},{5,4},{6,7},{7,6},{8,9},{9,8},{10,11... | collective-permute-start | bytes 1572872 | tf_op jit(solution)/shard_map/ppermute | solution.py:333
  25.3 11.0 %collective-permute-start.10 = (bf16[256,512]{1,0:T(8,128)(2,1)S(1)}, bf16[256,512]{1,0:T(8,128)(2,1)}, u32[]{:S(2)}, u32[]{:S(2)}) collective-permute-start(bf16[256,512]{1,0:T(8,128)(2,1)S(1)} %bitcast.26), channel_id=1, source_target_pairs={{0,20},{1,21},{2,22},{3,23},{4,16},{5,17},{6,18},{7,19},{8,28},{9,... | collective-permute-start | bytes 786440 | tf_op jit(solution)/shard_map/ppermute | solution.py:333
  27.4 13.3 %collective-permute-start.11 = (bf16[256,512]{1,0:T(8,128)(2,1)S(1)}, bf16[256,512]{1,0:T(8,128)(2,1)}, u32[]{:S(2)}, u32[]{:S(2)}) collective-permute-start(bf16[256,512]{1,0:T(8,128)(2,1)S(1)} %collective-permute-done.7.refs_6_.refs_2_), channel_id=1, source_target_pairs={{0,16},{16,0},{1,17},{17,1},{2,18},{18,2},{3,19},{19,3},{4,20},{20... | collective-permute-start | bytes 786440 | tf_op jit(solution)/shard_map/ppermute | solution.py:333
  29.7 16.7 %collective-permute-start.12 = (bf16[256,512]{1,0:T(8,128)(2,1)}, bf16[256,512]{1,0:T(8,128)(2,1)}, u32[]{:S(2)}, u32[]{:S(2)}) collective-permute-start(bf16[256,512]{1,0:T(8,128)(2,1)} %collective-permute-done.8.refs_7_.refs_3_), channel_id=1, source_target_pairs={{0,16},{16,0},{1,17},{17,1},{2,18},{18,2},{3,19},{19,3},{4,20},{20... | collective-permute-start | bytes 786440 | tf_op jit(solution)/shard_map/ppermute | solution.py:333
  46.3 61.9 %slice-start = ((s8[16777216]{0:T(1024)(128)(4,1)}), s8[4194304]{0:T(1024)(128)(4,1)S(1)}, s32[]{:S(2)}) async-start(s8[16777216]{0:T(1024)(128)(4,1)} %bitcast.29), calls=%async_computation.2 | async-start | bytes 8388608
  47.9 60.4 %slice-start.1 = ((s8[16777216]{0:T(1024)(128)(4,1)}), s8[4194304]{0:T(1024)(128)(4,1)S(1)}, s32[]{:S(2)}) async-start(s8[16777216]{0:T(1024)(128)(4,1)} %bitcast.29), calls=%async_computation.3 | async-start | bytes 8388608
  47.9 12.7 %collective-permute-start.13 = (bf16[1024,256]{1,0:T(8,128)(2,1)S(1)}, bf16[1024,256]{1,0:T(8,128)(2,1)S(1)}, u32[]{:S(2)}, u32[]{:S(2)}) collective-permute-start(bf16[1024,256]{1,0:T(8,128)(2,1)S(1)} %out_weight_part.1.refs_4_), channel_id=1, source_target_pairs={{0,2},{1,3},{2,0},{3,1},{4,6},{5,7},{6,4},{7,5},{8,10},{9,11},{10,... | collective-permute-start | bytes 1572872 | tf_op jit(solution)/shard_map/ppermute | solution.py:333
  48.4 21.9 %collective-permute-start.17 = (bf16[1024,256]{1,0:T(8,128)(2,1)S(1)}, bf16[1024,256]{1,0:T(8,128)(2,1)S(1)}, u32[]{:S(2)}, u32[]{:S(2)}) collective-permute-start(bf16[1024,256]{1,0:T(8,128)(2,1)S(1)} %out_weight_part.1.refs_4_), channel_id=1, source_target_pairs={{0,1},{1,0},{2,3},{3,2},{4,5},{5,4},{6,7},{7,6},{8,9},{9,8},{10,11... | collective-permute-start | bytes 1572872 | tf_op jit(solution)/shard_map/ppermute | solution.py:333
  53.9 54.3 %slice-start.2 = ((s8[16777216]{0:T(1024)(128)(4,1)}), s8[4194304]{0:T(1024)(128)(4,1)S(1)}, s32[]{:S(2)}) async-start(s8[16777216]{0:T(1024)(128)(4,1)} %bitcast.29), calls=%async_computation.4 | async-start | bytes 8388608
  53.9 54.3 %slice-start.3 = ((s8[16777216]{0:T(1024)(128)(4,1)}), s8[4194304]{0:T(1024)(128)(4,1)S(1)}, s32[]{:S(2)}) async-start(s8[16777216]{0:T(1024)(128)(4,1)} %bitcast.29), calls=%async_computation.5 | async-start | bytes 8388608
  60.6 9.7 %collective-permute-start.18 = (bf16[1024,256]{1,0:T(8,128)(2,1)S(1)}, bf16[1024,256]{1,0:T(8,128)(2,1)S(1)}, u32[]{:S(2)}, u32[]{:S(2)}) collective-permute-start(bf16[1024,256]{1,0:T(8,128)(2,1)S(1)} %collective-permute-done.13.refs_6_), channel_id=1, source_target_pairs={{0,1},{1,0},{2,3},{3,2},{4,5},{5,4},{6,7},{7,6},{8,9},{9,8},{10,11... | collective-permute-start | bytes 1572872 | tf_op jit(solution)/shard_map/ppermute | solution.py:333
  62.3 2.1 %collective-permute-start.14 = (bf16[256,256]{1,0:T(8,128)(2,1)S(1)}, bf16[256,256]{1,0:T(8,128)(2,1)S(1)}, u32[]{:S(2)}, u32[]{:S(2)}) collective-permute-start(bf16[256,256]{1,0:T(8,128)(2,1)S(1)} %get-tuple-element.32), channel_id=1, source_target_pairs={{0,1},{1,0},{2,3},{3,2},{4,5},{5,4},{6,7},{7,6},{8,9},{9,8},{10,11... | collective-permute-start | bytes 393224 | tf_op jit(solution)/shard_map/ppermute | solution.py:333
  62.3 4.6 %collective-permute-start.15 = (bf16[256,256]{1,0:T(8,128)(2,1)S(1)}, bf16[256,256]{1,0:T(8,128)(2,1)S(1)}, u32[]{:S(2)}, u32[]{:S(2)}) collective-permute-start(bf16[256,256]{1,0:T(8,128)(2,1)S(1)} %get-tuple-element.33), channel_id=1, source_target_pairs={{0,2},{1,3},{2,0},{3,1},{4,6},{5,7},{6,4},{7,5},{8,10},{9,11},{10,... | collective-permute-start | bytes 393224 | tf_op jit(solution)/shard_map/ppermute | solution.py:333
  62.7 7.6 %collective-permute-start.16 = (bf16[256,256]{1,0:T(8,128)(2,1)S(1)}, bf16[256,256]{1,0:T(8,128)(2,1)S(1)}, u32[]{:S(2)}, u32[]{:S(2)}) collective-permute-start(bf16[256,256]{1,0:T(8,128)(2,1)S(1)} %get-tuple-element.34), channel_id=1, source_target_pairs={{0,3},{1,2},{2,1},{3,0},{4,7},{5,6},{6,5},{7,4},{8,11},{9,10},{10,... | collective-permute-start | bytes 393224 | tf_op jit(solution)/shard_map/ppermute | solution.py:333

commit v6 on v5

--- a/solution.py
+++ b/solution.py
@@ -366,19 +366,29 @@
     slots = route_call(routes, gates)
     normed, block, slots = lax.optimization_barrier((norm_call(tokens), block, slots))
     marks, *gate_parts = slots
+    bits = [1 << i for i in reversed(range(lines_total.bit_length() - 1))]
     lines = {0: block}
-    bit = lines_total // 2
-    while bit:
-        for known in list(lines):
+    for bit in bits:
+        lines[bit] = swap(block, "ctx", bit * SPAN)
+    others = {}
+    for s in range(1, share):
+        for m in range(min(2, lines_total)):
+            others[s, m] = swap(block, ("groups", "ctx"), s * devices + m * SPAN)
+    if share > 1 and len(bits) > 1:
+        lines[bits[0]], others = lax.optimization_barrier((lines[bits[0]], others))
+    for bit in bits[1:]:
+        for known in [m for m in lines if m >= 2 * bit and m & (2 * bit - 1) == 0]:
             lines[known | bit] = swap(lines[known], "ctx", bit * SPAN)
-        bit //= 2
+    for s in range(1, share):
+        for m in range(2, lines_total):
+            others[s, m] = swap(lines[m], "groups", s)
     shares = [lines[m] for m in range(lines_total)]
-    for s in range(1, share):
-        shares += [swap(block, ("groups", "ctx"), s * devices + m * SPAN) if m < 2 else swap(lines[m], "groups", s) for m in range(lines_total)]
+    shares += [others[s, m] for s in range(1, share) for m in range(lines_total)]
 
     far = swap(normed, "ctx", 2)
     near = swap(normed, "ctx", 1)
     both = swap(far, "ctx", 1)
+
     place = jnp.stack([line, group % share])
     part = part_call(place, shares, lines_total, share)
     part_far = swap(part, "ctx", 2)

time: 161 us -> 156 us (0.969)
  waiting for transfers between devices: 35.1 us -> 28.3 us
    ppermute x19, waiting for transfers between devices: 35.1 us -> 28.3 us  [swap(): return lax.ppermute(value, axis, [(i, i ^ bits) for i in range(size)])]
  transfers between devices with their start and end apart: 19 -> 19, of which waited for: 9 -> 8; matrix products, arithmetic and copies ran while one was open for 0% -> 0% of each run, Pallas kernels for 8% -> 9%
where the time goes in v6:
time: 156 us
  blocking collectives  71.8 us (46%)
  Pallas kernels  32.5 us (21%)
  waiting for transfers between devices  28.3 us (18%)
  starting transfers between devices  21.7 us (14%)
    all_to_all x1, blocking collectives, per_device(): lax.all_to_all(outgoing, 'ctx', split_axis=0, concat_axis=0, tiled=True)  36.6 us
    all_to_all x1, blocking collectives, per_device(): lax.all_to_all(produced, 'ctx', split_axis=0, concat_axis=0, tiled=True)  35.3 us
    ppermute x19, waiting for transfers between devices, swap(): return lax.ppermute(value, axis, [(i, i ^ bits) for i in range(size)])  28.3 us
    ppermute x19, starting transfers between devices, swap(): return lax.ppermute(value, axis, [(i, i ^ bits) for i in range(size)])  21.7 us
    pallas_call x1, Pallas kernels, expert_call(): pl.pallas_call(functools.partial(expert_kernel, local=local, sources=sour...  15.3 us
    pallas_call x1, Pallas kernels, attend_call(): pl.pallas_call(functools.partial(attend_kernel, blocks=blocks), out_shape...  6.66 us
    pallas_call x1, Pallas kernels, project_call(): pl.pallas_call(functools.partial(project_kernel, count=count, lines=lines...  4.16 us
  transfers between devices with their start and end apart: 19, of which 8 were waited for; matrix products, arithmetic and copies ran while one was open for 0% of the time, Pallas kernels for 9%

profile of v6, /device:TPU:1, one launch (start us, length us, event | category | flops | bytes accessed | tf_op | source)
XLA Modules:
  0.0 155.9 jit_solution(13191266618786866539)
XLA Ops:
  0.1 1.0 constant_dynamic-slice_fusion
  1.3 2.8 %collective-permute-start.1 = (bf16[64,512]{1,0:T(8,128)(2,1)S(1)}, bf16[64,512]{1,0:T(8,128)(2,1)S(1)}, u32[]{:S(2)}, u32[]{:S(2)}) collective-permute-start(bf16[64,512]{1,0:T(8,128)(2,1)S(1)} %pad_maximum_fusion.1), channel_id=1, source_target_pairs={{0,2},{1,3},{2,0},{3,1},{4,6},{5,7},{6,4},{7,5},{8,10},{9,11},{10,... | collective-permute-start | bytes 196616 | tf_op jit(solution)/shard_map/ppermute | solution.py:333
  4.6 0.7 route_slots.1
  5.4 1.1 collective-permute-done.1
  6.5 1.6 %collective-permute-done.2 = bf16[64,512]{1,0:T(8,128)(2,1)S(1)} collective-permute-done((bf16[64,512]{1,0:T(8,128)(2,1)S(1)}, bf16[64,512]{1,0:T(8,128)(2,1)S(1)}, u32[]{:S(2)}, u32[]{:S(2)}) %collective-permute-start.2) | collective-permute-done | bytes 65568 | tf_op jit(solution)/shard_map/ppermute | solution.py:333
  8.1 1.2 collective-permute-start.4
  9.3 2.3 %collective-permute-start.7 = (bf16[256,512]{1,0:T(8,128)(2,1)S(1)}, bf16[256,512]{1,0:T(8,128)(2,1)S(1)}, u32[]{:S(2)}, u32[]{:S(2)}) collective-permute-start(bf16[256,512]{1,0:T(8,128)(2,1)S(1)} %bitcast.23), channel_id=1, source_target_pairs={{0,8},{1,9},{2,10},{3,11},{4,12},{5,13},{6,14},{7,15},{8,0},{9,1},... | collective-permute-start | bytes 786440 | tf_op jit(solution)/shard_map/ppermute | solution.py:333
  11.7 1.2 collective-permute-start.8
  12.9 1.3 collective-permute-start.9
  14.1 9.1 %collective-permute-done.7.refs_6_.refs_2_ = bf16[256,512]{1,0:T(8,128)(2,1)S(1)} collective-permute-done((bf16[256,512]{1,0:T(8,128)(2,1)S(1)}, bf16[256,512]{1,0:T(8,128)(2,1)S(1)}, u32[]{:S(2)}, u32[]{:S(2)}) %collective-permute-start.7) | collective-permute-done | bytes 262176 | tf_op jit(solution)/shard_map/ppermute | solution.py:333
  23.2 2.4 %collective-permute-start.10 = (bf16[256,512]{1,0:T(8,128)(2,1)S(1)}, bf16[256,512]{1,0:T(8,128)(2,1)}, u32[]{:S(2)}, u32[]{:S(2)}) collective-permute-start(bf16[256,512]{1,0:T(8,128)(2,1)S(1)} %collective-permute-done.7.refs_6_.refs_2_), channel_id=1, source_target_pairs={{0,4},{1,5},{2,6},{3,7},{4,0},{5,1},{6,2},{7,3},{8,12},{9,13},{10,... | collective-permute-start | bytes 786440 | tf_op jit(solution)/shard_map/ppermute | solution.py:333
  25.6 2.0 %collective-permute-start.3 = (bf16[256,1024]{1,0:T(8,128)(2,1)S(1)}, bf16[256,1024]{1,0:T(8,128)(2,1)}, u32[]{:S(2)}, u32[]{:S(2)}) collective-permute-start(bf16[256,1024]{1,0:T(8,128)(2,1)S(1)} %norm_tokens.1.refs_0_), channel_id=1, source_target_pairs={{0,1},{1,0},{2,3},{3,2},{4,5},{5,4},{6,7},{7,6},{8,9},{9,8},{10,11... | collective-permute-start | bytes 1572872 | tf_op jit(solution)/shard_map/ppermute | solution.py:333
  27.6 1.2 collective-permute-start.6
  29.1 0.4 collective-permute-done.10.refs_7_.refs_3_
  29.5 0.8 collective-permute-start.12
  30.3 5.7 %collective-permute-done.6.refs_5_.refs_1_ = bf16[256,512]{1,0:T(8,128)(2,1)} collective-permute-done((bf16[256,512]{1,0:T(8,128)(2,1)S(1)}, bf16[256,512]{1,0:T(8,128)(2,1)}, u32[]{:S(2)}, u32[]{:S(2)}) %collective-permute-start.6) | collective-permute-done | bytes 262176 | tf_op jit(solution)/shard_map/ppermute | solution.py:333
  36.0 4.3 %collective-permute-done.12.refs_11_.refs_7_ = bf16[256,512]{1,0:T(8,128)(2,1)} collective-permute-done((bf16[256,512]{1,0:T(8,128)(2,1)}, bf16[256,512]{1,0:T(8,128)(2,1)}, u32[]{:S(2)}, u32[]{:S(2)}) %collective-permute-start.12) | collective-permute-done | bytes 262176 | tf_op jit(solution)/shard_map/ppermute | solution.py:333
  40.3 1.5 out_weight_part.1.refs_4_
  41.8 0.4 collective-permute-start.13
  42.2 3.2 %collective-permute-start.17 = (bf16[1024,256]{1,0:T(8,128)(2,1)S(1)}, bf16[1024,256]{1,0:T(8,128)(2,1)S(1)}, u32[]{:S(2)}, u32[]{:S(2)}) collective-permute-start(bf16[1024,256]{1,0:T(8,128)(2,1)S(1)} %out_weight_part.1.refs_4_), channel_id=1, source_target_pairs={{0,1},{1,0},{2,3},{3,2},{4,5},{5,4},{6,7},{7,6},{8,9},{9,8},{10,11... | collective-permute-start | bytes 1572872 | tf_op jit(solution)/shard_map/ppermute | solution.py:333
  45.5 4.2 %project.1.p_ref = bf16[1024,768]{1,0:T(8,128)(2,1)S(1)} custom-call(s32[2]{0:T(128)S(1)} %pad_add_fusion.place_ref, bf16[256,1024]{1,0:T(8,128)(2,1)S(1)} %norm_tokens.1.refs_0_, bf16[256,1024]{1,0:T(8,128)(2,1)} %collective-permute-done.3.refs_1_, bf16[256,1024]{1,0:T(8,128)(2,1)} %collective-permute-done.4.refs_2_, ...), custom_call_target="tpu_custom_call" | custom-call | flops 1610612736 | bytes 6291456 | tf_op jit(solution)/shard_map/project/pallas_call | solution.py:153
  49.7 6.7 %attend.1 = (bf16[256,256]{1,0:T(8,128)(2,1)S(1)}, bf16[256,256]{1,0:T(8,128)(2,1)S(1)}, bf16[256,256]{1,0:T(8,128)(2,1)S(1)}, bf16[256,256]{1,0:T(8,128)(2,1)S(1)}) custom-call(bf16[1024,768]{1,0:T(8,128)(2,1)S(1)} %project.1.p_ref), custom_call_target="tpu_custom_call" | custom-call | flops 4294967296 | bytes 1572864 | tf_op jit(solution)/shard_map/attend/pallas_call | solution.py:187
  56.3 0.4 collective-permute-start.18
  56.9 1.2 collective-permute-start.15
  58.1 0.8 collective-permute-start.16
  58.9 2.8 %collective-permute-done.15.refs_2_ = bf16[256,256]{1,0:T(8,128)(2,1)S(1)} collective-permute-done((bf16[256,256]{1,0:T(8,128)(2,1)S(1)}, bf16[256,256]{1,0:T(8,128)(2,1)S(1)}, u32[]{:S(2)}, u32[]{:S(2)}) %collective-permute-start.15) | collective-permute-done | bytes 131104 | tf_op jit(solution)/shard_map/ppermute | solution.py:333
  61.7 3.3 %collective-permute-done.16.refs_3_ = bf16[256,256]{1,0:T(8,128)(2,1)S(1)} collective-permute-done((bf16[256,256]{1,0:T(8,128)(2,1)S(1)}, bf16[256,256]{1,0:T(8,128)(2,1)S(1)}, u32[]{:S(2)}, u32[]{:S(2)}) %collective-permute-start.16) | collective-permute-done | bytes 131104 | tf_op jit(solution)/shard_map/ppermute | solution.py:333
  65.0 1.6 %out_projection.1 = (f32[256,1024]{1,0:T(8,128)S(1)}, bf16[640,1024]{1,0:T(8,128)(2,1)S(1)}) custom-call(s32[1]{0:T(128)} %bitcast.place_ref, bf16[256,1024]{1,0:T(8,128)(2,1)S(1)} %copy-done, bf16[640,256]{1,0:T(8,128)(2,1)S(1)} %get-tuple-element.30.d_ref, bf16[256,256]{1,0:T(8,128)(2,1)S(1)} %get-tuple-element.37.refs_0_, ...), custom_call_target="tpu_custom_call" | custom-call | flops 872415232 | bytes 6291456 | tf_op jit(solution)/shard_map/out_projection/pallas_call | solution.py:215
  66.5 36.6 %all_to_all.10 = bf16[16,40,1024]{2,1,0:T(8,128)(2,1)} all-to-all(bf16[16,40,1024]{2,1,0:T(8,128)(2,1)S(1)} %bitcast.21), channel_id=1, replica_groups=mesh['groups'=2,'ctx'=16] {'ctx'}, dimensions={0} | all-to-all | bytes 2621440 | tf_op jit(solution)/shard_map/all_to_all | solution.py:410
  103.1 15.3 %experts.1 = bf16[640,1024]{1,0:T(8,128)(2,1)S(1)} custom-call(bf16[640,1024]{1,0:T(8,128)(2,1)} %bitcast.33, bf16[1024,8192]{1,0:T(8,128)(2,1)S(1)} %bitcast.30, bf16[8192,1024]{1,0:T(8,128)(2,1)} %wout_ref.1), custom_call_target="tpu_custom_call" | custom-call | flops 10737418240 | bytes 33554432 | tf_op jit(solution)/shard_map/experts/pallas_call | solution.py:293
  118.4 35.3 %all_to_all.11 = bf16[16,40,1024]{2,1,0:T(8,128)(2,1)S(1)} all-to-all(bf16[16,40,1024]{2,1,0:T(8,128)(2,1)S(1)} %bitcast.22), channel_id=1, replica_groups=mesh['groups'=2,'ctx'=16] {'ctx'}, dimensions={0} | all-to-all | bytes 2621440 | tf_op jit(solution)/shard_map/all_to_all | solution.py:413
  153.7 2.2 %combine.1 = bf16[256,1024]{1,0:T(8,128)(2,1)} custom-call(f32[256,1024]{1,0:T(8,128)S(1)} %get-tuple-element.42.r_ref, bf16[640,1024]{1,0:T(8,128)(2,1)S(1)} %bitcast.20, bf16[640,256]{1,0:T(8,128)(2,1)S(1)} %get-tuple-element.44.hi_ref, bf16[640,256]{1,0:T(8,128)(2,1)S(1)} %get-tuple-element.45.mid_ref, bf16[640,256]{1,0:T(8,128)(2,1)S(1)} %get-tuple-element.46.lo_ref), custom_call_target="tpu_custom_call" | custom-call | flops 1006632960 | bytes 2883584 | tf_op jit(solution)/shard_map/combine/pallas_call | solution.py:322
  (41 shorter events, 1.1 us)
Async XLA Ops:
  0.0 4.2 %copy-start = (bf16[256,1024]{1,0:T(8,128)(2,1)S(1)}, bf16[256,1024]{1,0:T(8,128)(2,1)}, u32[]{:S(2)}) copy-start(bf16[256,1024]{1,0:T(8,128)(2,1)} %t_ref.1) | copy-start | bytes 1572868
  0.0 4.5 %copy-start.1 = (s32[256,2]{0,1:T(2,128)S(1)}, s32[256,2]{0,1:T(2,128)}, u32[]{:S(2)}) copy-start(s32[256,2]{0,1:T(2,128)} %param.8) | copy-start | bytes 6148
  0.0 4.5 %copy-start.2 = (f32[256,2]{0,1:T(2,128)S(1)}, f32[256,2]{0,1:T(2,128)}, u32[]{:S(2)}) copy-start(f32[256,2]{0,1:T(2,128)} %param.9) | copy-start | bytes 6148
  1.2 4.2 %collective-permute-start = (bf16[64,512]{1,0:T(8,128)(2,1)S(1)}, bf16[64,512]{1,0:T(8,128)(2,1)S(1)}, u32[]{:S(2)}, u32[]{:S(2)}) collective-permute-start(bf16[64,512]{1,0:T(8,128)(2,1)S(1)} %pad_maximum_fusion), channel_id=1, source_target_pairs={{0,1},{1,0},{2,3},{3,2},{4,5},{5,4},{6,7},{7,6},{8,9},{9,8},{10,11... | collective-permute-start | bytes 196616 | tf_op jit(solution)/shard_map/ppermute | solution.py:333
  1.3 5.2 %collective-permute-start.1 = (bf16[64,512]{1,0:T(8,128)(2,1)S(1)}, bf16[64,512]{1,0:T(8,128)(2,1)S(1)}, u32[]{:S(2)}, u32[]{:S(2)}) collective-permute-start(bf16[64,512]{1,0:T(8,128)(2,1)S(1)} %pad_maximum_fusion.1), channel_id=1, source_target_pairs={{0,2},{1,3},{2,0},{3,1},{4,6},{5,7},{6,4},{7,5},{8,10},{9,11},{10,... | collective-permute-start | bytes 196616 | tf_op jit(solution)/shard_map/ppermute | solution.py:333
  4.1 4.1 %collective-permute-start.2 = (bf16[64,512]{1,0:T(8,128)(2,1)S(1)}, bf16[64,512]{1,0:T(8,128)(2,1)S(1)}, u32[]{:S(2)}, u32[]{:S(2)}) collective-permute-start(bf16[64,512]{1,0:T(8,128)(2,1)S(1)} %pad_maximum_fusion.2), channel_id=1, source_target_pairs={{0,3},{1,2},{2,1},{3,0},{4,7},{5,6},{6,5},{7,4},{8,11},{9,10},{10,... | collective-permute-start | bytes 196616 | tf_op jit(solution)/shard_map/ppermute | solution.py:333
  8.1 19.4 %collective-permute-start.4 = (bf16[256,1024]{1,0:T(8,128)(2,1)S(1)}, bf16[256,1024]{1,0:T(8,128)(2,1)}, u32[]{:S(2)}, u32[]{:S(2)}) collective-permute-start(bf16[256,1024]{1,0:T(8,128)(2,1)S(1)} %norm_tokens.1.refs_0_), channel_id=1, source_target_pairs={{0,2},{1,3},{2,0},{3,1},{4,6},{5,7},{6,4},{7,5},{8,10},{9,11},{10,... | collective-permute-start | bytes 1572872 | tf_op jit(solution)/shard_map/ppermute | solution.py:333
  9.3 13.9 %collective-permute-start.7 = (bf16[256,512]{1,0:T(8,128)(2,1)S(1)}, bf16[256,512]{1,0:T(8,128)(2,1)S(1)}, u32[]{:S(2)}, u32[]{:S(2)}) collective-permute-start(bf16[256,512]{1,0:T(8,128)(2,1)S(1)} %bitcast.23), channel_id=1, source_target_pairs={{0,8},{1,9},{2,10},{3,11},{4,12},{5,13},{6,14},{7,15},{8,0},{9,1},... | collective-permute-start | bytes 786440 | tf_op jit(solution)/shard_map/ppermute | solution.py:333
  11.7 11.6 %collective-permute-start.8 = (bf16[256,512]{1,0:T(8,128)(2,1)S(1)}, bf16[256,512]{1,0:T(8,128)(2,1)S(1)}, u32[]{:S(2)}, u32[]{:S(2)}) collective-permute-start(bf16[256,512]{1,0:T(8,128)(2,1)S(1)} %bitcast.24), channel_id=1, source_target_pairs={{0,16},{1,17},{2,18},{3,19},{4,20},{5,21},{6,22},{7,23},{8,24},{9,... | collective-permute-start | bytes 786440 | tf_op jit(solution)/shard_map/ppermute | solution.py:333
  12.9 10.4 %collective-permute-start.9 = (bf16[256,512]{1,0:T(8,128)(2,1)S(1)}, bf16[256,512]{1,0:T(8,128)(2,1)S(1)}, u32[]{:S(2)}, u32[]{:S(2)}) collective-permute-start(bf16[256,512]{1,0:T(8,128)(2,1)S(1)} %bitcast.25), channel_id=1, source_target_pairs={{0,20},{1,21},{2,22},{3,23},{4,16},{5,17},{6,18},{7,19},{8,28},{9,... | collective-permute-start | bytes 786440 | tf_op jit(solution)/shard_map/ppermute | solution.py:333
  23.2 6.3 %collective-permute-start.10 = (bf16[256,512]{1,0:T(8,128)(2,1)S(1)}, bf16[256,512]{1,0:T(8,128)(2,1)}, u32[]{:S(2)}, u32[]{:S(2)}) collective-permute-start(bf16[256,512]{1,0:T(8,128)(2,1)S(1)} %collective-permute-done.7.refs_6_.refs_2_), channel_id=1, source_target_pairs={{0,4},{1,5},{2,6},{3,7},{4,0},{5,1},{6,2},{7,3},{8,12},{9,13},{10,... | collective-permute-start | bytes 786440 | tf_op jit(solution)/shard_map/ppermute | solution.py:333
  25.6 19.9 %collective-permute-start.3 = (bf16[256,1024]{1,0:T(8,128)(2,1)S(1)}, bf16[256,1024]{1,0:T(8,128)(2,1)}, u32[]{:S(2)}, u32[]{:S(2)}) collective-permute-start(bf16[256,1024]{1,0:T(8,128)(2,1)S(1)} %norm_tokens.1.refs_0_), channel_id=1, source_target_pairs={{0,1},{1,0},{2,3},{3,2},{4,5},{5,4},{6,7},{7,6},{8,9},{9,8},{10,11... | collective-permute-start | bytes 1572872 | tf_op jit(solution)/shard_map/ppermute | solution.py:333
  27.6 17.9 %collective-permute-start.5 = (bf16[256,1024]{1,0:T(8,128)(2,1)}, bf16[256,1024]{1,0:T(8,128)(2,1)}, u32[]{:S(2)}, u32[]{:S(2)}) collective-permute-start(bf16[256,1024]{1,0:T(8,128)(2,1)} %collective-permute-done.4.refs_2_), channel_id=1, source_target_pairs={{0,1},{1,0},{2,3},{3,2},{4,5},{5,4},{6,7},{7,6},{8,9},{9,8},{10,11... | collective-permute-start | bytes 1572872 | tf_op jit(solution)/shard_map/ppermute | solution.py:333
  27.6 8.4 %collective-permute-start.6 = (bf16[256,512]{1,0:T(8,128)(2,1)S(1)}, bf16[256,512]{1,0:T(8,128)(2,1)}, u32[]{:S(2)}, u32[]{:S(2)}) collective-permute-start(bf16[256,512]{1,0:T(8,128)(2,1)S(1)} %bitcast.26), channel_id=1, source_target_pairs={{0,4},{1,5},{2,6},{3,7},{4,0},{5,1},{6,2},{7,3},{8,12},{9,13},{10,... | collective-permute-start | bytes 786440 | tf_op jit(solution)/shard_map/ppermute | solution.py:333
  28.8 7.2 %collective-permute-start.11 = (bf16[256,512]{1,0:T(8,128)(2,1)S(1)}, bf16[256,512]{1,0:T(8,128)(2,1)}, u32[]{:S(2)}, u32[]{:S(2)}) collective-permute-start(bf16[256,512]{1,0:T(8,128)(2,1)S(1)} %collective-permute-done.7.refs_6_.refs_2_), channel_id=1, source_target_pairs={{0,16},{16,0},{1,17},{17,1},{2,18},{18,2},{3,19},{19,3},{4,20},{20... | collective-permute-start | bytes 786440 | tf_op jit(solution)/shard_map/ppermute | solution.py:333
  29.5 10.8 %collective-permute-start.12 = (bf16[256,512]{1,0:T(8,128)(2,1)}, bf16[256,512]{1,0:T(8,128)(2,1)}, u32[]{:S(2)}, u32[]{:S(2)}) collective-permute-start(bf16[256,512]{1,0:T(8,128)(2,1)} %collective-permute-done.10.refs_7_.refs_3_), channel_id=1, source_target_pairs={{0,16},{16,0},{1,17},{17,1},{2,18},{18,2},{3,19},{19,3},{4,20},{20... | collective-permute-start | bytes 786440 | tf_op jit(solution)/shard_map/ppermute | solution.py:333
  40.3 62.8 %slice-start = ((s8[16777216]{0:T(1024)(128)(4,1)}), s8[4194304]{0:T(1024)(128)(4,1)S(1)}, s32[]{:S(2)}) async-start(s8[16777216]{0:T(1024)(128)(4,1)} %bitcast.29), calls=%async_computation.2 | async-start | bytes 8388608
  41.8 61.3 %slice-start.1 = ((s8[16777216]{0:T(1024)(128)(4,1)}), s8[4194304]{0:T(1024)(128)(4,1)S(1)}, s32[]{:S(2)}) async-start(s8[16777216]{0:T(1024)(128)(4,1)} %bitcast.29), calls=%async_computation.3 | async-start | bytes 8388608
  41.8 14.5 %collective-permute-start.13 = (bf16[1024,256]{1,0:T(8,128)(2,1)S(1)}, bf16[1024,256]{1,0:T(8,128)(2,1)S(1)}, u32[]{:S(2)}, u32[]{:S(2)}) collective-permute-start(bf16[1024,256]{1,0:T(8,128)(2,1)S(1)} %out_weight_part.1.refs_4_), channel_id=1, source_target_pairs={{0,2},{1,3},{2,0},{3,1},{4,6},{5,7},{6,4},{7,5},{8,10},{9,11},{10,... | collective-permute-start | bytes 1572872 | tf_op jit(solution)/shard_map/ppermute | solution.py:333
  42.2 22.7 %collective-permute-start.17 = (bf16[1024,256]{1,0:T(8,128)(2,1)S(1)}, bf16[1024,256]{1,0:T(8,128)(2,1)S(1)}, u32[]{:S(2)}, u32[]{:S(2)}) collective-permute-start(bf16[1024,256]{1,0:T(8,128)(2,1)S(1)} %out_weight_part.1.refs_4_), channel_id=1, source_target_pairs={{0,1},{1,0},{2,3},{3,2},{4,5},{5,4},{6,7},{7,6},{8,9},{9,8},{10,11... | collective-permute-start | bytes 1572872 | tf_op jit(solution)/shard_map/ppermute | solution.py:333
  49.6 53.5 %slice-start.2 = ((s8[16777216]{0:T(1024)(128)(4,1)}), s8[4194304]{0:T(1024)(128)(4,1)S(1)}, s32[]{:S(2)}) async-start(s8[16777216]{0:T(1024)(128)(4,1)} %bitcast.29), calls=%async_computation.4 | async-start | bytes 8388608
  49.6 53.5 %slice-start.3 = ((s8[16777216]{0:T(1024)(128)(4,1)}), s8[4194304]{0:T(1024)(128)(4,1)S(1)}, s32[]{:S(2)}) async-start(s8[16777216]{0:T(1024)(128)(4,1)} %bitcast.29), calls=%async_computation.5 | async-start | bytes 8388608
  56.3 8.6 %collective-permute-start.18 = (bf16[1024,256]{1,0:T(8,128)(2,1)S(1)}, bf16[1024,256]{1,0:T(8,128)(2,1)S(1)}, u32[]{:S(2)}, u32[]{:S(2)}) collective-permute-start(bf16[1024,256]{1,0:T(8,128)(2,1)S(1)} %collective-permute-done.13.refs_6_), channel_id=1, source_target_pairs={{0,1},{1,0},{2,3},{3,2},{4,5},{5,4},{6,7},{7,6},{8,9},{9,8},{10,11... | collective-permute-start | bytes 1572872 | tf_op jit(solution)/shard_map/ppermute | solution.py:333
  56.7 2.1 %collective-permute-start.14 = (bf16[256,256]{1,0:T(8,128)(2,1)S(1)}, bf16[256,256]{1,0:T(8,128)(2,1)S(1)}, u32[]{:S(2)}, u32[]{:S(2)}) collective-permute-start(bf16[256,256]{1,0:T(8,128)(2,1)S(1)} %get-tuple-element.38), channel_id=1, source_target_pairs={{0,1},{1,0},{2,3},{3,2},{4,5},{5,4},{6,7},{7,6},{8,9},{9,8},{10,11... | collective-permute-start | bytes 393224 | tf_op jit(solution)/shard_map/ppermute | solution.py:333
  56.9 4.8 %collective-permute-start.15 = (bf16[256,256]{1,0:T(8,128)(2,1)S(1)}, bf16[256,256]{1,0:T(8,128)(2,1)S(1)}, u32[]{:S(2)}, u32[]{:S(2)}) collective-permute-start(bf16[256,256]{1,0:T(8,128)(2,1)S(1)} %get-tuple-element.39), channel_id=1, source_target_pairs={{0,2},{1,3},{2,0},{3,1},{4,6},{5,7},{6,4},{7,5},{8,10},{9,11},{10,... | collective-permute-start | bytes 393224 | tf_op jit(solution)/shard_map/ppermute | solution.py:333
  58.1 6.9 %collective-permute-start.16 = (bf16[256,256]{1,0:T(8,128)(2,1)S(1)}, bf16[256,256]{1,0:T(8,128)(2,1)S(1)}, u32[]{:S(2)}, u32[]{:S(2)}) collective-permute-start(bf16[256,256]{1,0:T(8,128)(2,1)S(1)} %get-tuple-element.40), channel_id=1, source_target_pairs={{0,3},{1,2},{2,1},{3,0},{4,7},{5,6},{6,5},{7,4},{8,11},{9,10},{10,... | collective-permute-start | bytes 393224 | tf_op jit(solution)/shard_map/ppermute | solution.py:333

commit v7 on v6

--- a/solution.py
+++ b/solution.py
@@ -96,32 +96,25 @@
     )(routes.T, gates.T)
 
 
-def part_kernel(place_ref, *refs, lines, share):
-    ws, o_ref, full = refs[: lines * share], refs[lines * share], refs[lines * share + 1]
-    size, wide = ws[0].shape
-    cols = wide // 4
-    for s in range(share):
-        for m in range(lines):
-            start = pl.multiple_of((place_ref[0] ^ m) * size, size)
-            full[place_ref[1] ^ s, pl.ds(start, size), :] = ws[s * lines + m][:, 3 * cols :]
-    for s in range(share):
-        o_ref[:, s * cols : (s + 1) * cols] = full[s]
-
-
-def part_call(place, ws, lines, share):
-    size, wide = ws[0].shape
-    cols = wide // 4
+def part_kernel(line_ref, *refs):
+    ws, o_ref = refs[:-1], refs[-1]
+    size = ws[0].shape[0]
+    for m, w_ref in enumerate(ws):
+        o_ref[pl.ds(pl.multiple_of((line_ref[0] ^ m) * size, size), size), :] = w_ref[...]
+
+
+def part_call(line, ws):
+    size, cols = ws[0].shape
     vm = pl.BlockSpec(memory_space=pltpu.VMEM)
     return pl.pallas_call(
-        functools.partial(part_kernel, lines=lines, share=share),
-        out_shape=jax.ShapeDtypeStruct((lines * size, share * cols), bf16),
-        in_specs=[pl.BlockSpec(memory_space=pltpu.SMEM)] + [vm] * (lines * share),
+        part_kernel,
+        out_shape=jax.ShapeDtypeStruct((len(ws) * size, cols), bf16),
+        in_specs=[pl.BlockSpec(memory_space=pltpu.SMEM)] + [vm] * len(ws),
         out_specs=vm,
-        scratch_shapes=[pltpu.VMEM((share, lines * size, cols), bf16)],
-        compiler_params=params(),
-        cost_estimate=cost(1, 4 * lines * size * share * cols),
+        compiler_params=params(),
+        cost_estimate=cost(1, 4 * len(ws) * size * cols),
         name="out_weight_part",
-    )(place, *ws)
+    )(line, *ws)
 
 
 def project_kernel(place_ref, *refs, count, lines, share):
@@ -129,13 +122,13 @@
     ws = refs[count : count + lines * share]
     o_ref, full = refs[count + lines * share :]
     size, wide = ws[0].shape
-    cols = wide // 4
+    cols = wide // 3
     rows = xs[0].shape[0]
     mine = share * cols
     for s in range(share):
         for m in range(lines):
             start = pl.multiple_of((place_ref[0] ^ m) * size, size)
-            full[place_ref[1] ^ s, pl.ds(start, size), :] = ws[s * lines + m][:, : 3 * cols]
+            full[place_ref[1] ^ s, pl.ds(start, size), :] = ws[s * lines + m][...]
     for s in range(share):
         for j in range(count):
             got = mm(xs[j][...], full[s]).astype(bf16)
@@ -148,7 +141,7 @@
 def project_call(place, xs, ws, lines, share):
     rows, width = xs[0].shape
     count = len(xs)
-    cols = ws[0].shape[1] // 4
+    cols = ws[0].shape[1] // 3
     vm = pl.BlockSpec(memory_space=pltpu.VMEM)
     return pl.pallas_call(
         functools.partial(project_kernel, count=count, lines=lines, share=share),
@@ -195,25 +188,36 @@
     )(projected)
 
 
-def output_kernel(place_ref, t_ref, d_ref, *refs):
+def output_kernel(place_ref, t_ref, d_ref, *refs, share):
     ctxs, parts = refs[:SPAN], refs[SPAN : 2 * SPAN]
     r_ref, o_ref, c_ref, a_ref = refs[2 * SPAN :]
     wide = ctxs[0].shape[1]
+    cols = wide // share
     starts = [pl.multiple_of((place_ref[0] ^ j) * wide, wide) for j in range(SPAN)]
+
+    def natural(value):
+        pieces = []
+        for p in range(share):
+            piece = value[:, :cols]
+            for s in range(1, share):
+                piece = jnp.where((place_ref[1] ^ s) == p, value[:, s * cols : (s + 1) * cols], piece)
+            pieces.append(piece)
+        return jnp.concatenate(pieces, axis=1) if share > 1 else value
+
     for j in range(SPAN):
         c_ref[:, pl.ds(starts[j], wide)] = ctxs[j][...]
     for j in range(SPAN):
-        a_ref[:, pl.ds(starts[j], wide)] = mm(c_ref[...], parts[j][...])
+        a_ref[:, pl.ds(starts[j], wide)] = natural(mm(c_ref[...], parts[j][...]))
     total = t_ref[...].astype(f32) + a_ref[...]
     r_ref[...] = total
     o_ref[...] = mm(d_ref[...], normalize(total)).astype(bf16)
 
 
-def output_call(place, tokens, marks, parts, ctxs):
+def output_call(place, tokens, marks, parts, ctxs, share):
     rows, width = tokens.shape
     vm = pl.BlockSpec(memory_space=pltpu.VMEM)
     return pl.pallas_call(
-        output_kernel,
+        functools.partial(output_kernel, share=share),
         out_shape=[
             jax.ShapeDtypeStruct((rows, width), f32),
             jax.ShapeDtypeStruct((marks.shape[0], width), bf16),
@@ -363,8 +367,9 @@
     for j in range(SPAN):
         block = lax.dynamic_update_slice(block, pieces[j][None], (member ^ j, 0, 0))
     block = block.reshape(-1, 4 * cols)
+    block, last = block[:, : 3 * cols], block[:, 3 * cols :]
     slots = route_call(routes, gates)
-    normed, block, slots = lax.optimization_barrier((norm_call(tokens), block, slots))
+    normed, block, last, slots = lax.optimization_barrier((norm_call(tokens), block, last, slots))
     marks, *gate_parts = slots
     bits = [1 << i for i in reversed(range(lines_total.bit_length() - 1))]
     lines = {0: block}
@@ -380,8 +385,14 @@
         for known in [m for m in lines if m >= 2 * bit and m & (2 * bit - 1) == 0]:
             lines[known | bit] = swap(lines[known], "ctx", bit * SPAN)
     for s in range(1, share):
-        for m in range(2, lines_total):
+        for m in bits[:-1]:
             others[s, m] = swap(lines[m], "groups", s)
+    if share > 1 and len(bits) > 1:
+        lines[lines_total - 1], others = lax.optimization_barrier((lines[lines_total - 1], others))
+    for s in range(1, share):
+        for m in range(lines_total):
+            if (s, m) not in others:
+                others[s, m] = swap(lines[m], "groups", s)
     shares = [lines[m] for m in range(lines_total)]
     shares += [others[s, m] for s in range(1, share) for m in range(lines_total)]
 
@@ -389,10 +400,16 @@
     near = swap(normed, "ctx", 1)
     both = swap(far, "ctx", 1)
 
-    place = jnp.stack([line, group % share])
-    part = part_call(place, shares, lines_total, share)
+    pieces = {0: last}
+    for bit in bits:
+        for known in list(pieces):
+            pieces[known | bit] = swap(pieces[known], "ctx", bit * SPAN)
+    part = part_call(line.reshape(1), [pieces[m] for m in range(lines_total)])
+    part = jnp.concatenate([part] + [swap(part, "groups", s) for s in range(1, share)], axis=1)
     part_far = swap(part, "ctx", 2)
     part_near = swap(part, "ctx", 1)
+
+    place = jnp.stack([line, group % share])
     projected = project_call(place, [normed, near, far, both], shares, lines_total, share)
     ctxs = attend_call(projected, (0, 1, 2, 3), rows)
     own, part_far = lax.optimization_barrier((ctxs[0], part_far))
@@ -400,7 +417,7 @@
     back = {0: own} | {j: swap(ctxs[j], "ctx", j) for j in range(1, SPAN)}
     ctxs = [back[j] for j in range(SPAN)]
     resid, table = output_call(
-        member.reshape(1), tokens, marks, [part, part_near, part_far, part_both], ctxs
+        jnp.stack([member, group % share]), tokens, marks, [part, part_near, part_far, part_both], ctxs, share
     )
 
     table = table.reshape(EXPERTS, CAP, width)

time: 156 us -> 161 us (1.032)
  local copies, waits for them, and re-layouts: 1.11 us -> 8.26 us
  waiting for transfers between devices: 28.3 us -> 21.3 us
  starting transfers between devices: 21.7 us -> 27.9 us
    unnamed x14 -> x16, local copies, waits for them, and re-layouts: 0.04 us -> 7.15 us
    ppermute x19 -> x23, waiting for transfers between devices: 28.3 us -> 21.3 us  [swap(): return lax.ppermute(value, axis, [(i, i ^ bits) for i in range(size)])]
    ppermute x19 -> x23, starting transfers between devices: 21.7 us -> 27.9 us  [swap(): return lax.ppermute(value, axis, [(i, i ^ bits) for i in range(size)])]
  transfers between devices with their start and end apart: 19 -> 23, of which waited for: 8 -> 8; matrix products, arithmetic and copies ran while one was open for 0% -> 0% of each run, Pallas kernels for 9% -> 7%
where the time goes in v7:
time: 161 us
  blocking collectives  71.9 us (45%)
  Pallas kernels  31.2 us (19%)
  starting transfers between devices  27.9 us (17%)
  waiting for transfers between devices  21.3 us (13%)
  local copies, waits for them, and re-layouts  8.26 us (5%)
    all_to_all x1, blocking collectives, per_device(): lax.all_to_all(outgoing, 'ctx', split_axis=0, concat_axis=0, tiled=True)  36.6 us
    all_to_all x1, blocking collectives, per_device(): lax.all_to_all(produced, 'ctx', split_axis=0, concat_axis=0, tiled=True)  35.3 us
    ppermute x23, starting transfers between devices, swap(): return lax.ppermute(value, axis, [(i, i ^ bits) for i in range(size)])  27.9 us
    ppermute x23, waiting for transfers between devices, swap(): return lax.ppermute(value, axis, [(i, i ^ bits) for i in range(size)])  21.3 us
    pallas_call x1, Pallas kernels, expert_call(): pl.pallas_call(functools.partial(expert_kernel, local=local, sources=sour...  15.3 us
    unnamed x16, local copies, waits for them, and re-layouts  7.15 us
    pallas_call x1, Pallas kernels, attend_call(): pl.pallas_call(functools.partial(attend_kernel, blocks=blocks), out_shape...  6.66 us
    pallas_call x1, Pallas kernels, project_call(): pl.pallas_call(functools.partial(project_kernel, count=count, lines=lines...  3.8 us
  transfers between devices with their start and end apart: 23, of which 8 were waited for; matrix products, arithmetic and copies ran while one was open for 0% of the time, Pallas kernels for 7%

profile of v7, /device:TPU:1, one launch (start us, length us, event | category | flops | bytes accessed | tf_op | source)
XLA Modules:
  0.0 161.1 jit_solution(10760471197292572543)
XLA Ops:
  0.1 1.0 constant_dynamic-slice_fusion
  1.3 2.8 %collective-permute-start.1 = (bf16[64,512]{1,0:T(8,128)(2,1)S(1)}, bf16[64,512]{1,0:T(8,128)(2,1)S(1)}, u32[]{:S(2)}, u32[]{:S(2)}) collective-permute-start(bf16[64,512]{1,0:T(8,128)(2,1)S(1)} %pad_maximum_fusion.2), channel_id=1, source_target_pairs={{0,2},{1,3},{2,0},{3,1},{4,6},{5,7},{6,4},{7,5},{8,10},{9,11},{10,... | collective-permute-start | bytes 196616 | tf_op jit(solution)/shard_map/ppermute | solution.py:337
  4.6 0.7 route_slots.1
  5.4 1.1 collective-permute-done.1
  6.5 1.6 %collective-permute-done.2 = bf16[64,512]{1,0:T(8,128)(2,1)S(1)} collective-permute-done((bf16[64,512]{1,0:T(8,128)(2,1)S(1)}, bf16[64,512]{1,0:T(8,128)(2,1)S(1)}, u32[]{:S(2)}, u32[]{:S(2)}) %collective-permute-start.2) | collective-permute-done | bytes 65568 | tf_op jit(solution)/shard_map/ppermute | solution.py:337
  8.2 1.2 collective-permute-start.4
  9.4 2.3 %collective-permute-start.7 = (bf16[256,384]{1,0:T(8,128)(2,1)S(1)}, bf16[256,384]{1,0:T(8,128)(2,1)S(1)}, u32[]{:S(2)}, u32[]{:S(2)}) collective-permute-start(bf16[256,384]{1,0:T(8,128)(2,1)S(1)} %slice.8.refs_4_), channel_id=1, source_target_pairs={{0,8},{1,9},{2,10},{3,11},{4,12},{5,13},{6,14},{7,15},{8,0},{9,1},... | collective-permute-start | bytes 589832 | tf_op jit(solution)/shard_map/ppermute | solution.py:337
  11.7 1.2 collective-permute-start.8
  12.9 1.3 collective-permute-start.9
  14.2 7.9 %collective-permute-done.14.refs_2_ = bf16[256,128]{1,0:T(8,128)(2,1)S(1)} collective-permute-done((bf16[256,128]{1,0:T(8,128)(2,1)S(1)}, bf16[256,128]{1,0:T(8,128)(2,1)S(1)}, u32[]{:S(2)}, u32[]{:S(2)}) %collective-permute-start.14) | collective-permute-done | bytes 65568 | tf_op jit(solution)/shard_map/ppermute | solution.py:337
  22.2 2.6 %collective-permute-start.3 = (bf16[256,1024]{1,0:T(8,128)(2,1)S(1)}, bf16[256,1024]{1,0:T(8,128)(2,1)}, u32[]{:S(2)}, u32[]{:S(2)}) collective-permute-start(bf16[256,1024]{1,0:T(8,128)(2,1)S(1)} %norm_tokens.1.refs_0_), channel_id=1, source_target_pairs={{0,1},{1,0},{2,3},{3,2},{4,5},{5,4},{6,7},{7,6},{8,9},{9,8},{10,11... | collective-permute-start | bytes 1572872 | tf_op jit(solution)/shard_map/ppermute | solution.py:337
  25.8 1.1 collective-permute-start.15
  28.0 1.2 collective-permute-start.11
  29.2 0.7 collective-permute-done.15.refs_3_
  30.0 1.3 collective-permute-start.16
  31.3 2.2 %collective-permute-done.10.refs_7_ = bf16[256,384]{1,0:T(8,128)(2,1)} collective-permute-done((bf16[256,384]{1,0:T(8,128)(2,1)S(1)}, bf16[256,384]{1,0:T(8,128)(2,1)}, u32[]{:S(2)}, u32[]{:S(2)}) %collective-permute-start.10) | collective-permute-done | bytes 196640 | tf_op jit(solution)/shard_map/ppermute | solution.py:337
  33.5 1.3 collective-permute-start.6
  34.8 1.2 collective-permute-start.12
  36.1 1.7 %collective-permute-done.16 = bf16[1024,128]{1,0:T(8,128)(2,1)S(1)} collective-permute-done((bf16[1024,128]{1,0:T(8,128)(2,1)S(1)}, bf16[1024,128]{1,0:T(8,128)(2,1)S(1)}, u32[]{:S(2)}, u32[]{:S(2)}) %collective-permute-start.16) | collective-permute-done | bytes 262176 | tf_op jit(solution)/shard_map/ppermute | solution.py:337
  38.3 5.4 %collective-permute-start.21 = (bf16[1024,256]{1,0:T(8,128)(2,1)S(1)}, bf16[1024,256]{1,0:T(8,128)(2,1)S(1)}, u32[]{:S(2)}, u32[]{:S(2)}) collective-permute-start(bf16[1024,256]{1,0:T(8,128)(2,1)S(1)} %pad_maximum_fusion.refs_4_), channel_id=1, source_target_pairs={{0,1},{1,0},{2,3},{3,2},{4,5},{5,4},{6,7},{7,6},{8,9},{9,8},{10,11... | collective-permute-start | bytes 1572872 | tf_op jit(solution)/shard_map/ppermute | solution.py:337
  43.8 3.8 %project.1.p_ref = bf16[1024,768]{1,0:T(8,128)(2,1)S(1)} custom-call(s32[2]{0:T(128)S(1)} %pad_add_fusion.1.place_ref, bf16[256,1024]{1,0:T(8,128)(2,1)S(1)} %norm_tokens.1.refs_0_, bf16[256,1024]{1,0:T(8,128)(2,1)} %collective-permute-done.3.refs_1_, bf16[256,1024]{1,0:T(8,128)(2,1)S(1)} %collective-permute-done.4.refs_2_, ...), custom_call_target="tpu_custom_call" | custom-call | flops 1610612736 | bytes 6291456 | tf_op jit(solution)/shard_map/project/pallas_call | solution.py:146
  47.6 6.7 %attend.1 = (bf16[256,256]{1,0:T(8,128)(2,1)S(1)}, bf16[256,256]{1,0:T(8,128)(2,1)S(1)}, bf16[256,256]{1,0:T(8,128)(2,1)S(1)}, bf16[256,256]{1,0:T(8,128)(2,1)S(1)}) custom-call(bf16[1024,768]{1,0:T(8,128)(2,1)S(1)} %project.1.p_ref), custom_call_target="tpu_custom_call" | custom-call | flops 4294967296 | bytes 1572864 | tf_op jit(solution)/shard_map/attend/pallas_call | solution.py:180
  54.3 1.4 collective-permute-start.22
  56.1 1.7 %collective-permute-start.20 = (bf16[256,256]{1,0:T(8,128)(2,1)S(1)}, bf16[256,256]{1,0:T(8,128)(2,1)S(1)}, u32[]{:S(2)}, u32[]{:S(2)}) collective-permute-start(bf16[256,256]{1,0:T(8,128)(2,1)S(1)} %get-tuple-element.50), channel_id=1, source_target_pairs={{0,3},{1,2},{2,1},{3,0},{4,7},{5,6},{6,5},{7,4},{8,11},{9,10},{10,... | collective-permute-start | bytes 393224 | tf_op jit(solution)/shard_map/ppermute | solution.py:337
  57.9 2.5 %collective-permute-done.19.refs_2_ = bf16[256,256]{1,0:T(8,128)(2,1)S(1)} collective-permute-done((bf16[256,256]{1,0:T(8,128)(2,1)S(1)}, bf16[256,256]{1,0:T(8,128)(2,1)S(1)}, u32[]{:S(2)}, u32[]{:S(2)}) %collective-permute-start.19) | collective-permute-done | bytes 131104 | tf_op jit(solution)/shard_map/ppermute | solution.py:337
  60.4 3.4 %collective-permute-done.20.refs_3_ = bf16[256,256]{1,0:T(8,128)(2,1)S(1)} collective-permute-done((bf16[256,256]{1,0:T(8,128)(2,1)S(1)}, bf16[256,256]{1,0:T(8,128)(2,1)S(1)}, u32[]{:S(2)}, u32[]{:S(2)}) %collective-permute-start.20) | collective-permute-done | bytes 131104 | tf_op jit(solution)/shard_map/ppermute | solution.py:337
  63.8 2.1 %out_projection.1 = (f32[256,1024]{1,0:T(8,128)S(1)}, bf16[640,1024]{1,0:T(8,128)(2,1)S(1)}) custom-call(s32[2]{0:T(128)S(1)} %pad_add_fusion.place_ref, bf16[256,1024]{1,0:T(8,128)(2,1)S(1)} %copy-done, bf16[640,256]{1,0:T(8,128)(2,1)S(1)} %get-tuple-element.35.d_ref, bf16[256,256]{1,0:T(8,128)(2,1)S(1)} %get-tuple-element.47.refs_0_, ...), custom_call_target="tpu_custom_call" | custom-call | flops 872415232 | bytes 6291456 | tf_op jit(solution)/shard_map/out_projection/pallas_call | solution.py:219
  66.0 36.6 %all_to_all.10 = bf16[16,40,1024]{2,1,0:T(8,128)(2,1)} all-to-all(bf16[16,40,1024]{2,1,0:T(8,128)(2,1)S(1)} %bitcast.21), channel_id=1, replica_groups=mesh['groups'=2,'ctx'=16] {'ctx'}, dimensions={0} | all-to-all | bytes 2621440 | tf_op jit(solution)/shard_map/all_to_all | solution.py:427
  102.6 5.8 %copy-done.1 = bf16[1024,8192]{1,0:T(8,128)(2,1)S(1)} copy-done((bf16[1024,8192]{1,0:T(8,128)(2,1)S(1)}, bf16[1024,8192]{1,0:T(8,128)(2,1)}, u32[]{:S(2)}) %copy-start.1) | copy-done | bytes 16777240
  108.3 15.3 %experts.1 = bf16[640,1024]{1,0:T(8,128)(2,1)S(1)} custom-call(bf16[640,1024]{1,0:T(8,128)(2,1)} %bitcast.25, bf16[1024,8192]{1,0:T(8,128)(2,1)S(1)} %copy-done.1, bf16[8192,1024]{1,0:T(8,128)(2,1)} %wout_ref.1), custom_call_target="tpu_custom_call" | custom-call | flops 10737418240 | bytes 33554432 | tf_op jit(solution)/shard_map/experts/pallas_call | solution.py:297
  123.6 35.3 %all_to_all.11 = bf16[16,40,1024]{2,1,0:T(8,128)(2,1)S(1)} all-to-all(bf16[16,40,1024]{2,1,0:T(8,128)(2,1)S(1)} %bitcast.22), channel_id=1, replica_groups=mesh['groups'=2,'ctx'=16] {'ctx'}, dimensions={0} | all-to-all | bytes 2621440 | tf_op jit(solution)/shard_map/all_to_all | solution.py:430
  158.9 2.2 %combine.1 = bf16[256,1024]{1,0:T(8,128)(2,1)} custom-call(f32[256,1024]{1,0:T(8,128)S(1)} %get-tuple-element.52.r_ref, bf16[640,1024]{1,0:T(8,128)(2,1)S(1)} %bitcast.20, bf16[640,256]{1,0:T(8,128)(2,1)S(1)} %get-tuple-element.54.hi_ref, bf16[640,256]{1,0:T(8,128)(2,1)S(1)} %get-tuple-element.55.mid_ref, bf16[640,256]{1,0:T(8,128)(2,1)S(1)} %get-tuple-element.56.lo_ref), custom_call_target="tpu_custom_call" | custom-call | flops 1006632960 | bytes 2883584 | tf_op jit(solution)/shard_map/combine/pallas_call | solution.py:326
  (54 shorter events, 3.8 us)
Async XLA Ops:
  0.0 4.2 %copy-start = (bf16[256,1024]{1,0:T(8,128)(2,1)S(1)}, bf16[256,1024]{1,0:T(8,128)(2,1)}, u32[]{:S(2)}) copy-start(bf16[256,1024]{1,0:T(8,128)(2,1)} %t_ref.1) | copy-start | bytes 1572868
  0.0 4.5 %copy-start.6 = (s32[256,2]{0,1:T(2,128)S(1)}, s32[256,2]{0,1:T(2,128)}, u32[]{:S(2)}) copy-start(s32[256,2]{0,1:T(2,128)} %param.8) | copy-start | bytes 6148
  0.0 4.5 %copy-start.7 = (f32[256,2]{0,1:T(2,128)S(1)}, f32[256,2]{0,1:T(2,128)}, u32[]{:S(2)}) copy-start(f32[256,2]{0,1:T(2,128)} %param.9) | copy-start | bytes 6148
  1.2 4.2 %collective-permute-start = (bf16[64,512]{1,0:T(8,128)(2,1)S(1)}, bf16[64,512]{1,0:T(8,128)(2,1)S(1)}, u32[]{:S(2)}, u32[]{:S(2)}) collective-permute-start(bf16[64,512]{1,0:T(8,128)(2,1)S(1)} %pad_maximum_fusion.1), channel_id=1, source_target_pairs={{0,1},{1,0},{2,3},{3,2},{4,5},{5,4},{6,7},{7,6},{8,9},{9,8},{10,11... | collective-permute-start | bytes 196616 | tf_op jit(solution)/shard_map/ppermute | solution.py:337
  1.3 5.2 %collective-permute-start.1 = (bf16[64,512]{1,0:T(8,128)(2,1)S(1)}, bf16[64,512]{1,0:T(8,128)(2,1)S(1)}, u32[]{:S(2)}, u32[]{:S(2)}) collective-permute-start(bf16[64,512]{1,0:T(8,128)(2,1)S(1)} %pad_maximum_fusion.2), channel_id=1, source_target_pairs={{0,2},{1,3},{2,0},{3,1},{4,6},{5,7},{6,4},{7,5},{8,10},{9,11},{10,... | collective-permute-start | bytes 196616 | tf_op jit(solution)/shard_map/ppermute | solution.py:337
  4.1 4.1 %collective-permute-start.2 = (bf16[64,512]{1,0:T(8,128)(2,1)S(1)}, bf16[64,512]{1,0:T(8,128)(2,1)S(1)}, u32[]{:S(2)}, u32[]{:S(2)}) collective-permute-start(bf16[64,512]{1,0:T(8,128)(2,1)S(1)} %pad_maximum_fusion.3), channel_id=1, source_target_pairs={{0,3},{1,2},{2,1},{3,0},{4,7},{5,6},{6,5},{7,4},{8,11},{9,10},{10,... | collective-permute-start | bytes 196616 | tf_op jit(solution)/shard_map/ppermute | solution.py:337
  8.2 16.6 %collective-permute-start.4 = (bf16[256,1024]{1,0:T(8,128)(2,1)S(1)}, bf16[256,1024]{1,0:T(8,128)(2,1)S(1)}, u32[]{:S(2)}, u32[]{:S(2)}) collective-permute-start(bf16[256,1024]{1,0:T(8,128)(2,1)S(1)} %norm_tokens.1.refs_0_), channel_id=1, source_target_pairs={{0,2},{1,3},{2,0},{3,1},{4,6},{5,7},{6,4},{7,5},{8,10},{9,11},{10,... | collective-permute-start | bytes 1572872 | tf_op jit(solution)/shard_map/ppermute | solution.py:337
  9.4 15.4 %collective-permute-start.7 = (bf16[256,384]{1,0:T(8,128)(2,1)S(1)}, bf16[256,384]{1,0:T(8,128)(2,1)S(1)}, u32[]{:S(2)}, u32[]{:S(2)}) collective-permute-start(bf16[256,384]{1,0:T(8,128)(2,1)S(1)} %slice.8.refs_4_), channel_id=1, source_target_pairs={{0,8},{1,9},{2,10},{3,11},{4,12},{5,13},{6,14},{7,15},{8,0},{9,1},... | collective-permute-start | bytes 589832 | tf_op jit(solution)/shard_map/ppermute | solution.py:337
  11.7 13.4 %collective-permute-start.8 = (bf16[256,384]{1,0:T(8,128)(2,1)S(1)}, bf16[256,384]{1,0:T(8,128)(2,1)S(1)}, u32[]{:S(2)}, u32[]{:S(2)}) collective-permute-start(bf16[256,384]{1,0:T(8,128)(2,1)S(1)} %slice.8.refs_4_), channel_id=1, source_target_pairs={{0,16},{1,17},{2,18},{3,19},{4,20},{5,21},{6,22},{7,23},{8,24},{9,... | collective-permute-start | bytes 589832 | tf_op jit(solution)/shard_map/ppermute | solution.py:337
  12.9 14.1 %collective-permute-start.9 = (bf16[256,384]{1,0:T(8,128)(2,1)S(1)}, bf16[256,384]{1,0:T(8,128)(2,1)S(1)}, u32[]{:S(2)}, u32[]{:S(2)}) collective-permute-start(bf16[256,384]{1,0:T(8,128)(2,1)S(1)} %slice.8.refs_4_), channel_id=1, source_target_pairs={{0,20},{1,21},{2,22},{3,23},{4,16},{5,17},{6,18},{7,19},{8,28},{9,... | collective-permute-start | bytes 589832 | tf_op jit(solution)/shard_map/ppermute | solution.py:337
  14.2 8.0 %collective-permute-start.14 = (bf16[256,128]{1,0:T(8,128)(2,1)S(1)}, bf16[256,128]{1,0:T(8,128)(2,1)S(1)}, u32[]{:S(2)}, u32[]{:S(2)}) collective-permute-start(bf16[256,128]{1,0:T(8,128)(2,1)S(1)} %slice.9.refs_0_), channel_id=1, source_target_pairs={{0,8},{1,9},{2,10},{3,11},{4,12},{5,13},{6,14},{7,15},{8,0},{9,1},... | collective-permute-start | bytes 196616 | tf_op jit(solution)/shard_map/ppermute | solution.py:337
  22.2 21.6 %collective-permute-start.3 = (bf16[256,1024]{1,0:T(8,128)(2,1)S(1)}, bf16[256,1024]{1,0:T(8,128)(2,1)}, u32[]{:S(2)}, u32[]{:S(2)}) collective-permute-start(bf16[256,1024]{1,0:T(8,128)(2,1)S(1)} %norm_tokens.1.refs_0_), channel_id=1, source_target_pairs={{0,1},{1,0},{2,3},{3,2},{4,5},{5,4},{6,7},{7,6},{8,9},{9,8},{10,11... | collective-permute-start | bytes 1572872 | tf_op jit(solution)/shard_map/ppermute | solution.py:337
  24.8 19.0 %collective-permute-start.5 = (bf16[256,1024]{1,0:T(8,128)(2,1)S(1)}, bf16[256,1024]{1,0:T(8,128)(2,1)}, u32[]{:S(2)}, u32[]{:S(2)}) collective-permute-start(bf16[256,1024]{1,0:T(8,128)(2,1)S(1)} %collective-permute-done.4.refs_2_), channel_id=1, source_target_pairs={{0,1},{1,0},{2,3},{3,2},{4,5},{5,4},{6,7},{7,6},{8,9},{9,8},{10,11... | collective-permute-start | bytes 1572872 | tf_op jit(solution)/shard_map/ppermute | solution.py:337
  24.8 3.2 %collective-permute-start.13 = (bf16[256,128]{1,0:T(8,128)(2,1)S(1)}, bf16[256,128]{1,0:T(8,128)(2,1)S(1)}, u32[]{:S(2)}, u32[]{:S(2)}) collective-permute-start(bf16[256,128]{1,0:T(8,128)(2,1)S(1)} %slice.9.refs_0_), channel_id=1, source_target_pairs={{0,4},{1,5},{2,6},{3,7},{4,0},{5,1},{6,2},{7,3},{8,12},{9,13},{10,... | collective-permute-start | bytes 196616 | tf_op jit(solution)/shard_map/ppermute | solution.py:337
  25.2 0.7 copy-start.2
  25.8 4.1 %collective-permute-start.15 = (bf16[256,128]{1,0:T(8,128)(2,1)S(1)}, bf16[256,128]{1,0:T(8,128)(2,1)S(1)}, u32[]{:S(2)}, u32[]{:S(2)}) collective-permute-start(bf16[256,128]{1,0:T(8,128)(2,1)S(1)} %collective-permute-done.14.refs_2_), channel_id=1, source_target_pairs={{0,4},{1,5},{2,6},{3,7},{4,0},{5,1},{6,2},{7,3},{8,12},{9,13},{10,... | collective-permute-start | bytes 196616 | tf_op jit(solution)/shard_map/ppermute | solution.py:337
  27.0 0.7 copy-start.4
  27.7 5.8 %collective-permute-start.10 = (bf16[256,384]{1,0:T(8,128)(2,1)S(1)}, bf16[256,384]{1,0:T(8,128)(2,1)}, u32[]{:S(2)}, u32[]{:S(2)}) collective-permute-start(bf16[256,384]{1,0:T(8,128)(2,1)S(1)} %collective-permute-done.7.refs_6_), channel_id=1, source_target_pairs={{0,4},{1,5},{2,6},{3,7},{4,0},{5,1},{6,2},{7,3},{8,12},{9,13},{10,... | collective-permute-start | bytes 589832 | tf_op jit(solution)/shard_map/ppermute | solution.py:337
  28.0 6.9 %collective-permute-start.11 = (bf16[256,384]{1,0:T(8,128)(2,1)S(1)}, bf16[256,384]{1,0:T(8,128)(2,1)}, u32[]{:S(2)}, u32[]{:S(2)}) collective-permute-start(bf16[256,384]{1,0:T(8,128)(2,1)S(1)} %collective-permute-done.7.refs_6_), channel_id=1, source_target_pairs={{0,16},{16,0},{1,17},{17,1},{2,18},{18,2},{3,19},{19,3},{4,20},{20... | collective-permute-start | bytes 589832 | tf_op jit(solution)/shard_map/ppermute | solution.py:337
  29.2 14.6 %copy-start.3 = (bf16[256,384]{1,0:T(8,128)(2,1)S(1)}, bf16[256,384]{1,0:T(8,128)(2,1)}, u32[]{:S(2)}) copy-start(bf16[256,384]{1,0:T(8,128)(2,1)} %copy-done.2) | copy-start | bytes 589828
  29.2 14.6 %copy-start.5 = (bf16[256,384]{1,0:T(8,128)(2,1)S(1)}, bf16[256,384]{1,0:T(8,128)(2,1)}, u32[]{:S(2)}) copy-start(bf16[256,384]{1,0:T(8,128)(2,1)} %copy-done.4) | copy-start | bytes 589828
  30.0 7.9 %collective-permute-start.16 = (bf16[1024,128]{1,0:T(8,128)(2,1)S(1)}, bf16[1024,128]{1,0:T(8,128)(2,1)S(1)}, u32[]{:S(2)}, u32[]{:S(2)}) collective-permute-start(bf16[1024,128]{1,0:T(8,128)(2,1)S(1)} %out_weight_part.1), channel_id=1, source_target_pairs={{0,16},{16,0},{1,17},{17,1},{2,18},{18,2},{3,19},{19,3},{4,20},{20... | collective-permute-start | bytes 786440 | tf_op jit(solution)/shard_map/ppermute | solution.py:337
  33.5 4.8 %collective-permute-start.6 = (bf16[256,384]{1,0:T(8,128)(2,1)S(1)}, bf16[256,384]{1,0:T(8,128)(2,1)S(1)}, u32[]{:S(2)}, u32[]{:S(2)}) collective-permute-start(bf16[256,384]{1,0:T(8,128)(2,1)S(1)} %slice.8.refs_4_), channel_id=1, source_target_pairs={{0,4},{1,5},{2,6},{3,7},{4,0},{5,1},{6,2},{7,3},{8,12},{9,13},{10,... | collective-permute-start | bytes 589832 | tf_op jit(solution)/shard_map/ppermute | solution.py:337
  34.8 8.9 %collective-permute-start.12 = (bf16[256,384]{1,0:T(8,128)(2,1)}, bf16[256,384]{1,0:T(8,128)(2,1)S(1)}, u32[]{:S(2)}, u32[]{:S(2)}) collective-permute-start(bf16[256,384]{1,0:T(8,128)(2,1)} %collective-permute-done.10.refs_7_), channel_id=1, source_target_pairs={{0,16},{16,0},{1,17},{17,1},{2,18},{18,2},{3,19},{19,3},{4,20},{20... | collective-permute-start | bytes 589832 | tf_op jit(solution)/shard_map/ppermute | solution.py:337
  37.9 16.4 %collective-permute-start.17 = (bf16[1024,256]{1,0:T(8,128)(2,1)S(1)}, bf16[1024,256]{1,0:T(8,128)(2,1)S(1)}, u32[]{:S(2)}, u32[]{:S(2)}) collective-permute-start(bf16[1024,256]{1,0:T(8,128)(2,1)S(1)} %pad_maximum_fusion.refs_4_), channel_id=1, source_target_pairs={{0,2},{1,3},{2,0},{3,1},{4,6},{5,7},{6,4},{7,5},{8,10},{9,11},{10,... | collective-permute-start | bytes 1572872 | tf_op jit(solution)/shard_map/ppermute | solution.py:337
  38.3 19.6 %collective-permute-start.21 = (bf16[1024,256]{1,0:T(8,128)(2,1)S(1)}, bf16[1024,256]{1,0:T(8,128)(2,1)S(1)}, u32[]{:S(2)}, u32[]{:S(2)}) collective-permute-start(bf16[1024,256]{1,0:T(8,128)(2,1)S(1)} %pad_maximum_fusion.refs_4_), channel_id=1, source_target_pairs={{0,1},{1,0},{2,3},{3,2},{4,5},{5,4},{6,7},{7,6},{8,9},{9,8},{10,11... | collective-permute-start | bytes 1572872 | tf_op jit(solution)/shard_map/ppermute | solution.py:337
  54.3 9.5 %collective-permute-start.22 = (bf16[1024,256]{1,0:T(8,128)(2,1)S(1)}, bf16[1024,256]{1,0:T(8,128)(2,1)S(1)}, u32[]{:S(2)}, u32[]{:S(2)}) collective-permute-start(bf16[1024,256]{1,0:T(8,128)(2,1)S(1)} %collective-permute-done.17.refs_6_), channel_id=1, source_target_pairs={{0,1},{1,0},{2,3},{3,2},{4,5},{5,4},{6,7},{7,6},{8,9},{9,8},{10,11... | collective-permute-start | bytes 1572872 | tf_op jit(solution)/shard_map/ppermute | solution.py:337
  55.7 2.2 %collective-permute-start.18 = (bf16[256,256]{1,0:T(8,128)(2,1)S(1)}, bf16[256,256]{1,0:T(8,128)(2,1)S(1)}, u32[]{:S(2)}, u32[]{:S(2)}) collective-permute-start(bf16[256,256]{1,0:T(8,128)(2,1)S(1)} %get-tuple-element.48), channel_id=1, source_target_pairs={{0,1},{1,0},{2,3},{3,2},{4,5},{5,4},{6,7},{7,6},{8,9},{9,8},{10,11... | collective-permute-start | bytes 393224 | tf_op jit(solution)/shard_map/ppermute | solution.py:337
  55.8 4.6 %collective-permute-start.19 = (bf16[256,256]{1,0:T(8,128)(2,1)S(1)}, bf16[256,256]{1,0:T(8,128)(2,1)S(1)}, u32[]{:S(2)}, u32[]{:S(2)}) collective-permute-start(bf16[256,256]{1,0:T(8,128)(2,1)S(1)} %get-tuple-element.49), channel_id=1, source_target_pairs={{0,2},{1,3},{2,0},{3,1},{4,6},{5,7},{6,4},{7,5},{8,10},{9,11},{10,... | collective-permute-start | bytes 393224 | tf_op jit(solution)/shard_map/ppermute | solution.py:337
  56.1 7.7 %collective-permute-start.20 = (bf16[256,256]{1,0:T(8,128)(2,1)S(1)}, bf16[256,256]{1,0:T(8,128)(2,1)S(1)}, u32[]{:S(2)}, u32[]{:S(2)}) collective-permute-start(bf16[256,256]{1,0:T(8,128)(2,1)S(1)} %get-tuple-element.50), channel_id=1, source_target_pairs={{0,3},{1,2},{2,1},{3,0},{4,7},{5,6},{6,5},{7,4},{8,11},{9,10},{10,... | collective-permute-start | bytes 393224 | tf_op jit(solution)/shard_map/ppermute | solution.py:337
  102.6 5.8 %copy-start.1 = (bf16[1024,8192]{1,0:T(8,128)(2,1)S(1)}, bf16[1024,8192]{1,0:T(8,128)(2,1)}, u32[]{:S(2)}) copy-start(bf16[1024,8192]{1,0:T(8,128)(2,1)} %win_ref.1) | copy-start | bytes 50331652

commit v8 on v7

--- a/solution.py
+++ b/solution.py
@@ -21,7 +21,7 @@
 f32 = jnp.float32
 
 
-def params(mib=16):
+def params(mib=12):
     return pltpu.CompilerParams(vmem_limit_bytes=mib * MIB)
 
 
@@ -96,25 +96,24 @@
     )(routes.T, gates.T)
 
 
-def part_kernel(line_ref, *refs):
-    ws, o_ref = refs[:-1], refs[-1]
-    size = ws[0].shape[0]
-    for m, w_ref in enumerate(ws):
-        o_ref[pl.ds(pl.multiple_of((line_ref[0] ^ m) * size, size), size), :] = w_ref[...]
-
-
-def part_call(line, ws):
-    size, cols = ws[0].shape
+def part_kernel(line_ref, w_ref, o_ref, *, lines):
+    size = w_ref.shape[0] // lines
+    for m in range(lines):
+        start = pl.multiple_of((line_ref[0] ^ m) * size, size)
+        o_ref[pl.ds(start, size), :] = w_ref[m * size : (m + 1) * size, :]
+
+
+def part_call(line, blocks, lines):
     vm = pl.BlockSpec(memory_space=pltpu.VMEM)
     return pl.pallas_call(
-        part_kernel,
-        out_shape=jax.ShapeDtypeStruct((len(ws) * size, cols), bf16),
-        in_specs=[pl.BlockSpec(memory_space=pltpu.SMEM)] + [vm] * len(ws),
+        functools.partial(part_kernel, lines=lines),
+        out_shape=jax.ShapeDtypeStruct(blocks.shape, bf16),
+        in_specs=[pl.BlockSpec(memory_space=pltpu.SMEM), vm],
         out_specs=vm,
-        compiler_params=params(),
-        cost_estimate=cost(1, 4 * len(ws) * size * cols),
+        compiler_params=params(4),
+        cost_estimate=cost(1, 4 * blocks.size),
         name="out_weight_part",
-    )(line, *ws)
+    )(line, blocks)
 
 
 def project_kernel(place_ref, *refs, count, lines, share):
@@ -243,8 +242,9 @@
     pack = 4 * CAP
 
     def load(e, n):
-        span = pl.ds(e * hidden + n * step, step)
-        return pltpu.make_async_copy(wout_ref.at[span, :], out_buf.at[span, :], sems.at[e, n])
+        return pltpu.make_async_copy(
+            wout_ref.at[pl.ds(e * hidden + n * step, step), :], out_buf.at[pl.ds(n * step, step), :], sems.at[n]
+        )
 
     for n in range(steps):
         load(0, n).start()
@@ -272,13 +272,14 @@
         hid_ref[:, (steps - 1) * step :] = gelu(pre_ref[(steps - 1) % 2]).astype(bf16)
         for n in range(steps):
             load(e, n).wait()
-            if e + 1 < local:
-                load(e + 1, n).start()
-        term = mm(hid_ref[...], out_buf[e * hidden : (e + 1) * hidden, :]).astype(bf16)
+        term = mm(hid_ref[...], out_buf[...]).astype(bf16)
         if local > 1:
             term_ref[e] = term
         else:
             o_ref[...] = term
+        if e + 1 < local:
+            for n in range(steps):
+                load(e + 1, n).start()
 
     if local > 1:
         for g in range(count // pack):
@@ -304,10 +305,10 @@
             pltpu.VMEM((count, hidden), bf16),
             pltpu.VMEM((2, count, step), f32),
             pltpu.VMEM(kept, bf16),
-            pltpu.VMEM(w_out.shape, bf16),
-            pltpu.SemaphoreType.DMA((local, hidden // step)),
+            pltpu.VMEM((hidden, width), bf16),
+            pltpu.SemaphoreType.DMA((hidden // step,)),
         ],
-        compiler_params=params(36),
+        compiler_params=params(26 if local > 1 else 40),
         cost_estimate=cost(4 * count * width * hidden * local, 4 * width * hidden * local, count * hidden * local),
         name="experts",
     )(arrived, w_in, w_out)
@@ -400,11 +401,9 @@
     near = swap(normed, "ctx", 1)
     both = swap(far, "ctx", 1)
 
-    pieces = {0: last}
-    for bit in bits:
-        for known in list(pieces):
-            pieces[known | bit] = swap(pieces[known], "ctx", bit * SPAN)
-    part = part_call(line.reshape(1), [pieces[m] for m in range(lines_total)])
+    for bit in reversed(bits):
+        last = jnp.concatenate([last, swap(last, "ctx", bit * SPAN)], axis=0)
+    part = part_call(line.reshape(1), last, lines_total)
     part = jnp.concatenate([part] + [swap(part, "groups", s) for s in range(1, share)], axis=1)
     part_far = swap(part, "ctx", 2)
     part_near = swap(part, "ctx", 1)

time: 161 us -> 158 us (0.981)
  starting transfers between devices: 27.9 us -> 24.2 us
    ppermute x23 -> x22, starting transfers between devices: 27.9 us -> 24.2 us  [swap(): return lax.ppermute(value, axis, [(i, i ^ bits) for i in range(size)])]
    unnamed x16 -> x10, local copies, waits for them, and re-layouts: 7.15 us -> 5.78 us
    ppermute x23 -> x22, waiting for transfers between devices: 21.3 us -> 22.3 us  [swap(): return lax.ppermute(value, axis, [(i, i ^ bits) for i in range(size)])]
  transfers between devices with their start and end apart: 23 -> 22, of which waited for: 8 -> 9; matrix products, arithmetic and copies ran while one was open for 0% -> 1% of each run, Pallas kernels for 7% -> 7%
where the time goes in v8:
time: 158 us
  blocking collectives  72.6 us (46%)
  Pallas kernels  29.8 us (19%)
  starting transfers between devices  24.2 us (15%)
  waiting for transfers between devices  22.3 us (14%)
  local copies, waits for them, and re-layouts  6.89 us (4%)
  other arithmetic  1.85 us (1%)
    all_to_all x1, blocking collectives, per_device(): lax.all_to_all(outgoing, 'ctx', split_axis=0, concat_axis=0, tiled=True)  37.3 us
    all_to_all x1, blocking collectives, per_device(): lax.all_to_all(produced, 'ctx', split_axis=0, concat_axis=0, tiled=True)  35.3 us
    ppermute x22, starting transfers between devices, swap(): return lax.ppermute(value, axis, [(i, i ^ bits) for i in range(size)])  24.2 us
    ppermute x22, waiting for transfers between devices, swap(): return lax.ppermute(value, axis, [(i, i ^ bits) for i in range(size)])  22.3 us
    pallas_call x1, Pallas kernels, expert_call(): pl.pallas_call(functools.partial(expert_kernel, local=local, sources=sour...  13.9 us
    pallas_call x1, Pallas kernels, attend_call(): pl.pallas_call(functools.partial(attend_kernel, blocks=blocks), out_shape...  6.66 us
    unnamed x10, local copies, waits for them, and re-layouts  5.78 us
    pallas_call x1, Pallas kernels, project_call(): pl.pallas_call(functools.partial(project_kernel, count=count, lines=lines...  3.76 us
  transfers between devices with their start and end apart: 22, of which 9 were waited for; matrix products, arithmetic and copies ran while one was open for 1% of the time, Pallas kernels for 7%

profile of v8, /device:TPU:1, one launch (start us, length us, event | category | flops | bytes accessed | tf_op | source)
XLA Modules:
  0.0 158.0 jit_solution(15042135503361813049)
XLA Ops:
  0.1 1.0 constant_dynamic-slice_fusion
  1.3 2.8 %collective-permute-start.1 = (bf16[64,512]{1,0:T(8,128)(2,1)S(1)}, bf16[64,512]{1,0:T(8,128)(2,1)S(1)}, u32[]{:S(2)}, u32[]{:S(2)}) collective-permute-start(bf16[64,512]{1,0:T(8,128)(2,1)S(1)} %pad_maximum_fusion.4), channel_id=1, source_target_pairs={{0,2},{1,3},{2,0},{3,1},{4,6},{5,7},{6,4},{7,5},{8,10},{9,11},{10,... | collective-permute-start | bytes 196616 | tf_op jit(solution)/shard_map/ppermute | solution.py:338
  5.4 1.1 collective-permute-done.1
  6.5 1.6 %collective-permute-done.2 = bf16[64,512]{1,0:T(8,128)(2,1)S(1)} collective-permute-done((bf16[64,512]{1,0:T(8,128)(2,1)S(1)}, bf16[64,512]{1,0:T(8,128)(2,1)S(1)}, u32[]{:S(2)}, u32[]{:S(2)}) %collective-permute-start.2) | collective-permute-done | bytes 65568 | tf_op jit(solution)/shard_map/ppermute | solution.py:338
  8.2 1.2 collective-permute-start.4
  9.4 1.3 collective-permute-start.13
  10.7 2.3 %collective-permute-start.7 = (bf16[256,384]{1,0:T(8,128)(2,1)S(1)}, bf16[256,384]{1,0:T(8,128)(2,1)S(1)}, u32[]{:S(2)}, u32[]{:S(2)}) collective-permute-start(bf16[256,384]{1,0:T(8,128)(2,1)S(1)} %slice.8.refs_4_), channel_id=1, source_target_pairs={{0,8},{1,9},{2,10},{3,11},{4,12},{5,13},{6,14},{7,15},{8,0},{9,1},... | collective-permute-start | bytes 589832 | tf_op jit(solution)/shard_map/ppermute | solution.py:338
  13.0 1.2 collective-permute-start.8
  15.0 0.8 collective-permute-start.14
  15.8 6.3 %collective-permute-done.7.refs_6_ = bf16[256,384]{1,0:T(8,128)(2,1)S(1)} collective-permute-done((bf16[256,384]{1,0:T(8,128)(2,1)S(1)}, bf16[256,384]{1,0:T(8,128)(2,1)S(1)}, u32[]{:S(2)}, u32[]{:S(2)}) %collective-permute-start.7) | collective-permute-done | bytes 196640 | tf_op jit(solution)/shard_map/ppermute | solution.py:338
  22.1 2.5 %collective-permute-start.3 = (bf16[256,1024]{1,0:T(8,128)(2,1)S(1)}, bf16[256,1024]{1,0:T(8,128)(2,1)}, u32[]{:S(2)}, u32[]{:S(2)}) collective-permute-start(bf16[256,1024]{1,0:T(8,128)(2,1)S(1)} %norm_tokens.1.refs_0_), channel_id=1, source_target_pairs={{0,1},{1,0},{2,3},{3,2},{4,5},{5,4},{6,7},{7,6},{8,9},{9,8},{10,11... | collective-permute-start | bytes 1572872 | tf_op jit(solution)/shard_map/ppermute | solution.py:338
  24.7 1.3 collective-permute-start.11
  26.0 1.7 %collective-permute-done.14 = bf16[512,128]{1,0:T(8,128)(2,1)} collective-permute-done((bf16[512,128]{1,0:T(8,128)(2,1)}, bf16[512,128]{1,0:T(8,128)(2,1)}, u32[]{:S(2)}, u32[]{:S(2)}) %collective-permute-start.14) | collective-permute-done | bytes 131104 | tf_op jit(solution)/shard_map/ppermute | solution.py:338
  27.7 0.9 pad_maximum_fusion.1.w_ref
  28.7 1.3 collective-permute-start.15
  29.9 1.0 collective-permute-done.10.refs_7_
  30.9 2.2 %collective-permute-start.12 = (bf16[256,384]{1,0:T(8,128)(2,1)S(1)}, bf16[256,384]{1,0:T(8,128)(2,1)S(1)}, u32[]{:S(2)}, u32[]{:S(2)}) collective-permute-start(bf16[256,384]{1,0:T(8,128)(2,1)S(1)} %collective-permute-done.10.refs_7_), channel_id=1, source_target_pairs={{0,16},{16,0},{1,17},{17,1},{2,18},{18,2},{3,19},{19,3},{4,20},{20... | collective-permute-start | bytes 589832 | tf_op jit(solution)/shard_map/ppermute | solution.py:338
  33.2 3.9 %collective-permute-done.15 = bf16[1024,128]{1,0:T(8,128)(2,1)S(1)} collective-permute-done((bf16[1024,128]{1,0:T(8,128)(2,1)S(1)}, bf16[1024,128]{1,0:T(8,128)(2,1)S(1)}, u32[]{:S(2)}, u32[]{:S(2)}) %collective-permute-start.15) | collective-permute-done | bytes 262176 | tf_op jit(solution)/shard_map/ppermute | solution.py:338
  37.5 3.0 %collective-permute-start.20 = (bf16[1024,256]{1,0:T(8,128)(2,1)S(1)}, bf16[1024,256]{1,0:T(8,128)(2,1)S(1)}, u32[]{:S(2)}, u32[]{:S(2)}) collective-permute-start(bf16[1024,256]{1,0:T(8,128)(2,1)S(1)} %pad_maximum_fusion.refs_4_), channel_id=1, source_target_pairs={{0,1},{1,0},{2,3},{3,2},{4,5},{5,4},{6,7},{7,6},{8,9},{9,8},{10,11... | collective-permute-start | bytes 1572872 | tf_op jit(solution)/shard_map/ppermute | solution.py:338
  40.5 0.8 collective-permute-done.12.refs_11_
  41.3 3.8 %project.1.p_ref = bf16[1024,768]{1,0:T(8,128)(2,1)S(1)} custom-call(s32[2]{0:T(128)S(1)} %pad_add_fusion.1.place_ref, bf16[256,1024]{1,0:T(8,128)(2,1)S(1)} %norm_tokens.1.refs_0_, bf16[256,1024]{1,0:T(8,128)(2,1)} %collective-permute-done.3.refs_1_, bf16[256,1024]{1,0:T(8,128)(2,1)S(1)} %collective-permute-done.4.refs_2_, ...), custom_call_target="tpu_custom_call" | custom-call | flops 1610612736 | bytes 6291456 | tf_op jit(solution)/shard_map/project/pallas_call | solution.py:145
  45.0 6.7 %attend.1 = (bf16[256,256]{1,0:T(8,128)(2,1)S(1)}, bf16[256,256]{1,0:T(8,128)(2,1)S(1)}, bf16[256,256]{1,0:T(8,128)(2,1)S(1)}, bf16[256,256]{1,0:T(8,128)(2,1)S(1)}) custom-call(bf16[1024,768]{1,0:T(8,128)(2,1)S(1)} %project.1.p_ref), custom_call_target="tpu_custom_call" | custom-call | flops 4294967296 | bytes 1572864 | tf_op jit(solution)/shard_map/attend/pallas_call | solution.py:179
  51.7 1.5 collective-permute-start.21
  53.7 1.6 %collective-permute-start.19 = (bf16[256,256]{1,0:T(8,128)(2,1)S(1)}, bf16[256,256]{1,0:T(8,128)(2,1)S(1)}, u32[]{:S(2)}, u32[]{:S(2)}) collective-permute-start(bf16[256,256]{1,0:T(8,128)(2,1)S(1)} %get-tuple-element.50), channel_id=1, source_target_pairs={{0,3},{1,2},{2,1},{3,0},{4,7},{5,6},{6,5},{7,4},{8,11},{9,10},{10,... | collective-permute-start | bytes 393224 | tf_op jit(solution)/shard_map/ppermute | solution.py:338
  55.4 2.5 %collective-permute-done.18.refs_2_ = bf16[256,256]{1,0:T(8,128)(2,1)S(1)} collective-permute-done((bf16[256,256]{1,0:T(8,128)(2,1)S(1)}, bf16[256,256]{1,0:T(8,128)(2,1)S(1)}, u32[]{:S(2)}, u32[]{:S(2)}) %collective-permute-start.18) | collective-permute-done | bytes 131104 | tf_op jit(solution)/shard_map/ppermute | solution.py:338
  57.9 3.4 %collective-permute-done.19.refs_3_ = bf16[256,256]{1,0:T(8,128)(2,1)S(1)} collective-permute-done((bf16[256,256]{1,0:T(8,128)(2,1)S(1)}, bf16[256,256]{1,0:T(8,128)(2,1)S(1)}, u32[]{:S(2)}, u32[]{:S(2)}) %collective-permute-start.19) | collective-permute-done | bytes 131104 | tf_op jit(solution)/shard_map/ppermute | solution.py:338
  61.3 2.1 %out_projection.1 = (f32[256,1024]{1,0:T(8,128)S(1)}, bf16[640,1024]{1,0:T(8,128)(2,1)S(1)}) custom-call(s32[2]{0:T(128)S(1)} %pad_add_fusion.place_ref, bf16[256,1024]{1,0:T(8,128)(2,1)S(1)} %copy-done, bf16[640,256]{1,0:T(8,128)(2,1)S(1)} %get-tuple-element.35.d_ref, bf16[256,256]{1,0:T(8,128)(2,1)S(1)} %get-tuple-element.47.refs_0_, ...), custom_call_target="tpu_custom_call" | custom-call | flops 872415232 | bytes 6291456 | tf_op jit(solution)/shard_map/out_projection/pallas_call | solution.py:218
  63.5 37.3 %all_to_all.10 = bf16[16,40,1024]{2,1,0:T(8,128)(2,1)S(1)} all-to-all(bf16[16,40,1024]{2,1,0:T(8,128)(2,1)S(1)} %bitcast.21), channel_id=1, replica_groups=mesh['groups'=2,'ctx'=16] {'ctx'}, dimensions={0} | all-to-all | bytes 2621440 | tf_op jit(solution)/shard_map/all_to_all | solution.py:426
  100.8 5.8 %copy-done.1 = bf16[1024,8192]{1,0:T(8,128)(2,1)S(1)} copy-done((bf16[1024,8192]{1,0:T(8,128)(2,1)S(1)}, bf16[1024,8192]{1,0:T(8,128)(2,1)}, u32[]{:S(2)}) %copy-start.1) | copy-done | bytes 16777240
  106.6 13.9 %experts.1 = bf16[640,1024]{1,0:T(8,128)(2,1)S(1)} custom-call(bf16[640,1024]{1,0:T(8,128)(2,1)S(1)} %bitcast.22, bf16[1024,8192]{1,0:T(8,128)(2,1)S(1)} %copy-done.1, bf16[8192,1024]{1,0:T(8,128)(2,1)} %wout_ref.1), custom_call_target="tpu_custom_call" | custom-call | flops 10737418240 | bytes 33554432 | tf_op jit(solution)/shard_map/experts/pallas_call | solution.py:298
  120.5 35.3 %all_to_all.11 = bf16[16,40,1024]{2,1,0:T(8,128)(2,1)S(1)} all-to-all(bf16[16,40,1024]{2,1,0:T(8,128)(2,1)S(1)} %bitcast.23), channel_id=1, replica_groups=mesh['groups'=2,'ctx'=16] {'ctx'}, dimensions={0} | all-to-all | bytes 2621440 | tf_op jit(solution)/shard_map/all_to_all | solution.py:429
  155.8 2.2 %combine.1 = bf16[256,1024]{1,0:T(8,128)(2,1)} custom-call(f32[256,1024]{1,0:T(8,128)S(1)} %get-tuple-element.52.r_ref, bf16[640,1024]{1,0:T(8,128)(2,1)S(1)} %bitcast.20, bf16[640,256]{1,0:T(8,128)(2,1)S(1)} %get-tuple-element.54.hi_ref, bf16[640,256]{1,0:T(8,128)(2,1)S(1)} %get-tuple-element.55.mid_ref, bf16[640,256]{1,0:T(8,128)(2,1)S(1)} %get-tuple-element.56.lo_ref), custom_call_target="tpu_custom_call" | custom-call | flops 1006632960 | bytes 2883584 | tf_op jit(solution)/shard_map/combine/pallas_call | solution.py:327
  (48 shorter events, 3.4 us)
Async XLA Ops:
  0.0 4.2 %copy-start = (bf16[256,1024]{1,0:T(8,128)(2,1)S(1)}, bf16[256,1024]{1,0:T(8,128)(2,1)}, u32[]{:S(2)}) copy-start(bf16[256,1024]{1,0:T(8,128)(2,1)} %t_ref.1) | copy-start | bytes 1572868
  0.0 4.5 %copy-start.2 = (s32[256,2]{0,1:T(2,128)S(1)}, s32[256,2]{0,1:T(2,128)}, u32[]{:S(2)}) copy-start(s32[256,2]{0,1:T(2,128)} %param.8) | copy-start | bytes 6148
  0.0 4.5 %copy-start.3 = (f32[256,2]{0,1:T(2,128)S(1)}, f32[256,2]{0,1:T(2,128)}, u32[]{:S(2)}) copy-start(f32[256,2]{0,1:T(2,128)} %param.9) | copy-start | bytes 6148
  1.2 4.2 %collective-permute-start = (bf16[64,512]{1,0:T(8,128)(2,1)S(1)}, bf16[64,512]{1,0:T(8,128)(2,1)S(1)}, u32[]{:S(2)}, u32[]{:S(2)}) collective-permute-start(bf16[64,512]{1,0:T(8,128)(2,1)S(1)} %pad_maximum_fusion.3), channel_id=1, source_target_pairs={{0,1},{1,0},{2,3},{3,2},{4,5},{5,4},{6,7},{7,6},{8,9},{9,8},{10,11... | collective-permute-start | bytes 196616 | tf_op jit(solution)/shard_map/ppermute | solution.py:338
  1.3 5.2 %collective-permute-start.1 = (bf16[64,512]{1,0:T(8,128)(2,1)S(1)}, bf16[64,512]{1,0:T(8,128)(2,1)S(1)}, u32[]{:S(2)}, u32[]{:S(2)}) collective-permute-start(bf16[64,512]{1,0:T(8,128)(2,1)S(1)} %pad_maximum_fusion.4), channel_id=1, source_target_pairs={{0,2},{1,3},{2,0},{3,1},{4,6},{5,7},{6,4},{7,5},{8,10},{9,11},{10,... | collective-permute-start | bytes 196616 | tf_op jit(solution)/shard_map/ppermute | solution.py:338
  4.1 4.1 %collective-permute-start.2 = (bf16[64,512]{1,0:T(8,128)(2,1)S(1)}, bf16[64,512]{1,0:T(8,128)(2,1)S(1)}, u32[]{:S(2)}, u32[]{:S(2)}) collective-permute-start(bf16[64,512]{1,0:T(8,128)(2,1)S(1)} %pad_maximum_fusion.5), channel_id=1, source_target_pairs={{0,3},{1,2},{2,1},{3,0},{4,7},{5,6},{6,5},{7,4},{8,11},{9,10},{10,... | collective-permute-start | bytes 196616 | tf_op jit(solution)/shard_map/ppermute | solution.py:338
  8.2 16.4 %collective-permute-start.4 = (bf16[256,1024]{1,0:T(8,128)(2,1)S(1)}, bf16[256,1024]{1,0:T(8,128)(2,1)S(1)}, u32[]{:S(2)}, u32[]{:S(2)}) collective-permute-start(bf16[256,1024]{1,0:T(8,128)(2,1)S(1)} %norm_tokens.1.refs_0_), channel_id=1, source_target_pairs={{0,2},{1,3},{2,0},{3,1},{4,6},{5,7},{6,4},{7,5},{8,10},{9,11},{10,... | collective-permute-start | bytes 1572872 | tf_op jit(solution)/shard_map/ppermute | solution.py:338
  9.4 5.0 %collective-permute-start.13 = (bf16[256,128]{1,0:T(8,128)(2,1)S(1)}, bf16[256,128]{1,0:T(8,128)(2,1)S(1)}, u32[]{:S(2)}, u32[]{:S(2)}) collective-permute-start(bf16[256,128]{1,0:T(8,128)(2,1)S(1)} %slice.9), channel_id=1, source_target_pairs={{0,4},{1,5},{2,6},{3,7},{4,0},{5,1},{6,2},{7,3},{8,12},{9,13},{10,... | collective-permute-start | bytes 196616 | tf_op jit(solution)/shard_map/ppermute | solution.py:338
  10.7 11.4 %collective-permute-start.7 = (bf16[256,384]{1,0:T(8,128)(2,1)S(1)}, bf16[256,384]{1,0:T(8,128)(2,1)S(1)}, u32[]{:S(2)}, u32[]{:S(2)}) collective-permute-start(bf16[256,384]{1,0:T(8,128)(2,1)S(1)} %slice.8.refs_4_), channel_id=1, source_target_pairs={{0,8},{1,9},{2,10},{3,11},{4,12},{5,13},{6,14},{7,15},{8,0},{9,1},... | collective-permute-start | bytes 589832 | tf_op jit(solution)/shard_map/ppermute | solution.py:338
  13.0 11.7 %collective-permute-start.8 = (bf16[256,384]{1,0:T(8,128)(2,1)S(1)}, bf16[256,384]{1,0:T(8,128)(2,1)S(1)}, u32[]{:S(2)}, u32[]{:S(2)}) collective-permute-start(bf16[256,384]{1,0:T(8,128)(2,1)S(1)} %slice.8.refs_4_), channel_id=1, source_target_pairs={{0,16},{1,17},{2,18},{3,19},{4,20},{5,21},{6,22},{7,23},{8,24},{9,... | collective-permute-start | bytes 589832 | tf_op jit(solution)/shard_map/ppermute | solution.py:338
  14.2 10.4 %collective-permute-start.9 = (bf16[256,384]{1,0:T(8,128)(2,1)S(1)}, bf16[256,384]{1,0:T(8,128)(2,1)}, u32[]{:S(2)}, u32[]{:S(2)}) collective-permute-start(bf16[256,384]{1,0:T(8,128)(2,1)S(1)} %slice.8.refs_4_), channel_id=1, source_target_pairs={{0,20},{1,21},{2,22},{3,23},{4,16},{5,17},{6,18},{7,19},{8,28},{9,... | collective-permute-start | bytes 589832 | tf_op jit(solution)/shard_map/ppermute | solution.py:338
  14.4 10.2 %copy-start.4 = (bf16[256,128]{1,0:T(8,128)(2,1)}, bf16[256,128]{1,0:T(8,128)(2,1)S(1)}, u32[]{:S(2)}) copy-start(bf16[256,128]{1,0:T(8,128)(2,1)S(1)} %collective-permute-done.13) | copy-start | bytes 196612
  15.0 12.7 %collective-permute-start.14 = (bf16[512,128]{1,0:T(8,128)(2,1)}, bf16[512,128]{1,0:T(8,128)(2,1)}, u32[]{:S(2)}, u32[]{:S(2)}) collective-permute-start(bf16[512,128]{1,0:T(8,128)(2,1)} %pad_maximum_fusion.2), channel_id=1, source_target_pairs={{0,8},{1,9},{2,10},{3,11},{4,12},{5,13},{6,14},{7,15},{8,0},{9,1},... | collective-permute-start | bytes 393224 | tf_op jit(solution)/shard_map/ppermute | solution.py:338
  22.1 18.4 %collective-permute-start.3 = (bf16[256,1024]{1,0:T(8,128)(2,1)S(1)}, bf16[256,1024]{1,0:T(8,128)(2,1)}, u32[]{:S(2)}, u32[]{:S(2)}) collective-permute-start(bf16[256,1024]{1,0:T(8,128)(2,1)S(1)} %norm_tokens.1.refs_0_), channel_id=1, source_target_pairs={{0,1},{1,0},{2,3},{3,2},{4,5},{5,4},{6,7},{7,6},{8,9},{9,8},{10,11... | collective-permute-start | bytes 1572872 | tf_op jit(solution)/shard_map/ppermute | solution.py:338
  24.6 16.7 %collective-permute-start.5 = (bf16[256,1024]{1,0:T(8,128)(2,1)S(1)}, bf16[256,1024]{1,0:T(8,128)(2,1)}, u32[]{:S(2)}, u32[]{:S(2)}) collective-permute-start(bf16[256,1024]{1,0:T(8,128)(2,1)S(1)} %collective-permute-done.4.refs_2_), channel_id=1, source_target_pairs={{0,1},{1,0},{2,3},{3,2},{4,5},{5,4},{6,7},{7,6},{8,9},{9,8},{10,11... | collective-permute-start | bytes 1572872 | tf_op jit(solution)/shard_map/ppermute | solution.py:338
  24.7 6.2 %collective-permute-start.10 = (bf16[256,384]{1,0:T(8,128)(2,1)S(1)}, bf16[256,384]{1,0:T(8,128)(2,1)S(1)}, u32[]{:S(2)}, u32[]{:S(2)}) collective-permute-start(bf16[256,384]{1,0:T(8,128)(2,1)S(1)} %collective-permute-done.7.refs_6_), channel_id=1, source_target_pairs={{0,4},{1,5},{2,6},{3,7},{4,0},{5,1},{6,2},{7,3},{8,12},{9,13},{10,... | collective-permute-start | bytes 589832 | tf_op jit(solution)/shard_map/ppermute | solution.py:338
  24.7 6.2 %collective-permute-start.11 = (bf16[256,384]{1,0:T(8,128)(2,1)S(1)}, bf16[256,384]{1,0:T(8,128)(2,1)S(1)}, u32[]{:S(2)}, u32[]{:S(2)}) collective-permute-start(bf16[256,384]{1,0:T(8,128)(2,1)S(1)} %collective-permute-done.7.refs_6_), channel_id=1, source_target_pairs={{0,16},{16,0},{1,17},{17,1},{2,18},{18,2},{3,19},{19,3},{4,20},{20... | collective-permute-start | bytes 589832 | tf_op jit(solution)/shard_map/ppermute | solution.py:338
  28.7 8.4 %collective-permute-start.15 = (bf16[1024,128]{1,0:T(8,128)(2,1)S(1)}, bf16[1024,128]{1,0:T(8,128)(2,1)S(1)}, u32[]{:S(2)}, u32[]{:S(2)}) collective-permute-start(bf16[1024,128]{1,0:T(8,128)(2,1)S(1)} %out_weight_part.1), channel_id=1, source_target_pairs={{0,16},{16,0},{1,17},{17,1},{2,18},{18,2},{3,19},{19,3},{4,20},{20... | collective-permute-start | bytes 786440 | tf_op jit(solution)/shard_map/ppermute | solution.py:338
  30.9 6.6 %collective-permute-start.6 = (bf16[256,384]{1,0:T(8,128)(2,1)S(1)}, bf16[256,384]{1,0:T(8,128)(2,1)S(1)}, u32[]{:S(2)}, u32[]{:S(2)}) collective-permute-start(bf16[256,384]{1,0:T(8,128)(2,1)S(1)} %slice.8.refs_4_), channel_id=1, source_target_pairs={{0,4},{1,5},{2,6},{3,7},{4,0},{5,1},{6,2},{7,3},{8,12},{9,13},{10,... | collective-permute-start | bytes 589832 | tf_op jit(solution)/shard_map/ppermute | solution.py:338
  30.9 10.4 %collective-permute-start.12 = (bf16[256,384]{1,0:T(8,128)(2,1)S(1)}, bf16[256,384]{1,0:T(8,128)(2,1)S(1)}, u32[]{:S(2)}, u32[]{:S(2)}) collective-permute-start(bf16[256,384]{1,0:T(8,128)(2,1)S(1)} %collective-permute-done.10.refs_7_), channel_id=1, source_target_pairs={{0,16},{16,0},{1,17},{17,1},{2,18},{18,2},{3,19},{19,3},{4,20},{20... | collective-permute-start | bytes 589832 | tf_op jit(solution)/shard_map/ppermute | solution.py:338
  37.1 14.6 %collective-permute-start.16 = (bf16[1024,256]{1,0:T(8,128)(2,1)S(1)}, bf16[1024,256]{1,0:T(8,128)(2,1)S(1)}, u32[]{:S(2)}, u32[]{:S(2)}) collective-permute-start(bf16[1024,256]{1,0:T(8,128)(2,1)S(1)} %pad_maximum_fusion.refs_4_), channel_id=1, source_target_pairs={{0,2},{1,3},{2,0},{3,1},{4,6},{5,7},{6,4},{7,5},{8,10},{9,11},{10,... | collective-permute-start | bytes 1572872 | tf_op jit(solution)/shard_map/ppermute | solution.py:338
  37.5 17.9 %collective-permute-start.20 = (bf16[1024,256]{1,0:T(8,128)(2,1)S(1)}, bf16[1024,256]{1,0:T(8,128)(2,1)S(1)}, u32[]{:S(2)}, u32[]{:S(2)}) collective-permute-start(bf16[1024,256]{1,0:T(8,128)(2,1)S(1)} %pad_maximum_fusion.refs_4_), channel_id=1, source_target_pairs={{0,1},{1,0},{2,3},{3,2},{4,5},{5,4},{6,7},{7,6},{8,9},{9,8},{10,11... | collective-permute-start | bytes 1572872 | tf_op jit(solution)/shard_map/ppermute | solution.py:338
  51.7 9.6 %collective-permute-start.21 = (bf16[1024,256]{1,0:T(8,128)(2,1)S(1)}, bf16[1024,256]{1,0:T(8,128)(2,1)S(1)}, u32[]{:S(2)}, u32[]{:S(2)}) collective-permute-start(bf16[1024,256]{1,0:T(8,128)(2,1)S(1)} %collective-permute-done.16.refs_6_), channel_id=1, source_target_pairs={{0,1},{1,0},{2,3},{3,2},{4,5},{5,4},{6,7},{7,6},{8,9},{9,8},{10,11... | collective-permute-start | bytes 1572872 | tf_op jit(solution)/shard_map/ppermute | solution.py:338
  53.2 2.2 %collective-permute-start.17 = (bf16[256,256]{1,0:T(8,128)(2,1)S(1)}, bf16[256,256]{1,0:T(8,128)(2,1)S(1)}, u32[]{:S(2)}, u32[]{:S(2)}) collective-permute-start(bf16[256,256]{1,0:T(8,128)(2,1)S(1)} %get-tuple-element.48), channel_id=1, source_target_pairs={{0,1},{1,0},{2,3},{3,2},{4,5},{5,4},{6,7},{7,6},{8,9},{9,8},{10,11... | collective-permute-start | bytes 393224 | tf_op jit(solution)/shard_map/ppermute | solution.py:338
  53.3 4.6 %collective-permute-start.18 = (bf16[256,256]{1,0:T(8,128)(2,1)S(1)}, bf16[256,256]{1,0:T(8,128)(2,1)S(1)}, u32[]{:S(2)}, u32[]{:S(2)}) collective-permute-start(bf16[256,256]{1,0:T(8,128)(2,1)S(1)} %get-tuple-element.49), channel_id=1, source_target_pairs={{0,2},{1,3},{2,0},{3,1},{4,6},{5,7},{6,4},{7,5},{8,10},{9,11},{10,... | collective-permute-start | bytes 393224 | tf_op jit(solution)/shard_map/ppermute | solution.py:338
  53.7 7.6 %collective-permute-start.19 = (bf16[256,256]{1,0:T(8,128)(2,1)S(1)}, bf16[256,256]{1,0:T(8,128)(2,1)S(1)}, u32[]{:S(2)}, u32[]{:S(2)}) collective-permute-start(bf16[256,256]{1,0:T(8,128)(2,1)S(1)} %get-tuple-element.50), channel_id=1, source_target_pairs={{0,3},{1,2},{2,1},{3,0},{4,7},{5,6},{6,5},{7,4},{8,11},{9,10},{10,... | collective-permute-start | bytes 393224 | tf_op jit(solution)/shard_map/ppermute | solution.py:338
  100.8 5.8 %copy-start.1 = (bf16[1024,8192]{1,0:T(8,128)(2,1)S(1)}, bf16[1024,8192]{1,0:T(8,128)(2,1)}, u32[]{:S(2)}) copy-start(bf16[1024,8192]{1,0:T(8,128)(2,1)} %win_ref.1) | copy-start | bytes 50331652

commit v9 on v8

--- a/solution.py
+++ b/solution.py
@@ -76,6 +76,7 @@
         marks = jnp.where(here, 1.0, marks)
         weights = jnp.where(here, gates_ref[r : r + 1, :], weights)
     d_ref[...] = marks.astype(bf16)
+    weights = weights.T
     high = weights.astype(bf16)
     rest = weights - high.astype(f32)
     middle = rest.astype(bf16)
@@ -86,10 +87,11 @@
 
 def route_call(routes, gates):
     rows = routes.shape[0]
-    shape = jax.ShapeDtypeStruct((EXPERTS * CAP, rows), bf16)
+    marks = jax.ShapeDtypeStruct((EXPERTS * CAP, rows), bf16)
+    gates_shape = jax.ShapeDtypeStruct((rows, EXPERTS * CAP), bf16)
     return pl.pallas_call(
         route_kernel,
-        out_shape=[shape] * 4,
+        out_shape=[marks] + [gates_shape] * 3,
         compiler_params=params(),
         cost_estimate=cost(20 * EXPERTS * CAP * rows, 8 * EXPERTS * CAP * rows),
         name="route_slots",
@@ -119,7 +121,7 @@
 def project_kernel(place_ref, *refs, count, lines, share):
     xs = refs[:count]
     ws = refs[count : count + lines * share]
-    o_ref, full = refs[count + lines * share :]
+    o_ref, x_ref, w_ref = refs[count + lines * share :]
     size, wide = ws[0].shape
     cols = wide // 3
     rows = xs[0].shape[0]
@@ -127,14 +129,17 @@
     for s in range(share):
         for m in range(lines):
             start = pl.multiple_of((place_ref[0] ^ m) * size, size)
-            full[place_ref[1] ^ s, pl.ds(start, size), :] = ws[s * lines + m][...]
-    for s in range(share):
-        for j in range(count):
-            got = mm(xs[j][...], full[s]).astype(bf16)
-            for t in range(3):
-                o_ref[j * rows : (j + 1) * rows, t * mine + s * cols : t * mine + (s + 1) * cols] = got[
-                    :, t * cols : (t + 1) * cols
-                ]
+            w_ref[pl.ds(start, size), s * wide : (s + 1) * wide] = ws[s * lines + m][...]
+    for j in range(count):
+        x_ref[j * rows : (j + 1) * rows, :] = xs[j][...]
+    got = mm(x_ref[...], w_ref[...]).astype(bf16)
+    for t in range(3):
+        for p in range(share):
+            piece = got[:, t * cols : (t + 1) * cols]
+            for s in range(1, share):
+                other = got[:, s * wide + t * cols : s * wide + (t + 1) * cols]
+                piece = jnp.where((place_ref[1] ^ s) == p, other, piece)
+            o_ref[:, t * mine + p * cols : t * mine + (p + 1) * cols] = piece
 
 
 def project_call(place, xs, ws, lines, share):
@@ -147,21 +152,24 @@
         out_shape=jax.ShapeDtypeStruct((count * rows, 3 * share * cols), bf16),
         in_specs=[pl.BlockSpec(memory_space=pltpu.SMEM)] + [vm] * (count + lines * share),
         out_specs=vm,
-        scratch_shapes=[pltpu.VMEM((share, width, 3 * cols), bf16)],
+        scratch_shapes=[
+            pltpu.VMEM((count * rows, width), bf16),
+            pltpu.VMEM((width, share * 3 * cols), bf16),
+        ],
         compiler_params=params(),
         cost_estimate=cost(6 * count * rows * width * cols * share, 2 * width * (count * rows + 8 * cols * share)),
         name="project",
     )(place, *xs, *ws)
 
 
-def attend_kernel(p_ref, *o_refs, blocks):
+def attend_kernel(p_ref, *o_refs, tile):
     cols = p_ref.shape[1] // 3
     rows = o_refs[0].shape[0]
-    lane = lax.broadcasted_iota(jnp.int32, (rows, cols), 1) // HD
+    lane = lax.broadcasted_iota(jnp.int32, (tile * rows, cols), 1) // HD
     keys = p_ref[:, cols : 2 * cols]
     values = p_ref[:, 2 * cols :]
-    for o_ref, j in zip(o_refs, blocks):
-        queries = p_ref[j * rows : (j + 1) * rows, :cols] * jnp.asarray(HD ** (-0.5), bf16)
+    for i in range(0, len(o_refs), tile):
+        queries = p_ref[i * rows : (i + tile) * rows, :cols] * jnp.asarray(HD ** (-0.5), bf16)
         mixed = None
         for h in range(cols // HD):
             mine = lane == h
@@ -171,13 +179,15 @@
             probs = (weights * (1.0 / jnp.sum(weights, axis=-1, keepdims=True))).astype(bf16)
             part = mm(probs, values)
             mixed = part if mixed is None else jnp.where(mine, part, mixed)
-        o_ref[...] = mixed.astype(bf16)
+        mixed = mixed.astype(bf16)
+        for k in range(tile):
+            o_refs[i + k][...] = mixed[k * rows : (k + 1) * rows]
 
 
 def attend_call(projected, blocks, rows):
     length, width = projected.shape[0], projected.shape[1] // 3
     return pl.pallas_call(
-        functools.partial(attend_kernel, blocks=blocks),
+        functools.partial(attend_kernel, tile=1),
         out_shape=[jax.ShapeDtypeStruct((rows, width), bf16)] * len(blocks),
         compiler_params=params(),
         cost_estimate=cost(
@@ -225,7 +235,7 @@
         out_specs=[vm, vm],
         scratch_shapes=[pltpu.VMEM((rows, width), bf16), pltpu.VMEM((rows, width), f32)],
         compiler_params=params(),
-        cost_estimate=cost(2 * rows * width * (width + marks.shape[0]), 6 * width * width),
+        cost_estimate=cost(80 * rows * width * (width + marks.shape[0]), 6 * width * width),
         name="out_projection",
     )(place, tokens, marks, *ctxs, *parts)
 
@@ -315,11 +325,10 @@
 
 
 def combine_kernel(r_ref, b_ref, hi_ref, mid_ref, lo_ref, o_ref):
-    dims = (((0,), (0,)), ((), ()))
     back = b_ref[...]
-    mixture = mm(lo_ref[...], back, dims)
-    mixture = mixture + mm(mid_ref[...], back, dims)
-    mixture = mixture + mm(hi_ref[...], back, dims)
+    mixture = mm(lo_ref[...], back)
+    mixture = mixture + mm(mid_ref[...], back)
+    mixture = mixture + mm(hi_ref[...], back)
     o_ref[...] = (r_ref[...] + mixture).astype(bf16)
 
 

time: 158 us -> 152 us (0.962)
  local copies, waits for them, and re-layouts: 6.89 us -> 1.16 us
    unnamed x10 -> x20, local copies, waits for them, and re-layouts: 5.78 us -> 0.05 us
where the time goes in v9:
time: 152 us
  blocking collectives  72.6 us (48%)
  Pallas kernels  28.9 us (19%)
  starting transfers between devices  24.2 us (16%)
  waiting for transfers between devices  22.6 us (15%)
  other arithmetic  1.85 us (1%)
    all_to_all x1, blocking collectives, per_device(): lax.all_to_all(outgoing, 'ctx', split_axis=0, concat_axis=0, tiled=True)  37.3 us
    all_to_all x1, blocking collectives, per_device(): lax.all_to_all(produced, 'ctx', split_axis=0, concat_axis=0, tiled=True)  35.3 us
    ppermute x22, starting transfers between devices, swap(): return lax.ppermute(value, axis, [(i, i ^ bits) for i in range(size)])  24.2 us
    ppermute x22, waiting for transfers between devices, swap(): return lax.ppermute(value, axis, [(i, i ^ bits) for i in range(size)])  22.6 us
    pallas_call x1, Pallas kernels, expert_call(): pl.pallas_call(functools.partial(expert_kernel, local=local, sources=sour...  13.9 us
    pallas_call x1, Pallas kernels, attend_call(): pl.pallas_call(functools.partial(attend_kernel, tile=1), out_shape=[jax.S...  6.66 us
    pallas_call x1, Pallas kernels, project_call(): pl.pallas_call(functools.partial(project_kernel, count=count, lines=lines...  3.14 us
  transfers between devices with their start and end apart: 22, of which 9 were waited for; matrix products, arithmetic and copies ran while one was open for 1% of the time, Pallas kernels for 7%

profile of v9, /device:TPU:1, one launch (start us, length us, event | category | flops | bytes accessed | tf_op | source)
XLA Modules:
  0.0 151.7 jit_solution(16307929005216459326)
XLA Ops:
  0.1 1.0 constant_dynamic-slice_fusion
  1.3 2.8 %collective-permute-start.1 = (bf16[64,512]{1,0:T(8,128)(2,1)S(1)}, bf16[64,512]{1,0:T(8,128)(2,1)S(1)}, u32[]{:S(2)}, u32[]{:S(2)}) collective-permute-start(bf16[64,512]{1,0:T(8,128)(2,1)S(1)} %pad_maximum_fusion.4), channel_id=1, source_target_pairs={{0,2},{1,3},{2,0},{3,1},{4,6},{5,7},{6,4},{7,5},{8,10},{9,11},{10,... | collective-permute-start | bytes 196616 | tf_op jit(solution)/shard_map/ppermute | solution.py:347
  5.1 1.4 collective-permute-done.1
  6.5 1.6 %collective-permute-done.2 = bf16[64,512]{1,0:T(8,128)(2,1)S(1)} collective-permute-done((bf16[64,512]{1,0:T(8,128)(2,1)S(1)}, bf16[64,512]{1,0:T(8,128)(2,1)S(1)}, u32[]{:S(2)}, u32[]{:S(2)}) %collective-permute-start.2) | collective-permute-done | bytes 65568 | tf_op jit(solution)/shard_map/ppermute | solution.py:347
  8.2 1.2 collective-permute-start.4
  9.4 1.3 collective-permute-start.13
  10.7 2.3 %collective-permute-start.7 = (bf16[256,384]{1,0:T(8,128)(2,1)S(1)}, bf16[256,384]{1,0:T(8,128)(2,1)S(1)}, u32[]{:S(2)}, u32[]{:S(2)}) collective-permute-start(bf16[256,384]{1,0:T(8,128)(2,1)S(1)} %slice.8.refs_4_), channel_id=1, source_target_pairs={{0,8},{1,9},{2,10},{3,11},{4,12},{5,13},{6,14},{7,15},{8,0},{9,1},... | collective-permute-start | bytes 589832 | tf_op jit(solution)/shard_map/ppermute | solution.py:347
  13.0 1.2 collective-permute-start.8
  14.4 0.7 pad_maximum_fusion.2
  15.0 0.8 collective-permute-start.14
  15.8 6.3 %collective-permute-done.7.refs_6_ = bf16[256,384]{1,0:T(8,128)(2,1)S(1)} collective-permute-done((bf16[256,384]{1,0:T(8,128)(2,1)S(1)}, bf16[256,384]{1,0:T(8,128)(2,1)S(1)}, u32[]{:S(2)}, u32[]{:S(2)}) %collective-permute-start.7) | collective-permute-done | bytes 196640 | tf_op jit(solution)/shard_map/ppermute | solution.py:347
  22.1 2.5 %collective-permute-start.3 = (bf16[256,1024]{1,0:T(8,128)(2,1)S(1)}, bf16[256,1024]{1,0:T(8,128)(2,1)S(1)}, u32[]{:S(2)}, u32[]{:S(2)}) collective-permute-start(bf16[256,1024]{1,0:T(8,128)(2,1)S(1)} %norm_tokens.1.refs_0_), channel_id=1, source_target_pairs={{0,1},{1,0},{2,3},{3,2},{4,5},{5,4},{6,7},{7,6},{8,9},{9,8},{10,11... | collective-permute-start | bytes 1572872 | tf_op jit(solution)/shard_map/ppermute | solution.py:347
  24.7 1.3 collective-permute-start.11
  26.0 1.7 %collective-permute-done.14 = bf16[512,128]{1,0:T(8,128)(2,1)} collective-permute-done((bf16[512,128]{1,0:T(8,128)(2,1)}, bf16[512,128]{1,0:T(8,128)(2,1)}, u32[]{:S(2)}, u32[]{:S(2)}) %collective-permute-start.14) | collective-permute-done | bytes 131104 | tf_op jit(solution)/shard_map/ppermute | solution.py:347
  27.7 0.9 pad_maximum_fusion.1.w_ref
  28.7 1.3 collective-permute-start.15
  29.9 1.0 collective-permute-done.10.refs_7_
  30.9 2.2 %collective-permute-start.12 = (bf16[256,384]{1,0:T(8,128)(2,1)S(1)}, bf16[256,384]{1,0:T(8,128)(2,1)S(1)}, u32[]{:S(2)}, u32[]{:S(2)}) collective-permute-start(bf16[256,384]{1,0:T(8,128)(2,1)S(1)} %collective-permute-done.10.refs_7_), channel_id=1, source_target_pairs={{0,16},{16,0},{1,17},{17,1},{2,18},{18,2},{3,19},{19,3},{4,20},{20... | collective-permute-start | bytes 589832 | tf_op jit(solution)/shard_map/ppermute | solution.py:347
  33.2 3.9 %collective-permute-done.15 = bf16[1024,128]{1,0:T(8,128)(2,1)S(1)} collective-permute-done((bf16[1024,128]{1,0:T(8,128)(2,1)S(1)}, bf16[1024,128]{1,0:T(8,128)(2,1)S(1)}, u32[]{:S(2)}, u32[]{:S(2)}) %collective-permute-start.15) | collective-permute-done | bytes 262176 | tf_op jit(solution)/shard_map/ppermute | solution.py:347
  37.5 3.0 %collective-permute-start.20 = (bf16[1024,256]{1,0:T(8,128)(2,1)S(1)}, bf16[1024,256]{1,0:T(8,128)(2,1)S(1)}, u32[]{:S(2)}, u32[]{:S(2)}) collective-permute-start(bf16[1024,256]{1,0:T(8,128)(2,1)S(1)} %pad_maximum_fusion.refs_4_), channel_id=1, source_target_pairs={{0,1},{1,0},{2,3},{3,2},{4,5},{5,4},{6,7},{7,6},{8,9},{9,8},{10,11... | collective-permute-start | bytes 1572872 | tf_op jit(solution)/shard_map/ppermute | solution.py:347
  40.5 0.8 collective-permute-done.12.refs_11_
  41.3 3.1 %project.1.p_ref = bf16[1024,768]{1,0:T(8,128)(2,1)S(1)} custom-call(s32[2]{0:T(128)S(1)} %pad_add_fusion.1.place_ref, bf16[256,1024]{1,0:T(8,128)(2,1)S(1)} %norm_tokens.1.refs_0_, bf16[256,1024]{1,0:T(8,128)(2,1)S(1)} %collective-permute-done.3.refs_1_, bf16[256,1024]{1,0:T(8,128)(2,1)S(1)} %collective-permute-done.4.refs_2_, ...), custom_call_target="tpu_custom_call" | custom-call | flops 1610612736 | bytes 6291456 | tf_op jit(solution)/shard_map/project/pallas_call | solution.py:150
  44.4 6.7 %attend.1 = (bf16[256,256]{1,0:T(8,128)(2,1)S(1)}, bf16[256,256]{1,0:T(8,128)(2,1)S(1)}, bf16[256,256]{1,0:T(8,128)(2,1)S(1)}, bf16[256,256]{1,0:T(8,128)(2,1)S(1)}) custom-call(bf16[1024,768]{1,0:T(8,128)(2,1)S(1)} %project.1.p_ref), custom_call_target="tpu_custom_call" | custom-call | flops 4294967296 | bytes 1572864 | tf_op jit(solution)/shard_map/attend/pallas_call | solution.py:189
  51.1 1.5 collective-permute-start.21
  53.1 1.6 %collective-permute-start.19 = (bf16[256,256]{1,0:T(8,128)(2,1)S(1)}, bf16[256,256]{1,0:T(8,128)(2,1)S(1)}, u32[]{:S(2)}, u32[]{:S(2)}) collective-permute-start(bf16[256,256]{1,0:T(8,128)(2,1)S(1)} %get-tuple-element.50), channel_id=1, source_target_pairs={{0,3},{1,2},{2,1},{3,0},{4,7},{5,6},{6,5},{7,4},{8,11},{9,10},{10,... | collective-permute-start | bytes 393224 | tf_op jit(solution)/shard_map/ppermute | solution.py:347
  54.8 2.5 %collective-permute-done.18.refs_2_ = bf16[256,256]{1,0:T(8,128)(2,1)S(1)} collective-permute-done((bf16[256,256]{1,0:T(8,128)(2,1)S(1)}, bf16[256,256]{1,0:T(8,128)(2,1)S(1)}, u32[]{:S(2)}, u32[]{:S(2)}) %collective-permute-start.18) | collective-permute-done | bytes 131104 | tf_op jit(solution)/shard_map/ppermute | solution.py:347
  57.3 3.4 %collective-permute-done.19.refs_3_ = bf16[256,256]{1,0:T(8,128)(2,1)S(1)} collective-permute-done((bf16[256,256]{1,0:T(8,128)(2,1)S(1)}, bf16[256,256]{1,0:T(8,128)(2,1)S(1)}, u32[]{:S(2)}, u32[]{:S(2)}) %collective-permute-start.19) | collective-permute-done | bytes 131104 | tf_op jit(solution)/shard_map/ppermute | solution.py:347
  60.7 2.1 %out_projection.1 = (f32[256,1024]{1,0:T(8,128)S(1)}, bf16[640,1024]{1,0:T(8,128)(2,1)S(1)}) custom-call(s32[2]{0:T(128)S(1)} %pad_add_fusion.place_ref, bf16[256,1024]{1,0:T(8,128)(2,1)S(1)} %copy-done, bf16[640,256]{1,0:T(8,128)(2,1)S(1)} %copy-done.4, bf16[256,256]{1,0:T(8,128)(2,1)S(1)} %get-tuple-element.47.refs_0_, ...), custom_call_target="tpu_custom_call" | custom-call | flops 34896609280 | bytes 6291456 | tf_op jit(solution)/shard_map/out_projection/pallas_call | solution.py:228
  62.9 37.3 %all_to_all.10 = bf16[16,40,1024]{2,1,0:T(8,128)(2,1)S(1)} all-to-all(bf16[16,40,1024]{2,1,0:T(8,128)(2,1)S(1)} %bitcast.21), channel_id=1, replica_groups=mesh['groups'=2,'ctx'=16] {'ctx'}, dimensions={0} | all-to-all | bytes 2621440 | tf_op jit(solution)/shard_map/all_to_all | solution.py:435
  100.2 13.9 %experts.1 = bf16[640,1024]{1,0:T(8,128)(2,1)S(1)} custom-call(bf16[640,1024]{1,0:T(8,128)(2,1)S(1)} %bitcast.22, bf16[1024,8192]{1,0:T(8,128)(2,1)S(1)} %bitcast.25, bf16[8192,1024]{1,0:T(8,128)(2,1)} %wout_ref.1), custom_call_target="tpu_custom_call" | custom-call | flops 10737418240 | bytes 33554432 | tf_op jit(solution)/shard_map/experts/pallas_call | solution.py:308
  114.2 35.3 %all_to_all.11 = bf16[16,40,1024]{2,1,0:T(8,128)(2,1)S(1)} all-to-all(bf16[16,40,1024]{2,1,0:T(8,128)(2,1)S(1)} %bitcast.23), channel_id=1, replica_groups=mesh['groups'=2,'ctx'=16] {'ctx'}, dimensions={0} | all-to-all | bytes 2621440 | tf_op jit(solution)/shard_map/all_to_all | solution.py:438
  149.5 2.2 %combine.1 = bf16[256,1024]{1,0:T(8,128)(2,1)} custom-call(f32[256,1024]{1,0:T(8,128)S(1)} %get-tuple-element.52.r_ref, bf16[640,1024]{1,0:T(8,128)(2,1)S(1)} %bitcast.20, bf16[256,640]{1,0:T(8,128)(2,1)S(1)} %get-tuple-element.54.hi_ref, bf16[256,640]{1,0:T(8,128)(2,1)S(1)} %get-tuple-element.55.mid_ref, bf16[256,640]{1,0:T(8,128)(2,1)S(1)} %get-tuple-element.56.lo_ref), custom_call_target="tpu_custom_call" | custom-call | flops 1006632960 | bytes 2883584 | tf_op jit(solution)/shard_map/combine/pallas_call | solution.py:336
  (59 shorter events, 2.5 us)
Async XLA Ops:
  0.0 4.2 %copy-start = (bf16[256,1024]{1,0:T(8,128)(2,1)S(1)}, bf16[256,1024]{1,0:T(8,128)(2,1)}, u32[]{:S(2)}) copy-start(bf16[256,1024]{1,0:T(8,128)(2,1)} %t_ref.1) | copy-start | bytes 1572868
  0.0 4.5 %copy-start.1 = (s32[256,2]{0,1:T(2,128)S(1)}, s32[256,2]{0,1:T(2,128)}, u32[]{:S(2)}) copy-start(s32[256,2]{0,1:T(2,128)} %param.8) | copy-start | bytes 6148
  0.0 4.5 %copy-start.2 = (f32[256,2]{0,1:T(2,128)S(1)}, f32[256,2]{0,1:T(2,128)}, u32[]{:S(2)}) copy-start(f32[256,2]{0,1:T(2,128)} %param.9) | copy-start | bytes 6148
  1.2 3.9 %collective-permute-start = (bf16[64,512]{1,0:T(8,128)(2,1)S(1)}, bf16[64,512]{1,0:T(8,128)(2,1)S(1)}, u32[]{:S(2)}, u32[]{:S(2)}) collective-permute-start(bf16[64,512]{1,0:T(8,128)(2,1)S(1)} %pad_maximum_fusion.3), channel_id=1, source_target_pairs={{0,1},{1,0},{2,3},{3,2},{4,5},{5,4},{6,7},{7,6},{8,9},{9,8},{10,11... | collective-permute-start | bytes 196616 | tf_op jit(solution)/shard_map/ppermute | solution.py:347
  1.3 5.2 %collective-permute-start.1 = (bf16[64,512]{1,0:T(8,128)(2,1)S(1)}, bf16[64,512]{1,0:T(8,128)(2,1)S(1)}, u32[]{:S(2)}, u32[]{:S(2)}) collective-permute-start(bf16[64,512]{1,0:T(8,128)(2,1)S(1)} %pad_maximum_fusion.4), channel_id=1, source_target_pairs={{0,2},{1,3},{2,0},{3,1},{4,6},{5,7},{6,4},{7,5},{8,10},{9,11},{10,... | collective-permute-start | bytes 196616 | tf_op jit(solution)/shard_map/ppermute | solution.py:347
  4.1 4.1 %collective-permute-start.2 = (bf16[64,512]{1,0:T(8,128)(2,1)S(1)}, bf16[64,512]{1,0:T(8,128)(2,1)S(1)}, u32[]{:S(2)}, u32[]{:S(2)}) collective-permute-start(bf16[64,512]{1,0:T(8,128)(2,1)S(1)} %pad_maximum_fusion.5), channel_id=1, source_target_pairs={{0,3},{1,2},{2,1},{3,0},{4,7},{5,6},{6,5},{7,4},{8,11},{9,10},{10,... | collective-permute-start | bytes 196616 | tf_op jit(solution)/shard_map/ppermute | solution.py:347
  5.0 19.6 %copy-start.3 = (bf16[640,256]{1,0:T(8,128)(2,1)}, bf16[640,256]{1,0:T(8,128)(2,1)S(1)}, u32[]{:S(2)}) copy-start(bf16[640,256]{1,0:T(8,128)(2,1)S(1)} %get-tuple-element.35.d_ref) | copy-start | bytes 983044
  8.2 16.4 %collective-permute-start.4 = (bf16[256,1024]{1,0:T(8,128)(2,1)S(1)}, bf16[256,1024]{1,0:T(8,128)(2,1)S(1)}, u32[]{:S(2)}, u32[]{:S(2)}) collective-permute-start(bf16[256,1024]{1,0:T(8,128)(2,1)S(1)} %norm_tokens.1.refs_0_), channel_id=1, source_target_pairs={{0,2},{1,3},{2,0},{3,1},{4,6},{5,7},{6,4},{7,5},{8,10},{9,11},{10,... | collective-permute-start | bytes 1572872 | tf_op jit(solution)/shard_map/ppermute | solution.py:347
  9.4 5.0 %collective-permute-start.13 = (bf16[256,128]{1,0:T(8,128)(2,1)S(1)}, bf16[256,128]{1,0:T(8,128)(2,1)S(1)}, u32[]{:S(2)}, u32[]{:S(2)}) collective-permute-start(bf16[256,128]{1,0:T(8,128)(2,1)S(1)} %slice.9), channel_id=1, source_target_pairs={{0,4},{1,5},{2,6},{3,7},{4,0},{5,1},{6,2},{7,3},{8,12},{9,13},{10,... | collective-permute-start | bytes 196616 | tf_op jit(solution)/shard_map/ppermute | solution.py:347
  10.7 11.4 %collective-permute-start.7 = (bf16[256,384]{1,0:T(8,128)(2,1)S(1)}, bf16[256,384]{1,0:T(8,128)(2,1)S(1)}, u32[]{:S(2)}, u32[]{:S(2)}) collective-permute-start(bf16[256,384]{1,0:T(8,128)(2,1)S(1)} %slice.8.refs_4_), channel_id=1, source_target_pairs={{0,8},{1,9},{2,10},{3,11},{4,12},{5,13},{6,14},{7,15},{8,0},{9,1},... | collective-permute-start | bytes 589832 | tf_op jit(solution)/shard_map/ppermute | solution.py:347
  13.0 11.7 %collective-permute-start.8 = (bf16[256,384]{1,0:T(8,128)(2,1)S(1)}, bf16[256,384]{1,0:T(8,128)(2,1)}, u32[]{:S(2)}, u32[]{:S(2)}) collective-permute-start(bf16[256,384]{1,0:T(8,128)(2,1)S(1)} %slice.8.refs_4_), channel_id=1, source_target_pairs={{0,16},{1,17},{2,18},{3,19},{4,20},{5,21},{6,22},{7,23},{8,24},{9,... | collective-permute-start | bytes 589832 | tf_op jit(solution)/shard_map/ppermute | solution.py:347
  14.2 10.4 %collective-permute-start.9 = (bf16[256,384]{1,0:T(8,128)(2,1)S(1)}, bf16[256,384]{1,0:T(8,128)(2,1)}, u32[]{:S(2)}, u32[]{:S(2)}) collective-permute-start(bf16[256,384]{1,0:T(8,128)(2,1)S(1)} %slice.8.refs_4_), channel_id=1, source_target_pairs={{0,20},{1,21},{2,22},{3,23},{4,16},{5,17},{6,18},{7,19},{8,28},{9,... | collective-permute-start | bytes 589832 | tf_op jit(solution)/shard_map/ppermute | solution.py:347
  14.4 1.4 copy-start.5
  15.0 12.7 %collective-permute-start.14 = (bf16[512,128]{1,0:T(8,128)(2,1)}, bf16[512,128]{1,0:T(8,128)(2,1)}, u32[]{:S(2)}, u32[]{:S(2)}) collective-permute-start(bf16[512,128]{1,0:T(8,128)(2,1)} %pad_maximum_fusion.2), channel_id=1, source_target_pairs={{0,8},{1,9},{2,10},{3,11},{4,12},{5,13},{6,14},{7,15},{8,0},{9,1},... | collective-permute-start | bytes 393224 | tf_op jit(solution)/shard_map/ppermute | solution.py:347
  22.1 18.4 %collective-permute-start.3 = (bf16[256,1024]{1,0:T(8,128)(2,1)S(1)}, bf16[256,1024]{1,0:T(8,128)(2,1)S(1)}, u32[]{:S(2)}, u32[]{:S(2)}) collective-permute-start(bf16[256,1024]{1,0:T(8,128)(2,1)S(1)} %norm_tokens.1.refs_0_), channel_id=1, source_target_pairs={{0,1},{1,0},{2,3},{3,2},{4,5},{5,4},{6,7},{7,6},{8,9},{9,8},{10,11... | collective-permute-start | bytes 1572872 | tf_op jit(solution)/shard_map/ppermute | solution.py:347
  24.6 16.7 %collective-permute-start.5 = (bf16[256,1024]{1,0:T(8,128)(2,1)S(1)}, bf16[256,1024]{1,0:T(8,128)(2,1)}, u32[]{:S(2)}, u32[]{:S(2)}) collective-permute-start(bf16[256,1024]{1,0:T(8,128)(2,1)S(1)} %collective-permute-done.4.refs_2_), channel_id=1, source_target_pairs={{0,1},{1,0},{2,3},{3,2},{4,5},{5,4},{6,7},{7,6},{8,9},{9,8},{10,11... | collective-permute-start | bytes 1572872 | tf_op jit(solution)/shard_map/ppermute | solution.py:347
  24.7 6.2 %collective-permute-start.10 = (bf16[256,384]{1,0:T(8,128)(2,1)S(1)}, bf16[256,384]{1,0:T(8,128)(2,1)S(1)}, u32[]{:S(2)}, u32[]{:S(2)}) collective-permute-start(bf16[256,384]{1,0:T(8,128)(2,1)S(1)} %collective-permute-done.7.refs_6_), channel_id=1, source_target_pairs={{0,4},{1,5},{2,6},{3,7},{4,0},{5,1},{6,2},{7,3},{8,12},{9,13},{10,... | collective-permute-start | bytes 589832 | tf_op jit(solution)/shard_map/ppermute | solution.py:347
  24.7 6.2 %collective-permute-start.11 = (bf16[256,384]{1,0:T(8,128)(2,1)S(1)}, bf16[256,384]{1,0:T(8,128)(2,1)S(1)}, u32[]{:S(2)}, u32[]{:S(2)}) collective-permute-start(bf16[256,384]{1,0:T(8,128)(2,1)S(1)} %collective-permute-done.7.refs_6_), channel_id=1, source_target_pairs={{0,16},{16,0},{1,17},{17,1},{2,18},{18,2},{3,19},{19,3},{4,20},{20... | collective-permute-start | bytes 589832 | tf_op jit(solution)/shard_map/ppermute | solution.py:347
  28.7 8.4 %collective-permute-start.15 = (bf16[1024,128]{1,0:T(8,128)(2,1)S(1)}, bf16[1024,128]{1,0:T(8,128)(2,1)S(1)}, u32[]{:S(2)}, u32[]{:S(2)}) collective-permute-start(bf16[1024,128]{1,0:T(8,128)(2,1)S(1)} %out_weight_part.1), channel_id=1, source_target_pairs={{0,16},{16,0},{1,17},{17,1},{2,18},{18,2},{3,19},{19,3},{4,20},{20... | collective-permute-start | bytes 786440 | tf_op jit(solution)/shard_map/ppermute | solution.py:347
  30.9 6.6 %collective-permute-start.6 = (bf16[256,384]{1,0:T(8,128)(2,1)S(1)}, bf16[256,384]{1,0:T(8,128)(2,1)S(1)}, u32[]{:S(2)}, u32[]{:S(2)}) collective-permute-start(bf16[256,384]{1,0:T(8,128)(2,1)S(1)} %slice.8.refs_4_), channel_id=1, source_target_pairs={{0,4},{1,5},{2,6},{3,7},{4,0},{5,1},{6,2},{7,3},{8,12},{9,13},{10,... | collective-permute-start | bytes 589832 | tf_op jit(solution)/shard_map/ppermute | solution.py:347
  30.9 10.4 %collective-permute-start.12 = (bf16[256,384]{1,0:T(8,128)(2,1)S(1)}, bf16[256,384]{1,0:T(8,128)(2,1)S(1)}, u32[]{:S(2)}, u32[]{:S(2)}) collective-permute-start(bf16[256,384]{1,0:T(8,128)(2,1)S(1)} %collective-permute-done.10.refs_7_), channel_id=1, source_target_pairs={{0,16},{16,0},{1,17},{17,1},{2,18},{18,2},{3,19},{19,3},{4,20},{20... | collective-permute-start | bytes 589832 | tf_op jit(solution)/shard_map/ppermute | solution.py:347
  37.1 14.0 %collective-permute-start.16 = (bf16[1024,256]{1,0:T(8,128)(2,1)S(1)}, bf16[1024,256]{1,0:T(8,128)(2,1)S(1)}, u32[]{:S(2)}, u32[]{:S(2)}) collective-permute-start(bf16[1024,256]{1,0:T(8,128)(2,1)S(1)} %pad_maximum_fusion.refs_4_), channel_id=1, source_target_pairs={{0,2},{1,3},{2,0},{3,1},{4,6},{5,7},{6,4},{7,5},{8,10},{9,11},{10,... | collective-permute-start | bytes 1572872 | tf_op jit(solution)/shard_map/ppermute | solution.py:347
  37.5 17.4 %collective-permute-start.20 = (bf16[1024,256]{1,0:T(8,128)(2,1)S(1)}, bf16[1024,256]{1,0:T(8,128)(2,1)S(1)}, u32[]{:S(2)}, u32[]{:S(2)}) collective-permute-start(bf16[1024,256]{1,0:T(8,128)(2,1)S(1)} %pad_maximum_fusion.refs_4_), channel_id=1, source_target_pairs={{0,1},{1,0},{2,3},{3,2},{4,5},{5,4},{6,7},{7,6},{8,9},{9,8},{10,11... | collective-permute-start | bytes 1572872 | tf_op jit(solution)/shard_map/ppermute | solution.py:347
  44.4 16.3 %copy-start.4 = (bf16[640,256]{1,0:T(8,128)(2,1)S(1)}, bf16[640,256]{1,0:T(8,128)(2,1)}, u32[]{:S(2)}) copy-start(bf16[640,256]{1,0:T(8,128)(2,1)} %copy-done.3) | copy-start | bytes 983044
  44.4 55.8 %slice-start = ((s8[16777216]{0:T(1024)(128)(4,1)}), s8[4194304]{0:T(1024)(128)(4,1)S(1)}, s32[]{:S(2)}) async-start(s8[16777216]{0:T(1024)(128)(4,1)} %bitcast.24), calls=%async_computation.2 | async-start | bytes 8388608
  51.1 9.6 %collective-permute-start.21 = (bf16[1024,256]{1,0:T(8,128)(2,1)S(1)}, bf16[1024,256]{1,0:T(8,128)(2,1)S(1)}, u32[]{:S(2)}, u32[]{:S(2)}) collective-permute-start(bf16[1024,256]{1,0:T(8,128)(2,1)S(1)} %collective-permute-done.16.refs_6_), channel_id=1, source_target_pairs={{0,1},{1,0},{2,3},{3,2},{4,5},{5,4},{6,7},{7,6},{8,9},{9,8},{10,11... | collective-permute-start | bytes 1572872 | tf_op jit(solution)/shard_map/ppermute | solution.py:347
  52.6 2.2 %collective-permute-start.17 = (bf16[256,256]{1,0:T(8,128)(2,1)S(1)}, bf16[256,256]{1,0:T(8,128)(2,1)S(1)}, u32[]{:S(2)}, u32[]{:S(2)}) collective-permute-start(bf16[256,256]{1,0:T(8,128)(2,1)S(1)} %get-tuple-element.48), channel_id=1, source_target_pairs={{0,1},{1,0},{2,3},{3,2},{4,5},{5,4},{6,7},{7,6},{8,9},{9,8},{10,11... | collective-permute-start | bytes 393224 | tf_op jit(solution)/shard_map/ppermute | solution.py:347
  52.7 4.6 %collective-permute-start.18 = (bf16[256,256]{1,0:T(8,128)(2,1)S(1)}, bf16[256,256]{1,0:T(8,128)(2,1)S(1)}, u32[]{:S(2)}, u32[]{:S(2)}) collective-permute-start(bf16[256,256]{1,0:T(8,128)(2,1)S(1)} %get-tuple-element.49), channel_id=1, source_target_pairs={{0,2},{1,3},{2,0},{3,1},{4,6},{5,7},{6,4},{7,5},{8,10},{9,11},{10,... | collective-permute-start | bytes 393224 | tf_op jit(solution)/shard_map/ppermute | solution.py:347
  53.1 7.6 %collective-permute-start.19 = (bf16[256,256]{1,0:T(8,128)(2,1)S(1)}, bf16[256,256]{1,0:T(8,128)(2,1)S(1)}, u32[]{:S(2)}, u32[]{:S(2)}) collective-permute-start(bf16[256,256]{1,0:T(8,128)(2,1)S(1)} %get-tuple-element.50), channel_id=1, source_target_pairs={{0,3},{1,2},{2,1},{3,0},{4,7},{5,6},{6,5},{7,4},{8,11},{9,10},{10,... | collective-permute-start | bytes 393224 | tf_op jit(solution)/shard_map/ppermute | solution.py:347
  54.8 45.4 %slice-start.1 = ((s8[16777216]{0:T(1024)(128)(4,1)}), s8[4194304]{0:T(1024)(128)(4,1)S(1)}, s32[]{:S(2)}) async-start(s8[16777216]{0:T(1024)(128)(4,1)} %bitcast.24), calls=%async_computation.3 | async-start | bytes 8388608
  54.8 45.4 %slice-start.2 = ((s8[16777216]{0:T(1024)(128)(4,1)}), s8[4194304]{0:T(1024)(128)(4,1)S(1)}, s32[]{:S(2)}) async-start(s8[16777216]{0:T(1024)(128)(4,1)} %bitcast.24), calls=%async_computation.4 | async-start | bytes 8388608
  54.8 45.4 %slice-start.3 = ((s8[16777216]{0:T(1024)(128)(4,1)}), s8[4194304]{0:T(1024)(128)(4,1)S(1)}, s32[]{:S(2)}) async-start(s8[16777216]{0:T(1024)(128)(4,1)} %bitcast.24), calls=%async_computation.5 | async-start | bytes 8388608

commit v10 on v9

--- a/solution.py
+++ b/solution.py
@@ -53,7 +53,7 @@
     )(tokens)
 
 
-def route_kernel(routes_ref, gates_ref, d_ref, hi_ref, mid_ref, lo_ref):
+def route_kernel(routes_ref, gates_ref, d_ref, g_ref):
     rows = routes_ref.shape[1]
     slots = d_ref.shape[0]
     expert = lax.broadcasted_iota(jnp.int32, (EXPERTS, rows), 0)
@@ -80,18 +80,18 @@
     high = weights.astype(bf16)
     rest = weights - high.astype(f32)
     middle = rest.astype(bf16)
-    hi_ref[...] = high
-    mid_ref[...] = middle
-    lo_ref[...] = (rest - middle.astype(f32)).astype(bf16)
+    g_ref[:rows, :] = (rest - middle.astype(f32)).astype(bf16)
+    g_ref[rows : 2 * rows, :] = middle
+    g_ref[2 * rows :, :] = high
 
 
 def route_call(routes, gates):
     rows = routes.shape[0]
     marks = jax.ShapeDtypeStruct((EXPERTS * CAP, rows), bf16)
-    gates_shape = jax.ShapeDtypeStruct((rows, EXPERTS * CAP), bf16)
+    parts = jax.ShapeDtypeStruct((3 * rows, EXPERTS * CAP), bf16)
     return pl.pallas_call(
         route_kernel,
-        out_shape=[marks] + [gates_shape] * 3,
+        out_shape=[marks, parts],
         compiler_params=params(),
         cost_estimate=cost(20 * EXPERTS * CAP * rows, 8 * EXPERTS * CAP * rows),
         name="route_slots",
@@ -235,7 +235,7 @@
         out_specs=[vm, vm],
         scratch_shapes=[pltpu.VMEM((rows, width), bf16), pltpu.VMEM((rows, width), f32)],
         compiler_params=params(),
-        cost_estimate=cost(80 * rows * width * (width + marks.shape[0]), 6 * width * width),
+        cost_estimate=cost(160 * rows * width * (width + marks.shape[0]), 6 * width * width),
         name="out_projection",
     )(place, tokens, marks, *ctxs, *parts)
 
@@ -324,22 +324,21 @@
     )(arrived, w_in, w_out)
 
 
-def combine_kernel(r_ref, b_ref, hi_ref, mid_ref, lo_ref, o_ref):
-    back = b_ref[...]
-    mixture = mm(lo_ref[...], back)
-    mixture = mixture + mm(mid_ref[...], back)
-    mixture = mixture + mm(hi_ref[...], back)
+def combine_kernel(r_ref, b_ref, g_ref, o_ref):
+    rows = r_ref.shape[0]
+    terms = mm(g_ref[...], b_ref[...])
+    mixture = terms[:rows] + terms[rows : 2 * rows] + terms[2 * rows :]
     o_ref[...] = (r_ref[...] + mixture).astype(bf16)
 
 
-def combine_call(resid, back, parts):
+def combine_call(resid, back, gate_parts):
     return pl.pallas_call(
         combine_kernel,
         out_shape=jax.ShapeDtypeStruct(resid.shape, bf16),
         compiler_params=params(),
         cost_estimate=cost(6 * back.size * resid.shape[0], 6 * resid.size + 2 * back.size),
         name="combine",
-    )(resid, back, *parts)
+    )(resid, back, gate_parts)
 
 
 def swap(value, axis, bits):
@@ -380,7 +379,7 @@
     block, last = block[:, : 3 * cols], block[:, 3 * cols :]
     slots = route_call(routes, gates)
     normed, block, last, slots = lax.optimization_barrier((norm_call(tokens), block, last, slots))
-    marks, *gate_parts = slots
+    marks, gate_parts = slots
     bits = [1 << i for i in reversed(range(lines_total.bit_length() - 1))]
     lines = {0: block}
     for bit in bits:

time: 152 us -> 152 us (level)
  no operation moved by 1% of the time
where the time goes in v10:
time: 152 us
  blocking collectives  72.6 us (48%)
  Pallas kernels  28.9 us (19%)
  starting transfers between devices  24.2 us (16%)
  waiting for transfers between devices  22.6 us (15%)
  other arithmetic  1.85 us (1%)
    all_to_all x1, blocking collectives, per_device(): lax.all_to_all(outgoing, 'ctx', split_axis=0, concat_axis=0, tiled=True)  37.3 us
    all_to_all x1, blocking collectives, per_device(): lax.all_to_all(produced, 'ctx', split_axis=0, concat_axis=0, tiled=True)  35.3 us
    ppermute x22, starting transfers between devices, swap(): return lax.ppermute(value, axis, [(i, i ^ bits) for i in range(size)])  24.2 us
    ppermute x22, waiting for transfers between devices, swap(): return lax.ppermute(value, axis, [(i, i ^ bits) for i in range(size)])  22.6 us
    pallas_call x1, Pallas kernels, expert_call(): pl.pallas_call(functools.partial(expert_kernel, local=local, sources=sour...  13.9 us
    pallas_call x1, Pallas kernels, attend_call(): pl.pallas_call(functools.partial(attend_kernel, tile=1), out_shape=[jax.S...  6.66 us
    pallas_call x1, Pallas kernels, project_call(): pl.pallas_call(functools.partial(project_kernel, count=count, lines=lines...  3.14 us
  transfers between devices with their start and end apart: 22, of which 9 were waited for; matrix products, arithmetic and copies ran while one was open for 1% of the time, Pallas kernels for 7%

profile of v10, /device:TPU:1, one launch (start us, length us, event | category | flops | bytes accessed | tf_op | source)
XLA Modules:
  0.0 151.7 jit_solution(2757778277986660139)
XLA Ops:
  0.1 1.0 constant_dynamic-slice_fusion
  1.3 2.8 %collective-permute-start.1 = (bf16[64,512]{1,0:T(8,128)(2,1)S(1)}, bf16[64,512]{1,0:T(8,128)(2,1)S(1)}, u32[]{:S(2)}, u32[]{:S(2)}) collective-permute-start(bf16[64,512]{1,0:T(8,128)(2,1)S(1)} %pad_maximum_fusion.4), channel_id=1, source_target_pairs={{0,2},{1,3},{2,0},{3,1},{4,6},{5,7},{6,4},{7,5},{8,10},{9,11},{10,... | collective-permute-start | bytes 196616 | tf_op jit(solution)/shard_map/ppermute | solution.py:346
  5.1 1.4 collective-permute-done.1
  6.5 1.6 %collective-permute-done.2 = bf16[64,512]{1,0:T(8,128)(2,1)S(1)} collective-permute-done((bf16[64,512]{1,0:T(8,128)(2,1)S(1)}, bf16[64,512]{1,0:T(8,128)(2,1)S(1)}, u32[]{:S(2)}, u32[]{:S(2)}) %collective-permute-start.2) | collective-permute-done | bytes 65568 | tf_op jit(solution)/shard_map/ppermute | solution.py:346
  8.2 1.2 collective-permute-start.4
  9.4 1.3 collective-permute-start.13
  10.7 2.3 %collective-permute-start.7 = (bf16[256,384]{1,0:T(8,128)(2,1)S(1)}, bf16[256,384]{1,0:T(8,128)(2,1)S(1)}, u32[]{:S(2)}, u32[]{:S(2)}) collective-permute-start(bf16[256,384]{1,0:T(8,128)(2,1)S(1)} %slice.8.refs_4_), channel_id=1, source_target_pairs={{0,8},{1,9},{2,10},{3,11},{4,12},{5,13},{6,14},{7,15},{8,0},{9,1},... | collective-permute-start | bytes 589832 | tf_op jit(solution)/shard_map/ppermute | solution.py:346
  13.0 1.2 collective-permute-start.8
  14.4 0.7 pad_maximum_fusion.2
  15.0 0.8 collective-permute-start.14
  15.8 6.3 %collective-permute-done.7.refs_6_ = bf16[256,384]{1,0:T(8,128)(2,1)S(1)} collective-permute-done((bf16[256,384]{1,0:T(8,128)(2,1)S(1)}, bf16[256,384]{1,0:T(8,128)(2,1)S(1)}, u32[]{:S(2)}, u32[]{:S(2)}) %collective-permute-start.7) | collective-permute-done | bytes 196640 | tf_op jit(solution)/shard_map/ppermute | solution.py:346
  22.1 2.5 %collective-permute-start.3 = (bf16[256,1024]{1,0:T(8,128)(2,1)S(1)}, bf16[256,1024]{1,0:T(8,128)(2,1)S(1)}, u32[]{:S(2)}, u32[]{:S(2)}) collective-permute-start(bf16[256,1024]{1,0:T(8,128)(2,1)S(1)} %norm_tokens.1.refs_0_), channel_id=1, source_target_pairs={{0,1},{1,0},{2,3},{3,2},{4,5},{5,4},{6,7},{7,6},{8,9},{9,8},{10,11... | collective-permute-start | bytes 1572872 | tf_op jit(solution)/shard_map/ppermute | solution.py:346
  24.7 1.3 collective-permute-start.11
  26.0 1.7 %collective-permute-done.14 = bf16[512,128]{1,0:T(8,128)(2,1)} collective-permute-done((bf16[512,128]{1,0:T(8,128)(2,1)}, bf16[512,128]{1,0:T(8,128)(2,1)}, u32[]{:S(2)}, u32[]{:S(2)}) %collective-permute-start.14) | collective-permute-done | bytes 131104 | tf_op jit(solution)/shard_map/ppermute | solution.py:346
  27.7 0.9 pad_maximum_fusion.1.w_ref
  28.7 1.3 collective-permute-start.15
  29.9 1.0 collective-permute-done.10.refs_7_
  30.9 2.2 %collective-permute-start.12 = (bf16[256,384]{1,0:T(8,128)(2,1)S(1)}, bf16[256,384]{1,0:T(8,128)(2,1)S(1)}, u32[]{:S(2)}, u32[]{:S(2)}) collective-permute-start(bf16[256,384]{1,0:T(8,128)(2,1)S(1)} %collective-permute-done.10.refs_7_), channel_id=1, source_target_pairs={{0,16},{16,0},{1,17},{17,1},{2,18},{18,2},{3,19},{19,3},{4,20},{20... | collective-permute-start | bytes 589832 | tf_op jit(solution)/shard_map/ppermute | solution.py:346
  33.2 3.9 %collective-permute-done.15 = bf16[1024,128]{1,0:T(8,128)(2,1)S(1)} collective-permute-done((bf16[1024,128]{1,0:T(8,128)(2,1)S(1)}, bf16[1024,128]{1,0:T(8,128)(2,1)S(1)}, u32[]{:S(2)}, u32[]{:S(2)}) %collective-permute-start.15) | collective-permute-done | bytes 262176 | tf_op jit(solution)/shard_map/ppermute | solution.py:346
  37.5 3.0 %collective-permute-start.20 = (bf16[1024,256]{1,0:T(8,128)(2,1)S(1)}, bf16[1024,256]{1,0:T(8,128)(2,1)S(1)}, u32[]{:S(2)}, u32[]{:S(2)}) collective-permute-start(bf16[1024,256]{1,0:T(8,128)(2,1)S(1)} %pad_maximum_fusion.refs_4_), channel_id=1, source_target_pairs={{0,1},{1,0},{2,3},{3,2},{4,5},{5,4},{6,7},{7,6},{8,9},{9,8},{10,11... | collective-permute-start | bytes 1572872 | tf_op jit(solution)/shard_map/ppermute | solution.py:346
  40.5 0.8 collective-permute-done.12.refs_11_
  41.3 3.1 %project.1.p_ref = bf16[1024,768]{1,0:T(8,128)(2,1)S(1)} custom-call(s32[2]{0:T(128)S(1)} %pad_add_fusion.1.place_ref, bf16[256,1024]{1,0:T(8,128)(2,1)S(1)} %norm_tokens.1.refs_0_, bf16[256,1024]{1,0:T(8,128)(2,1)S(1)} %collective-permute-done.3.refs_1_, bf16[256,1024]{1,0:T(8,128)(2,1)S(1)} %collective-permute-done.4.refs_2_, ...), custom_call_target="tpu_custom_call" | custom-call | flops 1610612736 | bytes 6291456 | tf_op jit(solution)/shard_map/project/pallas_call | solution.py:150
  44.4 6.7 %attend.1 = (bf16[256,256]{1,0:T(8,128)(2,1)S(1)}, bf16[256,256]{1,0:T(8,128)(2,1)S(1)}, bf16[256,256]{1,0:T(8,128)(2,1)S(1)}, bf16[256,256]{1,0:T(8,128)(2,1)S(1)}) custom-call(bf16[1024,768]{1,0:T(8,128)(2,1)S(1)} %project.1.p_ref), custom_call_target="tpu_custom_call" | custom-call | flops 4294967296 | bytes 1572864 | tf_op jit(solution)/shard_map/attend/pallas_call | solution.py:189
  51.1 1.5 collective-permute-start.21
  53.1 1.6 %collective-permute-start.19 = (bf16[256,256]{1,0:T(8,128)(2,1)S(1)}, bf16[256,256]{1,0:T(8,128)(2,1)S(1)}, u32[]{:S(2)}, u32[]{:S(2)}) collective-permute-start(bf16[256,256]{1,0:T(8,128)(2,1)S(1)} %get-tuple-element.44), channel_id=1, source_target_pairs={{0,3},{1,2},{2,1},{3,0},{4,7},{5,6},{6,5},{7,4},{8,11},{9,10},{10,... | collective-permute-start | bytes 393224 | tf_op jit(solution)/shard_map/ppermute | solution.py:346
  54.8 2.5 %collective-permute-done.18.refs_2_ = bf16[256,256]{1,0:T(8,128)(2,1)S(1)} collective-permute-done((bf16[256,256]{1,0:T(8,128)(2,1)S(1)}, bf16[256,256]{1,0:T(8,128)(2,1)S(1)}, u32[]{:S(2)}, u32[]{:S(2)}) %collective-permute-start.18) | collective-permute-done | bytes 131104 | tf_op jit(solution)/shard_map/ppermute | solution.py:346
  57.3 3.4 %collective-permute-done.19.refs_3_ = bf16[256,256]{1,0:T(8,128)(2,1)S(1)} collective-permute-done((bf16[256,256]{1,0:T(8,128)(2,1)S(1)}, bf16[256,256]{1,0:T(8,128)(2,1)S(1)}, u32[]{:S(2)}, u32[]{:S(2)}) %collective-permute-start.19) | collective-permute-done | bytes 131104 | tf_op jit(solution)/shard_map/ppermute | solution.py:346
  60.7 2.1 %out_projection.1 = (f32[256,1024]{1,0:T(8,128)S(1)}, bf16[640,1024]{1,0:T(8,128)(2,1)S(1)}) custom-call(s32[2]{0:T(128)S(1)} %pad_add_fusion.place_ref, bf16[256,1024]{1,0:T(8,128)(2,1)S(1)} %copy-done, bf16[640,256]{1,0:T(8,128)(2,1)S(1)} %copy-done.4, bf16[256,256]{1,0:T(8,128)(2,1)S(1)} %get-tuple-element.41.refs_0_, ...), custom_call_target="tpu_custom_call" | custom-call | flops 69793218560 | bytes 6291456 | tf_op jit(solution)/shard_map/out_projection/pallas_call | solution.py:228
  62.9 37.3 %all_to_all.10 = bf16[16,40,1024]{2,1,0:T(8,128)(2,1)S(1)} all-to-all(bf16[16,40,1024]{2,1,0:T(8,128)(2,1)S(1)} %bitcast.21), channel_id=1, replica_groups=mesh['groups'=2,'ctx'=16] {'ctx'}, dimensions={0} | all-to-all | bytes 2621440 | tf_op jit(solution)/shard_map/all_to_all | solution.py:434
  100.2 13.9 %experts.1 = bf16[640,1024]{1,0:T(8,128)(2,1)S(1)} custom-call(bf16[640,1024]{1,0:T(8,128)(2,1)S(1)} %bitcast.22, bf16[1024,8192]{1,0:T(8,128)(2,1)S(1)} %bitcast.25, bf16[8192,1024]{1,0:T(8,128)(2,1)} %wout_ref.1), custom_call_target="tpu_custom_call" | custom-call | flops 10737418240 | bytes 33554432 | tf_op jit(solution)/shard_map/experts/pallas_call | solution.py:308
  114.2 35.3 %all_to_all.11 = bf16[16,40,1024]{2,1,0:T(8,128)(2,1)S(1)} all-to-all(bf16[16,40,1024]{2,1,0:T(8,128)(2,1)S(1)} %bitcast.23), channel_id=1, replica_groups=mesh['groups'=2,'ctx'=16] {'ctx'}, dimensions={0} | all-to-all | bytes 2621440 | tf_op jit(solution)/shard_map/all_to_all | solution.py:437
  149.5 2.2 %combine.1 = bf16[256,1024]{1,0:T(8,128)(2,1)} custom-call(f32[256,1024]{1,0:T(8,128)S(1)} %get-tuple-element.46.r_ref, bf16[640,1024]{1,0:T(8,128)(2,1)S(1)} %bitcast.20, bf16[768,640]{1,0:T(8,128)(2,1)S(1)} %get-tuple-element.48.g_ref), custom_call_target="tpu_custom_call" | custom-call | flops 1006632960 | bytes 2883584 | tf_op jit(solution)/shard_map/combine/pallas_call | solution.py:335
  (59 shorter events, 2.5 us)
Async XLA Ops:
  0.0 4.2 %copy-start = (bf16[256,1024]{1,0:T(8,128)(2,1)S(1)}, bf16[256,1024]{1,0:T(8,128)(2,1)}, u32[]{:S(2)}) copy-start(bf16[256,1024]{1,0:T(8,128)(2,1)} %t_ref.1) | copy-start | bytes 1572868
  0.0 4.5 %copy-start.1 = (s32[256,2]{0,1:T(2,128)S(1)}, s32[256,2]{0,1:T(2,128)}, u32[]{:S(2)}) copy-start(s32[256,2]{0,1:T(2,128)} %param.8) | copy-start | bytes 6148
  0.0 4.5 %copy-start.2 = (f32[256,2]{0,1:T(2,128)S(1)}, f32[256,2]{0,1:T(2,128)}, u32[]{:S(2)}) copy-start(f32[256,2]{0,1:T(2,128)} %param.9) | copy-start | bytes 6148
  1.2 3.9 %collective-permute-start = (bf16[64,512]{1,0:T(8,128)(2,1)S(1)}, bf16[64,512]{1,0:T(8,128)(2,1)S(1)}, u32[]{:S(2)}, u32[]{:S(2)}) collective-permute-start(bf16[64,512]{1,0:T(8,128)(2,1)S(1)} %pad_maximum_fusion.3), channel_id=1, source_target_pairs={{0,1},{1,0},{2,3},{3,2},{4,5},{5,4},{6,7},{7,6},{8,9},{9,8},{10,11... | collective-permute-start | bytes 196616 | tf_op jit(solution)/shard_map/ppermute | solution.py:346
  1.3 5.2 %collective-permute-start.1 = (bf16[64,512]{1,0:T(8,128)(2,1)S(1)}, bf16[64,512]{1,0:T(8,128)(2,1)S(1)}, u32[]{:S(2)}, u32[]{:S(2)}) collective-permute-start(bf16[64,512]{1,0:T(8,128)(2,1)S(1)} %pad_maximum_fusion.4), channel_id=1, source_target_pairs={{0,2},{1,3},{2,0},{3,1},{4,6},{5,7},{6,4},{7,5},{8,10},{9,11},{10,... | collective-permute-start | bytes 196616 | tf_op jit(solution)/shard_map/ppermute | solution.py:346
  4.1 4.1 %collective-permute-start.2 = (bf16[64,512]{1,0:T(8,128)(2,1)S(1)}, bf16[64,512]{1,0:T(8,128)(2,1)S(1)}, u32[]{:S(2)}, u32[]{:S(2)}) collective-permute-start(bf16[64,512]{1,0:T(8,128)(2,1)S(1)} %pad_maximum_fusion.5), channel_id=1, source_target_pairs={{0,3},{1,2},{2,1},{3,0},{4,7},{5,6},{6,5},{7,4},{8,11},{9,10},{10,... | collective-permute-start | bytes 196616 | tf_op jit(solution)/shard_map/ppermute | solution.py:346
  5.0 19.6 %copy-start.3 = (bf16[640,256]{1,0:T(8,128)(2,1)}, bf16[640,256]{1,0:T(8,128)(2,1)S(1)}, u32[]{:S(2)}) copy-start(bf16[640,256]{1,0:T(8,128)(2,1)S(1)} %get-tuple-element.29.d_ref) | copy-start | bytes 983044
  8.2 16.4 %collective-permute-start.4 = (bf16[256,1024]{1,0:T(8,128)(2,1)S(1)}, bf16[256,1024]{1,0:T(8,128)(2,1)S(1)}, u32[]{:S(2)}, u32[]{:S(2)}) collective-permute-start(bf16[256,1024]{1,0:T(8,128)(2,1)S(1)} %norm_tokens.1.refs_0_), channel_id=1, source_target_pairs={{0,2},{1,3},{2,0},{3,1},{4,6},{5,7},{6,4},{7,5},{8,10},{9,11},{10,... | collective-permute-start | bytes 1572872 | tf_op jit(solution)/shard_map/ppermute | solution.py:346
  9.4 5.0 %collective-permute-start.13 = (bf16[256,128]{1,0:T(8,128)(2,1)S(1)}, bf16[256,128]{1,0:T(8,128)(2,1)S(1)}, u32[]{:S(2)}, u32[]{:S(2)}) collective-permute-start(bf16[256,128]{1,0:T(8,128)(2,1)S(1)} %slice.9), channel_id=1, source_target_pairs={{0,4},{1,5},{2,6},{3,7},{4,0},{5,1},{6,2},{7,3},{8,12},{9,13},{10,... | collective-permute-start | bytes 196616 | tf_op jit(solution)/shard_map/ppermute | solution.py:346
  10.7 11.4 %collective-permute-start.7 = (bf16[256,384]{1,0:T(8,128)(2,1)S(1)}, bf16[256,384]{1,0:T(8,128)(2,1)S(1)}, u32[]{:S(2)}, u32[]{:S(2)}) collective-permute-start(bf16[256,384]{1,0:T(8,128)(2,1)S(1)} %slice.8.refs_4_), channel_id=1, source_target_pairs={{0,8},{1,9},{2,10},{3,11},{4,12},{5,13},{6,14},{7,15},{8,0},{9,1},... | collective-permute-start | bytes 589832 | tf_op jit(solution)/shard_map/ppermute | solution.py:346
  13.0 11.7 %collective-permute-start.8 = (bf16[256,384]{1,0:T(8,128)(2,1)S(1)}, bf16[256,384]{1,0:T(8,128)(2,1)}, u32[]{:S(2)}, u32[]{:S(2)}) collective-permute-start(bf16[256,384]{1,0:T(8,128)(2,1)S(1)} %slice.8.refs_4_), channel_id=1, source_target_pairs={{0,16},{1,17},{2,18},{3,19},{4,20},{5,21},{6,22},{7,23},{8,24},{9,... | collective-permute-start | bytes 589832 | tf_op jit(solution)/shard_map/ppermute | solution.py:346
  14.2 10.4 %collective-permute-start.9 = (bf16[256,384]{1,0:T(8,128)(2,1)S(1)}, bf16[256,384]{1,0:T(8,128)(2,1)}, u32[]{:S(2)}, u32[]{:S(2)}) collective-permute-start(bf16[256,384]{1,0:T(8,128)(2,1)S(1)} %slice.8.refs_4_), channel_id=1, source_target_pairs={{0,20},{1,21},{2,22},{3,23},{4,16},{5,17},{6,18},{7,19},{8,28},{9,... | collective-permute-start | bytes 589832 | tf_op jit(solution)/shard_map/ppermute | solution.py:346
  14.4 1.4 copy-start.5
  15.0 12.7 %collective-permute-start.14 = (bf16[512,128]{1,0:T(8,128)(2,1)}, bf16[512,128]{1,0:T(8,128)(2,1)}, u32[]{:S(2)}, u32[]{:S(2)}) collective-permute-start(bf16[512,128]{1,0:T(8,128)(2,1)} %pad_maximum_fusion.2), channel_id=1, source_target_pairs={{0,8},{1,9},{2,10},{3,11},{4,12},{5,13},{6,14},{7,15},{8,0},{9,1},... | collective-permute-start | bytes 393224 | tf_op jit(solution)/shard_map/ppermute | solution.py:346
  22.1 18.4 %collective-permute-start.3 = (bf16[256,1024]{1,0:T(8,128)(2,1)S(1)}, bf16[256,1024]{1,0:T(8,128)(2,1)S(1)}, u32[]{:S(2)}, u32[]{:S(2)}) collective-permute-start(bf16[256,1024]{1,0:T(8,128)(2,1)S(1)} %norm_tokens.1.refs_0_), channel_id=1, source_target_pairs={{0,1},{1,0},{2,3},{3,2},{4,5},{5,4},{6,7},{7,6},{8,9},{9,8},{10,11... | collective-permute-start | bytes 1572872 | tf_op jit(solution)/shard_map/ppermute | solution.py:346
  24.6 16.7 %collective-permute-start.5 = (bf16[256,1024]{1,0:T(8,128)(2,1)S(1)}, bf16[256,1024]{1,0:T(8,128)(2,1)}, u32[]{:S(2)}, u32[]{:S(2)}) collective-permute-start(bf16[256,1024]{1,0:T(8,128)(2,1)S(1)} %collective-permute-done.4.refs_2_), channel_id=1, source_target_pairs={{0,1},{1,0},{2,3},{3,2},{4,5},{5,4},{6,7},{7,6},{8,9},{9,8},{10,11... | collective-permute-start | bytes 1572872 | tf_op jit(solution)/shard_map/ppermute | solution.py:346
  24.7 6.2 %collective-permute-start.10 = (bf16[256,384]{1,0:T(8,128)(2,1)S(1)}, bf16[256,384]{1,0:T(8,128)(2,1)S(1)}, u32[]{:S(2)}, u32[]{:S(2)}) collective-permute-start(bf16[256,384]{1,0:T(8,128)(2,1)S(1)} %collective-permute-done.7.refs_6_), channel_id=1, source_target_pairs={{0,4},{1,5},{2,6},{3,7},{4,0},{5,1},{6,2},{7,3},{8,12},{9,13},{10,... | collective-permute-start | bytes 589832 | tf_op jit(solution)/shard_map/ppermute | solution.py:346
  24.7 6.2 %collective-permute-start.11 = (bf16[256,384]{1,0:T(8,128)(2,1)S(1)}, bf16[256,384]{1,0:T(8,128)(2,1)S(1)}, u32[]{:S(2)}, u32[]{:S(2)}) collective-permute-start(bf16[256,384]{1,0:T(8,128)(2,1)S(1)} %collective-permute-done.7.refs_6_), channel_id=1, source_target_pairs={{0,16},{16,0},{1,17},{17,1},{2,18},{18,2},{3,19},{19,3},{4,20},{20... | collective-permute-start | bytes 589832 | tf_op jit(solution)/shard_map/ppermute | solution.py:346
  28.7 8.4 %collective-permute-start.15 = (bf16[1024,128]{1,0:T(8,128)(2,1)S(1)}, bf16[1024,128]{1,0:T(8,128)(2,1)S(1)}, u32[]{:S(2)}, u32[]{:S(2)}) collective-permute-start(bf16[1024,128]{1,0:T(8,128)(2,1)S(1)} %out_weight_part.1), channel_id=1, source_target_pairs={{0,16},{16,0},{1,17},{17,1},{2,18},{18,2},{3,19},{19,3},{4,20},{20... | collective-permute-start | bytes 786440 | tf_op jit(solution)/shard_map/ppermute | solution.py:346
  30.9 6.6 %collective-permute-start.6 = (bf16[256,384]{1,0:T(8,128)(2,1)S(1)}, bf16[256,384]{1,0:T(8,128)(2,1)S(1)}, u32[]{:S(2)}, u32[]{:S(2)}) collective-permute-start(bf16[256,384]{1,0:T(8,128)(2,1)S(1)} %slice.8.refs_4_), channel_id=1, source_target_pairs={{0,4},{1,5},{2,6},{3,7},{4,0},{5,1},{6,2},{7,3},{8,12},{9,13},{10,... | collective-permute-start | bytes 589832 | tf_op jit(solution)/shard_map/ppermute | solution.py:346
  30.9 10.4 %collective-permute-start.12 = (bf16[256,384]{1,0:T(8,128)(2,1)S(1)}, bf16[256,384]{1,0:T(8,128)(2,1)S(1)}, u32[]{:S(2)}, u32[]{:S(2)}) collective-permute-start(bf16[256,384]{1,0:T(8,128)(2,1)S(1)} %collective-permute-done.10.refs_7_), channel_id=1, source_target_pairs={{0,16},{16,0},{1,17},{17,1},{2,18},{18,2},{3,19},{19,3},{4,20},{20... | collective-permute-start | bytes 589832 | tf_op jit(solution)/shard_map/ppermute | solution.py:346
  37.1 14.0 %collective-permute-start.16 = (bf16[1024,256]{1,0:T(8,128)(2,1)S(1)}, bf16[1024,256]{1,0:T(8,128)(2,1)S(1)}, u32[]{:S(2)}, u32[]{:S(2)}) collective-permute-start(bf16[1024,256]{1,0:T(8,128)(2,1)S(1)} %pad_maximum_fusion.refs_4_), channel_id=1, source_target_pairs={{0,2},{1,3},{2,0},{3,1},{4,6},{5,7},{6,4},{7,5},{8,10},{9,11},{10,... | collective-permute-start | bytes 1572872 | tf_op jit(solution)/shard_map/ppermute | solution.py:346
  37.5 17.4 %collective-permute-start.20 = (bf16[1024,256]{1,0:T(8,128)(2,1)S(1)}, bf16[1024,256]{1,0:T(8,128)(2,1)S(1)}, u32[]{:S(2)}, u32[]{:S(2)}) collective-permute-start(bf16[1024,256]{1,0:T(8,128)(2,1)S(1)} %pad_maximum_fusion.refs_4_), channel_id=1, source_target_pairs={{0,1},{1,0},{2,3},{3,2},{4,5},{5,4},{6,7},{7,6},{8,9},{9,8},{10,11... | collective-permute-start | bytes 1572872 | tf_op jit(solution)/shard_map/ppermute | solution.py:346
  44.4 16.3 %copy-start.4 = (bf16[640,256]{1,0:T(8,128)(2,1)S(1)}, bf16[640,256]{1,0:T(8,128)(2,1)}, u32[]{:S(2)}) copy-start(bf16[640,256]{1,0:T(8,128)(2,1)} %copy-done.3) | copy-start | bytes 983044
  44.4 55.8 %slice-start = ((s8[16777216]{0:T(1024)(128)(4,1)}), s8[4194304]{0:T(1024)(128)(4,1)S(1)}, s32[]{:S(2)}) async-start(s8[16777216]{0:T(1024)(128)(4,1)} %bitcast.24), calls=%async_computation.2 | async-start | bytes 8388608
  51.1 9.6 %collective-permute-start.21 = (bf16[1024,256]{1,0:T(8,128)(2,1)S(1)}, bf16[1024,256]{1,0:T(8,128)(2,1)S(1)}, u32[]{:S(2)}, u32[]{:S(2)}) collective-permute-start(bf16[1024,256]{1,0:T(8,128)(2,1)S(1)} %collective-permute-done.16.refs_6_), channel_id=1, source_target_pairs={{0,1},{1,0},{2,3},{3,2},{4,5},{5,4},{6,7},{7,6},{8,9},{9,8},{10,11... | collective-permute-start | bytes 1572872 | tf_op jit(solution)/shard_map/ppermute | solution.py:346
  52.6 2.2 %collective-permute-start.17 = (bf16[256,256]{1,0:T(8,128)(2,1)S(1)}, bf16[256,256]{1,0:T(8,128)(2,1)S(1)}, u32[]{:S(2)}, u32[]{:S(2)}) collective-permute-start(bf16[256,256]{1,0:T(8,128)(2,1)S(1)} %get-tuple-element.42), channel_id=1, source_target_pairs={{0,1},{1,0},{2,3},{3,2},{4,5},{5,4},{6,7},{7,6},{8,9},{9,8},{10,11... | collective-permute-start | bytes 393224 | tf_op jit(solution)/shard_map/ppermute | solution.py:346
  52.7 4.6 %collective-permute-start.18 = (bf16[256,256]{1,0:T(8,128)(2,1)S(1)}, bf16[256,256]{1,0:T(8,128)(2,1)S(1)}, u32[]{:S(2)}, u32[]{:S(2)}) collective-permute-start(bf16[256,256]{1,0:T(8,128)(2,1)S(1)} %get-tuple-element.43), channel_id=1, source_target_pairs={{0,2},{1,3},{2,0},{3,1},{4,6},{5,7},{6,4},{7,5},{8,10},{9,11},{10,... | collective-permute-start | bytes 393224 | tf_op jit(solution)/shard_map/ppermute | solution.py:346
  53.1 7.6 %collective-permute-start.19 = (bf16[256,256]{1,0:T(8,128)(2,1)S(1)}, bf16[256,256]{1,0:T(8,128)(2,1)S(1)}, u32[]{:S(2)}, u32[]{:S(2)}) collective-permute-start(bf16[256,256]{1,0:T(8,128)(2,1)S(1)} %get-tuple-element.44), channel_id=1, source_target_pairs={{0,3},{1,2},{2,1},{3,0},{4,7},{5,6},{6,5},{7,4},{8,11},{9,10},{10,... | collective-permute-start | bytes 393224 | tf_op jit(solution)/shard_map/ppermute | solution.py:346
  54.8 45.4 %slice-start.1 = ((s8[16777216]{0:T(1024)(128)(4,1)}), s8[4194304]{0:T(1024)(128)(4,1)S(1)}, s32[]{:S(2)}) async-start(s8[16777216]{0:T(1024)(128)(4,1)} %bitcast.24), calls=%async_computation.3 | async-start | bytes 8388608
  54.8 45.4 %slice-start.2 = ((s8[16777216]{0:T(1024)(128)(4,1)}), s8[4194304]{0:T(1024)(128)(4,1)S(1)}, s32[]{:S(2)}) async-start(s8[16777216]{0:T(1024)(128)(4,1)} %bitcast.24), calls=%async_computation.4 | async-start | bytes 8388608
  54.8 45.4 %slice-start.3 = ((s8[16777216]{0:T(1024)(128)(4,1)}), s8[4194304]{0:T(1024)(128)(4,1)S(1)}, s32[]{:S(2)}) async-start(s8[16777216]{0:T(1024)(128)(4,1)} %bitcast.24), calls=%async_computation.5 | async-start | bytes 8388608

commit v11 on v10

--- a/solution.py
+++ b/solution.py
@@ -134,12 +134,15 @@
         x_ref[j * rows : (j + 1) * rows, :] = xs[j][...]
     got = mm(x_ref[...], w_ref[...]).astype(bf16)
     for t in range(3):
-        for p in range(share):
-            piece = got[:, t * cols : (t + 1) * cols]
-            for s in range(1, share):
-                other = got[:, s * wide + t * cols : s * wide + (t + 1) * cols]
-                piece = jnp.where((place_ref[1] ^ s) == p, other, piece)
-            o_ref[:, t * mine + p * cols : t * mine + (p + 1) * cols] = piece
+        for s in range(share):
+            piece = got[:, s * wide + t * cols : s * wide + (t + 1) * cols]
+            if cols % 128 == 0:
+                start = pl.multiple_of(t * mine + (place_ref[1] ^ s) * cols, 128)
+                o_ref[:, pl.ds(start, cols)] = piece
+            else:
+                for p in range(share):
+                    at = slice(t * mine + p * cols, t * mine + (p + 1) * cols)
+                    o_ref[:, at] = jnp.where((place_ref[1] ^ s) == p, piece, o_ref[:, at])
 
 
 def project_call(place, xs, ws, lines, share):
@@ -216,7 +219,13 @@
     for j in range(SPAN):
         c_ref[:, pl.ds(starts[j], wide)] = ctxs[j][...]
     for j in range(SPAN):
-        a_ref[:, pl.ds(starts[j], wide)] = natural(mm(c_ref[...], parts[j][...]))
+        got = mm(c_ref[...], parts[j][...])
+        if cols % 128:
+            a_ref[:, pl.ds(starts[j], wide)] = natural(got)
+            continue
+        for s in range(share):
+            start = pl.multiple_of(starts[j] + (place_ref[1] ^ s) * cols, 128)
+            a_ref[:, pl.ds(start, cols)] = got[:, s * cols : (s + 1) * cols]
     total = t_ref[...].astype(f32) + a_ref[...]
     r_ref[...] = total
     o_ref[...] = mm(d_ref[...], normalize(total)).astype(bf16)

time: 152 us -> 152 us (level)
  no operation moved by 1% of the time
where the time goes in v11:
time: 152 us
  blocking collectives  72.6 us (48%)
  Pallas kernels  29.1 us (19%)
  starting transfers between devices  24.2 us (16%)
  waiting for transfers between devices  22.6 us (15%)
  other arithmetic  1.85 us (1%)
    all_to_all x1, blocking collectives, per_device(): lax.all_to_all(outgoing, 'ctx', split_axis=0, concat_axis=0, tiled=True)  37.3 us
    all_to_all x1, blocking collectives, per_device(): lax.all_to_all(produced, 'ctx', split_axis=0, concat_axis=0, tiled=True)  35.3 us
    ppermute x22, starting transfers between devices, swap(): return lax.ppermute(value, axis, [(i, i ^ bits) for i in range(size)])  24.2 us
    ppermute x22, waiting for transfers between devices, swap(): return lax.ppermute(value, axis, [(i, i ^ bits) for i in range(size)])  22.6 us
    pallas_call x1, Pallas kernels, expert_call(): pl.pallas_call(functools.partial(expert_kernel, local=local, sources=sour...  13.9 us
    pallas_call x1, Pallas kernels, attend_call(): pl.pallas_call(functools.partial(attend_kernel, tile=1), out_shape=[jax.S...  6.66 us
    pallas_call x1, Pallas kernels, project_call(): pl.pallas_call(functools.partial(project_kernel, count=count, lines=lines...  3.29 us
  transfers between devices with their start and end apart: 22, of which 9 were waited for; matrix products, arithmetic and copies ran while one was open for 1% of the time, Pallas kernels for 7%

profile of v11, /device:TPU:1, one launch (start us, length us, event | category | flops | bytes accessed | tf_op | source)
XLA Modules:
  0.0 151.9 jit_solution(7351802993174041248)
XLA Ops:
  0.1 1.0 constant_dynamic-slice_fusion
  1.3 2.8 %collective-permute-start.1 = (bf16[64,512]{1,0:T(8,128)(2,1)S(1)}, bf16[64,512]{1,0:T(8,128)(2,1)S(1)}, u32[]{:S(2)}, u32[]{:S(2)}) collective-permute-start(bf16[64,512]{1,0:T(8,128)(2,1)S(1)} %pad_maximum_fusion.4), channel_id=1, source_target_pairs={{0,2},{1,3},{2,0},{3,1},{4,6},{5,7},{6,4},{7,5},{8,10},{9,11},{10,... | collective-permute-start | bytes 196616 | tf_op jit(solution)/shard_map/ppermute | solution.py:355
  5.1 1.4 collective-permute-done.1
  6.5 1.6 %collective-permute-done.2 = bf16[64,512]{1,0:T(8,128)(2,1)S(1)} collective-permute-done((bf16[64,512]{1,0:T(8,128)(2,1)S(1)}, bf16[64,512]{1,0:T(8,128)(2,1)S(1)}, u32[]{:S(2)}, u32[]{:S(2)}) %collective-permute-start.2) | collective-permute-done | bytes 65568 | tf_op jit(solution)/shard_map/ppermute | solution.py:355
  8.2 1.2 collective-permute-start.4
  9.4 1.3 collective-permute-start.13
  10.7 2.3 %collective-permute-start.7 = (bf16[256,384]{1,0:T(8,128)(2,1)S(1)}, bf16[256,384]{1,0:T(8,128)(2,1)S(1)}, u32[]{:S(2)}, u32[]{:S(2)}) collective-permute-start(bf16[256,384]{1,0:T(8,128)(2,1)S(1)} %slice.8.refs_4_), channel_id=1, source_target_pairs={{0,8},{1,9},{2,10},{3,11},{4,12},{5,13},{6,14},{7,15},{8,0},{9,1},... | collective-permute-start | bytes 589832 | tf_op jit(solution)/shard_map/ppermute | solution.py:355
  13.0 1.2 collective-permute-start.8
  14.4 0.7 pad_maximum_fusion.2
  15.0 0.8 collective-permute-start.14
  15.8 6.3 %collective-permute-done.7.refs_6_ = bf16[256,384]{1,0:T(8,128)(2,1)S(1)} collective-permute-done((bf16[256,384]{1,0:T(8,128)(2,1)S(1)}, bf16[256,384]{1,0:T(8,128)(2,1)S(1)}, u32[]{:S(2)}, u32[]{:S(2)}) %collective-permute-start.7) | collective-permute-done | bytes 196640 | tf_op jit(solution)/shard_map/ppermute | solution.py:355
  22.1 2.5 %collective-permute-start.3 = (bf16[256,1024]{1,0:T(8,128)(2,1)S(1)}, bf16[256,1024]{1,0:T(8,128)(2,1)S(1)}, u32[]{:S(2)}, u32[]{:S(2)}) collective-permute-start(bf16[256,1024]{1,0:T(8,128)(2,1)S(1)} %norm_tokens.1.refs_0_), channel_id=1, source_target_pairs={{0,1},{1,0},{2,3},{3,2},{4,5},{5,4},{6,7},{7,6},{8,9},{9,8},{10,11... | collective-permute-start | bytes 1572872 | tf_op jit(solution)/shard_map/ppermute | solution.py:355
  24.7 1.3 collective-permute-start.11
  26.0 1.7 %collective-permute-done.14 = bf16[512,128]{1,0:T(8,128)(2,1)} collective-permute-done((bf16[512,128]{1,0:T(8,128)(2,1)}, bf16[512,128]{1,0:T(8,128)(2,1)}, u32[]{:S(2)}, u32[]{:S(2)}) %collective-permute-start.14) | collective-permute-done | bytes 131104 | tf_op jit(solution)/shard_map/ppermute | solution.py:355
  27.7 0.9 pad_maximum_fusion.1.w_ref
  28.7 1.3 collective-permute-start.15
  29.9 1.0 collective-permute-done.10.refs_7_
  30.9 2.2 %collective-permute-start.12 = (bf16[256,384]{1,0:T(8,128)(2,1)S(1)}, bf16[256,384]{1,0:T(8,128)(2,1)S(1)}, u32[]{:S(2)}, u32[]{:S(2)}) collective-permute-start(bf16[256,384]{1,0:T(8,128)(2,1)S(1)} %collective-permute-done.10.refs_7_), channel_id=1, source_target_pairs={{0,16},{16,0},{1,17},{17,1},{2,18},{18,2},{3,19},{19,3},{4,20},{20... | collective-permute-start | bytes 589832 | tf_op jit(solution)/shard_map/ppermute | solution.py:355
  33.2 3.9 %collective-permute-done.15 = bf16[1024,128]{1,0:T(8,128)(2,1)S(1)} collective-permute-done((bf16[1024,128]{1,0:T(8,128)(2,1)S(1)}, bf16[1024,128]{1,0:T(8,128)(2,1)S(1)}, u32[]{:S(2)}, u32[]{:S(2)}) %collective-permute-start.15) | collective-permute-done | bytes 262176 | tf_op jit(solution)/shard_map/ppermute | solution.py:355
  37.5 3.0 %collective-permute-start.20 = (bf16[1024,256]{1,0:T(8,128)(2,1)S(1)}, bf16[1024,256]{1,0:T(8,128)(2,1)S(1)}, u32[]{:S(2)}, u32[]{:S(2)}) collective-permute-start(bf16[1024,256]{1,0:T(8,128)(2,1)S(1)} %pad_maximum_fusion.refs_4_), channel_id=1, source_target_pairs={{0,1},{1,0},{2,3},{3,2},{4,5},{5,4},{6,7},{7,6},{8,9},{9,8},{10,11... | collective-permute-start | bytes 1572872 | tf_op jit(solution)/shard_map/ppermute | solution.py:355
  40.5 0.8 collective-permute-done.12.refs_11_
  41.3 3.3 %project.1.p_ref = bf16[1024,768]{1,0:T(8,128)(2,1)S(1)} custom-call(s32[2]{0:T(128)S(1)} %pad_add_fusion.1.place_ref, bf16[256,1024]{1,0:T(8,128)(2,1)S(1)} %norm_tokens.1.refs_0_, bf16[256,1024]{1,0:T(8,128)(2,1)S(1)} %collective-permute-done.3.refs_1_, bf16[256,1024]{1,0:T(8,128)(2,1)S(1)} %collective-permute-done.4.refs_2_, ...), custom_call_target="tpu_custom_call" | custom-call | flops 1610612736 | bytes 6291456 | tf_op jit(solution)/shard_map/project/pallas_call | solution.py:153
  44.6 6.7 %attend.1 = (bf16[256,256]{1,0:T(8,128)(2,1)S(1)}, bf16[256,256]{1,0:T(8,128)(2,1)S(1)}, bf16[256,256]{1,0:T(8,128)(2,1)S(1)}, bf16[256,256]{1,0:T(8,128)(2,1)S(1)}) custom-call(bf16[1024,768]{1,0:T(8,128)(2,1)S(1)} %project.1.p_ref), custom_call_target="tpu_custom_call" | custom-call | flops 4294967296 | bytes 1572864 | tf_op jit(solution)/shard_map/attend/pallas_call | solution.py:192
  51.3 1.5 collective-permute-start.21
  53.3 1.6 %collective-permute-start.19 = (bf16[256,256]{1,0:T(8,128)(2,1)S(1)}, bf16[256,256]{1,0:T(8,128)(2,1)S(1)}, u32[]{:S(2)}, u32[]{:S(2)}) collective-permute-start(bf16[256,256]{1,0:T(8,128)(2,1)S(1)} %get-tuple-element.44), channel_id=1, source_target_pairs={{0,3},{1,2},{2,1},{3,0},{4,7},{5,6},{6,5},{7,4},{8,11},{9,10},{10,... | collective-permute-start | bytes 393224 | tf_op jit(solution)/shard_map/ppermute | solution.py:355
  55.0 2.5 %collective-permute-done.18.refs_2_ = bf16[256,256]{1,0:T(8,128)(2,1)S(1)} collective-permute-done((bf16[256,256]{1,0:T(8,128)(2,1)S(1)}, bf16[256,256]{1,0:T(8,128)(2,1)S(1)}, u32[]{:S(2)}, u32[]{:S(2)}) %collective-permute-start.18) | collective-permute-done | bytes 131104 | tf_op jit(solution)/shard_map/ppermute | solution.py:355
  57.5 3.4 %collective-permute-done.19.refs_3_ = bf16[256,256]{1,0:T(8,128)(2,1)S(1)} collective-permute-done((bf16[256,256]{1,0:T(8,128)(2,1)S(1)}, bf16[256,256]{1,0:T(8,128)(2,1)S(1)}, u32[]{:S(2)}, u32[]{:S(2)}) %collective-permute-start.19) | collective-permute-done | bytes 131104 | tf_op jit(solution)/shard_map/ppermute | solution.py:355
  60.9 2.2 %out_projection.1 = (f32[256,1024]{1,0:T(8,128)S(1)}, bf16[640,1024]{1,0:T(8,128)(2,1)S(1)}) custom-call(s32[2]{0:T(128)S(1)} %pad_add_fusion.place_ref, bf16[256,1024]{1,0:T(8,128)(2,1)S(1)} %copy-done, bf16[640,256]{1,0:T(8,128)(2,1)S(1)} %copy-done.4, bf16[256,256]{1,0:T(8,128)(2,1)S(1)} %get-tuple-element.41.refs_0_, ...), custom_call_target="tpu_custom_call" | custom-call | flops 69793218560 | bytes 6291456 | tf_op jit(solution)/shard_map/out_projection/pallas_call | solution.py:237
  63.1 37.3 %all_to_all.10 = bf16[16,40,1024]{2,1,0:T(8,128)(2,1)S(1)} all-to-all(bf16[16,40,1024]{2,1,0:T(8,128)(2,1)S(1)} %bitcast.21), channel_id=1, replica_groups=mesh['groups'=2,'ctx'=16] {'ctx'}, dimensions={0} | all-to-all | bytes 2621440 | tf_op jit(solution)/shard_map/all_to_all | solution.py:443
  100.5 13.9 %experts.1 = bf16[640,1024]{1,0:T(8,128)(2,1)S(1)} custom-call(bf16[640,1024]{1,0:T(8,128)(2,1)S(1)} %bitcast.22, bf16[1024,8192]{1,0:T(8,128)(2,1)S(1)} %bitcast.25, bf16[8192,1024]{1,0:T(8,128)(2,1)} %wout_ref.1), custom_call_target="tpu_custom_call" | custom-call | flops 10737418240 | bytes 33554432 | tf_op jit(solution)/shard_map/experts/pallas_call | solution.py:317
  114.4 35.3 %all_to_all.11 = bf16[16,40,1024]{2,1,0:T(8,128)(2,1)S(1)} all-to-all(bf16[16,40,1024]{2,1,0:T(8,128)(2,1)S(1)} %bitcast.23), channel_id=1, replica_groups=mesh['groups'=2,'ctx'=16] {'ctx'}, dimensions={0} | all-to-all | bytes 2621440 | tf_op jit(solution)/shard_map/all_to_all | solution.py:446
  149.7 2.2 %combine.1 = bf16[256,1024]{1,0:T(8,128)(2,1)} custom-call(f32[256,1024]{1,0:T(8,128)S(1)} %get-tuple-element.46.r_ref, bf16[640,1024]{1,0:T(8,128)(2,1)S(1)} %bitcast.20, bf16[768,640]{1,0:T(8,128)(2,1)S(1)} %get-tuple-element.48.g_ref), custom_call_target="tpu_custom_call" | custom-call | flops 1006632960 | bytes 2883584 | tf_op jit(solution)/shard_map/combine/pallas_call | solution.py:344
  (59 shorter events, 2.5 us)
Async XLA Ops:
  0.0 4.2 %copy-start = (bf16[256,1024]{1,0:T(8,128)(2,1)S(1)}, bf16[256,1024]{1,0:T(8,128)(2,1)}, u32[]{:S(2)}) copy-start(bf16[256,1024]{1,0:T(8,128)(2,1)} %t_ref.1) | copy-start | bytes 1572868
  0.0 4.5 %copy-start.1 = (s32[256,2]{0,1:T(2,128)S(1)}, s32[256,2]{0,1:T(2,128)}, u32[]{:S(2)}) copy-start(s32[256,2]{0,1:T(2,128)} %param.8) | copy-start | bytes 6148
  0.0 4.5 %copy-start.2 = (f32[256,2]{0,1:T(2,128)S(1)}, f32[256,2]{0,1:T(2,128)}, u32[]{:S(2)}) copy-start(f32[256,2]{0,1:T(2,128)} %param.9) | copy-start | bytes 6148
  1.2 3.9 %collective-permute-start = (bf16[64,512]{1,0:T(8,128)(2,1)S(1)}, bf16[64,512]{1,0:T(8,128)(2,1)S(1)}, u32[]{:S(2)}, u32[]{:S(2)}) collective-permute-start(bf16[64,512]{1,0:T(8,128)(2,1)S(1)} %pad_maximum_fusion.3), channel_id=1, source_target_pairs={{0,1},{1,0},{2,3},{3,2},{4,5},{5,4},{6,7},{7,6},{8,9},{9,8},{10,11... | collective-permute-start | bytes 196616 | tf_op jit(solution)/shard_map/ppermute | solution.py:355
  1.3 5.2 %collective-permute-start.1 = (bf16[64,512]{1,0:T(8,128)(2,1)S(1)}, bf16[64,512]{1,0:T(8,128)(2,1)S(1)}, u32[]{:S(2)}, u32[]{:S(2)}) collective-permute-start(bf16[64,512]{1,0:T(8,128)(2,1)S(1)} %pad_maximum_fusion.4), channel_id=1, source_target_pairs={{0,2},{1,3},{2,0},{3,1},{4,6},{5,7},{6,4},{7,5},{8,10},{9,11},{10,... | collective-permute-start | bytes 196616 | tf_op jit(solution)/shard_map/ppermute | solution.py:355
  4.1 4.1 %collective-permute-start.2 = (bf16[64,512]{1,0:T(8,128)(2,1)S(1)}, bf16[64,512]{1,0:T(8,128)(2,1)S(1)}, u32[]{:S(2)}, u32[]{:S(2)}) collective-permute-start(bf16[64,512]{1,0:T(8,128)(2,1)S(1)} %pad_maximum_fusion.5), channel_id=1, source_target_pairs={{0,3},{1,2},{2,1},{3,0},{4,7},{5,6},{6,5},{7,4},{8,11},{9,10},{10,... | collective-permute-start | bytes 196616 | tf_op jit(solution)/shard_map/ppermute | solution.py:355
  5.0 19.6 %copy-start.3 = (bf16[640,256]{1,0:T(8,128)(2,1)}, bf16[640,256]{1,0:T(8,128)(2,1)S(1)}, u32[]{:S(2)}) copy-start(bf16[640,256]{1,0:T(8,128)(2,1)S(1)} %get-tuple-element.29.d_ref) | copy-start | bytes 983044
  8.2 16.4 %collective-permute-start.4 = (bf16[256,1024]{1,0:T(8,128)(2,1)S(1)}, bf16[256,1024]{1,0:T(8,128)(2,1)S(1)}, u32[]{:S(2)}, u32[]{:S(2)}) collective-permute-start(bf16[256,1024]{1,0:T(8,128)(2,1)S(1)} %norm_tokens.1.refs_0_), channel_id=1, source_target_pairs={{0,2},{1,3},{2,0},{3,1},{4,6},{5,7},{6,4},{7,5},{8,10},{9,11},{10,... | collective-permute-start | bytes 1572872 | tf_op jit(solution)/shard_map/ppermute | solution.py:355
  9.4 5.0 %collective-permute-start.13 = (bf16[256,128]{1,0:T(8,128)(2,1)S(1)}, bf16[256,128]{1,0:T(8,128)(2,1)S(1)}, u32[]{:S(2)}, u32[]{:S(2)}) collective-permute-start(bf16[256,128]{1,0:T(8,128)(2,1)S(1)} %slice.9), channel_id=1, source_target_pairs={{0,4},{1,5},{2,6},{3,7},{4,0},{5,1},{6,2},{7,3},{8,12},{9,13},{10,... | collective-permute-start | bytes 196616 | tf_op jit(solution)/shard_map/ppermute | solution.py:355
  10.7 11.4 %collective-permute-start.7 = (bf16[256,384]{1,0:T(8,128)(2,1)S(1)}, bf16[256,384]{1,0:T(8,128)(2,1)S(1)}, u32[]{:S(2)}, u32[]{:S(2)}) collective-permute-start(bf16[256,384]{1,0:T(8,128)(2,1)S(1)} %slice.8.refs_4_), channel_id=1, source_target_pairs={{0,8},{1,9},{2,10},{3,11},{4,12},{5,13},{6,14},{7,15},{8,0},{9,1},... | collective-permute-start | bytes 589832 | tf_op jit(solution)/shard_map/ppermute | solution.py:355
  13.0 11.7 %collective-permute-start.8 = (bf16[256,384]{1,0:T(8,128)(2,1)S(1)}, bf16[256,384]{1,0:T(8,128)(2,1)}, u32[]{:S(2)}, u32[]{:S(2)}) collective-permute-start(bf16[256,384]{1,0:T(8,128)(2,1)S(1)} %slice.8.refs_4_), channel_id=1, source_target_pairs={{0,16},{1,17},{2,18},{3,19},{4,20},{5,21},{6,22},{7,23},{8,24},{9,... | collective-permute-start | bytes 589832 | tf_op jit(solution)/shard_map/ppermute | solution.py:355
  14.2 10.4 %collective-permute-start.9 = (bf16[256,384]{1,0:T(8,128)(2,1)S(1)}, bf16[256,384]{1,0:T(8,128)(2,1)}, u32[]{:S(2)}, u32[]{:S(2)}) collective-permute-start(bf16[256,384]{1,0:T(8,128)(2,1)S(1)} %slice.8.refs_4_), channel_id=1, source_target_pairs={{0,20},{1,21},{2,22},{3,23},{4,16},{5,17},{6,18},{7,19},{8,28},{9,... | collective-permute-start | bytes 589832 | tf_op jit(solution)/shard_map/ppermute | solution.py:355
  14.4 1.4 copy-start.5
  15.0 12.7 %collective-permute-start.14 = (bf16[512,128]{1,0:T(8,128)(2,1)}, bf16[512,128]{1,0:T(8,128)(2,1)}, u32[]{:S(2)}, u32[]{:S(2)}) collective-permute-start(bf16[512,128]{1,0:T(8,128)(2,1)} %pad_maximum_fusion.2), channel_id=1, source_target_pairs={{0,8},{1,9},{2,10},{3,11},{4,12},{5,13},{6,14},{7,15},{8,0},{9,1},... | collective-permute-start | bytes 393224 | tf_op jit(solution)/shard_map/ppermute | solution.py:355
  22.1 18.4 %collective-permute-start.3 = (bf16[256,1024]{1,0:T(8,128)(2,1)S(1)}, bf16[256,1024]{1,0:T(8,128)(2,1)S(1)}, u32[]{:S(2)}, u32[]{:S(2)}) collective-permute-start(bf16[256,1024]{1,0:T(8,128)(2,1)S(1)} %norm_tokens.1.refs_0_), channel_id=1, source_target_pairs={{0,1},{1,0},{2,3},{3,2},{4,5},{5,4},{6,7},{7,6},{8,9},{9,8},{10,11... | collective-permute-start | bytes 1572872 | tf_op jit(solution)/shard_map/ppermute | solution.py:355
  24.6 16.7 %collective-permute-start.5 = (bf16[256,1024]{1,0:T(8,128)(2,1)S(1)}, bf16[256,1024]{1,0:T(8,128)(2,1)}, u32[]{:S(2)}, u32[]{:S(2)}) collective-permute-start(bf16[256,1024]{1,0:T(8,128)(2,1)S(1)} %collective-permute-done.4.refs_2_), channel_id=1, source_target_pairs={{0,1},{1,0},{2,3},{3,2},{4,5},{5,4},{6,7},{7,6},{8,9},{9,8},{10,11... | collective-permute-start | bytes 1572872 | tf_op jit(solution)/shard_map/ppermute | solution.py:355
  24.7 6.2 %collective-permute-start.10 = (bf16[256,384]{1,0:T(8,128)(2,1)S(1)}, bf16[256,384]{1,0:T(8,128)(2,1)S(1)}, u32[]{:S(2)}, u32[]{:S(2)}) collective-permute-start(bf16[256,384]{1,0:T(8,128)(2,1)S(1)} %collective-permute-done.7.refs_6_), channel_id=1, source_target_pairs={{0,4},{1,5},{2,6},{3,7},{4,0},{5,1},{6,2},{7,3},{8,12},{9,13},{10,... | collective-permute-start | bytes 589832 | tf_op jit(solution)/shard_map/ppermute | solution.py:355
  24.7 6.2 %collective-permute-start.11 = (bf16[256,384]{1,0:T(8,128)(2,1)S(1)}, bf16[256,384]{1,0:T(8,128)(2,1)S(1)}, u32[]{:S(2)}, u32[]{:S(2)}) collective-permute-start(bf16[256,384]{1,0:T(8,128)(2,1)S(1)} %collective-permute-done.7.refs_6_), channel_id=1, source_target_pairs={{0,16},{16,0},{1,17},{17,1},{2,18},{18,2},{3,19},{19,3},{4,20},{20... | collective-permute-start | bytes 589832 | tf_op jit(solution)/shard_map/ppermute | solution.py:355
  28.7 8.4 %collective-permute-start.15 = (bf16[1024,128]{1,0:T(8,128)(2,1)S(1)}, bf16[1024,128]{1,0:T(8,128)(2,1)S(1)}, u32[]{:S(2)}, u32[]{:S(2)}) collective-permute-start(bf16[1024,128]{1,0:T(8,128)(2,1)S(1)} %out_weight_part.1), channel_id=1, source_target_pairs={{0,16},{16,0},{1,17},{17,1},{2,18},{18,2},{3,19},{19,3},{4,20},{20... | collective-permute-start | bytes 786440 | tf_op jit(solution)/shard_map/ppermute | solution.py:355
  30.9 6.6 %collective-permute-start.6 = (bf16[256,384]{1,0:T(8,128)(2,1)S(1)}, bf16[256,384]{1,0:T(8,128)(2,1)S(1)}, u32[]{:S(2)}, u32[]{:S(2)}) collective-permute-start(bf16[256,384]{1,0:T(8,128)(2,1)S(1)} %slice.8.refs_4_), channel_id=1, source_target_pairs={{0,4},{1,5},{2,6},{3,7},{4,0},{5,1},{6,2},{7,3},{8,12},{9,13},{10,... | collective-permute-start | bytes 589832 | tf_op jit(solution)/shard_map/ppermute | solution.py:355
  30.9 10.4 %collective-permute-start.12 = (bf16[256,384]{1,0:T(8,128)(2,1)S(1)}, bf16[256,384]{1,0:T(8,128)(2,1)S(1)}, u32[]{:S(2)}, u32[]{:S(2)}) collective-permute-start(bf16[256,384]{1,0:T(8,128)(2,1)S(1)} %collective-permute-done.10.refs_7_), channel_id=1, source_target_pairs={{0,16},{16,0},{1,17},{17,1},{2,18},{18,2},{3,19},{19,3},{4,20},{20... | collective-permute-start | bytes 589832 | tf_op jit(solution)/shard_map/ppermute | solution.py:355
  37.1 14.1 %collective-permute-start.16 = (bf16[1024,256]{1,0:T(8,128)(2,1)S(1)}, bf16[1024,256]{1,0:T(8,128)(2,1)S(1)}, u32[]{:S(2)}, u32[]{:S(2)}) collective-permute-start(bf16[1024,256]{1,0:T(8,128)(2,1)S(1)} %pad_maximum_fusion.refs_4_), channel_id=1, source_target_pairs={{0,2},{1,3},{2,0},{3,1},{4,6},{5,7},{6,4},{7,5},{8,10},{9,11},{10,... | collective-permute-start | bytes 1572872 | tf_op jit(solution)/shard_map/ppermute | solution.py:355
  37.5 17.5 %collective-permute-start.20 = (bf16[1024,256]{1,0:T(8,128)(2,1)S(1)}, bf16[1024,256]{1,0:T(8,128)(2,1)S(1)}, u32[]{:S(2)}, u32[]{:S(2)}) collective-permute-start(bf16[1024,256]{1,0:T(8,128)(2,1)S(1)} %pad_maximum_fusion.refs_4_), channel_id=1, source_target_pairs={{0,1},{1,0},{2,3},{3,2},{4,5},{5,4},{6,7},{7,6},{8,9},{9,8},{10,11... | collective-permute-start | bytes 1572872 | tf_op jit(solution)/shard_map/ppermute | solution.py:355
  44.6 16.3 %copy-start.4 = (bf16[640,256]{1,0:T(8,128)(2,1)S(1)}, bf16[640,256]{1,0:T(8,128)(2,1)}, u32[]{:S(2)}) copy-start(bf16[640,256]{1,0:T(8,128)(2,1)} %copy-done.3) | copy-start | bytes 983044
  44.6 55.9 %slice-start = ((s8[16777216]{0:T(1024)(128)(4,1)}), s8[4194304]{0:T(1024)(128)(4,1)S(1)}, s32[]{:S(2)}) async-start(s8[16777216]{0:T(1024)(128)(4,1)} %bitcast.24), calls=%async_computation.2 | async-start | bytes 8388608
  51.3 9.6 %collective-permute-start.21 = (bf16[1024,256]{1,0:T(8,128)(2,1)S(1)}, bf16[1024,256]{1,0:T(8,128)(2,1)S(1)}, u32[]{:S(2)}, u32[]{:S(2)}) collective-permute-start(bf16[1024,256]{1,0:T(8,128)(2,1)S(1)} %collective-permute-done.16.refs_6_), channel_id=1, source_target_pairs={{0,1},{1,0},{2,3},{3,2},{4,5},{5,4},{6,7},{7,6},{8,9},{9,8},{10,11... | collective-permute-start | bytes 1572872 | tf_op jit(solution)/shard_map/ppermute | solution.py:355
  52.8 2.2 %collective-permute-start.17 = (bf16[256,256]{1,0:T(8,128)(2,1)S(1)}, bf16[256,256]{1,0:T(8,128)(2,1)S(1)}, u32[]{:S(2)}, u32[]{:S(2)}) collective-permute-start(bf16[256,256]{1,0:T(8,128)(2,1)S(1)} %get-tuple-element.42), channel_id=1, source_target_pairs={{0,1},{1,0},{2,3},{3,2},{4,5},{5,4},{6,7},{7,6},{8,9},{9,8},{10,11... | collective-permute-start | bytes 393224 | tf_op jit(solution)/shard_map/ppermute | solution.py:355
  52.8 4.6 %collective-permute-start.18 = (bf16[256,256]{1,0:T(8,128)(2,1)S(1)}, bf16[256,256]{1,0:T(8,128)(2,1)S(1)}, u32[]{:S(2)}, u32[]{:S(2)}) collective-permute-start(bf16[256,256]{1,0:T(8,128)(2,1)S(1)} %get-tuple-element.43), channel_id=1, source_target_pairs={{0,2},{1,3},{2,0},{3,1},{4,6},{5,7},{6,4},{7,5},{8,10},{9,11},{10,... | collective-permute-start | bytes 393224 | tf_op jit(solution)/shard_map/ppermute | solution.py:355
  53.3 7.6 %collective-permute-start.19 = (bf16[256,256]{1,0:T(8,128)(2,1)S(1)}, bf16[256,256]{1,0:T(8,128)(2,1)S(1)}, u32[]{:S(2)}, u32[]{:S(2)}) collective-permute-start(bf16[256,256]{1,0:T(8,128)(2,1)S(1)} %get-tuple-element.44), channel_id=1, source_target_pairs={{0,3},{1,2},{2,1},{3,0},{4,7},{5,6},{6,5},{7,4},{8,11},{9,10},{10,... | collective-permute-start | bytes 393224 | tf_op jit(solution)/shard_map/ppermute | solution.py:355
  55.0 45.5 %slice-start.1 = ((s8[16777216]{0:T(1024)(128)(4,1)}), s8[4194304]{0:T(1024)(128)(4,1)S(1)}, s32[]{:S(2)}) async-start(s8[16777216]{0:T(1024)(128)(4,1)} %bitcast.24), calls=%async_computation.3 | async-start | bytes 8388608
  55.0 45.5 %slice-start.2 = ((s8[16777216]{0:T(1024)(128)(4,1)}), s8[4194304]{0:T(1024)(128)(4,1)S(1)}, s32[]{:S(2)}) async-start(s8[16777216]{0:T(1024)(128)(4,1)} %bitcast.24), calls=%async_computation.4 | async-start | bytes 8388608
  55.0 45.5 %slice-start.3 = ((s8[16777216]{0:T(1024)(128)(4,1)}), s8[4194304]{0:T(1024)(128)(4,1)S(1)}, s32[]{:S(2)}) async-start(s8[16777216]{0:T(1024)(128)(4,1)} %bitcast.24), calls=%async_computation.5 | async-start | bytes 8388608
